TPU v7x, 32 devices: a whole 2x2x4 slice. The times are simulated.
32 devices in a mesh: dp: 8 (over y, x, core), mp: 4 (over z).
Axes of the slice: x: 2, y: 2, z: 4, core: 2. Of those that a mesh axis runs over, the one named last changes fastest.
Arguments:
- x_long: bfloat16 [8, 1024, 768], P('dp', 'mp'), may hold values from -6 to 6
- x_short: bfloat16 [8, 512, 768], P('dp', 'mp'), may hold values from -6 to 6
- dy_long: bfloat16 [8, 1024, 768], P('dp', 'mp'), may hold values from -6 to 6
- dy_short: bfloat16 [8, 512, 768], P('dp', 'mp'), may hold values from -6 to 6
- ln_gain: bfloat16 [2, 2, 768], replicated, may hold values from 0.5 to 1.5
- ln_bias: bfloat16 [2, 2, 768], replicated, may hold values from -1 to 1
- w_qkv: bfloat16 [2, 768, 3, 768], P(None, None, None, 'mp'), may hold values from -0.21875 to 0.21875
- b_qv: bfloat16 [2, 2, 768], P(None, None, 'mp'), may hold values from -1.5 to 1.5
- w_out: bfloat16 [2, 768, 768], P(None, 'mp'), may hold values from -0.4375 to 0.4375
- b_out: bfloat16 [2, 768], replicated, may hold values from -1 to 1
- w_up: bfloat16 [2, 768, 3072], P(None, None, 'mp'), may hold values from -0.21875 to 0.21875
- b_up: bfloat16 [2, 3072], P(None, 'mp'), may hold values from -1.5 to 1.5
- w_down: bfloat16 [2, 3072, 768], P(None, 'mp'), may hold values from -0.109375 to 0.109375
- b_down: bfloat16 [2, 768], replicated, may hold values from -1 to 1
- threshold: int32 [2], replicated, may hold values from 16 to 79
Outputs:
- y_long: bfloat16 [8, 1024, 768], P('dp', 'mp')
- y_short: bfloat16 [8, 512, 768], P('dp', 'mp')
- dx_long: float32 [8, 1024, 768], P('dp', 'mp')
- dx_short: float32 [8, 512, 768], P('dp', 'mp')
- g_ln_gain: float32 [2, 2, 768], replicated
- g_ln_bias: float32 [2, 2, 768], replicated
- g_w_qkv: float32 [2, 768, 3, 768], P(None, 'dp', None, 'mp')
- g_b_qv: float32 [2, 2, 768], P(None, None, 'mp')
- g_w_out: float32 [2, 768, 768], P(None, 'mp', 'dp')
- g_b_out: float32 [2, 768], replicated
- g_w_up: float32 [2, 768, 3072], P(None, 'dp', 'mp')
- g_b_up: float32 [2, 3072], P(None, 'mp')
- g_w_down: float32 [2, 3072, 768], P(None, 'mp', 'dp')
- g_b_down: float32 [2, 768], replicated
- key_share: float32 [2], replicated
All inputs are finite; a program needn't handle non-finite values.
Results may differ from a plain program's by a relative error of at most 0.03.
Values may be sent and summed in bfloat16 or wider, within the bound.
A program may use at most 192 MiB of HBM per device.

v0:
```python
import math

import jax
import jax.numpy as jnp
from jax import lax
from jax.sharding import PartitionSpec as P

HEAD_DIM = 64


HIGHEST_PRECISION = lax.Precision.HIGHEST
norm_eps = 1e-05


def for_sending(x):

    def short(part):
        return part.astype(jnp.bfloat16) if part.dtype == jnp.float32 else part

    return jax.tree.map(short, x)


def spread(value, axis, source):
    kept = jnp.where(lax.axis_index(axis) == source, value, 0).astype(value.dtype)
    return lax.psum(kept, axis)


def layer_norm(resid, norm_gain, norm_shift):
    average = jnp.mean(resid, axis=-1, keepdims=True)
    centred = resid - average
    variance = jnp.mean(centred * centred, axis=-1, keepdims=True)
    return centred * lax.rsqrt(variance + norm_eps) * norm_gain + norm_shift


def gelu_tanh(upper):
    return jax.nn.gelu(upper, approximate=True)


def gather_rows(pieces):
    return (
        lax.all_gather(pieces[0], "mp", axis=1, tiled=True),
        lax.all_gather(pieces[1], "mp", axis=1, tiled=True),
    )


def scatter_rows(pieces):
    return (
        lax.psum_scatter(
            pieces[0].astype(jnp.bfloat16), "mp", scatter_dimension=1, tiled=True
        ).astype(jnp.float32),
        lax.psum_scatter(
            pieces[1].astype(jnp.bfloat16), "mp", scatter_dimension=1, tiled=True
        ).astype(jnp.float32),
    )


def gather_grads(pieces):
    return (
        lax.all_gather(pieces[0], "mp", axis=1, tiled=True),
        lax.all_gather(pieces[1], "mp", axis=1, tiled=True),
    )


def scatter_grads(pieces):
    return (
        lax.psum_scatter(
            pieces[0].astype(jnp.bfloat16), "mp", scatter_dimension=1, tiled=True
        ).astype(jnp.float32),
        lax.psum_scatter(
            pieces[1].astype(jnp.bfloat16), "mp", scatter_dimension=1, tiled=True
        ).astype(jnp.float32),
    )


def block_logits(
    query_blk, sel_blk, keys_all, sel_key, sel_start, row_start, lower_tri, score_scale
):
    seq_len = keys_all.shape[1]
    block_rows = query_blk.shape[1]
    row_ids = row_start + lax.broadcasted_iota(jnp.int32, (block_rows, seq_len), 0)
    col_ids = lax.broadcasted_iota(jnp.int32, (block_rows, seq_len), 1)
    sel_score = (
        jnp.einsum("nid,njd->nij", sel_blk, sel_key, preferred_element_type=jnp.float32)
        * score_scale
    )
    chosen = jnp.logical_and(col_ids >= 1, row_ids > col_ids)
    select = jnp.where(chosen, jax.nn.softplus(sel_score), 0.0)
    penalty = sel_start[:, None, :] + jnp.einsum(
        "ik,nkj->nij", lower_tri, select, precision=HIGHEST_PRECISION
    )
    scores = (
        jnp.einsum("nihd,njhd->nhij", query_blk, keys_all, preferred_element_type=jnp.float32)
        * score_scale
    )
    logits = jnp.where(row_ids >= col_ids, scores - penalty[:, None], -jnp.inf)
    return (sel_score, chosen, select, logits)


def triangles(block_rows):
    first = lax.broadcasted_iota(jnp.int32, (block_rows, block_rows), 0)
    second = lax.broadcasted_iota(jnp.int32, (block_rows, block_rows), 1)
    return ((first > second).astype(jnp.float32), (second > first).astype(jnp.float32))


def attend_forward(queries, keys_all, values, sel_query, sel_key):
    seq_count, seq_len, local_heads, head_size = queries.shape
    block_rows = min(512, seq_len // 2)
    score_scale = 1.0 / math.sqrt(head_size)
    lower_tri, upper_tri = triangles(block_rows)
    sel_carry = jnp.zeros((seq_count, seq_len), jnp.float32)
    starts, outputs, log_norms = ([], [], [])
    for row_start in range(0, seq_len, block_rows):
        starts.append(sel_carry)
        query_blk = queries[:, row_start : row_start + block_rows]
        sel_blk = sel_query[:, row_start : row_start + block_rows]
        sel_score, chosen, select, logits = block_logits(
            query_blk, sel_blk, keys_all, sel_key, sel_carry, row_start, lower_tri, score_scale
        )
        row_max = jnp.max(logits, axis=-1, keepdims=True)
        exp_terms = jnp.exp(logits - row_max)
        row_sum = jnp.sum(exp_terms, axis=-1, keepdims=True)
        weights_blk = (exp_terms / row_sum).astype(jnp.bfloat16)
        outputs.append(
            jnp.einsum("nhij,njhd->nihd", weights_blk, values, preferred_element_type=jnp.float32)
        )
        log_norms.append(row_max + jnp.log(row_sum))
        sel_carry = sel_carry + jnp.sum(select, axis=1)
    return (jnp.concatenate(outputs, axis=1), starts, log_norms, sel_carry)


def attend_backward(queries, keys_all, values, sel_query, sel_key, grad_out, starts, log_norms):
    seq_count, seq_len, local_heads, head_size = queries.shape
    block_rows = min(512, seq_len // 2)
    score_scale = 1.0 / math.sqrt(head_size)
    lower_tri, upper_tri = triangles(block_rows)
    grad_keys = jnp.zeros(queries.shape, jnp.float32)
    grad_values = jnp.zeros(queries.shape, jnp.float32)
    grad_sel_key = jnp.zeros(sel_key.shape, jnp.float32)
    later_sum = jnp.zeros((seq_count, seq_len), jnp.float32)
    sel_key_wide = sel_key.astype(jnp.float32)
    query_parts, sel_query_parts = ([], [])
    block_count = seq_len // block_rows
    for index in reversed(range(block_count)):
        row_start = index * block_rows
        query_blk = queries[:, row_start : row_start + block_rows]
        sel_blk = sel_query[:, row_start : row_start + block_rows]
        grad_blk = grad_out[:, row_start : row_start + block_rows]
        sel_score, chosen, select, logits = block_logits(
            query_blk, sel_blk, keys_all, sel_key, starts[index], row_start, lower_tri, score_scale
        )
        probs = jnp.exp(logits - log_norms[index])
        grad_probs = jnp.einsum(
            "nihd,njhd->nhij", grad_blk, values, preferred_element_type=jnp.float32
        )
        row_delta = jnp.sum(probs * grad_probs, axis=-1, keepdims=True)
        grad_scores = probs * (grad_probs - row_delta)
        grad_low = grad_scores.astype(jnp.bfloat16)
        query_parts.append(
            jnp.einsum("nhij,njhd->nihd", grad_low, keys_all, preferred_element_type=jnp.float32)
            * score_scale
        )
        grad_keys = (
            grad_keys
            + jnp.einsum("nhij,nihd->njhd", grad_low, query_blk, preferred_element_type=jnp.float32)
            * score_scale
        )
        grad_values = grad_values + jnp.einsum(
            "nhij,nihd->njhd",
            probs.astype(jnp.bfloat16),
            grad_blk,
            preferred_element_type=jnp.float32,
        )
        head_sum = jnp.sum(grad_scores, axis=1)
        grad_select = -(
            later_sum[:, None, :]
            + jnp.einsum("ki,nij->nkj", upper_tri, head_sum, precision=HIGHEST_PRECISION)
        )
        later_sum = later_sum + jnp.sum(head_sum, axis=1)
        grad_sel = jnp.where(chosen, grad_select * jax.nn.sigmoid(sel_score), 0.0)
        sel_query_parts.append(
            jnp.einsum("nij,njd->nid", grad_sel, sel_key_wide, precision=HIGHEST_PRECISION)
            * score_scale
        )
        grad_sel_key = (
            grad_sel_key
            + jnp.einsum(
                "nij,nid->njd", grad_sel, sel_blk.astype(jnp.float32), precision=HIGHEST_PRECISION
            )
            * score_scale
        )
    grad_queries = jnp.concatenate(query_parts[::-1], axis=1)
    grad_sel_query = jnp.concatenate(sel_query_parts[::-1], axis=1)
    return (grad_queries, grad_keys, grad_values, grad_sel_query, grad_sel_key)


def selection_inputs(queries, keys_all):
    packed = tuple(
        (
            jnp.concatenate([query_grp[:, :, 0], key_grp[:, :, 0]], axis=-1)
            for query_grp, key_grp in zip(queries, keys_all)
        )
    )
    arrived = jax.tree.map(
        lambda part, own: part.astype(own.dtype),
        jax.tree.map(lambda part: spread(part, "mp", 0), for_sending(packed)),
        packed,
    )
    return [
        (arrived_part[..., :HEAD_DIM], arrived_part[..., HEAD_DIM:]) for arrived_part in arrived
    ]


def layer_forward(resids, layer_params, limit_value):
    norm_gain, norm_shift, w_qkv_l, b_qv_l, w_out_l, b_out_l, w_up_l, b_up_l, w_down_l, b_down_l = (
        layer_params
    )
    gain_wide = norm_gain.astype(jnp.float32)
    shift_wide = norm_shift.astype(jnp.float32)
    bias_wide = b_qv_l.astype(jnp.float32)
    normed1 = tuple(
        (layer_norm(resid, gain_wide[0], shift_wide[0]).astype(jnp.bfloat16) for resid in resids)
    )
    full1 = gather_rows(normed1)
    queries, keys_all, values = ([], [], [])
    for normed in full1:
        projected = jnp.einsum("ntd,dce->ntce", normed, w_qkv_l, preferred_element_type=jnp.float32)
        head_shape = (normed.shape[0], normed.shape[1], projected.shape[-1] // HEAD_DIM, HEAD_DIM)
        queries.append((projected[:, :, 0] + bias_wide[0]).astype(jnp.bfloat16).reshape(head_shape))
        keys_all.append(projected[:, :, 1].astype(jnp.bfloat16).reshape(head_shape))
        values.append((projected[:, :, 2] + bias_wide[1]).astype(jnp.bfloat16).reshape(head_shape))
    selected = selection_inputs(queries, keys_all)
    attended, records, partials = ([], [], [])
    share_sum = jnp.zeros((), jnp.float32)
    for index in range(2):
        outputs, starts, log_norms, sel_sums = attend_forward(
            queries[index], keys_all[index], values[index], selected[index][0], selected[index][1]
        )
        seq_count, seq_len = (outputs.shape[0], outputs.shape[1])
        flat_out = outputs.astype(jnp.bfloat16).reshape(seq_count, seq_len, -1)
        attended.append(flat_out)
        records.append((starts, log_norms))
        partials.append(
            jnp.einsum("nte,ed->ntd", flat_out, w_out_l, preferred_element_type=jnp.float32)
        )
        later_rows = (seq_len - 1 - lax.broadcasted_iota(jnp.int32, (seq_len,), 0)).astype(
            jnp.float32
        )
        share_sum = share_sum + jnp.sum(
            jax.nn.sigmoid(4.0 * (sel_sums / jnp.maximum(later_rows, 1.0) - limit_value))
        )
    branch1 = scatter_rows(tuple(partials))
    middles = tuple(
        (resid + branch + b_out_l.astype(jnp.float32) for resid, branch in zip(resids, branch1))
    )
    normed2 = tuple(
        (layer_norm(middle, gain_wide[1], shift_wide[1]).astype(jnp.bfloat16) for middle in middles)
    )
    full2 = gather_rows(normed2)
    uppers, actives, partials2 = ([], [], [])
    for normed in full2:
        upper = jnp.einsum(
            "ntd,df->ntf", normed, w_up_l, preferred_element_type=jnp.float32
        ) + b_up_l.astype(jnp.float32)
        active = gelu_tanh(upper).astype(jnp.bfloat16)
        uppers.append(upper)
        actives.append(active)
        partials2.append(
            jnp.einsum("ntf,fd->ntd", active, w_down_l, preferred_element_type=jnp.float32)
        )
    branch2 = scatter_rows(tuple(partials2))
    news = tuple(
        (middle + branch + b_down_l.astype(jnp.float32) for middle, branch in zip(middles, branch2))
    )
    saved = (
        resids,
        middles,
        full1,
        queries,
        keys_all,
        values,
        selected,
        records,
        attended,
        full2,
        uppers,
        actives,
    )
    return (news, saved, share_sum)


def layer_backward(grads, saved, layer_params):
    norm_gain, norm_shift, w_qkv_l, b_qv_l, w_out_l, b_out_l, w_up_l, b_up_l, w_down_l, b_down_l = (
        layer_params
    )
    (
        resids,
        middles,
        full1,
        queries,
        keys_all,
        values,
        selected,
        records,
        attended,
        full2,
        uppers,
        actives,
    ) = saved
    gain_wide = norm_gain.astype(jnp.float32)
    shift_wide = norm_shift.astype(jnp.float32)
    g_bdown = sum((jnp.sum(grad_rows, axis=(0, 1)) for grad_rows in grads))
    full_grads = gather_grads(tuple((grad_rows.astype(jnp.bfloat16) for grad_rows in grads)))
    g_wdown = sum(
        (
            jnp.einsum("ntf,ntd->fd", active, grad_full, preferred_element_type=jnp.float32)
            for active, grad_full in zip(actives, full_grads)
        )
    )
    grad_uppers = []
    for upper, grad_full in zip(uppers, full_grads):
        grad_active = jnp.einsum(
            "ntd,fd->ntf", grad_full, w_down_l, preferred_element_type=jnp.float32
        )
        grad_uppers.append(jax.vjp(gelu_tanh, upper)[1](grad_active)[0].astype(jnp.bfloat16))
    g_bup = sum(
        (jnp.sum(grad_upper.astype(jnp.float32), axis=(0, 1)) for grad_upper in grad_uppers)
    )
    g_wup = sum(
        (
            jnp.einsum("ntd,ntf->df", normed, grad_upper, preferred_element_type=jnp.float32)
            for normed, grad_upper in zip(full2, grad_uppers)
        )
    )
    grad_norm2 = scatter_grads(
        tuple(
            (
                jnp.einsum("ntf,df->ntd", grad_upper, w_up_l, preferred_element_type=jnp.float32)
                for grad_upper in grad_uppers
            )
        )
    )
    grad_mids = []
    g_gain2 = jnp.zeros(gain_wide.shape[1:], jnp.float32)
    g_shift2 = jnp.zeros(gain_wide.shape[1:], jnp.float32)
    for middle, grad_norm, grad_rows in zip(middles, grad_norm2, grads):
        pulled = jax.vjp(layer_norm, middle, gain_wide[1], shift_wide[1])[1](grad_norm)
        grad_mids.append(grad_rows + pulled[0])
        g_gain2 = g_gain2 + pulled[1]
        g_shift2 = g_shift2 + pulled[2]
    g_bout = sum((jnp.sum(grad_mid, axis=(0, 1)) for grad_mid in grad_mids))
    full_mids = gather_grads(tuple((grad_mid.astype(jnp.bfloat16) for grad_mid in grad_mids)))
    g_wout = sum(
        (
            jnp.einsum("nte,ntd->ed", flat_out, grad_full, preferred_element_type=jnp.float32)
            for flat_out, grad_full in zip(attended, full_mids)
        )
    )
    pieces, sel_parts = ([], [])
    for index in range(2):
        grad_att = jnp.einsum(
            "ntd,ed->nte", full_mids[index], w_out_l, preferred_element_type=jnp.float32
        )
        grad_att = grad_att.astype(jnp.bfloat16).reshape(queries[index].shape)
        starts, log_norms = records[index]
        grad_q, grad_k, grad_v, grad_sq, grad_sk = attend_backward(
            queries[index],
            keys_all[index],
            values[index],
            selected[index][0],
            selected[index][1],
            grad_att,
            starts,
            log_norms,
        )
        pieces.append((grad_q, grad_k, grad_v))
        sel_parts.append(jnp.concatenate([grad_sq, grad_sk], axis=-1))
    sel_total = jax.tree.map(
        lambda part: part.astype(jnp.float32), lax.psum(for_sending(tuple(sel_parts)), "mp")
    )
    owner = lax.axis_index("mp") == 0
    g_wqkv = jnp.zeros(w_qkv_l.shape, jnp.float32)
    g_bq = jnp.zeros(b_qv_l.shape[1:], jnp.float32)
    g_bv = jnp.zeros(b_qv_l.shape[1:], jnp.float32)
    parts1 = []
    for index in range(2):
        grad_q, grad_k, grad_v = pieces[index]
        grad_q = grad_q.at[:, :, 0, :].add(jnp.where(owner, sel_total[index][..., :HEAD_DIM], 0.0))
        grad_k = grad_k.at[:, :, 0, :].add(jnp.where(owner, sel_total[index][..., HEAD_DIM:], 0.0))
        seq_count, seq_len = (grad_q.shape[0], grad_q.shape[1])
        packed = (
            jnp.stack([grad_q, grad_k, grad_v], axis=2)
            .reshape(seq_count, seq_len, 3, -1)
            .astype(jnp.bfloat16)
        )
        packed_wide = packed.astype(jnp.float32)
        g_bq = g_bq + jnp.sum(packed_wide[:, :, 0], axis=(0, 1))
        g_bv = g_bv + jnp.sum(packed_wide[:, :, 2], axis=(0, 1))
        g_wqkv = g_wqkv + jnp.einsum(
            "ntd,ntce->dce", full1[index], packed, preferred_element_type=jnp.float32
        )
        parts1.append(
            jnp.einsum("ntce,dce->ntd", packed, w_qkv_l, preferred_element_type=jnp.float32)
        )
    grad_norm1 = scatter_grads(tuple(parts1))
    new_grads = []
    g_gain1 = jnp.zeros(gain_wide.shape[1:], jnp.float32)
    g_shift1 = jnp.zeros(gain_wide.shape[1:], jnp.float32)
    for resid, grad_norm, grad_mid in zip(resids, grad_norm1, grad_mids):
        pulled = jax.vjp(layer_norm, resid, gain_wide[0], shift_wide[0])[1](grad_norm)
        new_grads.append(grad_mid + pulled[0])
        g_gain1 = g_gain1 + pulled[1]
        g_shift1 = g_shift1 + pulled[2]
    layer_grads = (
        jnp.stack([g_gain1, g_gain2]),
        jnp.stack([g_shift1, g_shift2]),
        g_wqkv,
        jnp.stack([g_bq, g_bv]),
        g_wout,
        g_bout,
        g_wup,
        g_bup,
        g_wdown,
        g_bdown,
    )
    return (tuple(new_grads), layer_grads)


def reduce_stacked(stacked):
    g_gain, g_shift, g_wqkv, g_bqv, g_wout, g_bout, g_wup, g_bup, g_wdown, g_bdown, shares = stacked
    g_wqkv, g_wout, g_wup, g_wdown = (
        lax.psum_scatter(g_wqkv, "dp", scatter_dimension=1, tiled=True),
        lax.psum_scatter(g_wout, "dp", scatter_dimension=2, tiled=True),
        lax.psum_scatter(g_wup, "dp", scatter_dimension=1, tiled=True),
        lax.psum_scatter(g_wdown, "dp", scatter_dimension=2, tiled=True),
    )
    g_gain, g_shift, g_bout, g_bdown = lax.psum((g_gain, g_shift, g_bout, g_bdown), ("dp", "mp"))
    shares, g_bqv, g_bup = lax.psum((shares, g_bqv, g_bup), "dp")
    return (g_gain, g_shift, g_wqkv, g_bqv, g_wout, g_bout, g_wup, g_bup, g_wdown, g_bdown, shares)


def body(
    x_long,
    x_short,
    dy_long,
    dy_short,
    ln_gain,
    ln_bias,
    w_qkv,
    b_qv,
    w_out,
    b_out,
    w_up,
    b_up,
    w_down,
    b_down,
    threshold,
):
    all_params = (ln_gain, ln_bias, w_qkv, b_qv, w_out, b_out, w_up, b_up, w_down, b_down)
    layer_count = w_qkv.shape[0]
    limits = threshold.astype(jnp.float32) / 64.0
    resids = (x_long.astype(jnp.float32), x_short.astype(jnp.float32))
    saved_all, shares = ([], [])
    for layer in range(layer_count):
        resids, saved, share_sum = layer_forward(
            resids, tuple((param[layer] for param in all_params)), limits[layer]
        )
        saved_all.append(saved)
        shares.append(share_sum)
    grads = (dy_long.astype(jnp.float32), dy_short.astype(jnp.float32))
    collected = [None] * layer_count
    for layer in reversed(range(layer_count)):
        grads, layer_grads = layer_backward(
            grads, saved_all[layer], tuple((param[layer] for param in all_params))
        )
        collected[layer] = layer_grads + (shares[layer],)
    stacked = tuple(
        (
            jnp.stack([collected[layer][member] for layer in range(layer_count)])
            for member in range(11)
        )
    )
    outputs = reduce_stacked(stacked)
    local_keys = x_long.shape[0] * x_long.shape[1] * lax.axis_size("mp") + x_short.shape[
        0
    ] * x_short.shape[1] * lax.axis_size("mp")
    total_keys = local_keys * lax.axis_size("dp")
    key_share = outputs[10] / total_keys
    return (
        resids[0].astype(jnp.bfloat16),
        resids[1].astype(jnp.bfloat16),
        grads[0],
        grads[1],
        outputs[0],
        outputs[1],
        outputs[2],
        outputs[3],
        outputs[4],
        outputs[5],
        outputs[6],
        outputs[7],
        outputs[8],
        outputs[9],
        key_share,
    )


def solution(mesh):
    in_specs = (
        P("dp", "mp", None),
        P("dp", "mp", None),
        P("dp", "mp", None),
        P("dp", "mp", None),
        P(),
        P(),
        P(None, None, None, "mp"),
        P(None, None, "mp"),
        P(None, "mp", None),
        P(),
        P(None, None, "mp"),
        P(None, "mp"),
        P(None, "mp", None),
        P(),
        P(),
    )
    out_specs = (
        P("dp", "mp", None),
        P("dp", "mp", None),
        P("dp", "mp", None),
        P("dp", "mp", None),
        P(),
        P(),
        P(None, "dp", None, "mp"),
        P(None, None, "mp"),
        P(None, "mp", "dp"),
        P(),
        P(None, "dp", "mp"),
        P(None, "mp"),
        P(None, "mp", "dp"),
        P(),
        P(),
    )
    return jax.shard_map(body, mesh=mesh, in_specs=in_specs, out_specs=out_specs, check_vma=False)
```

profile of v0, /device:TPU:1, one launch (start us, length us, event | category | flops | bytes accessed | tf_op | source)
XLA Modules:
  0.0 1434.5 jit_solution(14469124738378798430)
XLA Ops:
  18.0 26.6 %all_gather.52 = bf16[1,512,768]{2,1,0:T(8,128)(2,1)S(1)} all-gather(bf16[1,128,768]{2,1,0:T(8,128)(2,1)S(1)} %fusion.422), channel_id=1, replica_groups=mesh['dp'=8,'mp'=4] {'mp'}, dimensions={1}, use_global_device_ids=true | all-gather | bytes 983040 | tf_op jit(solution)/shard_map/all_gather | solution.py:42
  51.0 11.6 all-gather.9.cloned.1.call-done
  68.3 32.7 %all-reduce.21.cloned.1.call-done = (bf16[1,1024,128]{1,2,0:T(8,128)(2,1)}, bf16[1,512,128]{1,2,0:T(8,128)(2,1)}) async-done(((bf16[1,1024,128]{1,2,0:T(8,128)(2,1)}, bf16[1,512,128]{1,2,0:T(8,128)(2,1)}), (bf16[1,1024,128]{1,2,0:T(8,128)(2,1)}, bf16[1,512,128]{1,2,0:T(8,128)(2,1)})) %all-reduce.21.cloned.1.call-update) | async-done | bytes 393232 | tf_op jit(solution)/shard_map/psum | solution.py:25
  104.4 7.0 fusion.59
  150.4 23.3 %reduce-scatter.24.cloned.1.call-done = bf16[1,256,768]{2,1,0:T(8,128)(2,1)} async-done(((bf16[1,1024,768]{2,1,0:T(8,128)(2,1)}), bf16[1,256,768]{2,1,0:T(8,128)(2,1)}) %reduce-scatter.24.cloned.1.call-update) | async-done | bytes 393232 | tf_op jit(solution)/shard_map/reduce_scatter | solution.py:48
  178.9 18.8 %reduce-scatter.32.cloned.1.call-done = bf16[1,128,768]{2,1,0:T(8,128)(2,1)} async-done(((bf16[1,512,768]{2,1,0:T(8,128)(2,1)}), bf16[1,128,768]{2,1,0:T(8,128)(2,1)}) %reduce-scatter.32.cloned.1.call-update) | async-done | bytes 196624 | tf_op jit(solution)/shard_map/reduce_scatter | solution.py:51
  201.0 21.7 %all_gather.53 = bf16[1,512,768]{2,1,0:T(8,128)(2,1)S(1)} all-gather(bf16[1,128,768]{2,1,0:T(8,128)(2,1)S(1)} %add_convert_fusion.13), channel_id=1, replica_groups=mesh['dp'=8,'mp'=4] {'mp'}, dimensions={1}, use_global_device_ids=true | all-gather | bytes 983040 | tf_op jit(solution)/shard_map/all_gather | solution.py:42
  229.1 15.2 %all-gather.11.cloned.1.call-done = bf16[1,1024,768]{2,1,0:T(8,128)(2,1)} async-done(((bf16[1,256,768]{2,1,0:T(8,128)(2,1)}), bf16[1,1024,768]{2,1,0:T(8,128)(2,1)}) %all-gather.11.cloned.1.call-update) | async-done | bytes 1572880 | tf_op jit(solution)/shard_map/all_gather | solution.py:41
  254.5 14.2 reduce-scatter.34.cloned.1.call-done
  269.9 37.0 %reduce-scatter.26.cloned.1.call-done = bf16[1,256,768]{2,1,0:T(8,128)(2,1)} async-done(((bf16[1,1024,768]{2,1,0:T(8,128)(2,1)}), bf16[1,256,768]{2,1,0:T(8,128)(2,1)}) %reduce-scatter.26.cloned.1.call-update) | async-done | bytes 393232 | tf_op jit(solution)/shard_map/reduce_scatter | solution.py:48
  310.5 21.0 %all_gather.54 = bf16[1,512,768]{2,1,0:T(8,128)(2,1)S(1)} all-gather(bf16[1,128,768]{2,1,0:T(8,128)(2,1)S(1)} %add_convert_fusion.12), channel_id=1, replica_groups=mesh['dp'=8,'mp'=4] {'mp'}, dimensions={1}, use_global_device_ids=true | all-gather | bytes 983040 | tf_op jit(solution)/shard_map/all_gather | solution.py:42
  333.9 19.3 %all-gather.13.cloned.1.call-done = bf16[1,1024,768]{2,1,0:T(8,128)(2,1)} async-done(((bf16[1,256,768]{2,1,0:T(8,128)(2,1)}), bf16[1,1024,768]{2,1,0:T(8,128)(2,1)}) %all-gather.13.cloned.1.call-update) | async-done | bytes 1572880 | tf_op jit(solution)/shard_map/all_gather | solution.py:41
  358.0 33.5 %all-reduce.19.cloned.1.call-done = (bf16[1,1024,128]{1,2,0:T(8,128)(2,1)}, bf16[1,512,128]{1,2,0:T(8,128)(2,1)}) async-done(((bf16[1,1024,128]{1,2,0:T(8,128)(2,1)}, bf16[1,512,128]{1,2,0:T(8,128)(2,1)}), (bf16[1,1024,128]{1,2,0:T(8,128)(2,1)}, bf16[1,512,128]{1,2,0:T(8,128)(2,1)})) %all-reduce.19.cloned.1.call-update) | async-done | bytes 393232 | tf_op jit(solution)/shard_map/psum | solution.py:25
  396.7 7.7 fusion.508
  406.3 7.9 fusion.58
  442.6 24.4 %reduce-scatter.28.cloned.1.call-done = bf16[1,256,768]{2,1,0:T(8,128)(2,1)} async-done(((bf16[1,1024,768]{2,1,0:T(8,128)(2,1)}), bf16[1,256,768]{2,1,0:T(8,128)(2,1)}) %reduce-scatter.28.cloned.1.call-update) | async-done | bytes 393232 | tf_op jit(solution)/shard_map/reduce_scatter | solution.py:48
  471.6 28.0 %all_gather.60 = bf16[1,512,768]{2,1,0:T(8,128)(2,1)} all-gather(bf16[1,128,768]{2,1,0:T(8,128)(2,1)} %param.34), channel_id=1, replica_groups=mesh['dp'=8,'mp'=4] {'mp'}, dimensions={1}, use_global_device_ids=true | all-gather | bytes 983040 | tf_op jit(solution)/shard_map/all_gather | solution.py:60
  505.4 22.5 %all_gather.55 = bf16[1,512,768]{2,1,0:T(8,128)(2,1)S(1)} all-gather(bf16[1,128,768]{2,1,0:T(8,128)(2,1)S(1)} %add_convert_fusion.9), channel_id=1, replica_groups=mesh['dp'=8,'mp'=4] {'mp'}, dimensions={1}, use_global_device_ids=true | all-gather | bytes 983040 | tf_op jit(solution)/shard_map/all_gather | solution.py:42
  539.5 8.2 all-gather.15.cloned.1.call-done
  552.5 33.5 %all-gather.17.cloned.1.call-done = bf16[1,1024,768]{2,1,0:T(8,128)(2,1)} async-done(((bf16[1,256,768]{2,1,0:T(8,128)(2,1)}), bf16[1,1024,768]{2,1,0:T(8,128)(2,1)}) %all-gather.17.cloned.1.call-update) | async-done | bytes 1572880 | tf_op jit(solution)/shard_map/all_gather | solution.py:59
  586.0 6.5 convert_reduce_fusion
  596.3 5.5 fusion.129
  612.2 21.7 %reduce-scatter.38.cloned.1.call-done = bf16[1,128,768]{2,1,0:T(8,128)(2,1)} async-done(((bf16[1,512,768]{2,1,0:T(8,128)(2,1)}), bf16[1,128,768]{2,1,0:T(8,128)(2,1)}) %reduce-scatter.38.cloned.1.call-update) | async-done | bytes 196624 | tf_op jit(solution)/shard_map/reduce_scatter | solution.py:51
  637.8 24.5 %all_gather.61 = bf16[1,512,768]{2,1,0:T(8,128)(2,1)S(1)} all-gather(bf16[1,128,768]{2,1,0:T(8,128)(2,1)S(1)} %fusion.560), channel_id=1, replica_groups=mesh['dp'=8,'mp'=4] {'mp'}, dimensions={1}, use_global_device_ids=true | all-gather | bytes 983040 | tf_op jit(solution)/shard_map/all_gather | solution.py:60
  664.3 17.2 %reduce-scatter.40.cloned.1.call-done = bf16[1,256,768]{2,1,0:T(8,128)(2,1)} async-done(((bf16[1,1024,768]{2,1,0:T(8,128)(2,1)}), bf16[1,256,768]{2,1,0:T(8,128)(2,1)}) %reduce-scatter.40.cloned.1.call-update) | async-done | bytes 393232 | tf_op jit(solution)/shard_map/reduce_scatter | solution.py:66
  684.9 34.5 %reduce-scatter.30.cloned.1.call-done = bf16[1,256,768]{2,1,0:T(8,128)(2,1)} async-done(((bf16[1,1024,768]{2,1,0:T(8,128)(2,1)}), bf16[1,256,768]{2,1,0:T(8,128)(2,1)}) %reduce-scatter.30.cloned.1.call-update) | async-done | bytes 393232 | tf_op jit(solution)/shard_map/reduce_scatter | solution.py:48
  732.3 27.8 %all-gather.19.cloned.1.call-done = bf16[1,1024,768]{2,1,0:T(8,128)(2,1)} async-done(((bf16[1,256,768]{2,1,0:T(8,128)(2,1)}), bf16[1,1024,768]{2,1,0:T(8,128)(2,1)}) %all-gather.19.cloned.1.call-update) | async-done | bytes 1572880 | tf_op jit(solution)/shard_map/all_gather | solution.py:59
  801.8 27.6 %all-reduce.17.cloned.1.call-done = (bf16[1,1024,128]{1,2,0:T(8,128)(2,1)}, bf16[1,512,128]{1,2,0:T(8,128)(2,1)}) async-done(((bf16[1,1024,128]{1,2,0:T(8,128)(2,1)}, bf16[1,512,128]{1,2,0:T(8,128)(2,1)}), (bf16[1,1024,128]{1,2,0:T(8,128)(2,1)}, bf16[1,512,128]{1,2,0:T(8,128)(2,1)})) %all-reduce.17.cloned.1.call-update) | async-done | bytes 393232 | tf_op jit(solution)/shard_map/psum | solution.py:378
  846.2 28.3 %reduce-scatter.42.cloned.1.call-done = bf16[1,256,768]{2,1,0:T(8,128)(2,1)} async-done(((bf16[1,1024,768]{2,1,0:T(8,128)(2,1)}), bf16[1,256,768]{2,1,0:T(8,128)(2,1)}) %reduce-scatter.42.cloned.1.call-update) | async-done | bytes 393232 | tf_op jit(solution)/shard_map/reduce_scatter | solution.py:66
  882.6 15.5 %reduce-scatter.50.cloned.1.call-done = bf16[1,128,768]{2,1,0:T(8,128)(2,1)} async-done(((bf16[1,512,768]{2,1,0:T(8,128)(2,1)}), bf16[1,128,768]{2,1,0:T(8,128)(2,1)}) %reduce-scatter.50.cloned.1.call-update) | async-done | bytes 196624 | tf_op jit(solution)/shard_map/reduce_scatter | solution.py:69
  903.6 23.9 %all_gather.62 = bf16[1,512,768]{2,1,0:T(8,128)(2,1)S(1)} all-gather(bf16[1,128,768]{2,1,0:T(8,128)(2,1)S(1)} %convert_element_type.982), channel_id=1, replica_groups=mesh['dp'=8,'mp'=4] {'mp'}, dimensions={1}, use_global_device_ids=true | all-gather | bytes 983040 | tf_op jit(solution)/shard_map/all_gather | solution.py:60
  933.1 13.5 all-gather.21.cloned.1.call-done
  946.6 6.3 convert_reduce_fusion.1
  963.3 7.6 reduce-scatter.52.cloned.1.call-done
  976.4 28.2 %all_gather.63 = bf16[1,512,768]{2,1,0:T(8,128)(2,1)S(1)} all-gather(bf16[1,128,768]{2,1,0:T(8,128)(2,1)S(1)} %convert_element_type.987), channel_id=1, replica_groups=mesh['dp'=8,'mp'=4] {'mp'}, dimensions={1}, use_global_device_ids=true | all-gather | bytes 983040 | tf_op jit(solution)/shard_map/all_gather | solution.py:60
  1007.5 12.0 reduce-scatter.44.cloned.1.call-done
  1038.4 26.4 %all-gather.23.cloned.1.call-done = bf16[1,1024,768]{2,1,0:T(8,128)(2,1)} async-done(((bf16[1,256,768]{2,1,0:T(8,128)(2,1)}), bf16[1,1024,768]{2,1,0:T(8,128)(2,1)}) %all-gather.23.cloned.1.call-update) | async-done | bytes 1572880 | tf_op jit(solution)/shard_map/all_gather | solution.py:59
  1096.5 8.2 copy.64
  1162.6 6.9 copy.75
  1169.5 8.0 reshape.3820
  1200.4 15.5 %all-reduce.13.cloned.1.call-done = f32[2,768,768]{1,0,2:T(2,128)} async-done(((f32[2,768,768]{1,0,2:T(2,128)}), f32[2,768,768]{1,0,2:T(2,128)}) %all-reduce.13.cloned.1.call-update) | async-done | bytes 4718608
  1219.4 20.8 %all-reduce.2 = (f32[2,2,192]{2,1,0:T(2,128)}, f32[2,768]{1,0:T(2,128)}, f32[2]{0:T(128)S(1)}) all-reduce(f32[2,2,192]{2,1,0:T(2,128)S(1)} %pad_maximum_fusion.41, f32[2,768]{1,0:T(2,128)S(1)} %pad_maximum_fusion.39, f32[2]{0:T(128)S(1)} %pad_maximum_fusion.42), channel_id=1, replica_groups=mesh['dp'=8,'mp'=4] {'dp'}, use_global_device_ids=true, to_apply=%region_123.124 | all-reduce | flops 2306 | bytes 18448 | tf_op jit(solution)/shard_map/psum | solution.py:437
  1240.7 15.6 %reduce-scatter.60.cloned.1.call-done = f32[96,384]{1,0:T(8,128)} async-done(((f32[768,384]{1,0:T(8,128)}), f32[96,384]{1,0:T(8,128)}) %reduce-scatter.60.cloned.1.call-update) | async-done | bytes 147472
  1258.2 22.5 %reduce-scatter.54.cloned.1.call-done = bf16[1,128,768]{2,1,0:T(8,128)(2,1)} async-done(((bf16[1,512,768]{2,1,0:T(8,128)(2,1)}), bf16[1,128,768]{2,1,0:T(8,128)(2,1)}) %reduce-scatter.54.cloned.1.call-update) | async-done | bytes 196624 | tf_op jit(solution)/shard_map/reduce_scatter | solution.py:69
  1285.0 33.6 %reduce-scatter.46.cloned.1.call-done = bf16[1,256,768]{2,1,0:T(8,128)(2,1)} async-done(((bf16[1,1024,768]{2,1,0:T(8,128)(2,1)}), bf16[1,256,768]{2,1,0:T(8,128)(2,1)}) %reduce-scatter.46.cloned.1.call-update) | async-done | bytes 393232 | tf_op jit(solution)/shard_map/reduce_scatter | solution.py:66
  1321.6 39.7 %all-reduce.1 = (f32[2,2,768]{2,1,0:T(2,128)}, f32[2,2,768]{2,1,0:T(2,128)}, f32[2,768]{1,0:T(2,128)}, f32[2,768]{1,0:T(2,128)}) all-reduce(f32[2,2,768]{2,1,0:T(2,128)S(1)} %pad_maximum_fusion.36, f32[2,2,768]{2,1,0:T(2,128)S(1)} %pad_maximum_fusion.37, ...), channel_id=1, replica_groups=mesh['dp'=8,'mp'=4] {'dp','mp'}, use_global_device_ids=true, to_apply=%region_104.105 | all-reduce | flops 9216 | bytes 73728 | tf_op jit(solution)/shard_map/psum | solution.py:436
  1363.6 5.9 reduce-scatter.58.cloned.1.call-done
  1372.1 55.4 %reduce-scatter.56.cloned.1.call-done = f32[2,96,768]{2,1,0:T(8,128)} async-done(((f32[2,768,768]{2,1,0:T(8,128)}), f32[2,96,768]{2,1,0:T(8,128)}) %reduce-scatter.56.cloned.1.call-update) | async-done | bytes 589840 | tf_op jit(solution)/shard_map/reduce_scatter | solution.py:433
  (1159 shorter events, 438.5 us)
Async XLA Ops:
  7.2 55.4 %all-gather.9.cloned.1.call-start = ((), (), s32[]{:S(2)}) async-start(), calls=%async_computation.19 | async-start | bytes 1966080 | tf_op jit(solution)/shard_map/all_gather | solution.py:41
  11.7 188.3 %copy-start.176 = (f32[768]{0:T(1024)}, f32[768]{0:T(1024)S(1)}, u32[]{:S(2)}) copy-start(f32[768]{0:T(1024)S(1)} %get-tuple-element.342) | copy-start | bytes 9220
  14.3 86.6 %all-reduce.21.cloned.1.call-start = ((), (), s32[]{:S(2)}) async-start(), calls=%async_computation.50 | async-start | bytes 786432 | tf_op jit(solution)/shard_map/psum | solution.py:25
  46.2 99.2 %copy-start.43 = (bf16[1,512,1,192]{1,3,2,0:T(8,128)(2,1)}, bf16[1,512,1,192]{1,3,2,0:T(8,128)(2,1)S(1)}, u32[]{:S(2)}) copy-start(bf16[1,512,1,192]{1,3,2,0:T(8,128)(2,1)S(1)} %slice.1117) | copy-start | bytes 589828
  46.3 67.3 %copy-start.317 = (pred[1024]{0:T(1024)(128)(4,1)}, pred[1024]{0:T(1024)(128)(4,1)S(1)}, u32[]{:S(2)}) copy-start(pred[1024]{0:T(1024)(128)(4,1)S(1)} %iota_compare_fusion.32) | copy-start | bytes 3076
  48.5 96.9 %copy-start.91 = (bf16[1,512,3,64]{1,3,2,0:T(8,128)(2,1)}, bf16[1,512,3,64]{1,3,2,0:T(8,128)(2,1)S(1)}, u32[]{:S(2)}) copy-start(bf16[1,512,3,64]{1,3,2,0:T(8,128)(2,1)S(1)} %add_convert_fusion.14) | copy-start | bytes 589828
  66.3 107.4 %reduce-scatter.24.cloned.1.call-start = ((), (), s32[]{:S(2)}) async-start(), calls=%async_computation.20 | async-start | bytes 1966080 | tf_op jit(solution)/shard_map/reduce_scatter | solution.py:48
  66.4 73.1 %copy-start.291 = (s32[256]{0:T(256)}, s32[256]{0:T(256)S(1)}, u32[]{:S(2)}) copy-start(s32[256]{0:T(256)S(1)} %iota_add_fusion.1) | copy-start | bytes 3076
  137.3 60.4 %reduce-scatter.32.cloned.1.call-start = ((), (), s32[]{:S(2)}) async-start(), calls=%async_computation.27 | async-start | bytes 983040 | tf_op jit(solution)/shard_map/reduce_scatter | solution.py:51
  149.7 94.5 %all-gather.11.cloned.1.call-start = ((), (), s32[]{:S(2)}) async-start(), calls=%async_computation.21 | async-start | bytes 1966080 | tf_op jit(solution)/shard_map/all_gather | solution.py:41
  150.4 156.5 %copy-start.141 = (f32[768]{0:T(1024)}, f32[768]{0:T(1024)S(1)}, u32[]{:S(2)}) copy-start(f32[768]{0:T(1024)S(1)} %get-tuple-element.206) | copy-start | bytes 9220
  178.3 90.5 %reduce-scatter.34.cloned.1.call-start = ((), (), s32[]{:S(2)}) async-start(), calls=%async_computation.28 | async-start | bytes 983040 | tf_op jit(solution)/shard_map/reduce_scatter | solution.py:51
  178.9 68.5 %copy-start.269 = (f32[768]{0:T(1024)}, f32[768]{0:T(1024)S(1)}, u32[]{:S(2)}) copy-start(f32[768]{0:T(1024)S(1)} %get-tuple-element.204) | copy-start | bytes 9220
  229.0 77.9 %reduce-scatter.26.cloned.1.call-start = ((), (), s32[]{:S(2)}) async-start(), calls=%async_computation.22 | async-start | bytes 1966080 | tf_op jit(solution)/shard_map/reduce_scatter | solution.py:48
  253.6 99.6 %all-gather.13.cloned.1.call-start = ((), (), s32[]{:S(2)}) async-start(), calls=%async_computation.23 | async-start | bytes 1966080 | tf_op jit(solution)/shard_map/all_gather | solution.py:41
  310.0 81.5 %all-reduce.19.cloned.1.call-start = ((), (), s32[]{:S(2)}) async-start(), calls=%async_computation.49 | async-start | bytes 786432 | tf_op jit(solution)/shard_map/psum | solution.py:25
  355.8 64.8 %copy-start.22 = (bf16[1,1024,1,192]{1,3,2,0:T(8,128)(2,1)}, bf16[1,1024,1,192]{1,3,2,0:T(8,128)(2,1)S(1)}, u32[]{:S(2)}) copy-start(bf16[1,1024,1,192]{1,3,2,0:T(8,128)(2,1)S(1)} %slice.1114) | copy-start | bytes 1179652
  356.1 64.5 %copy-start.51 = (bf16[1,1024,3,64]{1,3,2,0:T(8,128)(2,1)}, bf16[1,1024,3,64]{1,3,2,0:T(8,128)(2,1)S(1)}, u32[]{:S(2)}) copy-start(bf16[1,1024,3,64]{1,3,2,0:T(8,128)(2,1)S(1)} %add_convert_fusion.2) | copy-start | bytes 1179652
  357.0 110.1 %reduce-scatter.28.cloned.1.call-start = ((), (), s32[]{:S(2)}) async-start(), calls=%async_computation.24 | async-start | bytes 1966080 | tf_op jit(solution)/shard_map/reduce_scatter | solution.py:48
  430.7 71.9 %reduce-scatter.36.cloned.1.call-start = ((), (), s32[]{:S(2)}) async-start(), calls=%async_computation.29 | async-start | bytes 983040 | tf_op jit(solution)/shard_map/reduce_scatter | solution.py:51
  442.6 105.1 %all-gather.15.cloned.1.call-start = ((), (), s32[]{:S(2)}) async-start(), calls=%async_computation.25 | async-start | bytes 1966080 | tf_op jit(solution)/shard_map/all_gather | solution.py:41
  470.8 115.2 %all-gather.17.cloned.1.call-start = ((), (), s32[]{:S(2)}) async-start(), calls=%async_computation.31 | async-start | bytes 1966080 | tf_op jit(solution)/shard_map/all_gather | solution.py:59
  471.6 137.6 %reduce-scatter.48.cloned.1.call-start = ((), (), s32[]{:S(2)}) async-start(), calls=%async_computation.39 | async-start | bytes 983040 | tf_op jit(solution)/shard_map/reduce_scatter | solution.py:69
  535.5 98.4 %reduce-scatter.38.cloned.1.call-start = ((), (), s32[]{:S(2)}) async-start(), calls=%async_computation.30 | async-start | bytes 983040 | tf_op jit(solution)/shard_map/reduce_scatter | solution.py:51
  539.3 142.2 %reduce-scatter.40.cloned.1.call-start = ((), (), s32[]{:S(2)}) async-start(), calls=%async_computation.32 | async-start | bytes 1966080 | tf_op jit(solution)/shard_map/reduce_scatter | solution.py:66
  596.2 123.2 %reduce-scatter.30.cloned.1.call-start = ((), (), s32[]{:S(2)}) async-start(), calls=%async_computation.26 | async-start | bytes 1966080 | tf_op jit(solution)/shard_map/reduce_scatter | solution.py:48
  601.8 158.3 %all-gather.19.cloned.1.call-start = ((), (), s32[]{:S(2)}) async-start(), calls=%async_computation.33 | async-start | bytes 1966080 | tf_op jit(solution)/shard_map/all_gather | solution.py:59
  723.8 105.7 %all-reduce.17.cloned.1.call-start = ((), (), s32[]{:S(2)}) async-start(), calls=%async_computation.48 | async-start | bytes 786432 | tf_op jit(solution)/shard_map/psum | solution.py:378
  794.9 79.6 %reduce-scatter.42.cloned.1.call-start = ((), (), s32[]{:S(2)}) async-start(), calls=%async_computation.34 | async-start | bytes 1966080 | tf_op jit(solution)/shard_map/reduce_scatter | solution.py:66
  838.1 60.0 %reduce-scatter.50.cloned.1.call-start = ((), (), s32[]{:S(2)}) async-start(), calls=%async_computation.40 | async-start | bytes 983040 | tf_op jit(solution)/shard_map/reduce_scatter | solution.py:69
  846.0 100.7 %all-gather.21.cloned.1.call-start = ((), (), s32[]{:S(2)}) async-start(), calls=%async_computation.35 | async-start | bytes 1966080 | tf_op jit(solution)/shard_map/all_gather | solution.py:59
  881.2 89.7 %reduce-scatter.52.cloned.1.call-start = ((), (), s32[]{:S(2)}) async-start(), calls=%async_computation.41 | async-start | bytes 983040 | tf_op jit(solution)/shard_map/reduce_scatter | solution.py:69
  932.4 87.1 %reduce-scatter.44.cloned.1.call-start = ((), (), s32[]{:S(2)}) async-start(), calls=%async_computation.36 | async-start | bytes 1966080 | tf_op jit(solution)/shard_map/reduce_scatter | solution.py:66
  956.8 108.0 %all-gather.23.cloned.1.call-start = ((), (), s32[]{:S(2)}) async-start(), calls=%async_computation.37 | async-start | bytes 1966080 | tf_op jit(solution)/shard_map/all_gather | solution.py:59
  1026.4 102.7 %all-reduce.15.cloned.1.call-start = ((), (), s32[]{:S(2)}) async-start(), calls=%async_computation.47 | async-start | bytes 786432 | tf_op jit(solution)/shard_map/psum | solution.py:378
  1090.3 125.6 %all-reduce.13.cloned.1.call-start = ((), (), s32[]{:S(2)}) async-start(), calls=%async_computation.46 | async-start | bytes 9437184
  1104.7 151.6 %reduce-scatter.60.cloned.1.call-start = ((), (), s32[]{:S(2)}) async-start(), calls=%async_computation.45 | async-start | bytes 1327104
  1120.8 160.0 %reduce-scatter.54.cloned.1.call-start = ((), (), s32[]{:S(2)}) async-start(), calls=%async_computation.42 | async-start | bytes 983040 | tf_op jit(solution)/shard_map/reduce_scatter | solution.py:69
  1137.7 180.9 %reduce-scatter.46.cloned.1.call-start = ((), (), s32[]{:S(2)}) async-start(), calls=%async_computation.38 | async-start | bytes 1966080 | tf_op jit(solution)/shard_map/reduce_scatter | solution.py:66
  1152.1 217.4 %reduce-scatter.58.cloned.1.call-start = ((), (), s32[]{:S(2)}) async-start(), calls=%async_computation.44 | async-start | bytes 3981312
  1177.6 249.9 %reduce-scatter.56.cloned.1.call-start = ((), (), s32[]{:S(2)}) async-start(), calls=%async_computation.43 | async-start | bytes 5308416 | tf_op jit(solution)/shard_map/reduce_scatter | solution.py:433
  1217.0 64.9 %copy-start.296 = (f32[128]{0:T(128)S(1)}, f32[128]{0:T(128)}, u32[]{:S(2)}) copy-start(f32[128]{0:T(128)} %copy-done.295) | copy-start | bytes 1540
  1217.0 64.9 %copy-start.261 = (f32[128]{0:T(128)S(1)}, f32[128]{0:T(128)}, u32[]{:S(2)}) copy-start(f32[128]{0:T(128)} %copy-done.260) | copy-start | bytes 1540
  1217.0 66.1 %copy-start.68 = (f32[1,128,768]{2,1,0:T(8,128)S(1)}, f32[1,128,768]{2,1,0:T(8,128)}, u32[]{:S(2)}) copy-start(f32[1,128,768]{2,1,0:T(8,128)} %copy-done.67) | copy-start | bytes 1179652
  1219.1 99.5 %copy-start.190 = (f32[256]{0:T(256)S(1)}, f32[256]{0:T(256)}, u32[]{:S(2)}) copy-start(f32[256]{0:T(256)} %copy-done.189) | copy-start | bytes 3076
  1219.3 100.6 %copy-start.252 = (f32[256]{0:T(256)S(1)}, f32[256]{0:T(256)}, u32[]{:S(2)}) copy-start(f32[256]{0:T(256)} %copy-done.251) | copy-start | bytes 3076
  1219.3 100.7 %copy-start.211 = (f32[256]{0:T(256)S(1)}, f32[256]{0:T(256)}, u32[]{:S(2)}) copy-start(f32[256]{0:T(256)} %copy-done.210) | copy-start | bytes 3076
  1257.4 103.9 %copy-start.33 = (f32[1,256,768]{2,1,0:T(8,128)S(1)}, f32[1,256,768]{2,1,0:T(8,128)}, u32[]{:S(2)}) copy-start(f32[1,256,768]{2,1,0:T(8,128)} %copy-done.32) | copy-start | bytes 2359300
  (330 other events, 2810.6 us)
Sparse Core Ops, SparseCore 0:
  14.5 48.1 all-gather.8
  66.5 34.4 all-reduce.20
  137.5 36.2 reduce-scatter.23
  176.6 21.0 reduce-scatter.31
  199.8 44.4 all-gather.10
  247.1 21.6 reduce-scatter.33
  271.2 35.6 reduce-scatter.25
  310.1 43.0 all-gather.12
  357.1 34.3 all-reduce.18
  430.8 36.2 reduce-scatter.27
  469.4 33.1 reduce-scatter.35
  504.5 43.1 all-gather.14
  549.3 36.6 all-gather.16
  588.1 20.9 reduce-scatter.47
  611.3 22.5 reduce-scatter.37
  636.0 45.4 reduce-scatter.39
  683.7 35.6 reduce-scatter.29
  723.9 36.1 all-gather.18
  795.0 34.3 all-reduce.16
  838.2 36.2 reduce-scatter.41
  876.9 21.1 reduce-scatter.49
  900.3 46.2 all-gather.20
  949.1 21.7 reduce-scatter.51
  973.2 46.2 reduce-scatter.43
  1026.5 38.2 all-gather.22
  1090.4 34.3 all-reduce.14
  1128.0 87.8 all-reduce.12
  1219.4 36.8 reduce-scatter.59
  1258.6 22.1 reduce-scatter.53
  1282.9 35.6 reduce-scatter.45
  1322.1 47.3 reduce-scatter.57
  1373.6 53.8 reduce-scatter.55
where the time goes:
time: 1450 us; the launch traced here: 1430 us
  waiting for transfers between devices  659 us (45%)
  blocking collectives  257 us (18%)
  matrix products  255 us (18%)
  other arithmetic  143 us (10%)
  local copies, waits for them, and re-layouts  94.3 us (7%)
  between operations  22.5 us (2%)
    reduce_scatter x4, waiting for transfers between devices, scatter_rows(): lax.psum_scatter(pieces[0].astype(jnp.bfloat16), 'mp', scatter_dimension=...  119 us
    all_gather x4, blocking collectives, gather_grads(): lax.all_gather(pieces[1], 'mp', axis=1, tiled=True)  105 us
    all_gather x4, waiting for transfers between devices, gather_grads(): lax.all_gather(pieces[0], 'mp', axis=1, tiled=True)  101 us
    all_gather x4, blocking collectives, gather_rows(): lax.all_gather(pieces[1], 'mp', axis=1, tiled=True)  91.8 us
    reduce_scatter x4, waiting for transfers between devices, scatter_grads(): lax.psum_scatter(pieces[0].astype(jnp.bfloat16), 'mp', scatter_dimension=...  91.1 us
    unnamed x707, local copies, waits for them, and re-layouts  67.2 us
    psum x2, waiting for transfers between devices, spread(): return lax.psum(kept, axis)  66.2 us
    reduce_scatter x4, waiting for transfers between devices, scatter_rows(): lax.psum_scatter(pieces[1].astype(jnp.bfloat16), 'mp', scatter_dimension=...  57.6 us
  transfers between devices with their start and end apart: 32, of which 31 were waited for; matrix products, arithmetic and copies ran while one was open for 20% of the time, Pallas kernels for 0%

commit v1 on v0

v1 whole, which is shorter than its diff:
```python
import functools

import jax, jax.numpy as jnp
from jax import lax
from jax.experimental import pallas as pl
from jax.experimental.pallas import tpu as pltpu
from jax.sharding import Mesh
from jax.sharding import PartitionSpec as P

HD = 64
BR = 256
BIG = 1e30
NT = (((1,), (1,)), ((), ()))
NN = (((1,), (0,)), ((), ()))


def mm(a, b, dims=NN):
    return lax.dot_general(a, b, dims, preferred_element_type=jnp.float32)


def halves(v):
    hi = v.astype(jnp.bfloat16)
    lo = (v - hi.astype(jnp.float32)).astype(jnp.bfloat16)
    return hi, lo


def softplus(v):
    return jnp.maximum(v, 0.0) + jnp.log(1.0 + jnp.exp(-jnp.abs(v)))


def fwd_one(x_ref, o_ref, lse_ref, carry_ref):
    size = x_ref.shape[0]
    nh = (x_ref.shape[1] - 2 * HD) // (3 * HD)
    w = nh * HD
    nb = size // BR
    first = lax.broadcasted_iota(jnp.int32, (BR, BR), 0)
    second = lax.broadcasted_iota(jnp.int32, (BR, BR), 1)
    tri = (first > second).astype(jnp.bfloat16)
    lanes = lax.broadcasted_iota(jnp.int32, (BR, 128), 1)
    lse_ref[...] = jnp.zeros_like(lse_ref)
    carry_ref[...] = jnp.zeros_like(carry_ref)
    for b in range(nb):
        rows = pl.ds(b * BR, BR)
        q0 = x_ref[rows, 3 * w : 3 * w + HD] * 0.125
        pens = []
        for c in range(b + 1):
            cols = pl.ds(c * BR, BR)
            sp = softplus(mm(q0, x_ref[cols, 3 * w + HD : 3 * w + 2 * HD], NT))
            if c == b:
                keep = first > second
                if c == 0:
                    keep = jnp.logical_and(keep, second >= 1)
                sp = jnp.where(keep, sp, 0.0)
            elif c == 0:
                sp = jnp.where(second >= 1, sp, 0.0)
            hi, lo = halves(sp)
            pen = mm(tri, hi) + mm(tri, lo) + carry_ref[b : b + 1, cols]
            carry_ref[b + 1 : b + 2, cols] = pen[BR - 1 :] + sp[BR - 1 :]
            if c == b:
                pen = jnp.where(first >= second, pen, BIG)
            pens.append(pen)
        stats = jnp.zeros((BR, 128), jnp.float32)
        for h in range(nh):
            qh = x_ref[rows, h * HD : (h + 1) * HD] * 0.125
            scores = [
                mm(qh, x_ref[c * BR : (c + 1) * BR, w + h * HD : w + (h + 1) * HD], NT) - pens[c]
                for c in range(b + 1)
            ]
            top = scores[0]
            for s in scores[1:]:
                top = jnp.maximum(top, s)
            top = jnp.max(top, axis=1, keepdims=True)
            total = None
            acc = None
            for c in range(b + 1):
                e = jnp.exp(scores[c] - top)
                total = e if total is None else total + e
                part = mm(
                    e.astype(jnp.bfloat16),
                    x_ref[c * BR : (c + 1) * BR, 2 * w + h * HD : 2 * w + (h + 1) * HD],
                )
                acc = part if acc is None else acc + part
            total = jnp.sum(total, axis=1, keepdims=True)
            o_ref[rows, h * HD : (h + 1) * HD] = (acc / total).astype(jnp.bfloat16)
            stats = jnp.where(lanes == h, top + jnp.log(total), stats)
        lse_ref[:, rows] = jnp.transpose(stats)[:8]


def bwd_one(x_ref, g_ref, o_ref, lse_ref, carry_ref, d_ref, acc, kt):
    size = x_ref.shape[0]
    nh = (x_ref.shape[1] - 2 * HD) // (3 * HD)
    w = nh * HD
    nb = size // BR
    jj = lax.broadcasted_iota(jnp.int32, (BR, BR), 0)
    ii = lax.broadcasted_iota(jnp.int32, (BR, BR), 1)
    below = (jj < ii).astype(jnp.bfloat16)
    above = (jj > ii).astype(jnp.bfloat16)
    ones = jnp.ones((8, HD), jnp.bfloat16)
    for h in range(nh + 1):
        lo = 3 * w + HD if h == nh else w + h * HD
        kt[h, :, :size] = jnp.transpose(x_ref[:, lo : lo + HD].astype(jnp.float32)).astype(
            jnp.bfloat16
        )
    later = [None] * nb
    for b in reversed(range(nb)):
        rows = pl.ds(b * BR, BR)
        q0 = x_ref[rows, 3 * w : 3 * w + HD] * 0.125
        pens, sigs, sums = [], [], [None] * (b + 1)
        for c in range(b + 1):
            sel = mm(x_ref[c * BR : (c + 1) * BR, 3 * w + HD : 3 * w + 2 * HD], q0, NT)
            small = jnp.exp(-jnp.abs(sel))
            sp = jnp.maximum(sel, 0.0) + jnp.log(1.0 + small)
            sig = jnp.where(sel >= 0, 1.0, small) / (1.0 + small)
            if c == b or c == 0:
                keep = None
                if c == b:
                    keep = ii > jj
                if c == 0:
                    keep = jj >= 1 if keep is None else jnp.logical_and(keep, jj >= 1)
                sp = jnp.where(keep, sp, 0.0)
                sig = jnp.where(keep, sig, 0.0)
            hi, lo = halves(sp)
            start = jnp.transpose(
                jnp.broadcast_to(carry_ref[b : b + 1, c * BR : (c + 1) * BR], (128, BR))
            )
            pen = mm(hi, below) + mm(lo, below) + start[:, :1]
            if c == b:
                pen = jnp.where(ii >= jj, pen, BIG)
            pens.append(pen)
            sigs.append(sig)
        for h in range(nh):
            qh = x_ref[rows, h * HD : (h + 1) * HD] * 0.125
            gh = g_ref[rows, h * HD : (h + 1) * HD]
            prod = gh.astype(jnp.float32) * o_ref[rows, h * HD : (h + 1) * HD].astype(jnp.float32)
            phi, plo = halves(prod)
            delta = (mm(ones, phi, NT) + mm(ones, plo, NT))[:1]
            lse = lse_ref[h : h + 1, rows]
            dqt = None
            for c in range(b + 1):
                cols = pl.ds(c * BR, BR)
                s = mm(x_ref[cols, w + h * HD : w + (h + 1) * HD], qh, NT)
                p = jnp.exp((s - pens[c]) - lse)
                dp = mm(x_ref[cols, 2 * w + h * HD : 2 * w + (h + 1) * HD], gh, NT)
                ds = p * (dp - delta)
                low = ds.astype(jnp.bfloat16)
                dk = mm(low, qh)
                dv = mm(p.astype(jnp.bfloat16), gh)
                part = mm(kt[h, :, c * BR : (c + 1) * BR], low)
                dqt = part if dqt is None else dqt + part
                if b == nb - 1:
                    acc[h, cols] = dk
                    acc[nh + h, cols] = dv
                else:
                    acc[h, cols] += dk
                    acc[nh + h, cols] += dv
                sums[c] = ds if sums[c] is None else sums[c] + ds
            d_ref[rows, h * HD : (h + 1) * HD] = jnp.transpose(dqt * 0.125).astype(jnp.bfloat16)
        dqt = None
        for c in range(b + 1):
            cols = pl.ds(c * BR, BR)
            hi, lo = halves(sums[c])
            grad = mm(hi, above) + mm(lo, above)
            full = grad[:, :1] + sums[c][:, :1]
            if later[c] is not None:
                grad = grad + later[c]
                full = full + later[c]
            later[c] = full
            low = (-(grad * sigs[c])).astype(jnp.bfloat16)
            dk = mm(low, q0)
            part = mm(kt[nh, :, c * BR : (c + 1) * BR], low)
            dqt = part if dqt is None else dqt + part
            if b == nb - 1:
                acc[2 * nh, cols] = dk
            else:
                acc[2 * nh, cols] += dk
        d_ref[rows, 3 * w : 3 * w + HD] = jnp.transpose(dqt * 0.125).astype(jnp.bfloat16)
        own = pl.ds(b * BR, BR)
    for h in range(nh):
        d_ref[:, w + h * HD : w + (h + 1) * HD] = acc[h, :size].astype(jnp.bfloat16)
        d_ref[:, 2 * w + h * HD : 2 * w + (h + 1) * HD] = acc[nh + h, :size].astype(jnp.bfloat16)
    d_ref[:, 3 * w + HD : 3 * w + 2 * HD] = acc[2 * nh, :size].astype(jnp.bfloat16)


VMEM = pl.BlockSpec(memory_space=pltpu.VMEM)
LIMIT = 48 * 1024 * 1024


def attend_fwd(x):
    size, w = x.shape[0], (x.shape[1] - 2 * HD) // 3
    return pl.pallas_call(
        fwd_one,
        out_shape=(
            jax.ShapeDtypeStruct((size, w), jnp.bfloat16),
            jax.ShapeDtypeStruct((8, size), jnp.float32),
            jax.ShapeDtypeStruct((8, size), jnp.float32),
        ),
        in_specs=[VMEM],
        out_specs=(VMEM,) * 3,
        compiler_params=pltpu.CompilerParams(vmem_limit_bytes=LIMIT),
        cost_estimate=pl.CostEstimate(
            flops=size * size * 64 * 40, bytes_accessed=size * 2000, transcendentals=size * size * 3
        ),
        name="attend_fwd",
    )(x)


def attend_bwd(x, g, o, lse, carry):
    size, w = x.shape[0], (x.shape[1] - 2 * HD) // 3
    nh = w // HD
    return pl.pallas_call(
        bwd_one,
        out_shape=jax.ShapeDtypeStruct(x.shape, jnp.bfloat16),
        in_specs=[VMEM] * 5,
        out_specs=VMEM,
        scratch_shapes=[
            pltpu.VMEM((2 * nh + 1, size, HD), jnp.float32),
            pltpu.VMEM((nh + 1, HD, size), jnp.bfloat16),
        ],
        compiler_params=pltpu.CompilerParams(vmem_limit_bytes=LIMIT),
        cost_estimate=pl.CostEstimate(
            flops=size * size * 64 * 80, bytes_accessed=size * 4000, transcendentals=size * size * 3
        ),
        name="attend_bwd",
    )(x, g, o, lse, carry)


EPS = 1e-05
F32 = jnp.float32
BF = jnp.bfloat16


def swap(v, *axes):
    count = 2 ** len(axes)
    return lax.ppermute(
        v, axes if len(axes) > 1 else axes[0], [(i, count - 1 - i) for i in range(count)]
    )


def ordered(own, other, index, axis):
    return jnp.where(
        index == 0,
        jnp.concatenate([own, other], axis=axis),
        jnp.concatenate([other, own], axis=axis),
    )


def pick(v, index, axis):
    return lax.dynamic_index_in_dim(v, index, axis, keepdims=False)


def normalize(v, gain, shift):
    mean = jnp.mean(v, axis=-1, keepdims=True)
    cen = v - mean
    var = jnp.mean(cen * cen, axis=-1, keepdims=True)
    inv = lax.rsqrt(var + EPS)
    hat = cen * inv
    return hat * gain + shift, hat, inv


def normalize_back(grad, hat, inv, gain):
    gh = grad * gain
    a = jnp.mean(gh, axis=-1, keepdims=True)
    b = jnp.mean(gh * hat, axis=-1, keepdims=True)
    return inv * (gh - a - hat * b), jnp.sum(grad * hat, axis=0), jnp.sum(grad, axis=0)


def gelu_both(u):
    k = 0.7978845608028654
    inner = k * (u + 0.044715 * u * u * u)
    t = jnp.tanh(inner)
    act = 0.5 * u * (1.0 + t)
    slope = 0.5 * (1.0 + t) + 0.5 * u * (1.0 - t * t) * k * (1.0 + 3 * 0.044715 * u * u)
    return act, slope


def dot(a, b, ca=1, cb=0):
    return lax.dot_general(a, b, (((ca,), (cb,)), ((), ())), preferred_element_type=F32)


class Plan:
    def __init__(self, dims, dp, mp):
        self.dims, self.dp, self.mp = dims, dp, mp
        self.core = dims[-1]
        self.plane = dims[:-1]
        self.c = lax.axis_index(self.core)
        self.zh = lax.axis_index("zh")
        self.zl = lax.axis_index("zl")
        self.z = lax.axis_index(("zh", "zl"))
        self.d = lax.axis_index(dims)

    def relabel(self, v):
        got = lax.ppermute(v, (self.core, "zh"), [(1, 2), (2, 1)])
        return jnp.where(self.c == self.zh, v, got)

    def ring(self, v, step):
        n = self.mp
        return lax.ppermute(v, ("zh", "zl"), [(i, (i + step) % n) for i in range(n)])

    def gather(self, v):
        v = ordered(v, swap(v, "zl"), self.zl, 0)
        return ordered(v, swap(v, self.core), self.c, 0)

    def scatter(self, v):
        rows = v.shape[0] // 4
        v = v.reshape(2, 2, rows, v.shape[1])
        got = swap(pick(v, 1 - self.c, 0), self.core)
        mine = pick(v, self.c, 0).astype(F32) + got.astype(F32)
        got = swap(pick(mine, 1 - self.zl, 0).astype(BF), "zl")
        return pick(mine, self.zl, 0) + got.astype(F32)

    def to_rows(self, o):
        rows = o.shape[0] // 4
        o = o.reshape(2, 2, rows, o.shape[1])
        got = []
        for dc in range(2):
            line = []
            for dz in range(2):
                part = pick(pick(o, self.c ^ dc, 0), self.zl ^ dz, 0)
                axes = ((self.core,) if dc else ()) + (("zl",) if dz else ())
                line.append(swap(part, *axes) if axes else part)
            got.append(ordered(line[0], line[1], self.zl, 1))
        return ordered(got[0], got[1], self.c, 1)

    def to_heads(self, g):
        rows, w = g.shape[0], g.shape[1] // 4
        g = g.reshape(rows, 2, 2, w)
        got = []
        for dc in range(2):
            line = []
            for dz in range(2):
                part = pick(pick(g, self.c ^ dc, 1), self.zl ^ dz, 1)
                axes = ((self.core,) if dc else ()) + (("zl",) if dz else ())
                line.append(swap(part, *axes) if axes else part)
            got.append(ordered(line[0], line[1], self.zl, 0))
        return ordered(got[0], got[1], self.c, 0)

    def piece(self, w):
        rows = w.shape[0] // self.dp
        return lax.dynamic_slice_in_dim(w, self.d * rows, rows, 0)

    def ring_gather(self, v):
        parts = []
        for _ in range(self.mp - 1):
            v = self.ring(v, 1)
            parts.append(v)
        return parts

    def plane_gather(self, v, axes):
        k, rows, n = v.shape
        have = []
        shape = [k]
        for ax in axes:
            pos = sum(self.dims.index(h) < self.dims.index(ax) for h in have)
            got = swap(v, ax)
            cur = v.reshape(k, *([2] * len(have)), rows, n)
            oth = got.reshape(cur.shape)
            a = jnp.stack([cur, oth], axis=1 + pos)
            b = jnp.stack([oth, cur], axis=1 + pos)
            v = jnp.where(lax.axis_index(ax) == 0, a, b)
            have.append(ax)
            v = v.reshape(k, -1, rows, n).reshape(k, -1, n)
            rows_all = v.shape[1]
            v = v.reshape(k, rows_all, n)
        return v.reshape(k, self.dp, rows, n)

    def plane_scatter(self, g, axes):
        n = g.shape[1]
        left = [ax for ax in self.dims]
        rows = g.shape[0] // self.dp
        v = g.reshape(*([2] * len(left)), rows, n)
        for ax in axes:
            pos = left.index(ax)
            i = lax.axis_index(ax)
            got = swap(pick(v, 1 - i, pos), ax)
            v = (pick(v, i, pos).astype(F32) + got.astype(F32)).astype(BF)
            left.remove(ax)
        return v.reshape(-1, n)

    def ring_scatter(self, chunks):
        t = chunks[-1]
        for r in range(self.mp - 2, -1, -1):
            got = self.ring(t, -1)
            t = chunks[r].astype(F32) + got.astype(F32)
            if r:
                t = t.astype(BF)
        return t


def body(
    dims, dp, mp,
    x_long, x_short, dy_long, dy_short, ln_gain, ln_bias, w_qkv, b_qv, w_out, b_out, w_up, b_up, w_down, b_down, threshold,
):
    plan = Plan(dims, dp, mp)
    layers = w_qkv.shape[0]
    d_model = x_long.shape[-1]
    heads_w = w_qkv.shape[-1]
    ffq = w_up.shape[-1]
    rl, rs = x_long.shape[1], x_short.shape[1]
    rows = rl + rs
    core_rest = tuple(plan.plane)
    fwd_axes = core_rest + (plan.core,)
    alt_axes = core_rest[::-1] + (plan.core,)
    gain = ln_gain.astype(F32)
    shift = ln_bias.astype(F32)

    x = jnp.concatenate([x_long[0], x_short[0]], axis=0)
    x = plan.relabel(x)

    small = jnp.concatenate([b_up.reshape(-1), b_qv.reshape(-1)])
    rel_small = jnp.stack([small] + plan.ring_gather(small))
    n_up = layers * ffq
    rel_bup = rel_small[:, :n_up].reshape(mp, layers, ffq).astype(F32)
    rel_bqv = rel_small[:, n_up:].reshape(mp, layers, 2, heads_w).astype(F32)
    mine = 2 * plan.c + plan.zl
    my_bqv = pick(rel_bqv, (plan.z - mine) % mp, 0)
    zero_bq = pick(rel_bqv, plan.z % mp, 0)[:, 0, :HD]

    exts = []
    for l in range(layers):
        quarter = plan.relabel(w_qkv[l].reshape(d_model, 3 * heads_w))
        head0 = w_qkv[l][:, :2, :HD].reshape(d_model, 2 * HD)
        got = lax.ppermute(head0, "zl", [(0, 1)])
        head0 = jnp.where(plan.zl == 0, head0, got)
        got = lax.ppermute(head0, "zh", [(0, 1)])
        head0 = jnp.where(plan.zh == 0, head0, got)
        exts.append(jnp.concatenate([quarter, head0], axis=1))

    ups, downs, outs = [], [], []
    for l in range(layers):
        po = plan.piece(w_out[l])
        pu = jnp.concatenate([plan.piece(w_up[l]), po], axis=0)
        pd = plan.piece(w_down[l])
        n_out, n_d = po.shape[0], pd.shape[0]
        both = plan.ring_gather(jnp.concatenate([pu, pd], axis=0))
        stacked = jnp.stack(both)
        n_u = pu.shape[0]
        gu = plan.plane_gather(stacked[:, :n_u], fwd_axes)
        gd = plan.plane_gather(stacked[:, n_u:], alt_axes)
        up = gu[:, :, : n_u - n_out].reshape(mp - 1, d_model, ffq)
        ups.append(jnp.concatenate([w_up[l]] + [up[r] for r in range(mp - 1)], axis=1))
        out = gu[:, :, n_u - n_out :].reshape(mp - 1, heads_w, d_model)
        out = jnp.concatenate([w_out[l][None], out], axis=0)
        outs.append(
            jnp.concatenate([pick(out, (plan.z - q) % mp, 0) for q in range(mp)], axis=0)
        )
        downs.append(
            jnp.concatenate([w_down[l], gd.reshape((mp - 1) * ffq, d_model)], axis=0)
        )

    dy = plan.relabel(jnp.concatenate([dy_long[0], dy_short[0]], axis=0))

    limits = threshold.astype(F32) / 64.0
    resid = x.astype(F32)
    saved = []
    shares = []
    for l in range(layers):
        normed, hat1, inv1 = normalize(resid, gain[l, 0], shift[l, 0])
        normed = normed.astype(BF)
        full = [plan.gather(normed[:rl]), plan.gather(normed[rl:])]
        bias = jnp.concatenate(
            [
                my_bqv[l, 0],
                jnp.zeros((heads_w,), F32),
                my_bqv[l, 1],
                zero_bq[l],
                jnp.zeros((HD,), F32),
            ]
        )
        proj = [(dot(n, exts[l]) + bias).astype(BF) for n in full]
        att = [attend_fwd(p) for p in proj]
        share = jnp.zeros((), F32)
        for p, a in zip(proj, att):
            size = p.shape[0]
            sel = a[2][size // BR]
            left = (size - 1 - lax.broadcasted_iota(jnp.int32, (size,), 0)).astype(F32)
            share = share + jnp.sum(
                jax.nn.sigmoid(4.0 * (sel / jnp.maximum(left, 1.0) - limits[l]))
            )
        shares.append(share)
        attended = jnp.concatenate([plan.to_rows(a[0]) for a in att], axis=0)
        middle = resid + dot(attended, outs[l]) + b_out[l].astype(F32)
        normed2, hat2, inv2 = normalize(middle, gain[l, 1], shift[l, 1])
        normed2 = normed2.astype(BF)
        upper = dot(normed2, ups[l]) + rel_bup[:, l].reshape(-1)
        active = gelu_both(upper)[0].astype(BF)
        saved.append((resid, middle, full, proj, att, attended, normed2, upper, active))
        resid = middle + dot(active, downs[l]) + b_down[l].astype(F32)

    y = plan.relabel(resid.astype(BF))

    g = dy.astype(F32)
    vec = {}
    weight_grads = [None] * layers
    for l in reversed(range(layers)):
        resid, middle, full, proj, att, attended, normed2, upper, active = saved[l]
        g_bdown = jnp.sum(g, axis=0)
        gm = g.astype(BF)
        gact = dot(gm, downs[l], 1, 1)
        slope = gelu_both(upper)[1]
        gu = (slope * gact).astype(BF)
        w_down_t = dot(gm, active, 0, 0).astype(BF)
        w_up_g = dot(normed2, gu, 0, 0).astype(BF)
        g_bup = jnp.sum(gu.astype(F32), axis=0)
        gn2 = dot(gu, ups[l], 1, 1)
        _, hat2, inv2 = normalize(middle, gain[l, 1], shift[l, 1])
        back, g_gain2, g_shift2 = normalize_back(gn2, hat2, inv2, gain[l, 1])
        gmid = g + back
        g_bout = jnp.sum(gmid, axis=0)
        ga = gmid.astype(BF)
        go = dot(ga, outs[l], 1, 1).astype(BF)
        w_out_t = dot(ga, attended, 0, 0).astype(BF)
        gh = [plan.to_heads(go[:rl]), plan.to_heads(go[rl:])]
        dext = [attend_bwd(p, h, a[0], a[1], a[2]) for p, h, a in zip(proj, gh, att)]
        gn1 = jnp.concatenate(
            [plan.scatter(dot(e, exts[l], 1, 1).astype(BF)) for e in dext], axis=0
        )
        w_ext_g = sum(dot(n, e, 0, 0) for n, e in zip(full, dext)).astype(BF)
        g_bext = sum(jnp.sum(e.astype(F32), axis=0) for e in dext)
        _, hat1, inv1 = normalize(resid, gain[l, 0], shift[l, 0])
        back, g_gain1, g_shift1 = normalize_back(gn1, hat1, inv1, gain[l, 0])
        g = gmid + back

        w_up_g = plan.plane_scatter(w_up_g, (plan.core,) + core_rest)
        w_up_g = plan.ring_scatter([w_up_g[:, r * ffq : (r + 1) * ffq] for r in range(mp)])
        w_down_t = plan.plane_scatter(w_down_t, (plan.core,) + core_rest[::-1])
        w_down_t = plan.ring_scatter([w_down_t[:, r * ffq : (r + 1) * ffq] for r in range(mp)])
        w_out_t = plan.plane_scatter(w_out_t, (plan.core,) + core_rest)
        w_out_t = w_out_t.reshape(-1, mp, heads_w)
        w_out_t = plan.ring_scatter([pick(w_out_t, (plan.z - r) % mp, 1) for r in range(mp)])
        w_ext_g = plan.plane_scatter(w_ext_g, core_rest[::-1])
        w_ext_g = w_ext_g.reshape(2, -1, w_ext_g.shape[1])
        part, zero = w_ext_g[..., : 3 * heads_w], w_ext_g[..., 3 * heads_w :]
        got = lax.ppermute(part, (plan.core, "zh"), [(1, 0), (2, 3)])
        part = part.astype(F32) + got.astype(F32)
        got = lax.ppermute(
            pick(part, 1 - plan.c, 0).astype(BF), (plan.core, "zh"), [(0, 2), (3, 1)]
        )
        w_qkv_g = jnp.where(plan.c == plan.zh, pick(part, plan.c, 0), got.astype(F32))
        got = swap(pick(zero, 1 - plan.c, 0), plan.core)
        zero = (pick(zero, plan.c, 0).astype(F32) + got.astype(F32)).astype(BF)
        zero = zero.astype(F32) + swap(zero, "zl").astype(F32)
        zero = zero + swap(zero.astype(BF), "zh").astype(F32)
        zero = jnp.where(plan.z == 0, zero, 0.0)
        w_qkv_g = w_qkv_g.reshape(-1, 3, heads_w)
        zero = zero.reshape(-1, 2, HD)
        w_qkv_g = w_qkv_g + jnp.pad(zero, ((0, 0), (0, 1), (0, heads_w - HD)))
        weight_grads[l] = (w_qkv_g, jnp.transpose(w_out_t), w_up_g, jnp.transpose(w_down_t))

        hot = (lax.broadcasted_iota(jnp.int32, (mp, 1), 0) == mine).astype(F32)
        gq = hot * g_bext[None, :heads_w]
        gv = hot * g_bext[None, 2 * heads_w : 3 * heads_w]
        gq = gq.reshape(-1).at[:HD].add(g_bext[3 * heads_w : 3 * heads_w + HD])
        g_bup = g_bup.reshape(mp, ffq)
        g_bup = jnp.stack([pick(g_bup, (plan.z - q) % mp, 0) for q in range(mp)])
        vec[l] = jnp.concatenate(
            [
                g_gain1, g_gain2, g_shift1, g_shift2, g_bout, g_bdown,
                gq, gv.reshape(-1), g_bup.reshape(-1), jnp.full((128,), shares[l] / mp),
            ]
        )

    dx = plan.relabel(g.astype(BF)).astype(F32)
    total = lax.psum(jnp.stack([vec[l] for l in range(layers)]), dims + ("zh", "zl"))
    n = d_model
    g_gain = total[:, : 2 * n].reshape(layers, 2, n)
    g_bias = total[:, 2 * n : 4 * n].reshape(layers, 2, n)
    g_bout = total[:, 4 * n : 5 * n]
    g_bdown = total[:, 5 * n : 6 * n]
    at = 6 * n
    g_bqv = total[:, at : at + 2 * mp * heads_w].reshape(layers, 2, mp, heads_w)
    at += 2 * mp * heads_w
    g_bup = total[:, at : at + mp * ffq].reshape(layers, mp, ffq)
    at += mp * ffq
    key_share = total[:, at] / (dp * (rows * mp))
    return (
        y[None, :rl],
        y[None, rl:],
        dx[None, :rl],
        dx[None, rl:],
        g_gain,
        g_bias,
        jnp.stack([weight_grads[l][0] for l in range(layers)]),
        pick(g_bqv, plan.z, 2),
        jnp.stack([weight_grads[l][1] for l in range(layers)]),
        g_bout,
        jnp.stack([weight_grads[l][2] for l in range(layers)]),
        pick(g_bup, plan.z, 1),
        jnp.stack([weight_grads[l][3] for l in range(layers)]),
        g_bdown,
        key_share,
    )


def solution(mesh):
    dp, mp = mesh.shape["dp"], mesh.shape["mp"]
    bits = dp.bit_length() - 1
    dims = tuple(f"d{i}" for i in range(bits))
    fine = Mesh(mesh.devices.reshape((2,) * bits + (2, mp // 2)), dims + ("zh", "zl"))
    z = ("zh", "zl")
    in_specs = (
        P(dims, z, None), P(dims, z, None), P(dims, z, None), P(dims, z, None),
        P(), P(), P(None, None, None, z), P(None, None, z), P(None, z, None), P(),
        P(None, None, z), P(None, z), P(None, z, None), P(), P(),
    )
    out_specs = (
        P(dims, z, None), P(dims, z, None), P(dims, z, None), P(dims, z, None),
        P(), P(), P(None, dims, None, z), P(None, None, z), P(None, z, dims), P(),
        P(None, dims, z), P(None, z), P(None, z, dims), P(), P(),
    )
    return jax.shard_map(
        functools.partial(body, dims, dp, mp), mesh=fine, in_specs=in_specs, out_specs=out_specs, check_vma=False
    )
```

time: 1450 us -> 878 us (0.61)
  waiting for transfers between devices: 659 us -> 307 us
  blocking collectives: 257 us -> 0 us
  starting transfers between devices: 3.29 us -> 202 us
  matrix products: 255 us -> 77 us
  Pallas kernels: 0 us -> 54.8 us
  other arithmetic: 143 us -> 98 us
    reduce_scatter x17 -> x0, waiting for transfers between devices: 372 us -> none  [the longest x4 119 us: scatter_rows(): lax.psum_scatter(pieces[0].astype(jnp.bfloat16), 'mp', scatter_dimension=...]
    ppermute x0 -> x121, starting transfers between devices: none -> 201 us  [the longest x27 79.4 us: ring(): lax.ppermute(v, ('zh', 'zl'), [(i, (i + step) % n) for i in range(n)])]
    all_gather x8 -> x0, blocking collectives: 196 us -> none  [the longest x4 105 us: gather_grads(): lax.all_gather(pieces[1], 'mp', axis=1, tiled=True)]
    ppermute x0 -> x121, waiting for transfers between devices: none -> 187 us  [the longest x80 109 us: swap(): lax.ppermute(v, axes if len(axes) > 1 else axes[0], [(i, count - 1 - i) f...]
    dot_general x128 -> x30, matrix products: 245 us -> 77 us  [dot(): lax.dot_general(a, b, (((ca,), (cb,)), ((), ())), preferred_element_type=...]
    all_gather x8 -> x0, waiting for transfers between devices: 155 us -> none  [the longest x4 101 us: gather_grads(): lax.all_gather(pieces[0], 'mp', axis=1, tiled=True)]
    psum x2 -> x0, blocking collectives: 60.5 us -> none  [the longest x1 39.7 us: reduce_stacked(): lax.psum((g_gain, g_shift, g_bout, g_bdown), ('dp', 'mp'))]
    reduce_sum x58 -> x23, other arithmetic: 77.3 us -> 17.5 us  [the longest x4 5.07 us: body(): jnp.sum(jax.nn.sigmoid(4.0 * (sel / jnp.maximum(left, 1.0) - limits[l])))]
  transfers between devices with their start and end apart: 32 -> 122, of which waited for: 31 -> 52; matrix products, arithmetic and copies ran while one was open for 20% -> 25% of each run, Pallas kernels for 0% -> 6%
where the time goes in v1:
time: 878 us; the launch traced here: 861 us
  waiting for transfers between devices  307 us (35%)
  starting transfers between devices  202 us (23%)
  local copies, waits for them, and re-layouts  102 us (12%)
  other arithmetic  98 us (11%)
  matrix products  77 us (9%)
  Pallas kernels  54.8 us (6%)
  between operations  20.9 us (2%)
    psum x1, waiting for transfers between devices, body(): lax.psum(jnp.stack([vec[l] for l in range(layers)]), dims + ('zh', 'zl'))  120 us
    ppermute x80, waiting for transfers between devices, swap(): lax.ppermute(v, axes if len(axes) > 1 else axes[0], [(i, count - 1 - i) f...  109 us
    ppermute x27, starting transfers between devices, ring(): lax.ppermute(v, ('zh', 'zl'), [(i, (i + step) % n) for i in range(n)])  79.4 us
    dot_general x30, matrix products, dot(): lax.dot_general(a, b, (((ca,), (cb,)), ((), ())), preferred_element_type=...  77 us
    ppermute x80, starting transfers between devices, swap(): lax.ppermute(v, axes if len(axes) > 1 else axes[0], [(i, count - 1 - i) f...  75 us
    pallas_call x4, Pallas kernels, attend_bwd(): pl.pallas_call(bwd_one, out_shape=jax.ShapeDtypeStruct(x.shape, jnp.bfloa...  35.1 us
    ppermute x27, waiting for transfers between devices, ring(): lax.ppermute(v, ('zh', 'zl'), [(i, (i + step) % n) for i in range(n)])  29.4 us
    ppermute x6, waiting for transfers between devices, relabel(): got = lax.ppermute(v, (self.core, 'zh'), [(1, 2), (2, 1)])  29.4 us
  transfers between devices with their start and end apart: 122, of which 52 were waited for; matrix products, arithmetic and copies ran while one was open for 25% of the time, Pallas kernels for 6%

profile of v1, /device:TPU:1, one launch (start us, length us, event | category | flops | bytes accessed | tf_op | source)
XLA Modules:
  0.0 861.4 jit_solution(9309518129828769928)
XLA Ops:
  7.2 4.1 slice_bitcast_fusion.12
  22.0 3.9 collective-permute-start
  28.6 4.1 collective-permute-start.4
  41.1 6.4 collective-permute-done.7
  47.5 16.4 %collective-permute-start.8 = (bf16[2304]{0:T(1024)(128)(2,1)S(1)}, bf16[2304]{0:T(1024)(128)(2,1)S(1)}, u32[]{:S(2)}, u32[]{:S(2)}) collective-permute-start(bf16[2304]{0:T(1024)(128)(2,1)S(1)} %collective-permute-done.7), channel_id=1, source_target_pairs={{0,1},{1,2},{2,3},{3,0},{4,5},{5,6},{6,7},{7,4},{8,9},{9,10},{10,1... | collective-permute-start | bytes 13832 | tf_op jit(solution)/shard_map/ppermute | solution.py:297
  70.9 4.6 collective-permute-done.29
  79.8 4.8 collective-permute-start.30
  89.8 4.5 collective-permute-start.49
  94.4 13.0 %collective-permute-start.18 = (bf16[216,768]{1,0:T(8,128)(2,1)S(1)}, bf16[216,768]{1,0:T(8,128)(2,1)S(1)}, u32[]{:S(2)}, u32[]{:S(2)}) collective-permute-start(bf16[216,768]{1,0:T(8,128)(2,1)S(1)} %collective-permute-done.17), channel_id=1, source_target_pairs={{0,1},{1,2},{2,3},{3,0},{4,5},{5,6},{6,7},{7,4},{8,9},{9,10},{10,1... | collective-permute-start | bytes 995336 | tf_op jit(solution)/shard_map/ppermute | solution.py:297
  109.5 29.4 %collective-permute-done.49 = bf16[384,768]{1,0:T(8,128)(2,1)S(1)} collective-permute-done((bf16[384,768]{1,0:T(8,128)(2,1)S(1)}, bf16[384,768]{1,0:T(8,128)(2,1)S(1)}, u32[]{:S(2)}, u32[]{:S(2)}) %collective-permute-start.49) | collective-permute-done | bytes 589856 | tf_op jit(solution)/shard_map/ppermute | solution.py:292
  152.8 4.1 collective-permute-done.19
  157.0 3.8 collective-permute-done.41
  167.3 4.2 collective-permute-start.15
  194.7 7.4 attend_fwd.4
  203.7 5.9 collective-permute-start.11
  227.5 4.3 collective-permute-start.47
  257.5 4.2 collective-permute-start.34
  269.8 5.6 collective-permute-done.26
  287.0 7.4 attend_fwd.6
  310.8 7.4 convert_reduce_fusion
  326.2 4.7 convolution_convert_fusion.2
  330.9 4.5 convolution_convert_fusion
  371.3 4.5 attend_bwd.5
  380.5 13.0 %attend_bwd.4 = bf16[1024,704]{1,0:T(8,128)(2,1)S(1)} custom-call(bf16[1024,704]{1,0:T(8,128)(2,1)S(1)} %add_convert_fusion.x_ref, bf16[1024,192]{1,0:T(8,128)(2,1)S(1)} %maximum_select_fusion.26.g_ref, bf16[1024,192]{1,0:T(8,128)(2,1)S(1)} %get-tuple-element.53.o_ref, f32[8,1024]{1,0:T(8,128)S(1)} %get-tuple-element.55.lse_ref, ...), custom_call_target="tpu_custom_call" | custom-call | flops 5368709120 | bytes 4096000 | tf_op jit(solution)/shard_map/attend_bwd/pallas_call | solution.py:210
  408.6 9.5 %collective-permute-done.78 = bf16[2,2,96,704]{3,2,1,0:T(8,128)(2,1)S(1)} collective-permute-done((bf16[2,2,96,704]{3,2,1,0:T(8,128)(2,1)S(1)}, bf16[2,2,96,704]{3,2,1,0:T(8,128)(2,1)S(1)}, u32[]{:S(2)}, u32[]{:S(2)}) %collective-permute-start.78) | collective-permute-done | bytes 540704 | tf_op jit(solution)/shard_map/ppermute | solution.py:234
  420.5 4.9 collective-permute-done.92
  426.0 5.7 collective-permute-done.79
  435.8 4.5 collective-permute-start.80
  441.6 7.5 collective-permute-done.83
  467.8 4.6 collective-permute-done.81
  479.8 8.7 %convert_reduce_fusion.1 = (f32[3072]{0:T(1024)S(1)}, bf16[384,3072]{1,0:T(8,128)(2,1)S(1)}) fusion(bf16[2304,768]{1,0:T(8,128)(2,1)S(1)} %bitcast.535, bf16[768,768]{1,0:T(8,128)(2,1)S(1)} %copy-done.59, f32[384,768]{1,0:T(8,128)S(1)} %get-tuple-element.105, f32[384,3072]{1,0:T(8,128)} %copy-done.172), kind=kOutput, calls=%fused_computation.35 | convolution fusion | flops 1846440960 | bytes 12988416 | tf_op jit(solution)/shard_map/dot_general | solution.py:277
  495.0 4.7 convolution_convert_fusion.3
  499.7 4.7 convolution_convert_fusion.1
  523.4 4.5 attend_bwd.7
  533.1 13.0 %attend_bwd.6 = bf16[1024,704]{1,0:T(8,128)(2,1)S(1)} custom-call(bf16[1024,704]{1,0:T(8,128)(2,1)S(1)} %copy-done.11, bf16[1024,192]{1,0:T(8,128)(2,1)S(1)} %maximum_select_fusion.27.g_ref, bf16[1024,192]{1,0:T(8,128)(2,1)S(1)} %copy-done.1, f32[8,1024]{1,0:T(8,128)S(1)} %get-tuple-element.59.lse_ref, f32[8,1024]{1,0:T(8,128)S(1)} %copy-done.5), custom_call_target="tpu_custom_call" | custom-call | flops 5368709120 | bytes 4096000 | tf_op jit(solution)/shard_map/attend_bwd/pallas_call | solution.py:210
  550.5 5.0 add_convert_fusion.3
  561.7 12.2 %collective-permute-done.71 = bf16[2,2,96,704]{3,2,1,0:T(8,128)(2,1)S(1)} collective-permute-done((bf16[2,2,96,704]{3,2,1,0:T(8,128)(2,1)S(1)}, bf16[2,2,96,704]{3,2,1,0:T(8,128)(2,1)S(1)}, u32[]{:S(2)}, u32[]{:S(2)}) %collective-permute-start.71) | collective-permute-done | bytes 540704 | tf_op jit(solution)/shard_map/ppermute | solution.py:234
  576.6 5.0 collective-permute-done.86
  586.0 6.1 collective-permute-done.72
  608.6 5.7 collective-permute-start.73
  630.9 5.1 collective-permute-done.74
  641.9 4.6 collective-permute-start.70
  646.5 119.8 %all-reduce.4.cloned.1.call-done = f32[2,9344]{1,0:T(2,128)} async-done(((f32[2,9344]{1,0:T(2,128)}), f32[2,9344]{1,0:T(2,128)}) %all-reduce.4.cloned.1.call-update) | async-done | bytes 74768 | tf_op jit(solution)/shard_map/psum | solution.py:563
  805.8 4.2 collective-permute-start.120
  813.7 5.3 collective-permute-done.98
  821.5 10.5 %collective-permute-done.99 = bf16[96,3072]{1,0:T(8,128)(2,1)S(1)} collective-permute-done((bf16[96,3072]{1,0:T(8,128)(2,1)S(1)}, bf16[96,3072]{1,0:T(8,128)(2,1)S(1)}, u32[]{:S(2)}, u32[]{:S(2)}) %collective-permute-start.99) | collective-permute-done | bytes 589856 | tf_op jit(solution)/shard_map/ppermute | solution.py:234
  833.1 4.1 collective-permute-start.112
  847.3 4.1 collective-permute-start.114
  (976 shorter events, 404.3 us)
Async XLA Ops:
  7.2 759.1 %all-reduce.4.cloned.1.call-start = ((), (), s32[]{:S(2)}) async-start(), calls=%async_computation | async-start | bytes 149504 | tf_op jit(solution)/shard_map/psum | solution.py:563
  17.2 72.7 %collective-permute-start.17 = (bf16[216,768]{1,0:T(8,128)(2,1)}, bf16[216,768]{1,0:T(8,128)(2,1)S(1)}, u32[]{:S(2)}, u32[]{:S(2)}) collective-permute-start(bf16[216,768]{1,0:T(8,128)(2,1)} %pad_maximum_fusion.43), channel_id=1, source_target_pairs={{0,1},{1,2},{2,3},{3,0},{4,5},{5,6},{6,7},{7,4},{8,9},{9,10},{10,1... | collective-permute-start | bytes 995336 | tf_op jit(solution)/shard_map/ppermute | solution.py:297
  19.8 20.7 %collective-permute-start.6 = (bf16[2304]{0:T(1024)(128)(2,1)S(1)}, bf16[2304]{0:T(1024)(128)(2,1)S(1)}, u32[]{:S(2)}, u32[]{:S(2)}) collective-permute-start(bf16[2304]{0:T(1024)(128)(2,1)S(1)} %dynamic-update-slice.25), channel_id=1, source_target_pairs={{0,1},{1,2},{2,3},{3,0},{4,5},{5,6},{6,7},{7,4},{8,9},{9,10},{10,1... | collective-permute-start | bytes 13832 | tf_op jit(solution)/shard_map/ppermute | solution.py:297
  22.0 85.3 %collective-permute-start = (bf16[384,768]{1,0:T(8,128)(2,1)}, bf16[384,768]{1,0:T(8,128)(2,1)}, u32[]{:S(2)}, u32[]{:S(2)}) collective-permute-start(bf16[384,768]{1,0:T(8,128)(2,1)} %pad_maximum_fusion.30), channel_id=1, source_target_pairs={{2,4},{4,2},{3,5},{5,3},{10,12},{12,10},{11,13},{13,11},{18,20},{2... | collective-permute-start | bytes 1769480 | tf_op jit(solution)/shard_map/ppermute | solution.py:292
  28.6 38.8 %collective-permute-start.4 = (bf16[768,128]{0,1:T(8,128)(2,1)S(1)}, bf16[768,128]{0,1:T(8,128)(2,1)}, u32[]{:S(2)}, u32[]{:S(2)}) collective-permute-start(bf16[768,128]{0,1:T(8,128)(2,1)S(1)} %bitcast.579), channel_id=1, source_target_pairs={{0,1},{2,3},{4,5},{6,7},{8,9},{10,11},{12,13},{14,15},{16,17},{18,... | collective-permute-start | bytes 589832 | tf_op jit(solution)/shard_map/ppermute | solution.py:422
  32.7 113.5 %collective-permute-start.3 = (bf16[768,576]{0,1:T(8,128)(2,1)S(1)}, bf16[768,576]{0,1:T(8,128)(2,1)}, u32[]{:S(2)}, u32[]{:S(2)}) collective-permute-start(bf16[768,576]{0,1:T(8,128)(2,1)S(1)} %bitcast.541), channel_id=1, source_target_pairs={{2,4},{4,2},{3,5},{5,3},{10,12},{12,10},{11,13},{13,11},{18,20},{2... | collective-permute-start | bytes 2654216 | tf_op jit(solution)/shard_map/ppermute | solution.py:292
  47.5 17.5 %collective-permute-start.8 = (bf16[2304]{0:T(1024)(128)(2,1)S(1)}, bf16[2304]{0:T(1024)(128)(2,1)S(1)}, u32[]{:S(2)}, u32[]{:S(2)}) collective-permute-start(bf16[2304]{0:T(1024)(128)(2,1)S(1)} %collective-permute-done.7), channel_id=1, source_target_pairs={{0,1},{1,2},{2,3},{3,0},{4,5},{5,6},{6,7},{7,4},{8,9},{9,10},{10,1... | collective-permute-start | bytes 13832 | tf_op jit(solution)/shard_map/ppermute | solution.py:297
  65.0 29.4 %collective-permute-start.39 = (bf16[216,768]{1,0:T(8,128)(2,1)}, bf16[216,768]{1,0:T(8,128)(2,1)S(1)}, u32[]{:S(2)}, u32[]{:S(2)}) collective-permute-start(bf16[216,768]{1,0:T(8,128)(2,1)} %pad_maximum_fusion.44), channel_id=1, source_target_pairs={{0,1},{1,2},{2,3},{3,0},{4,5},{5,6},{6,7},{7,4},{8,9},{9,10},{10,1... | collective-permute-start | bytes 995336 | tf_op jit(solution)/shard_map/ppermute | solution.py:297
  87.2 60.4 %collective-permute-start.28 = (bf16[768,576]{0,1:T(8,128)(2,1)S(1)}, bf16[768,576]{0,1:T(8,128)(2,1)S(1)}, u32[]{:S(2)}, u32[]{:S(2)}) collective-permute-start(bf16[768,576]{0,1:T(8,128)(2,1)S(1)} %bitcast.540), channel_id=1, source_target_pairs={{2,4},{4,2},{3,5},{5,3},{10,12},{12,10},{11,13},{13,11},{18,20},{2... | collective-permute-start | bytes 2654216 | tf_op jit(solution)/shard_map/ppermute | solution.py:292
  89.8 49.1 %collective-permute-start.49 = (bf16[384,768]{1,0:T(8,128)(2,1)S(1)}, bf16[384,768]{1,0:T(8,128)(2,1)S(1)}, u32[]{:S(2)}, u32[]{:S(2)}) collective-permute-start(bf16[384,768]{1,0:T(8,128)(2,1)S(1)} %copy-done.92), channel_id=1, source_target_pairs={{2,4},{4,2},{3,5},{5,3},{10,12},{12,10},{11,13},{13,11},{18,20},{2... | collective-permute-start | bytes 1769480 | tf_op jit(solution)/shard_map/ppermute | solution.py:292
  94.4 46.1 %collective-permute-start.18 = (bf16[216,768]{1,0:T(8,128)(2,1)S(1)}, bf16[216,768]{1,0:T(8,128)(2,1)S(1)}, u32[]{:S(2)}, u32[]{:S(2)}) collective-permute-start(bf16[216,768]{1,0:T(8,128)(2,1)S(1)} %collective-permute-done.17), channel_id=1, source_target_pairs={{0,1},{1,2},{2,3},{3,0},{4,5},{5,6},{6,7},{7,4},{8,9},{9,10},{10,1... | collective-permute-start | bytes 995336 | tf_op jit(solution)/shard_map/ppermute | solution.py:297
  107.4 34.7 %collective-permute-start.40 = (bf16[216,768]{1,0:T(8,128)(2,1)S(1)}, bf16[216,768]{1,0:T(8,128)(2,1)S(1)}, u32[]{:S(2)}, u32[]{:S(2)}) collective-permute-start(bf16[216,768]{1,0:T(8,128)(2,1)S(1)} %collective-permute-done.39), channel_id=1, source_target_pairs={{0,1},{1,2},{2,3},{3,0},{4,5},{5,6},{6,7},{7,4},{8,9},{9,10},{10,1... | collective-permute-start | bytes 995336 | tf_op jit(solution)/shard_map/ppermute | solution.py:297
  145.1 15.7 %collective-permute-start.41 = (bf16[216,768]{1,0:T(8,128)(2,1)S(1)}, bf16[216,768]{1,0:T(8,128)(2,1)S(1)}, u32[]{:S(2)}, u32[]{:S(2)}) collective-permute-start(bf16[216,768]{1,0:T(8,128)(2,1)S(1)} %collective-permute-done.40), channel_id=1, source_target_pairs={{0,1},{1,2},{2,3},{3,0},{4,5},{5,6},{6,7},{7,4},{8,9},{9,10},{10,1... | collective-permute-start | bytes 995336 | tf_op jit(solution)/shard_map/ppermute | solution.py:297
  146.2 17.6 %collective-permute-start.13 = (bf16[256,768]{1,0:T(8,128)(2,1)S(1)}, bf16[256,768]{1,0:T(8,128)(2,1)S(1)}, u32[]{:S(2)}, u32[]{:S(2)}) collective-permute-start(bf16[256,768]{1,0:T(8,128)(2,1)S(1)} %maximum_select_fusion.29), channel_id=1, source_target_pairs={{0,4},{4,0},{1,5},{5,1},{2,6},{6,2},{3,7},{7,3},{8,12},{12,8},{9,1... | collective-permute-start | bytes 1179656 | tf_op jit(solution)/shard_map/ppermute | solution.py:234
  152.7 40.5 %collective-permute-start.2 = (bf16[512,768]{1,0:T(8,128)(2,1)S(1)}, bf16[512,768]{1,0:T(8,128)(2,1)S(1)}, u32[]{:S(2)}, u32[]{:S(2)}) collective-permute-start(bf16[512,768]{1,0:T(8,128)(2,1)S(1)} %maximum_select_fusion.22), channel_id=1, source_target_pairs={{0,4},{4,0},{1,5},{5,1},{2,6},{6,2},{3,7},{7,3},{8,12},{12,8},{9,1... | collective-permute-start | bytes 2359304 | tf_op jit(solution)/shard_map/ppermute | solution.py:234
  161.0 26.7 %collective-permute-start.20 = (bf16[3,120,768]{2,1,0:T(8,128)(2,1)S(1)}, bf16[3,120,768]{2,1,0:T(8,128)(2,1)S(1)}, u32[]{:S(2)}, u32[]{:S(2)}) collective-permute-start(bf16[3,120,768]{2,1,0:T(8,128)(2,1)S(1)} %get-tuple-element.157), channel_id=1, source_target_pairs={{0,16},{16,0},{1,17},{17,1},{2,18},{18,2},{3,19},{19,3},{4,20},{20... | collective-permute-start | bytes 1658888 | tf_op jit(solution)/shard_map/ppermute | solution.py:234
  178.3 41.9 %collective-permute-start.24 = (bf16[3,192,768]{2,1,0:T(8,128)(2,1)}, bf16[3,192,768]{2,1,0:T(8,128)(2,1)}, u32[]{:S(2)}, u32[]{:S(2)}) collective-permute-start(bf16[3,192,768]{2,1,0:T(8,128)(2,1)} %bitcast.53), channel_id=1, source_target_pairs={{0,16},{16,0},{1,17},{17,1},{2,18},{18,2},{3,19},{19,3},{4,20},{20... | collective-permute-start | bytes 2654216 | tf_op jit(solution)/shard_map/ppermute | solution.py:234
  183.3 42.2 %collective-permute-start.46 = (bf16[3,192,768]{2,1,0:T(8,128)(2,1)}, bf16[3,192,768]{2,1,0:T(8,128)(2,1)}, u32[]{:S(2)}, u32[]{:S(2)}) collective-permute-start(bf16[3,192,768]{2,1,0:T(8,128)(2,1)} %bitcast.108), channel_id=1, source_target_pairs={{0,16},{16,0},{1,17},{17,1},{2,18},{18,2},{3,19},{19,3},{4,20},{20... | collective-permute-start | bytes 2654216 | tf_op jit(solution)/shard_map/ppermute | solution.py:234
  188.9 46.8 %collective-permute-start.21 = (bf16[3,240,768]{2,1,0:T(8,128)(2,1)}, bf16[3,240,768]{2,1,0:T(8,128)(2,1)}, u32[]{:S(2)}, u32[]{:S(2)}) collective-permute-start(bf16[3,240,768]{2,1,0:T(8,128)(2,1)} %bitcast.31), channel_id=1, source_target_pairs={{0,8},{8,0},{1,9},{9,1},{2,10},{10,2},{3,11},{11,3},{4,12},{12,4},... | collective-permute-start | bytes 3317768 | tf_op jit(solution)/shard_map/ppermute | solution.py:234
  212.9 25.8 %collective-permute-start.43 = (bf16[3,240,768]{2,1,0:T(8,128)(2,1)}, bf16[3,240,768]{2,1,0:T(8,128)(2,1)S(1)}, u32[]{:S(2)}, u32[]{:S(2)}) collective-permute-start(bf16[3,240,768]{2,1,0:T(8,128)(2,1)} %bitcast.574), channel_id=1, source_target_pairs={{0,8},{8,0},{1,9},{9,1},{2,10},{10,2},{3,11},{11,3},{4,12},{12,4},... | collective-permute-start | bytes 3317768 | tf_op jit(solution)/shard_map/ppermute | solution.py:234
  222.3 20.5 %collective-permute-start.25 = (bf16[3,384,768]{2,1,0:T(8,128)(2,1)S(1)}, bf16[3,384,768]{2,1,0:T(8,128)(2,1)S(1)}, u32[]{:S(2)}, u32[]{:S(2)}) collective-permute-start(bf16[3,384,768]{2,1,0:T(8,128)(2,1)S(1)} %bitcast.548), channel_id=1, source_target_pairs={{0,4},{4,0},{1,5},{5,1},{2,6},{6,2},{3,7},{7,3},{8,12},{12,8},{9,1... | collective-permute-start | bytes 5308424 | tf_op jit(solution)/shard_map/ppermute | solution.py:234
  227.5 16.5 %collective-permute-start.47 = (bf16[3,384,768]{2,1,0:T(8,128)(2,1)S(1)}, bf16[3,384,768]{2,1,0:T(8,128)(2,1)S(1)}, u32[]{:S(2)}, u32[]{:S(2)}) collective-permute-start(bf16[3,384,768]{2,1,0:T(8,128)(2,1)S(1)} %bitcast.549), channel_id=1, source_target_pairs={{0,4},{4,0},{1,5},{5,1},{2,6},{6,2},{3,7},{7,3},{8,12},{12,8},{9,1... | collective-permute-start | bytes 5308424 | tf_op jit(solution)/shard_map/ppermute | solution.py:234
  239.3 22.4 %collective-permute-start.44 = (bf16[3,480,768]{2,1,0:T(8,128)(2,1)S(1)}, bf16[3,480,768]{2,1,0:T(8,128)(2,1)S(1)}, u32[]{:S(2)}, u32[]{:S(2)}) collective-permute-start(bf16[3,480,768]{2,1,0:T(8,128)(2,1)S(1)} %bitcast.542), channel_id=1, source_target_pairs={{0,4},{4,0},{1,5},{5,1},{2,6},{6,2},{3,7},{7,3},{8,12},{12,8},{9,1... | collective-permute-start | bytes 6635528 | tf_op jit(solution)/shard_map/ppermute | solution.py:234
  339.1 64.4 %collective-permute-start.48 = (bf16[384,768]{1,0:T(8,128)(2,1)}, bf16[384,768]{1,0:T(8,128)(2,1)}, u32[]{:S(2)}, u32[]{:S(2)}) collective-permute-start(bf16[384,768]{1,0:T(8,128)(2,1)} %fusion.36), channel_id=1, source_target_pairs={{2,4},{4,2},{3,5},{5,3},{10,12},{12,10},{11,13},{13,11},{18,20},{2... | collective-permute-start | bytes 1769480 | tf_op jit(solution)/shard_map/ppermute | solution.py:292
  344.2 23.6 %collective-permute-start.57 = (bf16[128,192]{1,0:T(8,128)(2,1)}, bf16[128,192]{1,0:T(8,128)(2,1)}, u32[]{:S(2)}, u32[]{:S(2)}) collective-permute-start(bf16[128,192]{1,0:T(8,128)(2,1)} %bitcast.132), channel_id=1, source_target_pairs={{0,5},{1,4},{4,1},{5,0},{2,7},{3,6},{6,3},{7,2},{8,13},{9,12},{12,... | collective-permute-start | bytes 147464 | tf_op jit(solution)/shard_map/ppermute | solution.py:234
  344.9 23.1 %collective-permute-start.56 = (bf16[128,192]{1,0:T(8,128)(2,1)}, bf16[128,192]{1,0:T(8,128)(2,1)}, u32[]{:S(2)}, u32[]{:S(2)}) collective-permute-start(bf16[128,192]{1,0:T(8,128)(2,1)} %bitcast.131), channel_id=1, source_target_pairs={{0,4},{4,0},{1,5},{5,1},{2,6},{6,2},{3,7},{7,3},{8,12},{12,8},{9,1... | collective-permute-start | bytes 147464 | tf_op jit(solution)/shard_map/ppermute | solution.py:234
  346.9 22.6 %collective-permute-start.55 = (bf16[128,192]{1,0:T(8,128)(2,1)}, bf16[128,192]{1,0:T(8,128)(2,1)}, u32[]{:S(2)}, u32[]{:S(2)}) collective-permute-start(bf16[128,192]{1,0:T(8,128)(2,1)} %bitcast.130), channel_id=1, source_target_pairs={{0,1},{1,0},{2,3},{3,2},{4,5},{5,4},{6,7},{7,6},{8,9},{9,8},{10,11... | collective-permute-start | bytes 147464 | tf_op jit(solution)/shard_map/ppermute | solution.py:234
  353.5 24.9 %collective-permute-start.52 = (bf16[256,192]{1,0:T(8,128)(2,1)}, bf16[256,192]{1,0:T(8,128)(2,1)}, u32[]{:S(2)}, u32[]{:S(2)}) collective-permute-start(bf16[256,192]{1,0:T(8,128)(2,1)} %bitcast.603), channel_id=1, source_target_pairs={{0,5},{1,4},{4,1},{5,0},{2,7},{3,6},{6,3},{7,2},{8,13},{9,12},{12,... | collective-permute-start | bytes 294920 | tf_op jit(solution)/shard_map/ppermute | solution.py:234
  369.6 35.4 %collective-permute-start.91 = (bf16[2,2,96,768]{3,2,1,0:T(8,128)(2,1)}, bf16[2,2,96,768]{3,2,1,0:T(8,128)(2,1)}, u32[]{:S(2)}, u32[]{:S(2)}) collective-permute-start(bf16[2,2,96,768]{3,2,1,0:T(8,128)(2,1)} %dynamic-slice_bitcast_fusion.12), channel_id=1, source_target_pairs={{0,4},{4,0},{1,5},{5,1},{2,6},{6,2},{3,7},{7,3},{8,12},{12,8},{9,1... | collective-permute-start | bytes 1769480 | tf_op jit(solution)/shard_map/ppermute | solution.py:234
  378.5 230.1 %collective-permute-start.103 = (bf16[2,2,96,3072]{3,2,1,0:T(8,128)(2,1)}, bf16[2,2,96,3072]{3,2,1,0:T(8,128)(2,1)}, u32[]{:S(2)}, u32[]{:S(2)}) collective-permute-start(bf16[2,2,96,3072]{3,2,1,0:T(8,128)(2,1)} %dynamic-slice_bitcast_fusion), channel_id=1, source_target_pairs={{0,4},{4,0},{1,5},{5,1},{2,6},{6,2},{3,7},{7,3},{8,12},{12,8},{9,1... | collective-permute-start | bytes 7077896 | tf_op jit(solution)/shard_map/ppermute | solution.py:234
  378.5 240.2 %collective-permute-start.115 = (bf16[2,2,96,3072]{3,2,0,1:T(8,128)(2,1)}, bf16[2,2,96,3072]{3,2,0,1:T(8,128)(2,1)}, u32[]{:S(2)}, u32[]{:S(2)}) collective-permute-start(bf16[2,2,96,3072]{3,2,0,1:T(8,128)(2,1)} %bitcast.470), channel_id=1, source_target_pairs={{0,4},{4,0},{1,5},{5,1},{2,6},{6,2},{3,7},{7,3},{8,12},{12,8},{9,1... | collective-permute-start | bytes 7077896 | tf_op jit(solution)/shard_map/ppermute | solution.py:234
  380.1 21.9 %collective-permute-start.58 = (bf16[2,128,768]{2,1,0:T(8,128)(2,1)}, bf16[2,128,768]{2,1,0:T(8,128)(2,1)}, u32[]{:S(2)}, u32[]{:S(2)}) collective-permute-start(bf16[2,128,768]{2,1,0:T(8,128)(2,1)} %dynamic-slice_bitcast_fusion.17), channel_id=1, source_target_pairs={{0,4},{4,0},{1,5},{5,1},{2,6},{6,2},{3,7},{7,3},{8,12},{12,8},{9,1... | collective-permute-start | bytes 1179656 | tf_op jit(solution)/shard_map/ppermute | solution.py:234
  401.9 23.9 %collective-permute-start.53 = (bf16[2,256,768]{2,1,0:T(8,128)(2,1)S(1)}, bf16[2,256,768]{2,1,0:T(8,128)(2,1)S(1)}, u32[]{:S(2)}, u32[]{:S(2)}) collective-permute-start(bf16[2,256,768]{2,1,0:T(8,128)(2,1)S(1)} %dynamic-slice_bitcast_fusion.7), channel_id=1, source_target_pairs={{0,4},{4,0},{1,5},{5,1},{2,6},{6,2},{3,7},{7,3},{8,12},{12,8},{9,1... | collective-permute-start | bytes 2359304 | tf_op jit(solution)/shard_map/ppermute | solution.py:234
  434.9 40.1 %collective-permute-start.54 = (bf16[256,768]{1,0:T(8,128)(2,1)}, bf16[256,768]{1,0:T(8,128)(2,1)}, u32[]{:S(2)}, u32[]{:S(2)}) collective-permute-start(bf16[256,768]{1,0:T(8,128)(2,1)} %fusion.60), channel_id=1, source_target_pairs={{0,1},{1,0},{2,3},{3,2},{4,5},{5,4},{6,7},{7,6},{8,9},{9,8},{10,11... | collective-permute-start | bytes 1179656 | tf_op jit(solution)/shard_map/ppermute | solution.py:234
  435.8 28.9 %collective-permute-start.80 = (bf16[2,96,576]{2,1,0:T(8,128)(2,1)S(1)}, bf16[2,96,576]{2,1,0:T(8,128)(2,1)}, u32[]{:S(2)}, u32[]{:S(2)}) collective-permute-start(bf16[2,96,576]{2,1,0:T(8,128)(2,1)S(1)} %slice.487), channel_id=1, source_target_pairs={{2,0},{4,6},{3,1},{5,7},{10,8},{12,14},{11,9},{13,15},{18,16},{20,... | collective-permute-start | bytes 663560 | tf_op jit(solution)/shard_map/ppermute | solution.py:533
  531.9 28.5 %collective-permute-start.85 = (bf16[2,2,96,768]{3,2,1,0:T(8,128)(2,1)}, bf16[2,2,96,768]{3,2,1,0:T(8,128)(2,1)}, u32[]{:S(2)}, u32[]{:S(2)}) collective-permute-start(bf16[2,2,96,768]{3,2,1,0:T(8,128)(2,1)} %dynamic-slice_bitcast_fusion.13), channel_id=1, source_target_pairs={{0,4},{4,0},{1,5},{5,1},{2,6},{6,2},{3,7},{7,3},{8,12},{12,8},{9,1... | collective-permute-start | bytes 1769480 | tf_op jit(solution)/shard_map/ppermute | solution.py:234
  532.6 26.4 %collective-permute-start.68 = (bf16[2,128,768]{2,1,0:T(8,128)(2,1)}, bf16[2,128,768]{2,1,0:T(8,128)(2,1)}, u32[]{:S(2)}, u32[]{:S(2)}) collective-permute-start(bf16[2,128,768]{2,1,0:T(8,128)(2,1)} %dynamic-slice_bitcast_fusion.16), channel_id=1, source_target_pairs={{0,4},{4,0},{1,5},{5,1},{2,6},{6,2},{3,7},{7,3},{8,12},{12,8},{9,1... | collective-permute-start | bytes 1179656 | tf_op jit(solution)/shard_map/ppermute | solution.py:234
  549.0 34.4 %collective-permute-start.63 = (bf16[2,256,768]{2,1,0:T(8,128)(2,1)}, bf16[2,256,768]{2,1,0:T(8,128)(2,1)}, u32[]{:S(2)}, u32[]{:S(2)}) collective-permute-start(bf16[2,256,768]{2,1,0:T(8,128)(2,1)} %dynamic-slice_bitcast_fusion.6), channel_id=1, source_target_pairs={{0,4},{4,0},{1,5},{5,1},{2,6},{6,2},{3,7},{7,3},{8,12},{12,8},{9,1... | collective-permute-start | bytes 2359304 | tf_op jit(solution)/shard_map/ppermute | solution.py:234
  560.4 15.0 %collective-permute-start.69 = (bf16[128,768]{1,0:T(8,128)(2,1)S(1)}, bf16[128,768]{1,0:T(8,128)(2,1)S(1)}, u32[]{:S(2)}, u32[]{:S(2)}) collective-permute-start(bf16[128,768]{1,0:T(8,128)(2,1)S(1)} %fusion.87), channel_id=1, source_target_pairs={{0,1},{1,0},{2,3},{3,2},{4,5},{5,4},{6,7},{7,6},{8,9},{9,8},{10,11... | collective-permute-start | bytes 589832 | tf_op jit(solution)/shard_map/ppermute | solution.py:234
  575.4 204.8 %collective-permute-start.97 = (bf16[2,2,96,3072]{3,2,1,0:T(8,128)(2,1)}, bf16[2,2,96,3072]{3,2,1,0:T(8,128)(2,1)}, u32[]{:S(2)}, u32[]{:S(2)}) collective-permute-start(bf16[2,2,96,3072]{3,2,1,0:T(8,128)(2,1)} %dynamic-slice_bitcast_fusion.1), channel_id=1, source_target_pairs={{0,4},{4,0},{1,5},{5,1},{2,6},{6,2},{3,7},{7,3},{8,12},{12,8},{9,1... | collective-permute-start | bytes 7077896 | tf_op jit(solution)/shard_map/ppermute | solution.py:234
  581.6 203.2 %collective-permute-start.109 = (bf16[2,2,96,3072]{3,2,0,1:T(8,128)(2,1)}, bf16[2,2,96,3072]{3,2,0,1:T(8,128)(2,1)}, u32[]{:S(2)}, u32[]{:S(2)}) collective-permute-start(bf16[2,2,96,3072]{3,2,0,1:T(8,128)(2,1)} %bitcast.471), channel_id=1, source_target_pairs={{0,4},{4,0},{1,5},{5,1},{2,6},{6,2},{3,7},{7,3},{8,12},{12,8},{9,1... | collective-permute-start | bytes 7077896 | tf_op jit(solution)/shard_map/ppermute | solution.py:234
  608.5 29.2 %collective-permute-start.64 = (bf16[256,768]{1,0:T(8,128)(2,1)}, bf16[256,768]{1,0:T(8,128)(2,1)}, u32[]{:S(2)}, u32[]{:S(2)}) collective-permute-start(bf16[256,768]{1,0:T(8,128)(2,1)} %fusion.61), channel_id=1, source_target_pairs={{0,1},{1,0},{2,3},{3,2},{4,5},{5,4},{6,7},{7,6},{8,9},{9,8},{10,11... | collective-permute-start | bytes 1179656 | tf_op jit(solution)/shard_map/ppermute | solution.py:234
  608.6 17.3 %collective-permute-start.73 = (bf16[2,96,576]{2,1,0:T(8,128)(2,1)S(1)}, bf16[2,96,576]{2,1,0:T(8,128)(2,1)S(1)}, u32[]{:S(2)}, u32[]{:S(2)}) collective-permute-start(bf16[2,96,576]{2,1,0:T(8,128)(2,1)S(1)} %slice.485), channel_id=1, source_target_pairs={{2,0},{4,6},{3,1},{5,7},{10,8},{12,14},{11,9},{13,15},{18,16},{20,... | collective-permute-start | bytes 663560 | tf_op jit(solution)/shard_map/ppermute | solution.py:533
  624.6 150.2 %collective-permute-start.104 = (bf16[2,96,3072]{2,1,0:T(8,128)(2,1)}, bf16[2,96,3072]{2,1,0:T(8,128)(2,1)}, u32[]{:S(2)}, u32[]{:S(2)}) collective-permute-start(bf16[2,96,3072]{2,1,0:T(8,128)(2,1)} %dynamic-slice_bitcast_fusion.4), channel_id=1, source_target_pairs={{0,16},{16,0},{1,17},{17,1},{2,18},{18,2},{3,19},{19,3},{4,20},{20... | collective-permute-start | bytes 3538952 | tf_op jit(solution)/shard_map/ppermute | solution.py:234
  636.0 142.1 %collective-permute-start.116 = (bf16[2,96,3072]{2,1,0:T(8,128)(2,1)}, bf16[2,96,3072]{2,1,0:T(8,128)(2,1)}, u32[]{:S(2)}, u32[]{:S(2)}) collective-permute-start(bf16[2,96,3072]{2,1,0:T(8,128)(2,1)} %dynamic-slice_bitcast_fusion.2), channel_id=1, source_target_pairs={{0,8},{8,0},{1,9},{9,1},{2,10},{10,2},{3,11},{11,3},{4,12},{12,4},... | collective-permute-start | bytes 3538952 | tf_op jit(solution)/shard_map/ppermute | solution.py:234
  641.9 131.1 %collective-permute-start.70 = (bf16[384,768]{1,0:T(8,128)(2,1)}, bf16[384,768]{1,0:T(8,128)(2,1)S(1)}, u32[]{:S(2)}, u32[]{:S(2)}) collective-permute-start(bf16[384,768]{1,0:T(8,128)(2,1)} %fusion.43), channel_id=1, source_target_pairs={{2,4},{4,2},{3,5},{5,3},{10,12},{12,10},{11,13},{13,11},{18,20},{2... | collective-permute-start | bytes 1769480 | tf_op jit(solution)/shard_map/ppermute | solution.py:292
  783.6 35.4 %collective-permute-start.98 = (bf16[2,96,3072]{2,1,0:T(8,128)(2,1)S(1)}, bf16[2,96,3072]{2,1,0:T(8,128)(2,1)S(1)}, u32[]{:S(2)}, u32[]{:S(2)}) collective-permute-start(bf16[2,96,3072]{2,1,0:T(8,128)(2,1)S(1)} %dynamic-slice_bitcast_fusion.5), channel_id=1, source_target_pairs={{0,16},{16,0},{1,17},{17,1},{2,18},{18,2},{3,19},{19,3},{4,20},{20... | collective-permute-start | bytes 3538952 | tf_op jit(solution)/shard_map/ppermute | solution.py:234
  787.8 32.0 %collective-permute-start.110 = (bf16[2,96,3072]{2,1,0:T(8,128)(2,1)S(1)}, bf16[2,96,3072]{2,1,0:T(8,128)(2,1)S(1)}, u32[]{:S(2)}, u32[]{:S(2)}) collective-permute-start(bf16[2,96,3072]{2,1,0:T(8,128)(2,1)S(1)} %dynamic-slice_bitcast_fusion.3), channel_id=1, source_target_pairs={{0,8},{8,0},{1,9},{9,1},{2,10},{10,2},{3,11},{11,3},{4,12},{12,4},... | collective-permute-start | bytes 3538952 | tf_op jit(solution)/shard_map/ppermute | solution.py:234
  (251 other events, 2614.8 us)
Sparse Core Ops, SparseCore 0:
  640.8 125.4 all-reduce.3

commit v2 on v1

--- a/solution.py
+++ b/solution.py
@@ -28,7 +28,7 @@
     return jnp.maximum(v, 0.0) + jnp.log(1.0 + jnp.exp(-jnp.abs(v)))
 
 
-def fwd_one(x_ref, o_ref, lse_ref, carry_ref):
+def fwd_one(x_ref, o_ref, lse_ref, carry_ref, done=None):
     size = x_ref.shape[0]
     nh = (x_ref.shape[1] - 2 * HD) // (3 * HD)
     w = nh * HD
@@ -84,6 +84,8 @@
             o_ref[rows, h * HD : (h + 1) * HD] = (acc / total).astype(jnp.bfloat16)
             stats = jnp.where(lanes == h, top + jnp.log(total), stats)
         lse_ref[:, rows] = jnp.transpose(stats)[:8]
+        if done is not None:
+            done(b)
 
 
 def bwd_one(x_ref, g_ref, o_ref, lse_ref, carry_ref, d_ref, acc, kt):
@@ -224,6 +226,335 @@
     )(x, g, o, lse, carry)
 
 
+class Group:
+    def __init__(self, core):
+        self.core = core
+        self.c = lax.axis_index(core)
+        self.zl = lax.axis_index("zl")
+        self.me = 2 * self.c + self.zl
+
+    def peer(self, delta):
+        return {self.core: self.c ^ (delta >> 1), "zl": self.zl ^ (delta & 1)}
+
+    def member(self, m):
+        return {self.core: m >> 1, "zl": m & 1}
+
+    def greet(self, deltas):
+        barrier = pltpu.get_barrier_semaphore()
+        for delta in deltas:
+            pl.semaphore_signal(
+                barrier, inc=1, device_id=self.peer(delta), device_id_type=pl.DeviceIdType.MESH
+            )
+        pl.semaphore_wait(barrier, len(deltas))
+
+
+def send(src, dst, ssem, rsem, device):
+    return pltpu.make_async_remote_copy(
+        src_ref=src,
+        dst_ref=dst,
+        send_sem=ssem,
+        recv_sem=rsem,
+        device_id=device,
+        device_id_type=pl.DeviceIdType.MESH,
+    )
+
+
+def fwd_x(core, xl, xs, att, ol, os, lsel, lses, cl, cs, land, ssem, rsem):
+    group = Group(core)
+    nl, ns = xl.shape[0] // 4, xs.shape[0] // 4
+    group.greet((1, 2, 3))
+
+    def copy(k, m):
+        src, n, at = ((ol, nl, 0), (os, ns, nl))[k]
+        return send(
+            src.at[pl.ds(m * n, n)],
+            land.at[group.me, pl.ds(at, n)],
+            ssem.at[k, m],
+            rsem.at[k, group.me],
+            group.member(m),
+        )
+
+    def arrived(k, m):
+        src, n, at = ((ol, nl, 0), (os, ns, nl))[k]
+        return send(
+            src.at[pl.ds(0, n)], land.at[m, pl.ds(at, n)], ssem.at[k, m], rsem.at[k, m], group.member(m)
+        )
+
+    def start(k, m):
+        src, n, at = ((ol, nl, 0), (os, ns, nl))[k]
+
+        @pl.when(group.me != m)
+        def _():
+            copy(k, m).start()
+
+        @pl.when(group.me == m)
+        def _():
+            land[m, at : at + n] = src[m * n : (m + 1) * n]
+
+    def started(k, n):
+        def done(b):
+            for m in range(b * BR // n, (b + 1) * BR // n):
+                start(k, m)
+
+        return done
+
+    fwd_one(xs, os, lses, cs, started(1, ns))
+    fwd_one(xl, ol, lsel, cl, started(0, nl))
+    w = ol.shape[1]
+    for m in range(4):
+
+        @pl.when(group.me != m)
+        def _():
+            for k in range(2):
+                copy(k, m).wait_send()
+                arrived(k, m).wait_recv()
+
+    for m in range(4):
+        att[:, m * w : (m + 1) * w] = land[m]
+
+
+def bwd_x(core, xl, xs, go, ol, os, lsel, lses, cl, cs, dl, ds, acc, kt, out, gl, gs, ssem, rsem):
+    group = Group(core)
+    nl, ns = xl.shape[0] // 4, xs.shape[0] // 4
+    w = ol.shape[1]
+    for m in range(4):
+        out[m] = go[:, m * w : (m + 1) * w]
+    group.greet((1, 2, 3))
+
+    def part(k):
+        return ((gl, nl, 0), (gs, ns, nl))[k]
+
+    def copy(k, m):
+        dst, n, at = part(k)
+        return send(
+            out.at[m, pl.ds(at, n)],
+            dst.at[pl.ds(pl.multiple_of(group.me * n, 16), n)],
+            ssem.at[k, m],
+            rsem.at[k, group.me],
+            group.member(m),
+        )
+
+    def arrived(k, m):
+        dst, n, at = part(k)
+        return send(
+            out.at[m, pl.ds(at, n)], dst.at[pl.ds(m * n, n)], ssem.at[k, m], rsem.at[k, m], group.member(m)
+        )
+
+    for k in (1, 0):
+        for m in range(4):
+            dst, n, at = part(k)
+
+            @pl.when(group.me != m)
+            def _():
+                copy(k, m).start()
+
+            @pl.when(group.me == m)
+            def _():
+                dst[m * n : (m + 1) * n] = out[m, at : at + n]
+
+    for k in (1, 0):
+        for m in range(4):
+
+            @pl.when(group.me != m)
+            def _():
+                arrived(k, m).wait_recv()
+
+        if k:
+            bwd_one(xs, gs, os, lses, cs, ds, acc, kt)
+        else:
+            bwd_one(xl, gl, ol, lsel, cl, dl, acc, kt)
+    for m in range(4):
+
+        @pl.when(group.me != m)
+        def _():
+            for k in range(2):
+                copy(k, m).wait_send()
+
+
+def norm_rows(v):
+    mean = jnp.mean(v, axis=-1, keepdims=True)
+    cen = v - mean
+    inv = lax.rsqrt(jnp.mean(cen * cen, axis=-1, keepdims=True) + 1e-05)
+    return cen * inv, inv
+
+
+def project_x(core, resid, gain, shift, w, bias, nl_ref, ns_ref, pl_ref, ps_ref, ssem, rsem):
+    group = Group(core)
+    nl, ns = nl_ref.shape[0] // 4, ns_ref.shape[0] // 4
+    half = nl // 2
+    parts = ((ns_ref, ps_ref, ns, 0, ns, nl), (nl_ref, pl_ref, nl, 0, half, 0), (nl_ref, pl_ref, nl, half, half, half))
+
+    def rows(k, m):
+        ref, _, n, at, size, _ = parts[k]
+        return ref.at[pl.ds(pl.multiple_of(m * n + at, 16), size)]
+
+    def copy(k, j, m, delta):
+        return send(rows(k, m), rows(k, m), ssem.at[k, j], rsem.at[k, j], group.peer(delta))
+
+    def compute(k, m):
+        ref, out, n, at, size, _ = parts[k]
+        here = pl.ds(pl.multiple_of(m * n + at, 16), size)
+        out[here] = (mm(ref[here], w[...]) + bias[...]).astype(jnp.bfloat16)
+
+    me = group.me
+    for k in range(3):
+        ref, _, n, at, size, src = parts[k]
+        hat, _ = norm_rows(resid[src : src + size])
+        ref[pl.ds(pl.multiple_of(me * n + at, 16), size)] = (hat * gain[...] + shift[...]).astype(
+            jnp.bfloat16
+        )
+        if k == 0:
+            group.greet((1, 2))
+        copy(k, 0, me, 1).start()
+        copy(k, 1, me, 2).start()
+    for k in range(3):
+        compute(k, me)
+    for k in range(3):
+        copy(k, 1, me ^ 2, 2).wait_recv()
+        compute(k, me ^ 2)
+    for k in range(3):
+        copy(k, 0, me ^ 1, 1).wait_recv()
+        copy(k, 2, me ^ 1, 2).start()
+        compute(k, me ^ 1)
+    for k in range(3):
+        copy(k, 2, me ^ 3, 2).wait_recv()
+        compute(k, me ^ 3)
+    for k in range(3):
+        copy(k, 0, me, 1).wait_send()
+        copy(k, 1, me, 2).wait_send()
+        copy(k, 2, me ^ 1, 2).wait_send()
+
+
+def collect_x(core, dl, ds, w, resid, gain, gmid, g_ref, sums, mine, out, got, ssem, rsem):
+    group = Group(core)
+    nl, ns = dl.shape[0] // 4, ds.shape[0] // 4
+    me = group.me
+
+    def partial(m):
+        a = mm(dl[pl.ds(pl.multiple_of(m * nl, 16), nl)], w[...], NT)
+        b = mm(ds[pl.ds(pl.multiple_of(m * ns, 16), ns)], w[...], NT)
+        return jnp.concatenate([a, b], axis=0)
+
+    def copy(k, delta):
+        return send(out.at[k], got.at[k], ssem.at[k], rsem.at[k], group.peer(delta))
+
+    out[0] = partial(me ^ 3).astype(jnp.bfloat16)
+    group.greet((1, 2))
+    copy(0, 2).start()
+    mine[...] = partial(me ^ 1)
+    copy(0, 2).wait_recv()
+    out[1] = (mine[...] + got[0].astype(jnp.float32)).astype(jnp.bfloat16)
+    copy(1, 1).start()
+    out[2] = partial(me ^ 2).astype(jnp.bfloat16)
+    copy(2, 2).start()
+    mine[...] = partial(me)
+    hat, inv = norm_rows(resid[...])
+    copy(2, 2).wait_recv()
+    copy(1, 1).wait_recv()
+    grad = mine[...] + got[2].astype(jnp.float32) + got[1].astype(jnp.float32)
+    gh = grad * gain[...]
+    a = jnp.mean(gh, axis=-1, keepdims=True)
+    b = jnp.mean(gh * hat, axis=-1, keepdims=True)
+    g_ref[...] = gmid[...] + inv * (gh - a - hat * b)
+    sums[0:1] = jnp.sum(grad * hat, axis=0, keepdims=True)
+    sums[1:2] = jnp.sum(grad, axis=0, keepdims=True)
+    copy(0, 2).wait_send()
+    copy(1, 1).wait_send()
+    copy(2, 2).wait_send()
+
+
+def shape(dims, dtype):
+    return jax.ShapeDtypeStruct(tuple(dims), dtype)
+
+
+def remote(kernel, core, outs, scratch, ident, name, args, flops=10**9):
+    return pl.pallas_call(
+        functools.partial(kernel, core),
+        out_shape=tuple(outs),
+        in_specs=[VMEM] * len(args),
+        out_specs=(VMEM,) * len(outs),
+        scratch_shapes=scratch,
+        compiler_params=pltpu.CompilerParams(
+            vmem_limit_bytes=LIMIT, collective_id=ident, has_side_effects=True
+        ),
+        cost_estimate=pl.CostEstimate(flops=flops, bytes_accessed=10**7, transcendentals=10**6),
+        name=name,
+    )(*args)
+
+
+DMA = pltpu.SemaphoreType.DMA
+
+
+def attend_fwd_x(core, xl, xs):
+    w = (xl.shape[1] - 2 * HD) // 3
+    rows = (xl.shape[0] + xs.shape[0]) // 4
+    outs = [shape((rows, 4 * w), jnp.bfloat16)]
+    outs += [shape((x.shape[0], w), jnp.bfloat16) for x in (xl, xs)]
+    outs += [shape((8, x.shape[0]), jnp.float32) for x in (xl, xs)] * 2
+    scratch = [pltpu.VMEM((4, rows, w), jnp.bfloat16), DMA((2, 4)), DMA((2, 4))]
+    return remote(fwd_x, core, outs, scratch, 1, "attend_fwd_x", (xl, xs), 10**10)
+
+
+def attend_bwd_x(core, xl, xs, go, ol, os, lsel, lses, cl, cs):
+    w = ol.shape[1]
+    nh = w // HD
+    size = xl.shape[0]
+    outs = [shape(x.shape, jnp.bfloat16) for x in (xl, xs)]
+    scratch = [
+        pltpu.VMEM((2 * nh + 1, size, HD), jnp.float32),
+        pltpu.VMEM((nh + 1, HD, size), jnp.bfloat16),
+        pltpu.VMEM((4, go.shape[0], w), jnp.bfloat16),
+        pltpu.VMEM(ol.shape, jnp.bfloat16),
+        pltpu.VMEM(os.shape, jnp.bfloat16),
+        DMA((2, 4)),
+        DMA((2, 4)),
+    ]
+    args = (xl, xs, go, ol, os, lsel, lses, cl, cs)
+    return remote(bwd_x, core, outs, scratch, 2, "attend_bwd_x", args, 2 * 10**10)
+
+
+def project(core, resid, gain, shift, w, bias, nl, ns):
+    d, n = w.shape
+    outs = [shape((4 * nl, d), jnp.bfloat16), shape((4 * ns, d), jnp.bfloat16)]
+    outs += [shape((4 * nl, n), jnp.bfloat16), shape((4 * ns, n), jnp.bfloat16)]
+    args = (resid, gain[None], shift[None], w, bias[None])
+    return remote(project_x, core, outs, [DMA((3, 3)), DMA((3, 3))], 3, "project_x", args)
+
+
+def collect(core, dl, ds, w, resid, gain, gmid):
+    outs = [shape(resid.shape, jnp.float32), shape((8, w.shape[0]), jnp.float32)]
+    scratch = [
+        pltpu.VMEM(resid.shape, jnp.float32),
+        pltpu.VMEM((3,) + resid.shape, jnp.bfloat16),
+        pltpu.VMEM((3,) + resid.shape, jnp.bfloat16),
+        DMA((3,)),
+        DMA((3,)),
+    ]
+    return remote(collect_x, core, outs, scratch, 4, "collect_x", (dl, ds, w, resid, gain[None], gmid))
+
+
+def total_x(axes, v, out, land, ssem, rsem):
+    barrier = pltpu.get_barrier_semaphore()
+    peers = [{ax: 1 - lax.axis_index(ax)} for ax in axes]
+    for peer in peers:
+        pl.semaphore_signal(barrier, inc=1, device_id=peer, device_id_type=pl.DeviceIdType.MESH)
+    pl.semaphore_wait(barrier, len(peers))
+    land[0] = v[...]
+    n = len(axes)
+    for i, peer in enumerate(peers):
+        copy = send(land.at[i], land.at[n + 1 + i], ssem.at[i], rsem.at[i], peer)
+        copy.start()
+        copy.wait()
+        land[i + 1] = land[i] + land[n + 1 + i]
+    out[...] = land[n]
+
+
+def total(axes, v):
+    n = len(axes)
+    scratch = [pltpu.VMEM((2 * n + 1,) + v.shape, jnp.float32), DMA((n,)), DMA((n,))]
+    return remote(total_x, axes, [shape(v.shape, jnp.float32)], scratch, 5, "total_x", (v,))[0]
+
+
 EPS = 1e-05
 F32 = jnp.float32
 BF = jnp.bfloat16
@@ -376,6 +707,36 @@
             left.remove(ax)
         return v.reshape(-1, n)
 
+    def scatter_all(self, up, down, out):
+        n, e = up.shape[1], out.shape[1]
+        bits = len(self.dims)
+        view = lambda v: v.reshape(*([2] * bits), -1, v.shape[1])
+        mats = [view(up), view(down), view(out)]
+        pos = bits - 1
+        to_send = jnp.concatenate([pick(v, 1 - self.c, pos) for v in mats], axis=-1)
+        got = swap(to_send, self.core)
+        up, down, out = [
+            (pick(v, self.c, pos).astype(F32) + got[..., at : at + v.shape[-1]].astype(F32)).astype(BF)
+            for v, at in zip(mats, (0, n, 2 * n))
+        ]
+        down = jnp.concatenate([down, out], axis=-1)
+        res = []
+        for v, axes in ((up, self.plane), (down, self.plane[::-1])):
+            left = list(self.plane)
+            for ax in axes:
+                i, p = lax.axis_index(ax), left.index(ax)
+                got = swap(pick(v, 1 - i, p), ax)
+                v = (pick(v, i, p).astype(F32) + got.astype(F32)).astype(BF)
+                left.remove(ax)
+            res.append(v)
+        up, down = res
+        rows = up.shape[0]
+        cut = lambda v: v.reshape(rows, self.mp, -1)
+        v = jnp.concatenate([cut(up), cut(down[:, :n]), cut(down[:, n:])], axis=-1)
+        v = self.ring_scatter([pick(v, (self.z - r) % self.mp, 1) for r in range(self.mp)])
+        q = n // self.mp
+        return v[:, :q], v[:, q : 2 * q], v[:, 2 * q :]
+
     def ring_scatter(self, chunks):
         t = chunks[-1]
         for r in range(self.mp - 2, -1, -1):
@@ -410,6 +771,7 @@
     rel_small = jnp.stack([small] + plan.ring_gather(small))
     n_up = layers * ffq
     rel_bup = rel_small[:, :n_up].reshape(mp, layers, ffq).astype(F32)
+    bup = jnp.stack([pick(rel_bup, (plan.z - q) % mp, 0) for q in range(mp)])
     rel_bqv = rel_small[:, n_up:].reshape(mp, layers, 2, heads_w).astype(F32)
     mine = 2 * plan.c + plan.zl
     my_bqv = pick(rel_bqv, (plan.z - mine) % mp, 0)
@@ -426,26 +788,13 @@
         exts.append(jnp.concatenate([quarter, head0], axis=1))
 
     ups, downs, outs = [], [], []
+    order = ("zh", "zl") + dims
     for l in range(layers):
-        po = plan.piece(w_out[l])
-        pu = jnp.concatenate([plan.piece(w_up[l]), po], axis=0)
-        pd = plan.piece(w_down[l])
-        n_out, n_d = po.shape[0], pd.shape[0]
-        both = plan.ring_gather(jnp.concatenate([pu, pd], axis=0))
-        stacked = jnp.stack(both)
-        n_u = pu.shape[0]
-        gu = plan.plane_gather(stacked[:, :n_u], fwd_axes)
-        gd = plan.plane_gather(stacked[:, n_u:], alt_axes)
-        up = gu[:, :, : n_u - n_out].reshape(mp - 1, d_model, ffq)
-        ups.append(jnp.concatenate([w_up[l]] + [up[r] for r in range(mp - 1)], axis=1))
-        out = gu[:, :, n_u - n_out :].reshape(mp - 1, heads_w, d_model)
-        out = jnp.concatenate([w_out[l][None], out], axis=0)
-        outs.append(
-            jnp.concatenate([pick(out, (plan.z - q) % mp, 0) for q in range(mp)], axis=0)
-        )
-        downs.append(
-            jnp.concatenate([w_down[l], gd.reshape((mp - 1) * ffq, d_model)], axis=0)
-        )
+        outs.append(lax.all_gather(plan.piece(w_out[l]), order, axis=0, tiled=True))
+        n_up = ffq // dp
+        piece = lax.dynamic_slice_in_dim(w_up[l], plan.d * n_up, n_up, 1)
+        ups.append(lax.all_gather(jnp.transpose(piece), order, axis=0, tiled=True))
+        downs.append(lax.all_gather(plan.piece(w_down[l]), order, axis=0, tiled=True))
 
     dy = plan.relabel(jnp.concatenate([dy_long[0], dy_short[0]], axis=0))
 
@@ -454,9 +803,6 @@
     saved = []
     shares = []
     for l in range(layers):
-        normed, hat1, inv1 = normalize(resid, gain[l, 0], shift[l, 0])
-        normed = normed.astype(BF)
-        full = [plan.gather(normed[:rl]), plan.gather(normed[rl:])]
         bias = jnp.concatenate(
             [
                 my_bqv[l, 0],
@@ -466,22 +812,24 @@
                 jnp.zeros((HD,), F32),
             ]
         )
-        proj = [(dot(n, exts[l]) + bias).astype(BF) for n in full]
-        att = [attend_fwd(p) for p in proj]
+        full_l, full_s, pj_l, pj_s = project(
+            plan.core, resid, gain[l, 0], shift[l, 0], exts[l], bias, rl, rs
+        )
+        full, proj = (full_l, full_s), (pj_l, pj_s)
+        attended, *att = attend_fwd_x(plan.core, pj_l, pj_s)
         share = jnp.zeros((), F32)
-        for p, a in zip(proj, att):
-            size = p.shape[0]
-            sel = a[2][size // BR]
+        for carry in att[4:]:
+            size = carry.shape[1]
+            sel = carry[size // BR]
             left = (size - 1 - lax.broadcasted_iota(jnp.int32, (size,), 0)).astype(F32)
             share = share + jnp.sum(
                 jax.nn.sigmoid(4.0 * (sel / jnp.maximum(left, 1.0) - limits[l]))
             )
         shares.append(share)
-        attended = jnp.concatenate([plan.to_rows(a[0]) for a in att], axis=0)
         middle = resid + dot(attended, outs[l]) + b_out[l].astype(F32)
         normed2, hat2, inv2 = normalize(middle, gain[l, 1], shift[l, 1])
         normed2 = normed2.astype(BF)
-        upper = dot(normed2, ups[l]) + rel_bup[:, l].reshape(-1)
+        upper = dot(normed2, ups[l], 1, 1) + bup[:, l].reshape(-1)
         active = gelu_both(upper)[0].astype(BF)
         saved.append((resid, middle, full, proj, att, attended, normed2, upper, active))
         resid = middle + dot(active, downs[l]) + b_down[l].astype(F32)
@@ -501,7 +849,7 @@
         w_down_t = dot(gm, active, 0, 0).astype(BF)
         w_up_g = dot(normed2, gu, 0, 0).astype(BF)
         g_bup = jnp.sum(gu.astype(F32), axis=0)
-        gn2 = dot(gu, ups[l], 1, 1)
+        gn2 = dot(gu, ups[l])
         _, hat2, inv2 = normalize(middle, gain[l, 1], shift[l, 1])
         back, g_gain2, g_shift2 = normalize_back(gn2, hat2, inv2, gain[l, 1])
         gmid = g + back
@@ -509,24 +857,14 @@
         ga = gmid.astype(BF)
         go = dot(ga, outs[l], 1, 1).astype(BF)
         w_out_t = dot(ga, attended, 0, 0).astype(BF)
-        gh = [plan.to_heads(go[:rl]), plan.to_heads(go[rl:])]
-        dext = [attend_bwd(p, h, a[0], a[1], a[2]) for p, h, a in zip(proj, gh, att)]
-        gn1 = jnp.concatenate(
-            [plan.scatter(dot(e, exts[l], 1, 1).astype(BF)) for e in dext], axis=0
-        )
+        dext = attend_bwd_x(plan.core, *proj, go, *att)
+        new_g, ln1 = collect(plan.core, *dext, exts[l], resid, gain[l, 0], gmid)
+        g_gain1, g_shift1 = ln1[0], ln1[1]
         w_ext_g = sum(dot(n, e, 0, 0) for n, e in zip(full, dext)).astype(BF)
         g_bext = sum(jnp.sum(e.astype(F32), axis=0) for e in dext)
-        _, hat1, inv1 = normalize(resid, gain[l, 0], shift[l, 0])
-        back, g_gain1, g_shift1 = normalize_back(gn1, hat1, inv1, gain[l, 0])
-        g = gmid + back
-
-        w_up_g = plan.plane_scatter(w_up_g, (plan.core,) + core_rest)
-        w_up_g = plan.ring_scatter([w_up_g[:, r * ffq : (r + 1) * ffq] for r in range(mp)])
-        w_down_t = plan.plane_scatter(w_down_t, (plan.core,) + core_rest[::-1])
-        w_down_t = plan.ring_scatter([w_down_t[:, r * ffq : (r + 1) * ffq] for r in range(mp)])
-        w_out_t = plan.plane_scatter(w_out_t, (plan.core,) + core_rest)
-        w_out_t = w_out_t.reshape(-1, mp, heads_w)
-        w_out_t = plan.ring_scatter([pick(w_out_t, (plan.z - r) % mp, 1) for r in range(mp)])
+        g = new_g
+
+        w_up_g, w_down_t, w_out_t = plan.scatter_all(w_up_g, w_down_t, w_out_t)
         w_ext_g = plan.plane_scatter(w_ext_g, core_rest[::-1])
         w_ext_g = w_ext_g.reshape(2, -1, w_ext_g.shape[1])
         part, zero = w_ext_g[..., : 3 * heads_w], w_ext_g[..., 3 * heads_w :]
@@ -550,8 +888,6 @@
         gq = hot * g_bext[None, :heads_w]
         gv = hot * g_bext[None, 2 * heads_w : 3 * heads_w]
         gq = gq.reshape(-1).at[:HD].add(g_bext[3 * heads_w : 3 * heads_w + HD])
-        g_bup = g_bup.reshape(mp, ffq)
-        g_bup = jnp.stack([pick(g_bup, (plan.z - q) % mp, 0) for q in range(mp)])
         vec[l] = jnp.concatenate(
             [
                 g_gain1, g_gain2, g_shift1, g_shift2, g_bout, g_bdown,
@@ -560,18 +896,19 @@
         )
 
     dx = plan.relabel(g.astype(BF)).astype(F32)
-    total = lax.psum(jnp.stack([vec[l] for l in range(layers)]), dims + ("zh", "zl"))
+    total_v = jnp.stack([vec[l] for l in range(layers)])
+    total_v = total(dims + ("zh", "zl"), total_v.reshape(-1, 128)).reshape(total_v.shape)
     n = d_model
-    g_gain = total[:, : 2 * n].reshape(layers, 2, n)
-    g_bias = total[:, 2 * n : 4 * n].reshape(layers, 2, n)
-    g_bout = total[:, 4 * n : 5 * n]
-    g_bdown = total[:, 5 * n : 6 * n]
+    g_gain = total_v[:, : 2 * n].reshape(layers, 2, n)
+    g_bias = total_v[:, 2 * n : 4 * n].reshape(layers, 2, n)
+    g_bout = total_v[:, 4 * n : 5 * n]
+    g_bdown = total_v[:, 5 * n : 6 * n]
     at = 6 * n
-    g_bqv = total[:, at : at + 2 * mp * heads_w].reshape(layers, 2, mp, heads_w)
+    g_bqv = total_v[:, at : at + 2 * mp * heads_w].reshape(layers, 2, mp, heads_w)
     at += 2 * mp * heads_w
-    g_bup = total[:, at : at + mp * ffq].reshape(layers, mp, ffq)
+    g_bup = total_v[:, at : at + mp * ffq].reshape(layers, mp, ffq)
     at += mp * ffq
-    key_share = total[:, at] / (dp * (rows * mp))
+    key_share = total_v[:, at] / (dp * (rows * mp))
     return (
         y[None, :rl],
         y[None, rl:],

time: 878 us -> 902 us (1.027)
  Pallas kernels: 54.8 us -> 215 us
  starting transfers between devices: 202 us -> 106 us
  other arithmetic: 98 us -> 60.7 us
  matrix products: 77 us -> 92.8 us
  local copies, waits for them, and re-layouts: 102 us -> 90.7 us
    all_gather x0 -> x6, waiting for transfers between devices: none -> 166 us  [the longest x2 106 us: body(): lax.all_gather(plan.piece(w_down[l]), order, axis=0, tiled=True)]
    pallas_call x8 -> x9, Pallas kernels: 54.8 us -> 215 us  [remote(): pl.pallas_call(functools.partial(kernel, core), out_shape=tuple(outs), in...]
    psum x1 -> x0, waiting for transfers between devices: 120 us -> none  [body(): lax.psum(jnp.stack([vec[l] for l in range(layers)]), dims + ('zh', 'zl'))]
    ppermute x80 -> x20, starting transfers between devices: 75 us -> 15.2 us  [swap(): lax.ppermute(v, axes if len(axes) > 1 else axes[0], [(i, count - 1 - i) f...]
    ppermute x27 -> x9, starting transfers between devices: 79.4 us -> 45.2 us  [ring(): lax.ppermute(v, ('zh', 'zl'), [(i, (i + step) % n) for i in range(n)])]
    select_n x48 -> x0, other arithmetic: 33.1 us -> none  [the longest x20 21.9 us: plane_gather(): v = jnp.where(lax.axis_index(ax) == 0, a, b)]
    ppermute x6, waiting for transfers between devices: 29.4 us -> 0.02 us  [relabel(): got = lax.ppermute(v, (self.core, 'zh'), [(1, 2), (2, 1)])]
    convert_element_type x22 -> x4, other arithmetic: 19.7 us -> 2.56 us  [plane_scatter(): v = (pick(v, i, pos).astype(F32) + got.astype(F32)).astype(BF)]
  transfers between devices with their start and end apart: 122 -> 49, of which waited for: 52 -> 25; matrix products, arithmetic and copies ran while one was open for 25% -> 17% of each run, Pallas kernels for 6% -> 14%
where the time goes in v2:
time: 902 us; the launch traced here: 889 us
  waiting for transfers between devices  304 us (34%)
  Pallas kernels  215 us (24%)
  starting transfers between devices  106 us (12%)
  matrix products  92.8 us (10%)
  local copies, waits for them, and re-layouts  90.7 us (10%)
  other arithmetic  60.7 us (7%)
  between operations  19.6 us (2%)
    pallas_call x9, Pallas kernels, remote(): pl.pallas_call(functools.partial(kernel, core), out_shape=tuple(outs), in...  215 us
    all_gather x2, waiting for transfers between devices, body(): lax.all_gather(plan.piece(w_down[l]), order, axis=0, tiled=True)  106 us
    dot_general x22, matrix products, dot(): lax.dot_general(a, b, (((ca,), (cb,)), ((), ())), preferred_element_type=...  92.8 us
    ppermute x20, waiting for transfers between devices, swap(): lax.ppermute(v, axes if len(axes) > 1 else axes[0], [(i, count - 1 - i) f...  92.7 us
    all_gather x2, waiting for transfers between devices, body(): ups.append(lax.all_gather(jnp.transpose(piece), order, axis=0, tiled=True))  59.4 us
    ppermute x9, starting transfers between devices, ring(): lax.ppermute(v, ('zh', 'zl'), [(i, (i + step) % n) for i in range(n)])  45.2 us
    unnamed x278, local copies, waits for them, and re-layouts  28.5 us
    ppermute x9, waiting for transfers between devices, ring(): lax.ppermute(v, ('zh', 'zl'), [(i, (i + step) % n) for i in range(n)])  27 us
  transfers between devices with their start and end apart: 49, of which 25 were waited for; matrix products, arithmetic and copies ran while one was open for 17% of the time, Pallas kernels for 14%

profile of v2, /device:TPU:1, one launch (start us, length us, event | category | flops | bytes accessed | tf_op | source)
XLA Modules:
  0.0 889.5 jit_solution(13630911948023041952)
XLA Ops:
  16.5 5.7 collective-permute-start
  30.1 4.3 collective-permute-start.7
  40.3 3.5 collective-permute-done.4
  43.8 23.1 %collective-permute-start.5 = (bf16[2304]{0:T(1024)(128)(2,1)S(1)}, bf16[2304]{0:T(1024)(128)(2,1)S(1)}, u32[]{:S(2)}, u32[]{:S(2)}) collective-permute-start(bf16[2304]{0:T(1024)(128)(2,1)S(1)} %collective-permute-done.4), channel_id=1, source_target_pairs={{0,1},{1,2},{2,3},{3,0},{4,5},{5,6},{6,7},{7,4},{8,9},{9,10},{10,1... | collective-permute-start | bytes 13832 | tf_op jit(solution)/shard_map/ppermute | solution.py:628
  69.0 8.2 collective-permute-start.6
  80.7 3.8 collective-permute-start.8
  89.5 11.4 %collective-permute-done.3 = bf16[768,128]{1,0:T(8,128)(2,1)S(1)} collective-permute-done((bf16[768,128]{1,0:T(8,128)(2,1)S(1)}, bf16[768,128]{1,0:T(8,128)(2,1)S(1)}, u32[]{:S(2)}, u32[]{:S(2)}) %collective-permute-start.3) | collective-permute-done | bytes 196640 | tf_op jit(solution)/shard_map/ppermute | solution.py:786
  100.9 4.8 collective-permute-start.9
  116.0 39.1 %project_x.2 = (bf16[1024,768]{1,0:T(8,128)(2,1)S(1)}, bf16[512,768]{1,0:T(8,128)(2,1)S(1)}, bf16[1024,704]{1,0:T(8,128)(2,1)}, bf16[512,704]{1,0:T(8,128)(2,1)S(1)}) custom-call(f32[384,768]{1,0:T(8,128)S(1)} %select_convert_fusion.1.resid, f32[1,768]{1,0:T(1,128)S(1)} %get-tuple-element.235.gain, f32[1,768]{1,0:T(1,128)S(1)} %get-tuple-element.236.shift, ...), custom_call_target="tpu_custom_call" | custom-call | flops 1000000000 | bytes 10000000 | tf_op jit(solution)/shard_map/project_x/pallas_call | solution.py:471
  159.8 20.2 %attend_fwd_x.2 = (bf16[384,768]{1,0:T(8,128)(2,1)S(1)}, bf16[1024,192]{1,0:T(8,128)(2,1)S(1)}, bf16[512,192]{1,0:T(8,128)(2,1)S(1)}, f32[8,1024]{1,0:T(8,128)S(...) custom-call(bf16[1024,704]{1,0:T(8,128)(2,1)S(1)} %copy-done.21, ...), custom_call_target="tpu_custom_call" | custom-call | flops 10000000000 | bytes 10000000 | tf_op jit(solution)/shard_map/attend_fwd_x/pallas_call | solution.py:471
  194.3 7.0 convolution_add_fusion.1
  201.3 47.6 %all-gather.17.cloned.1.call-done = bf16[1,3072,768]{2,1,0:T(8,128)(2,1)} async-done(((bf16[1,96,768]{2,1,0:T(8,128)(2,1)}), bf16[1,3072,768]{2,1,0:T(8,128)(2,1)}) %all-gather.17.cloned.1.call-update) | async-done | bytes 4718608 | tf_op jit(solution)/shard_map/all_gather | solution.py:797
  248.9 6.9 fusion.55.resid
  255.7 19.8 %project_x.3 = (bf16[1024,768]{1,0:T(8,128)(2,1)S(1)}, bf16[512,768]{1,0:T(8,128)(2,1)S(1)}, bf16[1024,704]{1,0:T(8,128)(2,1)}, bf16[512,704]{1,0:T(8,128)(2,1)S(1)}) custom-call(f32[384,768]{1,0:T(8,128)S(1)} %fusion.55.resid, f32[1,768]{1,0:T(1,128)S(1)} %get-tuple-element.234.gain, f32[1,768]{1,0:T(1,128)S(1)} %get-tuple-element.233.shift, ...), custom_call_target="tpu_custom_call" | custom-call | flops 1000000000 | bytes 10000000 | tf_op jit(solution)/shard_map/project_x/pallas_call | solution.py:471
  280.0 24.4 %attend_fwd_x.3 = (bf16[384,768]{1,0:T(8,128)(2,1)S(1)}, bf16[1024,192]{1,0:T(8,128)(2,1)S(1)}, bf16[512,192]{1,0:T(8,128)(2,1)S(1)}, f32[8,1024]{1,0:T(8,128)S(...) custom-call(bf16[1024,704]{1,0:T(8,128)(2,1)S(1)} %copy-done.23, ...), custom_call_target="tpu_custom_call" | custom-call | flops 10000000000 | bytes 10000000 | tf_op jit(solution)/shard_map/attend_fwd_x/pallas_call | solution.py:471
  310.9 59.3 %all-gather.13.cloned.1.call-done = bf16[3072,768]{1,0:T(8,128)(2,1)} async-done(((bf16[96,768]{1,0:T(8,128)(2,1)}), bf16[3072,768]{1,0:T(8,128)(2,1)}) %all-gather.13.cloned.1.call-update) | async-done | bytes 4718608 | tf_op jit(solution)/shard_map/all_gather | solution.py:796
  370.2 7.1 convolution_add_fusion
  377.3 58.7 %all-gather.21.cloned.1.call-done = bf16[1,3072,768]{2,1,0:T(8,128)(2,1)} async-done(((bf16[1,96,768]{2,1,0:T(8,128)(2,1)}), bf16[1,3072,768]{2,1,0:T(8,128)(2,1)}) %all-gather.21.cloned.1.call-update) | async-done | bytes 4718608 | tf_op jit(solution)/shard_map/all_gather | solution.py:797
  436.0 8.4 convert_reduce_fusion
  450.1 24.5 %attend_bwd_x.2 = (bf16[1024,704]{1,0:T(8,128)(2,1)S(1)}, bf16[512,704]{1,0:T(8,128)(2,1)S(1)}) custom-call(bf16[1024,704]{1,0:T(8,128)(2,1)S(1)} %copy-done.24, bf16[512,704]{1,0:T(8,128)(2,1)S(1)} %copy-done.28, bf16[384,768]{1,0:T(8,128)(2,1)S(1)} %convolution_convert_fusion.7.go, bf16[1024,192]{1,0:T(8,128)(2,1)S(1)} %copy-done.32, ...), custom_call_target="tpu_custom_call" | custom-call | flops 20000000000 | bytes 10000000 | tf_op jit(solution)/shard_map/attend_bwd_x/pallas_call | solution.py:471
  475.8 20.4 %collect_x.2 = (f32[384,768]{1,0:T(8,128)S(1)}, f32[8,768]{1,0:T(8,128)S(1)}) custom-call(bf16[1024,704]{1,0:T(8,128)(2,1)} %copy-done, bf16[512,704]{1,0:T(8,128)(2,1)S(1)} %get-tuple-element.82.ds, bf16[768,704]{1,0:T(8,128)(2,1)S(1)} %pad_maximum_fusion.3.w, f32[384,768]{1,0:T(8,128)S(1)} %copy-done.9, f32[1,768]{1,0:T(1,128)S(1)} %get-tuple-element.234.gain, ...), custom_call_target="tpu_custom_call" | custom-call | flops 1000000000 | bytes 10000000 | tf_op jit(solution)/shard_map/collect_x/pallas_call | solution.py:471
  496.2 8.3 convert_reduce_fusion.1
  504.6 5.0 multiply_reduce_fusion.1
  513.8 25.0 %attend_bwd_x.3 = (bf16[1024,704]{1,0:T(8,128)(2,1)S(1)}, bf16[512,704]{1,0:T(8,128)(2,1)S(1)}) custom-call(bf16[1024,704]{1,0:T(8,128)(2,1)S(1)} %copy-done.22, bf16[512,704]{1,0:T(8,128)(2,1)S(1)} %copy-done.26, bf16[384,768]{1,0:T(8,128)(2,1)S(1)} %convolution_convert_fusion.6.go, bf16[1024,192]{1,0:T(8,128)(2,1)S(1)} %copy-done.30, ...), custom_call_target="tpu_custom_call" | custom-call | flops 20000000000 | bytes 10000000 | tf_op jit(solution)/shard_map/attend_bwd_x/pallas_call | solution.py:471
  540.6 18.1 %collect_x.3 = (f32[384,768]{1,0:T(8,128)S(1)}, f32[8,768]{1,0:T(8,128)S(1)}) custom-call(bf16[1024,704]{1,0:T(8,128)(2,1)} %copy-done.2, bf16[512,704]{1,0:T(8,128)(2,1)S(1)} %get-tuple-element.91.ds, bf16[768,704]{1,0:T(8,128)(2,1)S(1)} %copy-done.7, f32[384,768]{1,0:T(8,128)S(1)} %select_convert_fusion.1.resid, f32[1,768]{1,0:T(1,128)S(1)} %get-tuple-element.235.gain, ...), custom_call_target="tpu_custom_call" | custom-call | flops 1000000000 | bytes 10000000 | tf_op jit(solution)/shard_map/collect_x/pallas_call | solution.py:471
  562.0 7.5 convolution_convert_fusion
  569.6 4.9 convolution_convert_fusion.1
  576.3 7.4 convolution_convert_fusion.2
  583.6 6.0 convolution_convert_fusion.3
  589.8 3.8 fusion.58
  593.6 5.1 collective-permute-start.10
  606.5 23.9 %total_x.1 = f32[146,128]{1,0:T(8,128)S(1)} custom-call(f32[146,128]{1,0:T(8,128)S(1)} %reshape.303.v), custom_call_target="tpu_custom_call" | custom-call | flops 1000000000 | bytes 10000000 | tf_op jit(solution)/shard_map/total_x/pallas_call | solution.py:471
  631.7 3.3 fusion.113
  683.4 5.4 collective-permute-done.14
  689.1 3.6 collective-permute-start.22
  692.6 5.1 collective-permute-start.15
  707.1 3.6 collective-permute-done.26
  710.8 3.5 collective-permute-done.19
  725.9 4.2 fusion.14
  734.3 3.4 fusion.16
  740.9 16.8 %collective-permute-done.36 = bf16[2,96,3072]{2,1,0:T(8,128)(2,1)S(1)} collective-permute-done((bf16[2,96,3072]{2,1,0:T(8,128)(2,1)S(1)}, bf16[2,96,3072]{2,1,0:T(8,128)(2,1)S(1)}, u32[]{:S(2)}, u32[]{:S(2)}) %collective-permute-start.36) | collective-permute-done | bytes 1179680 | tf_op jit(solution)/shard_map/ppermute | solution.py:565
  759.7 23.3 %collective-permute-done.28 = bf16[2,96,3072]{2,1,0:T(8,128)(2,1)S(1)} collective-permute-done((bf16[2,96,3072]{2,1,0:T(8,128)(2,1)S(1)}, bf16[2,96,3072]{2,1,0:T(8,128)(2,1)S(1)}, u32[]{:S(2)}, u32[]{:S(2)}) %collective-permute-start.28) | collective-permute-done | bytes 1179680 | tf_op jit(solution)/shard_map/ppermute | solution.py:565
  786.3 11.7 %collective-permute-done.30 = bf16[2,96,3840]{2,1,0:T(8,128)(2,1)S(1)} collective-permute-done((bf16[2,96,3840]{2,1,0:T(8,128)(2,1)S(1)}, bf16[2,96,3840]{2,1,0:T(8,128)(2,1)S(1)}, u32[]{:S(2)}, u32[]{:S(2)}) %collective-permute-start.30) | collective-permute-done | bytes 1474592 | tf_op jit(solution)/shard_map/ppermute | solution.py:565
  801.1 22.1 %collective-permute-done.29 = bf16[96,3072]{1,0:T(8,128)(2,1)S(1)} collective-permute-done((bf16[96,3072]{1,0:T(8,128)(2,1)S(1)}, bf16[96,3072]{1,0:T(8,128)(2,1)S(1)}, u32[]{:S(2)}, u32[]{:S(2)}) %collective-permute-start.29) | collective-permute-done | bytes 589856 | tf_op jit(solution)/shard_map/ppermute | solution.py:565
  853.0 4.4 collective-permute-done.41
  860.4 4.3 collective-permute-done.33
  867.8 4.4 collective-permute-done.42
  872.3 7.2 collective-permute-done.34
  (594 shorter events, 220.5 us)
Async XLA Ops:
  7.2 182.4 %all-gather.15.cloned.1.call-start = ((), (), s32[]{:S(2)}) async-start(), calls=%async_computation.2 | async-start | bytes 1216512 | tf_op jit(solution)/shard_map/all_gather | solution.py:793
  9.0 185.3 %all-gather.11.cloned.1.call-start = ((), (), s32[]{:S(2)}) async-start(), calls=%async_computation | async-start | bytes 4866048 | tf_op jit(solution)/shard_map/all_gather | solution.py:796
  12.0 236.8 %all-gather.17.cloned.1.call-start = ((), (), s32[]{:S(2)}) async-start(), calls=%async_computation.3 | async-start | bytes 4866048 | tf_op jit(solution)/shard_map/all_gather | solution.py:797
  13.9 292.9 %all-gather.19.cloned.1.call-start = ((), (), s32[]{:S(2)}) async-start(), calls=%async_computation.4 | async-start | bytes 1216512 | tf_op jit(solution)/shard_map/all_gather | solution.py:793
  14.6 355.6 %all-gather.13.cloned.1.call-start = ((), (), s32[]{:S(2)}) async-start(), calls=%async_computation.1 | async-start | bytes 4866048 | tf_op jit(solution)/shard_map/all_gather | solution.py:796
  15.5 420.5 %all-gather.21.cloned.1.call-start = ((), (), s32[]{:S(2)}) async-start(), calls=%async_computation.5 | async-start | bytes 4866048 | tf_op jit(solution)/shard_map/all_gather | solution.py:797
  16.5 94.5 %collective-permute-start = (bf16[384,768]{1,0:T(8,128)(2,1)}, bf16[384,768]{1,0:T(8,128)(2,1)}, u32[]{:S(2)}, u32[]{:S(2)}) collective-permute-start(bf16[384,768]{1,0:T(8,128)(2,1)} %pad_maximum_fusion.4), channel_id=1, source_target_pairs={{2,4},{4,2},{3,5},{5,3},{10,12},{12,10},{11,13},{13,11},{18,20},{2... | collective-permute-start | bytes 1769480 | tf_op jit(solution)/shard_map/ppermute | solution.py:623
  24.1 61.5 %collective-permute-start.2 = (bf16[768,128]{1,0:T(8,128)(2,1)S(1)}, bf16[768,128]{1,0:T(8,128)(2,1)S(1)}, u32[]{:S(2)}, u32[]{:S(2)}) collective-permute-start(bf16[768,128]{1,0:T(8,128)(2,1)S(1)} %copy.113), channel_id=1, source_target_pairs={{0,1},{2,3},{4,5},{6,7},{8,9},{10,11},{12,13},{14,15},{16,17},{18,... | collective-permute-start | bytes 589832 | tf_op jit(solution)/shard_map/ppermute | solution.py:784
  27.3 84.9 %collective-permute-start.1 = (bf16[768,576]{0,1:T(8,128)(2,1)}, bf16[768,576]{0,1:T(8,128)(2,1)}, u32[]{:S(2)}, u32[]{:S(2)}) collective-permute-start(bf16[768,576]{0,1:T(8,128)(2,1)} %bitcast.4), channel_id=1, source_target_pairs={{2,4},{4,2},{3,5},{5,3},{10,12},{12,10},{11,13},{13,11},{18,20},{2... | collective-permute-start | bytes 2654216 | tf_op jit(solution)/shard_map/ppermute | solution.py:623
  30.1 13.7 %collective-permute-start.4 = (bf16[2304]{0:T(1024)(128)(2,1)S(1)}, bf16[2304]{0:T(1024)(128)(2,1)S(1)}, u32[]{:S(2)}, u32[]{:S(2)}) collective-permute-start(bf16[2304]{0:T(1024)(128)(2,1)S(1)} %dynamic-update-slice.31), channel_id=1, source_target_pairs={{0,1},{1,2},{2,3},{3,0},{4,5},{5,6},{6,7},{7,4},{8,9},{9,10},{10,1... | collective-permute-start | bytes 13832 | tf_op jit(solution)/shard_map/ppermute | solution.py:628
  30.1 154.8 %collective-permute-start.7 = (bf16[768,576]{0,1:T(8,128)(2,1)}, bf16[768,576]{0,1:T(8,128)(2,1)}, u32[]{:S(2)}, u32[]{:S(2)}) collective-permute-start(bf16[768,576]{0,1:T(8,128)(2,1)} %bitcast.19), channel_id=1, source_target_pairs={{2,4},{4,2},{3,5},{5,3},{10,12},{12,10},{11,13},{13,11},{18,20},{2... | collective-permute-start | bytes 2654216 | tf_op jit(solution)/shard_map/ppermute | solution.py:623
  43.8 25.2 %collective-permute-start.5 = (bf16[2304]{0:T(1024)(128)(2,1)S(1)}, bf16[2304]{0:T(1024)(128)(2,1)S(1)}, u32[]{:S(2)}, u32[]{:S(2)}) collective-permute-start(bf16[2304]{0:T(1024)(128)(2,1)S(1)} %collective-permute-done.4), channel_id=1, source_target_pairs={{0,1},{1,2},{2,3},{3,0},{4,5},{5,6},{6,7},{7,4},{8,9},{9,10},{10,1... | collective-permute-start | bytes 13832 | tf_op jit(solution)/shard_map/ppermute | solution.py:628
  69.0 11.7 %collective-permute-start.6 = (bf16[2304]{0:T(1024)(128)(2,1)S(1)}, bf16[2304]{0:T(1024)(128)(2,1)S(1)}, u32[]{:S(2)}, u32[]{:S(2)}) collective-permute-start(bf16[2304]{0:T(1024)(128)(2,1)S(1)} %collective-permute-done.5), channel_id=1, source_target_pairs={{0,1},{1,2},{2,3},{3,0},{4,5},{5,6},{6,7},{7,4},{8,9},{9,10},{10,1... | collective-permute-start | bytes 13832 | tf_op jit(solution)/shard_map/ppermute | solution.py:628
  80.7 7.4 collective-permute-start.8
  85.6 23.7 %collective-permute-start.11 = (bf16[384,768]{1,0:T(8,128)(2,1)}, bf16[384,768]{1,0:T(8,128)(2,1)S(1)}, u32[]{:S(2)}, u32[]{:S(2)}) collective-permute-start(bf16[384,768]{1,0:T(8,128)(2,1)} %pad_maximum_fusion.5), channel_id=1, source_target_pairs={{2,4},{4,2},{3,5},{5,3},{10,12},{12,10},{11,13},{13,11},{18,20},{2... | collective-permute-start | bytes 1769480 | tf_op jit(solution)/shard_map/ppermute | solution.py:623
  88.2 12.7 %collective-permute-start.3 = (bf16[768,128]{1,0:T(8,128)(2,1)S(1)}, bf16[768,128]{1,0:T(8,128)(2,1)S(1)}, u32[]{:S(2)}, u32[]{:S(2)}) collective-permute-start(bf16[768,128]{1,0:T(8,128)(2,1)S(1)} %broadcast_select_fusion.5), channel_id=1, source_target_pairs={{0,2},{1,3},{4,6},{5,7},{8,10},{9,11},{12,14},{13,15},{16,18},{17,... | collective-permute-start | bytes 589832 | tf_op jit(solution)/shard_map/ppermute | solution.py:786
  100.9 7.8 collective-permute-start.9
  593.6 86.1 %collective-permute-start.10 = (bf16[384,768]{1,0:T(8,128)(2,1)}, bf16[384,768]{1,0:T(8,128)(2,1)}, u32[]{:S(2)}, u32[]{:S(2)}) collective-permute-start(bf16[384,768]{1,0:T(8,128)(2,1)} %fusion.58), channel_id=1, source_target_pairs={{2,4},{4,2},{3,5},{5,3},{10,12},{12,10},{11,13},{13,11},{18,20},{2... | collective-permute-start | bytes 1769480 | tf_op jit(solution)/shard_map/ppermute | solution.py:623
  599.6 76.3 %collective-permute-start.12 = (bf16[384,768]{1,0:T(8,128)(2,1)}, bf16[384,768]{1,0:T(8,128)(2,1)}, u32[]{:S(2)}, u32[]{:S(2)}) collective-permute-start(bf16[384,768]{1,0:T(8,128)(2,1)} %convert_element_type.524), channel_id=1, source_target_pairs={{2,4},{4,2},{3,5},{5,3},{10,12},{12,10},{11,13},{13,11},{18,20},{2... | collective-permute-start | bytes 1769480 | tf_op jit(solution)/shard_map/ppermute | solution.py:623
  639.6 32.3 %collective-permute-start.20 = (bf16[2,2,96,704]{3,2,1,0:T(8,128)(2,1)}, bf16[2,2,96,704]{3,2,1,0:T(8,128)(2,1)}, u32[]{:S(2)}, u32[]{:S(2)}) collective-permute-start(bf16[2,2,96,704]{3,2,1,0:T(8,128)(2,1)} %dynamic-slice_bitcast_fusion.6), channel_id=1, source_target_pairs={{0,8},{8,0},{1,9},{9,1},{2,10},{10,2},{3,11},{11,3},{4,12},{12,4},... | collective-permute-start | bytes 1622024 | tf_op jit(solution)/shard_map/ppermute | solution.py:565
  644.6 29.3 %collective-permute-start.13 = (bf16[2,2,96,704]{3,2,1,0:T(8,128)(2,1)}, bf16[2,2,96,704]{3,2,1,0:T(8,128)(2,1)}, u32[]{:S(2)}, u32[]{:S(2)}) collective-permute-start(bf16[2,2,96,704]{3,2,1,0:T(8,128)(2,1)} %dynamic-slice_bitcast_fusion.7), channel_id=1, source_target_pairs={{0,8},{8,0},{1,9},{9,1},{2,10},{10,2},{3,11},{11,3},{4,12},{12,4},... | collective-permute-start | bytes 1622024 | tf_op jit(solution)/shard_map/ppermute | solution.py:565
  655.8 70.1 %collective-permute-start.35 = (bf16[2,2,96,6912]{3,2,0,1:T(8,128)(2,1)}, bf16[2,2,96,6912]{3,2,0,1:T(8,128)(2,1)}, u32[]{:S(2)}, u32[]{:S(2)}) collective-permute-start(bf16[2,2,96,6912]{3,2,0,1:T(8,128)(2,1)} %pad_maximum_fusion.1), channel_id=1, source_target_pairs={{0,4},{4,0},{1,5},{5,1},{2,6},{6,2},{3,7},{7,3},{8,12},{12,8},{9,1... | collective-permute-start | bytes 15925256 | tf_op jit(solution)/shard_map/ppermute | solution.py:565
  671.9 61.4 %collective-permute-start.27 = (bf16[2,2,96,6912]{3,2,0,1:T(8,128)(2,1)}, bf16[2,2,96,6912]{3,2,0,1:T(8,128)(2,1)}, u32[]{:S(2)}, u32[]{:S(2)}) collective-permute-start(bf16[2,2,96,6912]{3,2,0,1:T(8,128)(2,1)} %pad_maximum_fusion), channel_id=1, source_target_pairs={{0,4},{4,0},{1,5},{5,1},{2,6},{6,2},{3,7},{7,3},{8,12},{12,8},{9,1... | collective-permute-start | bytes 15925256 | tf_op jit(solution)/shard_map/ppermute | solution.py:565
  673.9 8.6 collective-permute-start.21
  676.0 12.9 %collective-permute-start.14 = (bf16[2,96,704]{2,1,0:T(8,128)(2,1)S(1)}, bf16[2,96,704]{2,1,0:T(8,128)(2,1)S(1)}, u32[]{:S(2)}, u32[]{:S(2)}) collective-permute-start(bf16[2,96,704]{2,1,0:T(8,128)(2,1)S(1)} %dynamic-slice_bitcast_fusion.10), channel_id=1, source_target_pairs={{0,16},{16,0},{1,17},{17,1},{2,18},{18,2},{3,19},{19,3},{4,20},{20... | collective-permute-start | bytes 811016 | tf_op jit(solution)/shard_map/ppermute | solution.py:565
  689.1 25.3 %collective-permute-start.22 = (bf16[2,96,576]{2,1,0:T(8,128)(2,1)}, bf16[2,96,576]{2,1,0:T(8,128)(2,1)}, u32[]{:S(2)}, u32[]{:S(2)}) collective-permute-start(bf16[2,96,576]{2,1,0:T(8,128)(2,1)} %slice.385), channel_id=1, source_target_pairs={{2,0},{4,6},{3,1},{5,7},{10,8},{12,14},{11,9},{13,15},{18,16},{20,... | collective-permute-start | bytes 663560 | tf_op jit(solution)/shard_map/ppermute | solution.py:871
  692.6 5.1 collective-permute-start.24
  692.6 24.0 %collective-permute-start.15 = (bf16[2,96,576]{2,1,0:T(8,128)(2,1)S(1)}, bf16[2,96,576]{2,1,0:T(8,128)(2,1)}, u32[]{:S(2)}, u32[]{:S(2)}) collective-permute-start(bf16[2,96,576]{2,1,0:T(8,128)(2,1)S(1)} %slice.383), channel_id=1, source_target_pairs={{2,0},{4,6},{3,1},{5,7},{10,8},{12,14},{11,9},{13,15},{18,16},{20,... | collective-permute-start | bytes 663560 | tf_op jit(solution)/shard_map/ppermute | solution.py:871
  699.0 3.7 collective-permute-start.25
  702.7 4.4 collective-permute-start.18
  707.1 3.6 collective-permute-start.26
  710.6 3.6 collective-permute-start.19
  715.4 4.9 collective-permute-start.23
  718.4 5.2 collective-permute-start.16
  730.2 27.5 %collective-permute-start.36 = (bf16[2,96,3072]{2,1,0:T(8,128)(2,1)S(1)}, bf16[2,96,3072]{2,1,0:T(8,128)(2,1)S(1)}, u32[]{:S(2)}, u32[]{:S(2)}) collective-permute-start(bf16[2,96,3072]{2,1,0:T(8,128)(2,1)S(1)} %dynamic-slice_bitcast_fusion), channel_id=1, source_target_pairs={{0,16},{16,0},{1,17},{17,1},{2,18},{18,2},{3,19},{19,3},{4,20},{20... | collective-permute-start | bytes 3538952 | tf_op jit(solution)/shard_map/ppermute | solution.py:565
  732.6 51.5 %collective-permute-start.38 = (bf16[2,96,3840]{2,1,0:T(8,128)(2,1)S(1)}, bf16[2,96,3840]{2,1,0:T(8,128)(2,1)S(1)}, u32[]{:S(2)}, u32[]{:S(2)}) collective-permute-start(bf16[2,96,3840]{2,1,0:T(8,128)(2,1)S(1)} %fusion.35), channel_id=1, source_target_pairs={{0,8},{8,0},{1,9},{9,1},{2,10},{10,2},{3,11},{11,3},{4,12},{12,4},... | collective-permute-start | bytes 4423688 | tf_op jit(solution)/shard_map/ppermute | solution.py:565
  737.9 45.1 %collective-permute-start.28 = (bf16[2,96,3072]{2,1,0:T(8,128)(2,1)S(1)}, bf16[2,96,3072]{2,1,0:T(8,128)(2,1)S(1)}, u32[]{:S(2)}, u32[]{:S(2)}) collective-permute-start(bf16[2,96,3072]{2,1,0:T(8,128)(2,1)S(1)} %dynamic-slice_bitcast_fusion.1), channel_id=1, source_target_pairs={{0,16},{16,0},{1,17},{17,1},{2,18},{18,2},{3,19},{19,3},{4,20},{20... | collective-permute-start | bytes 3538952 | tf_op jit(solution)/shard_map/ppermute | solution.py:565
  740.1 57.9 %collective-permute-start.30 = (bf16[2,96,3840]{2,1,0:T(8,128)(2,1)S(1)}, bf16[2,96,3840]{2,1,0:T(8,128)(2,1)S(1)}, u32[]{:S(2)}, u32[]{:S(2)}) collective-permute-start(bf16[2,96,3840]{2,1,0:T(8,128)(2,1)S(1)} %fusion.39), channel_id=1, source_target_pairs={{0,8},{8,0},{1,9},{9,1},{2,10},{10,2},{3,11},{11,3},{4,12},{12,4},... | collective-permute-start | bytes 4423688 | tf_op jit(solution)/shard_map/ppermute | solution.py:565
  759.0 65.0 %collective-permute-start.37 = (bf16[96,3072]{1,0:T(8,128)(2,1)}, bf16[96,3072]{1,0:T(8,128)(2,1)}, u32[]{:S(2)}, u32[]{:S(2)}) collective-permute-start(bf16[96,3072]{1,0:T(8,128)(2,1)} %dynamic-slice_bitcast_fusion.4), channel_id=1, source_target_pairs={{0,8},{8,0},{1,9},{9,1},{2,10},{10,2},{3,11},{11,3},{4,12},{12,4},... | collective-permute-start | bytes 1769480 | tf_op jit(solution)/shard_map/ppermute | solution.py:565
  783.4 39.8 %collective-permute-start.29 = (bf16[96,3072]{1,0:T(8,128)(2,1)S(1)}, bf16[96,3072]{1,0:T(8,128)(2,1)S(1)}, u32[]{:S(2)}, u32[]{:S(2)}) collective-permute-start(bf16[96,3072]{1,0:T(8,128)(2,1)S(1)} %dynamic-slice_bitcast_fusion.5), channel_id=1, source_target_pairs={{0,8},{8,0},{1,9},{9,1},{2,10},{10,2},{3,11},{11,3},{4,12},{12,4},... | collective-permute-start | bytes 1769480 | tf_op jit(solution)/shard_map/ppermute | solution.py:565
  785.4 40.9 %collective-permute-start.39 = (bf16[96,3840]{1,0:T(8,128)(2,1)}, bf16[96,3840]{1,0:T(8,128)(2,1)}, u32[]{:S(2)}, u32[]{:S(2)}) collective-permute-start(bf16[96,3840]{1,0:T(8,128)(2,1)} %dynamic-slice_bitcast_fusion.2), channel_id=1, source_target_pairs={{0,16},{16,0},{1,17},{17,1},{2,18},{18,2},{3,19},{19,3},{4,20},{20... | collective-permute-start | bytes 2211848 | tf_op jit(solution)/shard_map/ppermute | solution.py:565
  800.4 28.1 %collective-permute-start.31 = (bf16[96,3840]{1,0:T(8,128)(2,1)}, bf16[96,3840]{1,0:T(8,128)(2,1)}, u32[]{:S(2)}, u32[]{:S(2)}) collective-permute-start(bf16[96,3840]{1,0:T(8,128)(2,1)} %dynamic-slice_bitcast_fusion.3), channel_id=1, source_target_pairs={{0,16},{16,0},{1,17},{17,1},{2,18},{18,2},{3,19},{19,3},{4,20},{20... | collective-permute-start | bytes 2211848 | tf_op jit(solution)/shard_map/ppermute | solution.py:565
  834.1 9.1 %collective-permute-start.40 = (bf16[96,1728]{1,0:T(8,128)(2,1)}, bf16[96,1728]{1,0:T(8,128)(2,1)}, u32[]{:S(2)}, u32[]{:S(2)}) collective-permute-start(bf16[96,1728]{1,0:T(8,128)(2,1)} %dynamic-slice_bitcast_fusion.8), channel_id=1, source_target_pairs={{0,3},{1,0},{2,1},{3,2},{4,7},{5,4},{6,5},{7,6},{8,11},{9,8},{10,9... | collective-permute-start | bytes 995336 | tf_op jit(solution)/shard_map/ppermute | solution.py:628
  842.0 8.0 collective-permute-start.32
  844.2 13.1 %collective-permute-start.41 = (bf16[96,1728]{1,0:T(8,128)(2,1)S(1)}, bf16[96,1728]{1,0:T(8,128)(2,1)S(1)}, u32[]{:S(2)}, u32[]{:S(2)}) collective-permute-start(bf16[96,1728]{1,0:T(8,128)(2,1)S(1)} %fusion.72), channel_id=1, source_target_pairs={{0,3},{1,0},{2,1},{3,2},{4,7},{5,4},{6,5},{7,6},{8,11},{9,8},{10,9... | collective-permute-start | bytes 995336 | tf_op jit(solution)/shard_map/ppermute | solution.py:628
  850.1 14.7 %collective-permute-start.33 = (bf16[96,1728]{1,0:T(8,128)(2,1)S(1)}, bf16[96,1728]{1,0:T(8,128)(2,1)S(1)}, u32[]{:S(2)}, u32[]{:S(2)}) collective-permute-start(bf16[96,1728]{1,0:T(8,128)(2,1)S(1)} %fusion.71), channel_id=1, source_target_pairs={{0,3},{1,0},{2,1},{3,2},{4,7},{5,4},{6,5},{7,6},{8,11},{9,8},{10,9... | collective-permute-start | bytes 995336 | tf_op jit(solution)/shard_map/ppermute | solution.py:628
  857.5 14.7 %collective-permute-start.42 = (bf16[96,1728]{1,0:T(8,128)(2,1)S(1)}, bf16[96,1728]{1,0:T(8,128)(2,1)S(1)}, u32[]{:S(2)}, u32[]{:S(2)}) collective-permute-start(bf16[96,1728]{1,0:T(8,128)(2,1)S(1)} %fusion.73), channel_id=1, source_target_pairs={{0,3},{1,0},{2,1},{3,2},{4,7},{5,4},{6,5},{7,6},{8,11},{9,8},{10,9... | collective-permute-start | bytes 995336 | tf_op jit(solution)/shard_map/ppermute | solution.py:628
  864.8 14.7 %collective-permute-start.34 = (bf16[96,1728]{1,0:T(8,128)(2,1)S(1)}, bf16[96,1728]{1,0:T(8,128)(2,1)S(1)}, u32[]{:S(2)}, u32[]{:S(2)}) collective-permute-start(bf16[96,1728]{1,0:T(8,128)(2,1)S(1)} %fusion.74), channel_id=1, source_target_pairs={{0,3},{1,0},{2,1},{3,2},{4,7},{5,4},{6,5},{7,6},{8,11},{9,8},{10,9... | collective-permute-start | bytes 995336 | tf_op jit(solution)/shard_map/ppermute | solution.py:628
  (128 other events, 1417.8 us)
Sparse Core Ops, SparseCore 0:
  10.9 91.1 all-gather.14
  105.6 73.1 all-gather.10
  182.3 66.5 all-gather.16
  251.6 53.4 all-gather.18
  307.8 62.3 all-gather.12
  373.5 62.4 all-gather.20

commit v3 on v2

--- a/solution.py
+++ b/solution.py
@@ -707,36 +707,6 @@
             left.remove(ax)
         return v.reshape(-1, n)
 
-    def scatter_all(self, up, down, out):
-        n, e = up.shape[1], out.shape[1]
-        bits = len(self.dims)
-        view = lambda v: v.reshape(*([2] * bits), -1, v.shape[1])
-        mats = [view(up), view(down), view(out)]
-        pos = bits - 1
-        to_send = jnp.concatenate([pick(v, 1 - self.c, pos) for v in mats], axis=-1)
-        got = swap(to_send, self.core)
-        up, down, out = [
-            (pick(v, self.c, pos).astype(F32) + got[..., at : at + v.shape[-1]].astype(F32)).astype(BF)
-            for v, at in zip(mats, (0, n, 2 * n))
-        ]
-        down = jnp.concatenate([down, out], axis=-1)
-        res = []
-        for v, axes in ((up, self.plane), (down, self.plane[::-1])):
-            left = list(self.plane)
-            for ax in axes:
-                i, p = lax.axis_index(ax), left.index(ax)
-                got = swap(pick(v, 1 - i, p), ax)
-                v = (pick(v, i, p).astype(F32) + got.astype(F32)).astype(BF)
-                left.remove(ax)
-            res.append(v)
-        up, down = res
-        rows = up.shape[0]
-        cut = lambda v: v.reshape(rows, self.mp, -1)
-        v = jnp.concatenate([cut(up), cut(down[:, :n]), cut(down[:, n:])], axis=-1)
-        v = self.ring_scatter([pick(v, (self.z - r) % self.mp, 1) for r in range(self.mp)])
-        q = n // self.mp
-        return v[:, :q], v[:, q : 2 * q], v[:, 2 * q :]
-
     def ring_scatter(self, chunks):
         t = chunks[-1]
         for r in range(self.mp - 2, -1, -1):
@@ -771,7 +741,6 @@
     rel_small = jnp.stack([small] + plan.ring_gather(small))
     n_up = layers * ffq
     rel_bup = rel_small[:, :n_up].reshape(mp, layers, ffq).astype(F32)
-    bup = jnp.stack([pick(rel_bup, (plan.z - q) % mp, 0) for q in range(mp)])
     rel_bqv = rel_small[:, n_up:].reshape(mp, layers, 2, heads_w).astype(F32)
     mine = 2 * plan.c + plan.zl
     my_bqv = pick(rel_bqv, (plan.z - mine) % mp, 0)
@@ -788,13 +757,26 @@
         exts.append(jnp.concatenate([quarter, head0], axis=1))
 
     ups, downs, outs = [], [], []
-    order = ("zh", "zl") + dims
     for l in range(layers):
-        outs.append(lax.all_gather(plan.piece(w_out[l]), order, axis=0, tiled=True))
-        n_up = ffq // dp
-        piece = lax.dynamic_slice_in_dim(w_up[l], plan.d * n_up, n_up, 1)
-        ups.append(lax.all_gather(jnp.transpose(piece), order, axis=0, tiled=True))
-        downs.append(lax.all_gather(plan.piece(w_down[l]), order, axis=0, tiled=True))
+        po = plan.piece(w_out[l])
+        pu = jnp.concatenate([plan.piece(w_up[l]), po], axis=0)
+        pd = plan.piece(w_down[l])
+        n_out, n_d = po.shape[0], pd.shape[0]
+        both = plan.ring_gather(jnp.concatenate([pu, pd], axis=0))
+        stacked = jnp.stack(both)
+        n_u = pu.shape[0]
+        gu = plan.plane_gather(stacked[:, :n_u], fwd_axes)
+        gd = plan.plane_gather(stacked[:, n_u:], alt_axes)
+        up = gu[:, :, : n_u - n_out].reshape(mp - 1, d_model, ffq)
+        ups.append(jnp.concatenate([w_up[l]] + [up[r] for r in range(mp - 1)], axis=1))
+        out = gu[:, :, n_u - n_out :].reshape(mp - 1, heads_w, d_model)
+        out = jnp.concatenate([w_out[l][None], out], axis=0)
+        outs.append(
+            jnp.concatenate([pick(out, (plan.z - q) % mp, 0) for q in range(mp)], axis=0)
+        )
+        downs.append(
+            jnp.concatenate([w_down[l], gd.reshape((mp - 1) * ffq, d_model)], axis=0)
+        )
 
     dy = plan.relabel(jnp.concatenate([dy_long[0], dy_short[0]], axis=0))
 
@@ -803,6 +785,9 @@
     saved = []
     shares = []
     for l in range(layers):
+        normed, hat1, inv1 = normalize(resid, gain[l, 0], shift[l, 0])
+        normed = normed.astype(BF)
+        full = [plan.gather(normed[:rl]), plan.gather(normed[rl:])]
         bias = jnp.concatenate(
             [
                 my_bqv[l, 0],
@@ -812,24 +797,22 @@
                 jnp.zeros((HD,), F32),
             ]
         )
-        full_l, full_s, pj_l, pj_s = project(
-            plan.core, resid, gain[l, 0], shift[l, 0], exts[l], bias, rl, rs
-        )
-        full, proj = (full_l, full_s), (pj_l, pj_s)
-        attended, *att = attend_fwd_x(plan.core, pj_l, pj_s)
+        proj = [(dot(n, exts[l]) + bias).astype(BF) for n in full]
+        att = [attend_fwd(p) for p in proj]
         share = jnp.zeros((), F32)
-        for carry in att[4:]:
-            size = carry.shape[1]
-            sel = carry[size // BR]
+        for p, a in zip(proj, att):
+            size = p.shape[0]
+            sel = a[2][size // BR]
             left = (size - 1 - lax.broadcasted_iota(jnp.int32, (size,), 0)).astype(F32)
             share = share + jnp.sum(
                 jax.nn.sigmoid(4.0 * (sel / jnp.maximum(left, 1.0) - limits[l]))
             )
         shares.append(share)
+        attended = jnp.concatenate([plan.to_rows(a[0]) for a in att], axis=0)
         middle = resid + dot(attended, outs[l]) + b_out[l].astype(F32)
         normed2, hat2, inv2 = normalize(middle, gain[l, 1], shift[l, 1])
         normed2 = normed2.astype(BF)
-        upper = dot(normed2, ups[l], 1, 1) + bup[:, l].reshape(-1)
+        upper = dot(normed2, ups[l]) + rel_bup[:, l].reshape(-1)
         active = gelu_both(upper)[0].astype(BF)
         saved.append((resid, middle, full, proj, att, attended, normed2, upper, active))
         resid = middle + dot(active, downs[l]) + b_down[l].astype(F32)
@@ -849,7 +832,7 @@
         w_down_t = dot(gm, active, 0, 0).astype(BF)
         w_up_g = dot(normed2, gu, 0, 0).astype(BF)
         g_bup = jnp.sum(gu.astype(F32), axis=0)
-        gn2 = dot(gu, ups[l])
+        gn2 = dot(gu, ups[l], 1, 1)
         _, hat2, inv2 = normalize(middle, gain[l, 1], shift[l, 1])
         back, g_gain2, g_shift2 = normalize_back(gn2, hat2, inv2, gain[l, 1])
         gmid = g + back
@@ -857,14 +840,24 @@
         ga = gmid.astype(BF)
         go = dot(ga, outs[l], 1, 1).astype(BF)
         w_out_t = dot(ga, attended, 0, 0).astype(BF)
-        dext = attend_bwd_x(plan.core, *proj, go, *att)
-        new_g, ln1 = collect(plan.core, *dext, exts[l], resid, gain[l, 0], gmid)
-        g_gain1, g_shift1 = ln1[0], ln1[1]
+        gh = [plan.to_heads(go[:rl]), plan.to_heads(go[rl:])]
+        dext = [attend_bwd(p, h, a[0], a[1], a[2]) for p, h, a in zip(proj, gh, att)]
+        gn1 = jnp.concatenate(
+            [plan.scatter(dot(e, exts[l], 1, 1).astype(BF)) for e in dext], axis=0
+        )
         w_ext_g = sum(dot(n, e, 0, 0) for n, e in zip(full, dext)).astype(BF)
         g_bext = sum(jnp.sum(e.astype(F32), axis=0) for e in dext)
-        g = new_g
-
-        w_up_g, w_down_t, w_out_t = plan.scatter_all(w_up_g, w_down_t, w_out_t)
+        _, hat1, inv1 = normalize(resid, gain[l, 0], shift[l, 0])
+        back, g_gain1, g_shift1 = normalize_back(gn1, hat1, inv1, gain[l, 0])
+        g = gmid + back
+
+        w_up_g = plan.plane_scatter(w_up_g, (plan.core,) + core_rest)
+        w_up_g = plan.ring_scatter([w_up_g[:, r * ffq : (r + 1) * ffq] for r in range(mp)])
+        w_down_t = plan.plane_scatter(w_down_t, (plan.core,) + core_rest[::-1])
+        w_down_t = plan.ring_scatter([w_down_t[:, r * ffq : (r + 1) * ffq] for r in range(mp)])
+        w_out_t = plan.plane_scatter(w_out_t, (plan.core,) + core_rest)
+        w_out_t = w_out_t.reshape(-1, mp, heads_w)
+        w_out_t = plan.ring_scatter([pick(w_out_t, (plan.z - r) % mp, 1) for r in range(mp)])
         w_ext_g = plan.plane_scatter(w_ext_g, core_rest[::-1])
         w_ext_g = w_ext_g.reshape(2, -1, w_ext_g.shape[1])
         part, zero = w_ext_g[..., : 3 * heads_w], w_ext_g[..., 3 * heads_w :]
@@ -888,6 +881,8 @@
         gq = hot * g_bext[None, :heads_w]
         gv = hot * g_bext[None, 2 * heads_w : 3 * heads_w]
         gq = gq.reshape(-1).at[:HD].add(g_bext[3 * heads_w : 3 * heads_w + HD])
+        g_bup = g_bup.reshape(mp, ffq)
+        g_bup = jnp.stack([pick(g_bup, (plan.z - q) % mp, 0) for q in range(mp)])
         vec[l] = jnp.concatenate(
             [
                 g_gain1, g_gain2, g_shift1, g_shift2, g_bout, g_bdown,
@@ -896,19 +891,18 @@
         )
 
     dx = plan.relabel(g.astype(BF)).astype(F32)
-    total_v = jnp.stack([vec[l] for l in range(layers)])
-    total_v = total(dims + ("zh", "zl"), total_v.reshape(-1, 128)).reshape(total_v.shape)
+    total = lax.psum(jnp.stack([vec[l] for l in range(layers)]), dims + ("zh", "zl"))
     n = d_model
-    g_gain = total_v[:, : 2 * n].reshape(layers, 2, n)
-    g_bias = total_v[:, 2 * n : 4 * n].reshape(layers, 2, n)
-    g_bout = total_v[:, 4 * n : 5 * n]
-    g_bdown = total_v[:, 5 * n : 6 * n]
+    g_gain = total[:, : 2 * n].reshape(layers, 2, n)
+    g_bias = total[:, 2 * n : 4 * n].reshape(layers, 2, n)
+    g_bout = total[:, 4 * n : 5 * n]
+    g_bdown = total[:, 5 * n : 6 * n]
     at = 6 * n
-    g_bqv = total_v[:, at : at + 2 * mp * heads_w].reshape(layers, 2, mp, heads_w)
+    g_bqv = total[:, at : at + 2 * mp * heads_w].reshape(layers, 2, mp, heads_w)
     at += 2 * mp * heads_w
-    g_bup = total_v[:, at : at + mp * ffq].reshape(layers, mp, ffq)
+    g_bup = total[:, at : at + mp * ffq].reshape(layers, mp, ffq)
     at += mp * ffq
-    key_share = total_v[:, at] / (dp * (rows * mp))
+    key_share = total[:, at] / (dp * (rows * mp))
     return (
         y[None, :rl],
         y[None, rl:],
@@ -928,6 +922,1073 @@
     )
 
 
+MESH = pl.DeviceIdType.MESH
+ANY = pl.BlockSpec(memory_space=pl.ANY)
+
+
+class Net:
+    def __init__(self, dims):
+        self.dims = dims
+        self.y, self.x, self.c = (lax.axis_index(ax) for ax in dims)
+        self.zh, self.zl = lax.axis_index("zh"), lax.axis_index("zl")
+        self.z = 2 * self.zh + self.zl
+        self.yx = 2 * self.y + self.x
+        self.me = 2 * self.c + self.zl
+        self.moves = self.c != self.zh
+
+    def group(self, delta):
+        return {self.dims[2]: self.c ^ (delta >> 1), "zl": self.zl ^ (delta & 1)}
+
+    def member(self, m):
+        return {self.dims[2]: m >> 1, "zl": m & 1}
+
+    def plane(self, e):
+        return {self.dims[0]: self.y ^ (e >> 1), self.dims[1]: self.x ^ (e & 1)}
+
+    def line(self, r):
+        to = (self.z + r) % 4
+        return {"zh": to // 2, "zl": to % 2}
+
+    def partner(self):
+        return {self.dims[2]: 1 - self.c, "zh": 1 - self.zh}
+
+    def greet(self, peers):
+        barrier = pltpu.get_barrier_semaphore()
+        for peer in peers:
+            pl.semaphore_signal(barrier, inc=1, device_id=peer, device_id_type=MESH)
+        pl.semaphore_wait(barrier, len(peers))
+
+
+class Sems:
+    def __init__(self, ssem, rsem):
+        self.ssem, self.rsem, self.used = ssem, rsem, 0
+
+    def copy(self, src, dst, device):
+        i = self.used
+        self.used += 1
+        return send(src, dst, self.ssem.at[i], self.rsem.at[i], device)
+
+
+class Batch:
+    def __init__(self, copies, when=None):
+        self.copies, self.when = copies, when
+
+    def _do(self, f):
+        if self.when is None:
+            f()
+        else:
+            pl.when(self.when)(f)
+
+    def start(self):
+        self._do(lambda: [c.start() for c in self.copies] and None)
+
+    def recv(self):
+        self._do(lambda: [c.wait_recv() for c in self.copies] and None)
+
+    def sent(self):
+        self._do(lambda: [c.wait_send() for c in self.copies] and None)
+
+    def end(self):
+        self.recv()
+        self.sent()
+
+
+def aligned(v, n=16):
+    return pl.multiple_of(v, n)
+
+
+def z_weights(net, sems, layer, w_up, w_down, zup, zdn):
+    rows, n = zup.shape[1], zup.shape[2]
+    part = zdn.shape[1]
+    out = []
+    for r in (1, 2, 3):
+        dev, slot = net.line(r), 3 - r
+        src = w_up.at[layer, pl.ds(aligned(net.yx * rows), rows), pl.ds(aligned(net.c * n, 128), n)]
+        out.append(sems.copy(src, zup.at[slot], dev))
+        src = w_down.at[layer, pl.ds(aligned(net.c * n + net.yx * part), part)]
+        out.append(sems.copy(src, zdn.at[slot], dev))
+    return Batch(out)
+
+
+def plane_weights(net, sems, lsem, layer, w_up, w_down, zup, zdn, wup, wdn):
+    rows, n = zup.shape[1], zup.shape[2]
+    part = zdn.shape[1]
+    at_up = pl.ds(aligned(net.yx * rows), rows)
+    at_dn = pl.ds(aligned(net.yx * part), part)
+    out = []
+    for e in (1, 2, 3):
+        out.append(sems.copy(zup, wup.at[pl.ds(1, 3), at_up], net.plane(e)))
+        out.append(sems.copy(zdn, wdn.at[pl.ds(1, 3), at_dn], net.plane(e)))
+    cols = pl.ds(aligned(net.c * n, 128), n)
+    local = [
+        pltpu.make_async_copy(zup, wup.at[pl.ds(1, 3), at_up], lsem.at[0]),
+        pltpu.make_async_copy(zdn, wdn.at[pl.ds(1, 3), at_dn], lsem.at[1]),
+        pltpu.make_async_copy(w_up.at[layer, :, cols], wup.at[0], lsem.at[2]),
+        pltpu.make_async_copy(w_down.at[layer, pl.ds(aligned(net.c * n), n)], wdn.at[0], lsem.at[3]),
+    ]
+    return Batch(out), local
+
+
+class Projections:
+    def __init__(self, net, sems, wq, w0, qland, zland, ext):
+        self.net, self.wq, self.w0, self.qland, self.zland, self.ext = net, wq, w0, qland, zland, ext
+        rows = qland.shape[1]
+        here = pl.ds(aligned(net.yx * rows), rows)
+        at = net.yx
+        self.q1 = Batch([sems.copy(wq.at[here], qland.at[at], net.partner())], net.moves)
+        self.q2 = Batch([sems.copy(qland.at[at], qland.at[at], net.plane(e)) for e in (1, 2, 3)], net.moves)
+        self.h1 = []
+        for r in (1, 2, 3):
+            copy = sems.copy(w0.at[here], zland.at[at], net.line(r))
+            self.h1.append(copy)
+        self.h2 = Batch([sems.copy(zland.at[at], zland.at[at], net.plane(e)) for e in (1, 2, 3)], net.z != 0)
+
+    def start(self):
+        self.q1.start()
+
+        @pl.when(self.net.z == 0)
+        def _():
+            for copy in self.h1:
+                copy.start()
+
+    def forward(self):
+        self.q1.recv()
+        self.q2.start()
+        for r in (1, 2, 3):
+            pl.when(self.net.z == r)(lambda: self.h1[r - 1].wait_recv())
+        self.h2.start()
+
+    def finish(self):
+        rows, n = self.qland.shape[1:]
+        self.q2.recv()
+        self.h2.recv()
+
+        @pl.when(self.net.moves)
+        def _():
+            for k in range(4):
+                self.ext[k * rows : (k + 1) * rows, :n] = self.qland[k]
+
+        @pl.when(jnp.logical_not(self.net.moves))
+        def _():
+            self.ext[:, :n] = self.wq[...]
+
+        @pl.when(self.net.z != 0)
+        def _():
+            for k in range(4):
+                self.ext[k * rows : (k + 1) * rows, n:] = self.zland[k]
+
+        @pl.when(self.net.z == 0)
+        def _():
+            self.ext[:, n:] = self.w0[...]
+
+        self.q1.sent()
+        self.q2.sent()
+        self.h2.sent()
+
+        @pl.when(self.net.z == 0)
+        def _():
+            for copy in self.h1:
+                copy.wait_send()
+
+
+def first_x(dims, x, wq, w0, small, w_up, w_down, xr, ext, smalls, zup, zdn, qland, zland, lsem, ssem, rsem):
+    net, sems = Net(dims), Sems(ssem, rsem)
+    moved = Batch([sems.copy(x, xr, net.partner())], net.moves)
+    proj = Projections(net, sems, wq, w0, qland, zland, ext)
+    tiny = Batch([sems.copy(small, smalls.at[4 - r], net.line(r)) for r in (1, 2, 3)])
+    weights = z_weights(net, sems, 0, w_up, w_down, zup, zdn)
+    net.greet([net.partner()] + [net.line(r) for r in (1, 2, 3)] + [net.plane(e) for e in (1, 2, 3)])
+    proj.start()
+    moved.start()
+    tiny.start()
+    weights.start()
+    smalls[0] = small[...]
+
+    @pl.when(jnp.logical_not(net.moves))
+    def _():
+        xr[...] = x[...]
+
+    proj.forward()
+    proj.finish()
+    moved.end()
+    tiny.end()
+    weights.end()
+
+
+def project_part(net, sems, resid, gain, shift, w, bias, fl, fs, pj_l, pj_s):
+    nl, ns = fl.shape[0] // 4, fs.shape[0] // 4
+    half = nl // 2
+    parts = ((fs, pj_s, ns, 0, ns, nl), (fl, pj_l, nl, 0, half, 0), (fl, pj_l, nl, half, half, half))
+    me = net.me
+
+    def rows(k, m):
+        ref, _, n, at, size, _ = parts[k]
+        return ref.at[pl.ds(aligned(m * n + at), size)]
+
+    def compute(k, m):
+        ref, out, n, at, size, _ = parts[k]
+        here = pl.ds(aligned(m * n + at), size)
+        out[here] = (mm(ref[here], w[...]) + bias[...]).astype(jnp.bfloat16)
+
+    chip = [sems.copy(rows(k, me), rows(k, me), net.group(1)) for k in range(3)]
+    core = [sems.copy(rows(k, me), rows(k, me), net.group(2)) for k in range(3)]
+    over = [sems.copy(rows(k, me ^ 1), rows(k, me ^ 1), net.group(2)) for k in range(3)]
+    for k in range(3):
+        ref, _, n, at, size, src = parts[k]
+        hat, _ = norm_rows(resid[src : src + size].astype(jnp.float32))
+        ref[pl.ds(aligned(me * n + at), size)] = (hat * gain[...] + shift[...]).astype(jnp.bfloat16)
+        chip[k].start()
+        core[k].start()
+    for k in range(3):
+        compute(k, me)
+    for k in range(3):
+        core[k].wait_recv()
+        compute(k, me ^ 2)
+    for k in range(3):
+        chip[k].wait_recv()
+        over[k].start()
+        compute(k, me ^ 1)
+    for k in range(3):
+        over[k].wait_recv()
+        compute(k, me ^ 3)
+    return chip + core + over
+
+
+def attend_part(net, sems, xl, xs, att, ol, os, lsel, lses, cl, cs, land):
+    nl, ns = xl.shape[0] // 4, xs.shape[0] // 4
+    w = ol.shape[1]
+    base = sems.used
+    sems.used += 8
+
+    def part(k):
+        return ((ol, nl, 0), (os, ns, nl))[k]
+
+    def copy(k, m):
+        src, n, at = part(k)
+        return send(
+            src.at[pl.ds(m * n, n)],
+            land.at[net.me, pl.ds(at, n)],
+            sems.ssem.at[base + 4 * k + m],
+            sems.rsem.at[base + 4 * k + net.me],
+            net.member(m),
+        )
+
+    def arrived(k, m):
+        src, n, at = part(k)
+        i = base + 4 * k + m
+        return send(src.at[pl.ds(0, n)], land.at[m, pl.ds(at, n)], sems.ssem.at[i], sems.rsem.at[i], net.member(m))
+
+    def start(k, m):
+        src, n, at = part(k)
+
+        @pl.when(net.me != m)
+        def _():
+            copy(k, m).start()
+
+        @pl.when(net.me == m)
+        def _():
+            land[m, at : at + n] = src[m * n : (m + 1) * n]
+
+    def started(k, n):
+        def done(b):
+            for m in range(b * BR // n, (b + 1) * BR // n):
+                start(k, m)
+
+        return done
+
+    fwd_one(xs, os, lses, cs, started(1, ns))
+    fwd_one(xl, ol, lsel, cl, started(0, nl))
+    for m in range(4):
+
+        @pl.when(net.me != m)
+        def _():
+            for k in range(2):
+                copy(k, m).wait_send()
+                arrived(k, m).wait_recv()
+
+    for m in range(4):
+        att[:, m * w : (m + 1) * w] = land[m]
+
+
+def layer_x(
+    dims, first, resid, gain, shift, w, bias, w_up, w_down, zup, zdn, *rest
+):
+    net = Net(dims)
+    if first:
+        wq, w0, *rest = rest
+    else:
+        dy, *rest = rest
+    att, fl, fs, pj_l, pj_s, ol, os, lsel, lses, cl, cs, wup, wdn, extra, *rest = rest
+    land, lsem, ssem, rsem, *rest = rest
+    sems = Sems(ssem, rsem)
+    weights, local = plane_weights(net, sems, lsem, 0 if first else 1, w_up, w_down, zup, zdn, wup, wdn)
+    peers = [net.group(2), net.group(3), net.partner()]
+    peers += [net.plane(e) for e in (1, 2, 3)] + [net.line(r) for r in (1, 2, 3)]
+    if first:
+        qland, zland = rest
+        proj = Projections(net, sems, wq, w0, qland, zland, extra)
+    else:
+        moved = Batch([sems.copy(dy, extra, net.partner())], net.moves)
+    net.greet(peers)
+    weights.start()
+    for copy in local:
+        copy.start()
+    pending = project_part(net, sems, resid, gain, shift, w, bias, fl, fs, pj_l, pj_s)
+    if first:
+        proj.start()
+    else:
+        moved.start()
+
+        @pl.when(jnp.logical_not(net.moves))
+        def _():
+            extra[...] = dy[...]
+
+    attend_part(net, sems, pj_l, pj_s, att, ol, os, lsel, lses, cl, cs, land)
+    if first:
+        proj.forward()
+    for copy in pending:
+        copy.wait_send()
+    if first:
+        proj.finish()
+    else:
+        moved.end()
+    for copy in local:
+        copy.wait()
+    weights.end()
+
+
+def gelu_pair(u):
+    k = 0.7978845608028654
+    sq = u * u
+    t = jnp.tanh(u * (k + k * 0.044715 * sq))
+    h = 0.5 * (1.0 + t)
+    act = u * h
+    slope = h + act * (1.0 - t) * (k + 3 * k * 0.044715 * sq)
+    return act, slope
+
+
+def mlp_x(
+    dims, last, att, resid, wout, bout, gain, shift, wup, wdn, bup, bdown, w_up, w_down, *rest
+):
+    net = Net(dims)
+    if last:
+        middle, n2, act, slope, new, out, got, ssem, rsem = rest
+    else:
+        middle, n2, act, slope, new, zup, zdn, out, got, ssem, rsem = rest
+    sems = Sems(ssem, rsem)
+    n = att.shape[0]
+    f = wup.shape[2]
+    there = sems.copy(n2.at[pl.ds(0, n)], n2.at[pl.ds(n, n)], net.group(2))
+    back = sems.copy(out, got, net.group(2))
+    peers = [net.group(2)]
+    if not last:
+        weights = z_weights(net, sems, 1, w_up, w_down, zup, zdn)
+        peers += [net.line(r) for r in (1, 2, 3)]
+    net.greet(peers)
+    if not last:
+        weights.start()
+    half = n // 2
+    for i in range(2):
+        at = slice(i * half, (i + 1) * half)
+        middle[at] = resid[at].astype(jnp.float32) + mm(att[at], wout[...]) + bout[...]
+        hat, _ = norm_rows(middle[at])
+        n2[at] = (hat * gain[...] + shift[...]).astype(jnp.bfloat16)
+    there.start()
+
+    def hidden(at):
+        for r in range(4):
+            cols = slice(r * f, (r + 1) * f)
+            u = mm(n2[at], wup[r]) + bup[r : r + 1]
+            a, s = gelu_pair(u)
+            act[at, cols] = a.astype(jnp.bfloat16)
+            slope[at, cols] = s.astype(jnp.bfloat16)
+
+    def down(at):
+        total = mm(act[at, :f], wdn[0])
+        for r in range(1, 4):
+            total = total + mm(act[at, r * f : (r + 1) * f], wdn[r])
+        return total
+
+    quarter = n // 4
+    for i in range(4):
+        hidden(slice(i * quarter, (i + 1) * quarter))
+    there.wait_recv()
+    for i in range(4):
+        hidden(slice(n + i * quarter, n + (i + 1) * quarter))
+    for i in range(2):
+        out[i * half : (i + 1) * half] = down(slice(n + i * half, n + (i + 1) * half)).astype(
+            jnp.bfloat16
+        )
+    back.start()
+    for i in range(2):
+        at = slice(i * half, (i + 1) * half)
+        new[at] = middle[at] + down(at) + bdown[...]
+    back.wait_recv()
+    new[...] += got[...].astype(jnp.float32)
+    there.wait_send()
+    back.wait_send()
+    if not last:
+        weights.end()
+
+
+TN = (((0,), (0,)), ((), ()))
+
+
+def ext_scatter(net, sems, dw, land):
+    return [sems.copy(dw.at[net.yx ^ e], land.at[e - 1], net.plane(e)) for e in (1, 2, 3)]
+
+
+def mlp_back_x(
+    dims, last, g, att, wout, gain, wup, wdn, middle, n2, act, slope, *rest
+):
+    net = Net(dims)
+    if last:
+        ins = ()
+    else:
+        s_in, so_in, dq_in, d0_in, *rest = rest
+    gmid, go, dup, ddn, dout, sums, sums_up, *rest = rest
+    if not last:
+        f_out, fo_out, q_out, z_out, *rest = rest
+    gm, gu, gact, out, got, oself, olands, *rest = rest
+    if not last:
+        land, oland, qland, zland, *rest = rest
+    ssem, rsem = rest
+    sems = Sems(ssem, rsem)
+    n, d = g.shape
+    f = wup.shape[2]
+    there = sems.copy(gm.at[pl.ds(0, n)], gm.at[pl.ds(n, n)], net.group(2))
+    back = sems.copy(out, got, net.group(2))
+    cross = sems.copy(oself, olands, net.group(2))
+    peers = [net.group(2)]
+    if not last:
+        carry = FinishLine(net, sems, s_in, so_in, land, oland)
+        ext = Batch(ext_scatter(net, sems, dq_in, qland) + ext_scatter(net, sems, d0_in, zland))
+        peers += [net.line(r) for r in (1, 2, 3)] + [net.plane(e) for e in (1, 2, 3)]
+    gm[:n] = g[...].astype(jnp.bfloat16)
+    net.greet(peers)
+    there.start()
+    if not last:
+        carry.start()
+        ext.start()
+    sums[...] = jnp.zeros_like(sums)
+    sums[0:1] = jnp.sum(g[...], axis=0, keepdims=True)
+    quarter = n // 4
+
+    def hidden(at):
+        for r in range(4):
+            cols = slice(r * f, (r + 1) * f)
+            u = mm(gm[at], wdn[r], NT)
+            gu[at, cols] = (u * slope[at, cols].astype(jnp.float32)).astype(jnp.bfloat16)
+
+    def up(at):
+        total = mm(gu[at, :f], wup[0], NT)
+        for r in range(1, 4):
+            total = total + mm(gu[at, r * f : (r + 1) * f], wup[r], NT)
+        return total
+
+    for i in range(4):
+        hidden(slice(i * quarter, (i + 1) * quarter))
+    there.wait_recv()
+    for i in range(4):
+        hidden(slice(n + i * quarter, n + (i + 1) * quarter))
+    half = n // 2
+    for i in range(2):
+        out[i * half : (i + 1) * half] = up(slice(n + i * half, n + (i + 1) * half)).astype(
+            jnp.bfloat16
+        )
+    back.start()
+    for i in range(2):
+        at = slice(i * half, (i + 1) * half)
+        gact[at] = up(at)
+    chunk = d // 4
+
+    def products(left, right, dst):
+        for k in range(4):
+            for r in range(4):
+                dst[k, r] = mm(
+                    left[:, k * chunk : (k + 1) * chunk], right[:, r * f : (r + 1) * f], TN
+                ).astype(jnp.bfloat16)
+
+    products(gm, act, ddn)
+    back.wait_recv()
+    gn = gact[...] + got[...].astype(jnp.float32)
+    hat, inv = norm_rows(middle[...])
+    gh = gn * gain[...]
+    a = jnp.mean(gh, axis=-1, keepdims=True)
+    b = jnp.mean(gh * hat, axis=-1, keepdims=True)
+    gmid[...] = g[...] + inv * (gh - a - hat * b)
+    sums[1:2] = jnp.sum(gn * hat, axis=0, keepdims=True)
+    sums[2:3] = jnp.sum(gn, axis=0, keepdims=True)
+    sums[3:4] = jnp.sum(gmid[...], axis=0, keepdims=True)
+    ga = gmid[...].astype(jnp.bfloat16)
+    go[...] = mm(ga, wout[...], NT).astype(jnp.bfloat16)
+    e = att.shape[1] // 2
+    other = att[:, pl.ds(aligned((1 - net.c) * e, 128), e)]
+    oself[...] = mm(ga, other, TN).astype(jnp.bfloat16)
+    cross.start()
+    products(n2, gu, dup)
+    sums_up[...] = jnp.zeros_like(sums_up)
+    sums_up[0:1] = jnp.sum(gu[...].astype(jnp.float32), axis=0, keepdims=True)
+    mine = mm(ga, att[:, pl.ds(aligned(net.c * e, 128), e)], TN)
+    cross.wait_recv()
+    mine = mine + olands[...].astype(jnp.float32)
+    for k in range(4):
+        dout[k] = mine[k * chunk : (k + 1) * chunk].astype(jnp.bfloat16)
+    there.wait_send()
+    back.wait_send()
+    cross.wait_send()
+    if not last:
+        carry.finish(f_out, fo_out)
+        ext.recv()
+        for own, lands, dst in ((dq_in, qland, q_out), (d0_in, zland, z_out)):
+            t = own[net.yx].astype(jnp.float32)
+            for e in range(3):
+                t = t + lands[e].astype(jnp.float32)
+            dst[...] = t.astype(jnp.bfloat16)
+        ext.sent()
+
+
+class FinishLine:
+    def __init__(self, net, sems, s, so, land, oland):
+        self.net, self.s, self.so, self.land, self.oland = net, s, so, land, oland
+        self.main = Batch([sems.copy(s.at[r], land.at[3 - r], net.line(r)) for r in (1, 2, 3)])
+        self.out = []
+        for r in (1, 2, 3):
+            to = (net.z + r) % 4
+            copy = sems.copy(so.at[to % 2], oland.at[3 - r], net.line(r))
+            self.out.append((copy, to // 2 == net.c))
+        self.owner = net.zh == net.c
+
+    def start(self):
+        self.main.start()
+        for copy, use in self.out:
+            pl.when(use)(copy.start)
+
+    def finish(self, f_out, fo_out):
+        self.main.recv()
+        f_out[...] = (
+            self.s[0].astype(jnp.float32)
+            + self.land[0].astype(jnp.float32)
+            + self.land[1].astype(jnp.float32)
+            + self.land[2].astype(jnp.float32)
+        ).astype(f_out.dtype)
+
+        @pl.when(self.owner)
+        def _():
+            for copy, _ in self.out:
+                copy.wait_recv()
+            fo_out[...] = (
+                self.so[self.net.zl].astype(jnp.float32)
+                + self.oland[0].astype(jnp.float32)
+                + self.oland[1].astype(jnp.float32)
+                + self.oland[2].astype(jnp.float32)
+            ).astype(fo_out.dtype)
+
+        @pl.when(jnp.logical_not(self.owner))
+        def _():
+            fo_out[...] = jnp.zeros_like(fo_out)
+
+        self.main.sent()
+        for copy, use in self.out:
+            pl.when(use)(copy.wait_send)
+
+
+def layer_back_x(
+    dims, xl, xs, go, ol, os, lsel, lses, cl, cs, w, resid, gain, gmid, fl, fs, dup, ddn, dout,
+    g_ref, sums, bsum, dq, d0, s, so,
+    dl, ds, acc, kt, outg, gl, gs, mine, out, got, rup, rdn, rout, ssem, rsem,
+):
+    net, sems = Net(dims), Sems(ssem, rsem)
+    nl, ns = xl.shape[0] // 4, xs.shape[0] // 4
+    wid = ol.shape[1]
+    me = net.me
+    base = sems.used
+    sems.used += 8
+    big = []
+    for e in (1, 2, 3):
+        at = net.yx ^ e
+        big.append(sems.copy(ddn.at[at], rdn.at[e - 1], net.plane(e)))
+        big.append(sems.copy(dup.at[at], rup.at[e - 1], net.plane(e)))
+        big.append(sems.copy(dout.at[at], rout.at[e - 1], net.plane(e)))
+    big = Batch(big)
+    for m in range(4):
+        outg[m] = go[:, m * wid : (m + 1) * wid]
+    net.greet([net.group(d) for d in (1, 2, 3)] + [net.plane(e) for e in (1, 2, 3)])
+
+    def part(k):
+        return ((gl, nl, 0), (gs, ns, nl))[k]
+
+    def copy(k, m):
+        dst, n, at = part(k)
+        return send(
+            outg.at[m, pl.ds(at, n)],
+            dst.at[pl.ds(aligned(me * n), n)],
+            sems.ssem.at[base + 4 * k + m],
+            sems.rsem.at[base + 4 * k + me],
+            net.member(m),
+        )
+
+    def arrived(k, m):
+        dst, n, at = part(k)
+        i = base + 4 * k + m
+        return send(outg.at[m, pl.ds(at, n)], dst.at[pl.ds(m * n, n)], sems.ssem.at[i], sems.rsem.at[i], net.member(m))
+
+    for k in (1, 0):
+        for m in range(4):
+            dst, n, at = part(k)
+
+            @pl.when(me != m)
+            def _():
+                copy(k, m).start()
+
+            @pl.when(me == m)
+            def _():
+                dst[m * n : (m + 1) * n] = outg[m, at : at + n]
+
+    big.start()
+    for k in (1, 0):
+        for m in range(4):
+
+            @pl.when(me != m)
+            def _():
+                arrived(k, m).wait_recv()
+
+        if k:
+            bwd_one(xs, gs, os, lses, cs, ds, acc, kt)
+        else:
+            bwd_one(xl, gl, ol, lsel, cl, dl, acc, kt)
+    for m in range(4):
+
+        @pl.when(me != m)
+        def _():
+            for k in range(2):
+                copy(k, m).wait_send()
+
+    def partial(m):
+        a = mm(dl[pl.ds(aligned(m * nl), nl)], w[...], NT)
+        b = mm(ds[pl.ds(aligned(m * ns), ns)], w[...], NT)
+        return jnp.concatenate([a, b], axis=0)
+
+    to_core = [sems.copy(out.at[k], got.at[k], net.group(2)) for k in (0, 1)]
+    to_chip = sems.copy(out.at[2], got.at[2], net.group(1))
+    out[0] = partial(me ^ 3).astype(jnp.bfloat16)
+    to_core[0].start()
+    mine[...] = partial(me ^ 1)
+    to_core[0].wait_recv()
+    out[2] = (mine[...] + got[0].astype(jnp.float32)).astype(jnp.bfloat16)
+    to_chip.start()
+    out[1] = partial(me ^ 2).astype(jnp.bfloat16)
+    to_core[1].start()
+    mine[...] = partial(me)
+    chunk = w.shape[0] // 4
+    nq = dq.shape[2]
+    for k in range(4):
+        at = slice(k * chunk, (k + 1) * chunk)
+        both = mm(fl[:, at], dl[...], TN) + mm(fs[:, at], ds[...], TN)
+        dq[k] = both[:, :nq].astype(jnp.bfloat16)
+        d0[k] = both[:, nq:].astype(jnp.bfloat16)
+    bsum[...] = jnp.zeros_like(bsum)
+    bsum[0:1] = jnp.sum(dl[...].astype(jnp.float32), axis=0, keepdims=True) + jnp.sum(
+        ds[...].astype(jnp.float32), axis=0, keepdims=True
+    )
+    hat, inv = norm_rows(resid[...].astype(jnp.float32))
+    to_core[1].wait_recv()
+    to_chip.wait_recv()
+    grad = mine[...] + got[1].astype(jnp.float32) + got[2].astype(jnp.float32)
+    gh = grad * gain[...]
+    a = jnp.mean(gh, axis=-1, keepdims=True)
+    b = jnp.mean(gh * hat, axis=-1, keepdims=True)
+    g_ref[...] = gmid[...] + inv * (gh - a - hat * b)
+    sums[...] = jnp.zeros_like(sums)
+    sums[0:1] = jnp.sum(grad * hat, axis=0, keepdims=True)
+    sums[1:2] = jnp.sum(grad, axis=0, keepdims=True)
+    for c in to_core + [to_chip]:
+        c.wait_send()
+    big.recv()
+    yx = net.yx
+    for r in range(4):
+        for i, (own, land) in enumerate(((dup, rup), (ddn, rdn))):
+            t = own[yx, r].astype(jnp.float32)
+            for e in range(3):
+                t = t + land[e, r].astype(jnp.float32)
+            s[r, i] = t.astype(jnp.bfloat16)
+    t = dout[yx].astype(jnp.float32)
+    for e in range(3):
+        t = t + rout[e].astype(jnp.float32)
+    n = so.shape[2]
+    for i in range(2):
+        so[i] = t[:, i * n : (i + 1) * n].astype(jnp.bfloat16)
+    big.sent()
+
+
+def tail_x(
+    axes, s, so, dq, d0, f1, fo1, q1, z1, vec, dx,
+    gup, gdn, gout, gqkv, dxr, total_ref,
+    land, oland, f0, fo0, qland, zland, qs, zs, qline, zline, fself, fland, oself, olands, qself, qlands, zself, zlands, vland,
+    ssem, rsem,
+):
+    dims = axes[:-2]
+    net, sems = Net(dims), Sems(ssem, rsem)
+    moved = Batch([sems.copy(dx, dxr, net.partner())], net.moves)
+    line = FinishLine(net, sems, s, so, land, oland)
+    ext = Batch(ext_scatter(net, sems, dq, qland) + ext_scatter(net, sems, d0, zland))
+    rounds = [{ax: 1 - lax.axis_index(ax)} for ax in axes]
+    nv = len(axes)
+    steps = [sems.copy(vland.at[i], vland.at[nv + 1 + i], peer) for i, peer in enumerate(rounds)]
+    qsend = Batch([sems.copy(qs, qline, net.line(2))], net.moves)
+    qrecv = jnp.logical_not(net.moves)
+    zsend = [sems.copy(zs, zline.at[r - 1], net.line(r)) for r in (1, 2, 3)]
+    cross = Batch([sems.copy(fself, fland, net.group(2)), sems.copy(zself, zlands, net.group(2))])
+    owned = Batch([sems.copy(oself, olands, net.group(2)), sems.copy(qself, qlands, net.group(2))])
+    net.greet(
+        [net.partner(), net.group(2)]
+        + [net.line(r) for r in (1, 2, 3)]
+        + [net.plane(e) for e in (1, 2, 3)]
+    )
+    f32 = jnp.float32
+    ext.start()
+    moved.start()
+    line.start()
+
+    @pl.when(jnp.logical_not(net.moves))
+    def _():
+        dxr[...] = dx[...]
+
+    vland[0] = vec[...]
+    for i in range(nv):
+        steps[i].start()
+        steps[i].wait()
+        vland[i + 1] = vland[i] + vland[nv + 1 + i]
+    total_ref[...] = vland[nv]
+
+    ext.recv()
+    yx = net.yx
+    for own, lands, dst in ((dq, qland, qs), (d0, zland, zs)):
+        t = own[yx].astype(f32)
+        for e in range(3):
+            t = t + lands[e].astype(f32)
+        dst[0] = t.astype(jnp.bfloat16)
+    qs[1] = q1[...]
+    zs[1] = z1[...]
+    qsend.start()
+    for r in (1, 2, 3):
+        pl.when(net.z == 4 - r)(zsend[r - 1].start)
+    line.finish(f0, fo0)
+    half = f0.shape[1] // 2
+    theirs = pl.ds(aligned((1 - net.c) * half), half)
+    ours = pl.ds(aligned(net.c * half), half)
+
+    @pl.when(qrecv)
+    def _():
+        qsend.copies[0].wait_recv()
+        for l in range(2):
+            qself[l] = (qs[l, theirs].astype(f32) + qline[l, theirs].astype(f32)).astype(jnp.bfloat16)
+            gqkv[l] = qs[l, ours].astype(f32) + qline[l, ours].astype(f32)
+        for l, fo in ((0, fo0), (1, fo1)):
+            oself[l] = fo[theirs].astype(jnp.bfloat16)
+            gout[l] = fo[ours].astype(f32)
+        for c in owned.copies:
+            c.start()
+
+    @pl.when(net.z == 0)
+    def _():
+        for r in (1, 2, 3):
+            zsend[r - 1].wait_recv()
+        for l in range(2):
+            t = zs[l].astype(f32)
+            for r in range(3):
+                t = t + zline[r, l].astype(f32)
+            zs[l] = t.astype(jnp.bfloat16)
+
+    for l, f in ((0, f0), (1, f1)):
+        for i in range(2):
+            fself[l, i] = f[i, theirs].astype(jnp.bfloat16)
+        zself[l] = zs[l, theirs]
+    cross.start()
+    cross.recv()
+    n = f0.shape[2]
+
+    @pl.when(net.moves)
+    def _():
+        for c in owned.copies:
+            c.wait_recv()
+        gqkv[...] = qlands[...].astype(f32)
+        gout[...] = olands[...].astype(f32)
+
+    for c in range(2):
+
+        @pl.when(net.c == c)
+        def _():
+            for l, f in ((0, f0), (1, f1)):
+                for i, dst in ((0, gup), (1, gdn)):
+                    dst[l, :, c * n : (c + 1) * n] = f[i, ours].astype(f32)
+                    dst[l, :, (1 - c) * n : (2 - c) * n] = fland[l, i].astype(f32)
+
+    @pl.when(net.z == 0)
+    def _():
+        wid = gout.shape[2]
+        for l in range(2):
+            t = zs[l, ours].astype(f32) + zlands[l].astype(f32)
+            gqkv[l, :, :HD] += t[:, :HD]
+            gqkv[l, :, wid : wid + HD] += t[:, HD:]
+
+    pl.when(qrecv)(lambda: [c.wait_send() for c in owned.copies] and None)
+    cross.sent()
+    qsend.sent()
+    for r in (1, 2, 3):
+        pl.when(net.z == 4 - r)(zsend[r - 1].wait_send)
+    ext.sent()
+    moved.end()
+
+
+def call(kernel, static, args, outs, scratch, ident, name, flops):
+    return pl.pallas_call(
+        functools.partial(kernel, *static),
+        out_shape=tuple(jax.ShapeDtypeStruct(tuple(s), t) for s, t, _ in outs),
+        in_specs=[VMEM if v else ANY for _, v in args],
+        out_specs=tuple(VMEM if v else ANY for _, _, v in outs),
+        scratch_shapes=scratch,
+        compiler_params=pltpu.CompilerParams(
+            vmem_limit_bytes=56 * 1024 * 1024, collective_id=ident, has_side_effects=True
+        ),
+        cost_estimate=pl.CostEstimate(flops=flops, bytes_accessed=10**7, transcendentals=10**6),
+        name=name,
+    )(*[a for a, _ in args])
+
+
+def sems_of(n):
+    return [DMA((n,)), DMA((n,))]
+
+
+def fast_body(
+    dims, x_long, x_short, dy_long, dy_short, ln_gain, ln_bias, w_qkv, b_qv, w_out, b_out, w_up, b_up, w_down, b_down, threshold
+):
+    bf, f32 = jnp.bfloat16, jnp.float32
+    layers, d = w_qkv.shape[0], w_qkv.shape[1]
+    wid, ffq = w_qkv.shape[3], w_up.shape[2]
+    rl, rs = x_long.shape[1], x_short.shape[1]
+    rows = rl + rs
+    nq, nx = 3 * wid, 3 * wid + 2 * HD
+    f = ffq // 2
+    chunk, part = d // 4, f // 4
+    net = Net(dims)
+    axes = dims + ("zh", "zl")
+    vm = lambda *s: pltpu.VMEM(tuple(s), bf)
+    vf = lambda *s: pltpu.VMEM(tuple(s), f32)
+
+    x = jnp.concatenate([x_long[0], x_short[0]], axis=0)
+    dy = jnp.concatenate([dy_long[0], dy_short[0]], axis=0)
+    wqs = [w_qkv[l].reshape(d, nq) for l in range(layers)]
+    w0s = [w_qkv[l][:, :2, :HD].reshape(d, 2 * HD) for l in range(layers)]
+    flat = jnp.concatenate([b_up.reshape(-1), b_qv.reshape(-1)])
+    flat = jnp.pad(flat, (0, -flat.shape[0] % 4096)).reshape(16, -1)
+    order = ("zh", "zl") + dims
+    share_rows = wid // 8
+    wo = lax.dynamic_slice_in_dim(w_out, (4 * net.y + 2 * net.x + net.c) * share_rows, share_rows, 1)
+    wo = lax.all_gather(wo, order, axis=0, tiled=False)
+    wo = jnp.moveaxis(wo, 1, 0).reshape(layers, 4 * wid, d)
+
+    lands = [vm(4, chunk, nq), vm(4, chunk, 2 * HD)]
+    xr, ext0, smalls, zup, zdn = call(
+        first_x,
+        (dims,),
+        [(x, 1), (wqs[0], 1), (w0s[0], 1), (flat, 1), (w_up, 0), (w_down, 0)],
+        [((rows, d), bf, 1), ((d, nx), bf, 1), ((4,) + flat.shape, bf, 1), ((3, chunk, f), bf, 0), ((3, part, d), bf, 0)],
+        lands + [DMA((1,))] + sems_of(24),
+        1,
+        "first_x",
+        10**9,
+    )
+    n_up = layers * ffq
+    smalls = smalls.reshape(4, -1)
+    rel_bup = smalls[:, :n_up].reshape(4, layers, 2, f).astype(f32)
+    rel_bup = lax.dynamic_index_in_dim(rel_bup, net.c, 2, keepdims=False)
+    rel_bqv = smalls[:, n_up : n_up + layers * 2 * wid].reshape(4, layers, 2, wid).astype(f32)
+    my_bqv = lax.dynamic_index_in_dim(rel_bqv, (net.me - net.z) % 4, 0, keepdims=False)
+    zero_bq = lax.dynamic_index_in_dim(rel_bqv, (0 - net.z) % 4, 0, keepdims=False)[:, 0, :HD]
+    none = jnp.zeros((layers, wid), f32)
+    bias = jnp.concatenate([my_bqv[:, 0], none, my_bqv[:, 1], zero_bq, none[:, :HD]], axis=1)
+    gain, shift = ln_gain.astype(f32), ln_bias.astype(f32)
+    bo, bd = b_out.astype(f32), b_down.astype(f32)
+    limits = threshold.astype(f32) / 64.0
+
+    resid = xr
+    exts = [ext0, None]
+    saved, shares = [], []
+    for l in range(layers):
+        first = l == 0
+        extra = [(wqs[1], 1), (w0s[1], 1)] if first else [(dy, 1)]
+        extra_out = ((d, nx), bf, 1) if first else ((rows, d), bf, 1)
+        size = ((4 * rl), (4 * rs))
+        att, fl, fs, pj_l, pj_s, ol, os, lsel, lses, cl, cs, wup, wdn, got = call(
+            layer_x,
+            (dims, first),
+            [
+                (resid, 1), (gain[l, :1], 1), (shift[l, :1], 1), (exts[l], 1), (bias[l : l + 1], 1),
+                (w_up, 0), (w_down, 0), (zup, 0), (zdn, 0),
+            ] + extra,
+            [((rows, 4 * wid), bf, 1)]
+            + [((n, d), bf, 1) for n in size]
+            + [((n, nx), bf, 1) for n in size]
+            + [((n, wid), bf, 1) for n in size]
+            + [((8, n), f32, 1) for n in size] * 2
+            + [((4, d, f), bf, 0), ((4, f, d), bf, 0), extra_out],
+            [vm(4, rows, wid), DMA((4,))] + sems_of(40) + (lands if first else []),
+            2 + l,
+            "layer_x",
+            10**10,
+        )
+        if first:
+            exts[1] = got
+        else:
+            dyr = got
+        share = jnp.zeros((), f32)
+        for carry in (cl, cs):
+            n = carry.shape[1]
+            left = (n - 1 - lax.broadcasted_iota(jnp.int32, (n,), 0)).astype(f32)
+            ratio = carry[n // BR] / jnp.maximum(left, 1.0)
+            share = share + jnp.sum(jax.nn.sigmoid(4.0 * (ratio - limits[l])))
+        shares.append(share)
+        last = l == layers - 1
+        outs = [
+            ((rows, d), f32, 1), ((2 * rows, d), bf, 1), ((2 * rows, 4 * f), bf, 1), ((2 * rows, 4 * f), bf, 1),
+            ((rows, d), f32, 1),
+        ]
+        if not last:
+            outs += [((3, chunk, f), bf, 0), ((3, part, d), bf, 0)]
+        middle, n2, act, slope, new, *z = call(
+            mlp_x,
+            (dims, last),
+            [
+                (att, 1), (resid, 1), (wo[l], 1), (bo[l : l + 1], 1), (gain[l, 1:], 1), (shift[l, 1:], 1),
+                (wup, 1), (wdn, 1), (rel_bup[:, l], 1), (bd[l : l + 1], 1), (w_up, 0), (w_down, 0),
+            ],
+            outs,
+            [vm(rows, d), vm(rows, d)] + sems_of(10),
+            4 + l,
+            "mlp_x",
+            10**10,
+        )
+        if not last:
+            zup, zdn = z
+        saved.append((resid, middle, n2, act, slope, att, fl, fs, pj_l, pj_s, ol, os, lsel, lses, cl, cs, wup, wdn))
+        resid = new
+
+    y = Plan(dims, 8, 4).relabel(resid.astype(bf))
+    g = dyr.astype(f32)
+    vec = [None] * layers
+    carried = []
+    for l in reversed(range(layers)):
+        resid, middle, n2, act, slope, att, fl, fs, pj_l, pj_s, ol, os, lsel, lses, cl, cs, wup, wdn = saved[l]
+        last = l == layers - 1
+        outs = [
+            ((rows, d), f32, 1), ((rows, d), bf, 1), ((4, 4, chunk, f), bf, 1), ((4, 4, chunk, f), bf, 1),
+            ((4, chunk, 2 * wid), bf, 1), ((8, d), f32, 1), ((8, 4 * f), f32, 1),
+        ]
+        scratch = [
+            vm(2 * rows, d), vm(2 * rows, 4 * f), vf(rows, d), vm(rows, d), vm(rows, d), vm(d, 2 * wid), vm(d, 2 * wid)
+        ]
+        args = [
+            (g, 1), (att, 1), (wo[l], 1), (gain[l, 1:], 1), (wup, 1), (wdn, 1), (middle, 1), (n2, 1), (act, 1), (slope, 1)
+        ]
+        if not last:
+            args += [(v, 1) for v in carried]
+            outs += [((2, chunk, f), bf, 1), ((chunk, wid), bf, 1), ((chunk, nq), bf, 1), ((chunk, 2 * HD), bf, 1)]
+            scratch += [vm(3, 2, chunk, f), vm(3, chunk, wid), vm(3, chunk, nq), vm(3, chunk, 2 * HD)]
+        gmid, go, dup, ddn, dout, sums2, sums_up, *done = call(
+            mlp_back_x, (dims, last), args, outs, scratch + sems_of(20), 6 + l, "mlp_back_x", 10**10
+        )
+        size = ((4 * rl), (4 * rs))
+        g, sums1, bsum, dq, d0, s, so = call(
+            layer_back_x,
+            (dims,),
+            [
+                (v, 1)
+                for v in (
+                    pj_l, pj_s, go, ol, os, lsel, lses, cl, cs, exts[l], resid, gain[l, :1], gmid, fl, fs, dup, ddn, dout
+                )
+            ],
+            [
+                ((rows, d), f32, 1), ((8, d), f32, 1), ((8, nx), f32, 1), ((4, chunk, nq), bf, 1),
+                ((4, chunk, 2 * HD), bf, 1), ((4, 2, chunk, f), bf, 1), ((2, chunk, wid), bf, 1),
+            ],
+            [
+                vm(size[0], nx), vm(size[1], nx), vf(2 * (wid // HD) + 1, size[0], HD), vm(wid // HD + 1, HD, size[0]),
+                vm(4, rows, wid), vm(size[0], wid), vm(size[1], wid), vf(rows, d), vm(3, rows, d), vm(3, rows, d),
+                vm(3, 4, chunk, f), vm(3, 4, chunk, f), vm(3, chunk, 2 * wid),
+            ] + sems_of(24),
+            8 + l,
+            "layer_back_x",
+            2 * 10**10,
+        )
+        carried = [s, so, dq, d0]
+        hot = (lax.broadcasted_iota(jnp.int32, (4, 1), 0) == net.me).astype(f32)
+        b = bsum[0]
+        gq = (hot * b[None, :wid]).reshape(-1).at[:HD].add(b[nq : nq + HD])
+        gv = (hot * b[None, 2 * wid : nq]).reshape(-1)
+        up = sums_up[0].reshape(4, f)
+        up = jnp.stack([lax.dynamic_index_in_dim(up, (q - net.z) % 4, 0, keepdims=False) for q in range(4)])
+        side = (lax.broadcasted_iota(jnp.int32, (1, 2, 1), 1) == net.c).astype(f32)
+        up = (up[:, None] * side).reshape(-1)
+        vec[l] = jnp.concatenate(
+            [
+                sums1[0], sums2[1], sums1[1], sums2[2], sums2[3], sums2[0], gq, gv, up,
+                jnp.full((128,), shares[l] / 4),
+            ]
+        )
+
+    v = jnp.stack(vec)
+    flat_v = v.reshape(-1, 128)
+    pad = -flat_v.shape[0] % 8
+    flat_v = jnp.pad(flat_v, ((0, pad), (0, 0)))
+    f1, fo1, q1, z1 = done
+    s, so, dq, d0 = carried
+    half = chunk // 2
+    nv = len(axes)
+    gup, gdn, gout, gqkv, dx, tot = call(
+        tail_x,
+        (axes,),
+        [(a, 1) for a in (s, so, dq, d0, f1, fo1, q1, z1, flat_v, g.astype(bf))],
+        [
+            ((2, half, ffq), f32, 1), ((2, half, ffq), f32, 1), ((2, half, wid), f32, 1), ((2, half, nq), f32, 1),
+            ((rows, d), bf, 1), (flat_v.shape, f32, 1),
+        ],
+        [
+            vm(3, 2, chunk, f), vm(3, chunk, wid), vf(2, chunk, f), vf(chunk, wid),
+            vm(3, chunk, nq), vm(3, chunk, 2 * HD), vm(2, chunk, nq), vm(2, chunk, 2 * HD), vm(2, chunk, nq),
+            vm(3, 2, chunk, 2 * HD), vm(2, 2, half, f), vm(2, 2, half, f), vm(2, half, wid), vm(2, half, wid),
+            vm(2, half, nq), vm(2, half, nq), vm(2, half, 2 * HD), vm(2, half, 2 * HD), vf(2 * nv + 1, *flat_v.shape),
+        ] + sems_of(32),
+        10,
+        "tail_x",
+        10**9,
+    )
+    tot = tot[: flat_v.shape[0] - pad].reshape(v.shape) if pad else tot.reshape(v.shape)
+    dx = dx.astype(f32)
+    at = 6 * d
+    g_bqv = tot[:, at : at + 8 * wid].reshape(layers, 2, 4, wid)
+    at += 8 * wid
+    g_bup = tot[:, at : at + 4 * ffq].reshape(layers, 4, ffq)
+    at += 4 * ffq
+    return (
+        y[None, :rl],
+        y[None, rl:],
+        dx[None, :rl],
+        dx[None, rl:],
+        tot[:, : 2 * d].reshape(layers, 2, d),
+        tot[:, 2 * d : 4 * d].reshape(layers, 2, d),
+        gqkv.reshape(layers, half, 3, wid),
+        pick(g_bqv, net.z, 2),
+        jnp.swapaxes(gout, 1, 2),
+        tot[:, 4 * d : 5 * d],
+        gup,
+        pick(g_bup, net.z, 1),
+        jnp.swapaxes(gdn, 1, 2),
+        tot[:, 5 * d : 6 * d],
+        tot[:, at] / (8 * 4 * rows),
+    )
+
+
 def solution(mesh):
     dp, mp = mesh.shape["dp"], mesh.shape["mp"]
     bits = dp.bit_length() - 1
@@ -944,6 +2005,7 @@
         P(), P(), P(None, dims, None, z), P(None, None, z), P(None, z, dims), P(),
         P(None, dims, z), P(None, z), P(None, z, dims), P(), P(),
     )
+    run = functools.partial(fast_body, dims) if dp == 8 else functools.partial(body, dims, dp, mp)
     return jax.shard_map(
-        functools.partial(body, dims, dp, mp), mesh=fine, in_specs=in_specs, out_specs=out_specs, check_vma=False
+        run, mesh=fine, in_specs=in_specs, out_specs=out_specs, check_vma=False
     )

time: 902 us -> 624 us (0.69)
  Pallas kernels: 215 us -> 537 us
  waiting for transfers between devices: 304 us -> 0.02 us
  starting transfers between devices: 106 us -> 1.95 us
  matrix products: 92.8 us -> 0 us
  local copies, waits for them, and re-layouts: 90.7 us -> 42.6 us
  other arithmetic: 60.7 us -> 15.6 us
    pallas_call x9 -> x10, Pallas kernels: 215 us -> 537 us  [call(): pl.pallas_call(functools.partial(kernel, *static), out_shape=tuple((jax.S...]
    all_gather x6 -> x1, waiting for transfers between devices: 166 us -> 0.01 us  [fast_body(): wo = lax.all_gather(wo, order, axis=0, tiled=False)]
    ppermute x37 -> x0, waiting for transfers between devices: 138 us -> none  [the longest x20 92.7 us: swap(): lax.ppermute(v, axes if len(axes) > 1 else axes[0], [(i, count - 1 - i) f...]
    dot_general x22 -> x0, matrix products: 92.8 us -> none  [dot(): lax.dot_general(a, b, (((ca,), (cb,)), ((), ())), preferred_element_type=...]
    ppermute x37 -> x0, starting transfers between devices: 84.7 us -> none  [the longest x9 45.2 us: ring(): lax.ppermute(v, ('zh', 'zl'), [(i, (i + step) % n) for i in range(n)])]
    unnamed x278 -> x65, local copies, waits for them, and re-layouts: 28.5 us -> 7.61 us
    ppermute x6 -> x1, starting transfers between devices: 21.2 us -> 1.91 us  [relabel(): got = lax.ppermute(v, (self.core, 'zh'), [(1, 2), (2, 1)])]
    convert_element_type x32 -> x10, other arithmetic: 23.6 us -> 4.69 us  [the longest x1 2.14 us: fast_body(): g = dyr.astype(f32)]
  transfers between devices with their start and end apart: 49 -> 2, of which waited for: 25 -> 0; matrix products, arithmetic and copies ran while one was open for 17% -> 5% of each run, Pallas kernels for 14% -> 21%
where the time goes in v3:
time: 624 us; the launch traced here: 615 us
  Pallas kernels  537 us (86%)
  local copies, waits for them, and re-layouts  42.6 us (7%)
  between operations  17.9 us (3%)
  other arithmetic  15.6 us (2%)
    pallas_call x10, Pallas kernels, call(): pl.pallas_call(functools.partial(kernel, *static), out_shape=tuple((jax.S...  537 us
  transfers between devices with their start and end apart: 2, of which 0 were waited for; matrix products, arithmetic and copies ran while one was open for 5% of the time, Pallas kernels for 21%

profile of v3, /device:TPU:1, one launch (start us, length us, event | category | flops | bytes accessed | tf_op | source)
XLA Modules:
  0.0 614.9 jit_solution(16650286129083039055)
XLA Ops:
  7.3 1.0 copy-done
  8.9 1.8 slice_bitcast_fusion.16
  11.0 1.3 copy.57.wq
  12.3 0.8 copy.58.w0
  14.4 2.0 pad_maximum_fusion.x
  16.4 51.6 %first_x.1 = (bf16[384,768]{1,0:T(8,128)(2,1)}, bf16[768,704]{1,0:T(8,128)(2,1)}, bf16[4,16,256]{2,1,0:T(8,128)(2,1)}, bf16[3,192,384]{2,1,0:T(8,128)(2,1)}, bf16[3,96,768]{2,1,0:T(8,128)(2,1)}) custom-call(bf16[384,768]{1,0:T(8,128)(2,1)} %pad_maximum_fusion.x, bf16[768,576]{1,0:T(8,128)(2,1)} %copy.57.wq, bf16[768,128]{1,0:T(8,128)(2,1)} %copy.58.w0, ...), custom_call_target="tpu_custom_call" | custom-call | flops 1000000000 | bytes 10000000 | tf_op jit(solution)/shard_map/first_x/pallas_call | solution.py:1745
  68.0 0.8 copy.69
  68.9 1.4 copy.60.rest_0_
  70.3 0.8 copy.61.rest_1_
  73.1 79.7 %layer_x.2 = (bf16[384,768]{1,0:T(8,128)(2,1)}, bf16[1024,768]{1,0:T(8,128)(2,1)}, bf16[512,768]{1,0:T(8,128)(2,1)}, bf16[1024,704]{1,0:T(8,128)(2,1)}, bf16[512...) custom-call(bf16[384,768]{1,0:T(8,128)(2,1)} %get-tuple-element.122., ...), custom_call_target="tpu_custom_call" | custom-call | flops 10000000000 | bytes 10000000 | tf_op jit(solution)/shard_map/layer_x/pallas_call | solution.py:1745
  152.8 0.8 slice.293
  154.9 1.3 fusion.5
  156.1 1.3 divide_reduce_fusion.1
  158.7 0.9 pad_maximum_fusion.1.rest_0_
  161.4 1.8 copy.75
  163.2 1.5 fusion.8
  164.8 29.5 %mlp_x.2 = (f32[384,768]{1,0:T(8,128)}, bf16[768,768]{1,0:T(8,128)(2,1)}, bf16[768,1536]{1,0:T(8,128)(2,1)}, bf16[768,1536]{1,0:T(8,128)(2,1)}, f32[384,768]{1,0...) custom-call(bf16[384,768]{1,0:T(8,128)(2,1)} %get-tuple-element.127.att, ...), custom_call_target="tpu_custom_call" | custom-call | flops 10000000000 | bytes 10000000 | tf_op jit(solution)/shard_map/mlp_x/pallas_call | solution.py:1745
  194.3 76.3 %layer_x.3 = (bf16[384,768]{1,0:T(8,128)(2,1)}, bf16[1024,768]{1,0:T(8,128)(2,1)}, bf16[512,768]{1,0:T(8,128)(2,1)}, bf16[1024,704]{1,0:T(8,128)(2,1)}, bf16[512...) custom-call(f32[384,768]{1,0:T(8,128)} %get-tuple-element.130.resid,, ...), custom_call_target="tpu_custom_call" | custom-call | flops 10000000000 | bytes 10000000 | tf_op jit(solution)/shard_map/layer_x/pallas_call | solution.py:1745
  270.6 2.1 convert_element_type.82.g
  274.2 15.5 %mlp_x.3 = (f32[384,768]{1,0:T(8,128)}, bf16[768,768]{1,0:T(8,128)(2,1)}, bf16[768,1536]{1,0:T(8,128)(2,1)}, bf16[768,1536]{1,0:T(8,128)(2,1)}, f32[384,768]{1,0:T(8,128)}) custom-call(bf16[384,768]{1,0:T(8,128)(2,1)} %get-tuple-element.134.att, f32[384,768]{1,0:T(8,128)} %get-tuple-element.130.resid, bf16[768,768]{1,0:T(8,128)(2,1)} %bitcast.96, ...), custom_call_target="tpu_custom_call" | custom-call | flops 10000000000 | bytes 10000000 | tf_op jit(solution)/shard_map/mlp_x/pallas_call | solution.py:1745
  289.7 27.9 %mlp_back_x.2 = (f32[384,768]{1,0:T(8,128)}, bf16[384,768]{1,0:T(8,128)(2,1)}, bf16[4,4,192,384]{3,2,1,0:T(8,128)(2,1)}, bf16[4,4,192,384]{3,2,1,0:T(8,128)(2,1)...) custom-call(f32[384,768]{1,0:T(8,128)} %convert_element_type.82.g, ...), custom_call_target="tpu_custom_call" | custom-call | flops 10000000000 | bytes 10000000 | tf_op jit(solution)/shard_map/mlp_back_x/pallas_call | solution.py:1745
  317.6 70.1 %layer_back_x.2 = (f32[384,768]{1,0:T(8,128)}, f32[8,768]{1,0:T(8,128)}, f32[8,704]{1,0:T(8,128)}, bf16[4,192,576]{2,1,0:T(8,128)(2,1)}, bf16[4,192,128]{2,1,0:T...) custom-call(bf16[1024,704]{1,0:T(8,128)(2,1)} %get-tuple-element.140.xl, ...), custom_call_target="tpu_custom_call" | custom-call | flops 20000000000 | bytes 10000000 | tf_op jit(solution)/shard_map/layer_back_x/pallas_call | solution.py:1745
  387.7 0.8 slice_reduce_fusion.5
  388.6 34.5 %mlp_back_x.3 = (f32[384,768]{1,0:T(8,128)}, bf16[384,768]{1,0:T(8,128)(2,1)}, bf16[4,4,192,384]{3,2,1,0:T(8,128)(2,1)}, bf16[4,4,192,384]{3,2,1,0:T(8,128)(2,1)...) custom-call(f32[384,768]{1,0:T(8,128)} %get-tuple-element.160.g, ...), custom_call_target="tpu_custom_call" | custom-call | flops 10000000000 | bytes 10000000 | tf_op jit(solution)/shard_map/mlp_back_x/pallas_call | solution.py:1745
  423.1 77.8 %layer_back_x.3 = (f32[384,768]{1,0:T(8,128)}, f32[8,768]{1,0:T(8,128)}, f32[8,704]{1,0:T(8,128)}, bf16[4,192,576]{2,1,0:T(8,128)(2,1)}, bf16[4,192,128]{2,1,0:T...) custom-call(bf16[1024,704]{1,0:T(8,128)(2,1)} %get-tuple-element.138.xl, ...), custom_call_target="tpu_custom_call" | custom-call | flops 20000000000 | bytes 10000000 | tf_op jit(solution)/shard_map/layer_back_x/pallas_call | solution.py:1745
  500.9 0.8 fusion.11
  503.4 0.8 slice_reduce_fusion
  504.3 0.8 slice_reduce_fusion.1
  505.3 1.2 divide_reduce_fusion
  506.5 1.2 fusion.6
  509.1 0.8 slice_reduce_fusion.11
  511.9 0.9 convert_element_type.88.dx
  512.8 74.2 %tail_x.1 = (f32[2,96,768]{2,1,0:T(8,128)}, f32[2,96,768]{2,1,0:T(8,128)}, f32[2,96,192]{2,1,0:T(8,128)}, f32[2,96,576]{2,1,0:T(8,128)}, bf16[384,768]{1,0:T(8,128)(2,1)}, /*index=5*/f32[152,128]{1,0:T(8,128)}) custom-call(bf16[4,2,192,384]{3,2,1,0:T(8,128)(2,1)} %get-tuple-element.182.s, bf16[2,192,192]{2,1,0:T(8,128)(2,1)} %get-tuple-element.183.so, ...), custom_call_target="tpu_custom_call" | custom-call | flops 1000000000 | bytes 10000000 | tf_op jit(solution)/shard_map/tail_x/pallas_call | solution.py:1745
  587.0 1.0 reshape.185
  589.8 0.9 convert_element_type.81
  590.7 1.9 collective-permute-start
  592.7 1.3 reshape.186
  594.0 1.3 reshape.187
  595.3 1.3 copy.64
  596.6 1.1 copy.65
  598.4 1.7 copy.66
  600.1 0.8 reshape.190
  601.5 1.3 fusion.7
  602.8 0.8 slice_bitcast_fusion.1
  603.6 0.9 slice_bitcast_fusion
  604.6 0.8 slice_bitcast_fusion.2
  606.1 0.8 copy.104
  606.9 0.8 copy.105
  (134 shorter events, 16.7 us)
Async XLA Ops:
  7.2 1.1 copy-start
  7.2 154.2 %all-gather.3.cloned.1.call-start = ((), (), s32[]{:S(2)}) async-start(), calls=%async_computation | async-start | bytes 2433024 | tf_op jit(solution)/shard_map/all_gather | solution.py:1788
  8.9 1.8 copy-start.18
  8.9 1.9 copy-start.17
  11.0 2.8 copy-start.16
  73.1 81.2 %copy-start.19 = (s32[2]{0:T(128)S(1)}, s32[2]{0:T(128)}, u32[]{:S(2)}) copy-start(s32[2]{0:T(128)} %param.33) | copy-start | bytes 28
  73.1 85.7 %copy-start.7 = (bf16[1,256,768]{2,1,0:T(8,128)(2,1)S(1)}, bf16[1,256,768]{2,1,0:T(8,128)(2,1)}, u32[]{:S(2)}) copy-start(bf16[1,256,768]{2,1,0:T(8,128)(2,1)} %param.21) | copy-start | bytes 1179652
  73.1 85.7 %copy-start.9 = (bf16[1,128,768]{2,1,0:T(8,128)(2,1)S(1)}, bf16[1,128,768]{2,1,0:T(8,128)(2,1)}, u32[]{:S(2)}) copy-start(bf16[1,128,768]{2,1,0:T(8,128)(2,1)} %param.22) | copy-start | bytes 589828
  152.8 6.8 %copy-start.12 = (bf16[2,768]{1,0:T(2,128)(2,1)S(1)}, bf16[2,768]{1,0:T(2,128)(2,1)}, u32[]{:S(2)}) copy-start(bf16[2,768]{1,0:T(2,128)(2,1)} %param.28) | copy-start | bytes 9220
  152.8 7.4 %copy-start.13 = (bf16[2,768]{1,0:T(2,128)(2,1)S(1)}, bf16[2,768]{1,0:T(2,128)(2,1)}, u32[]{:S(2)}) copy-start(bf16[2,768]{1,0:T(2,128)(2,1)} %param.32) | copy-start | bytes 9220
  317.6 71.0 %copy-start.15 = (f32[8,768]{1,0:T(8,128)S(1)}, f32[8,768]{1,0:T(8,128)}, u32[]{:S(2)}) copy-start(f32[8,768]{1,0:T(8,128)} %get-tuple-element.195) | copy-start | bytes 73732
  423.1 85.8 %copy-start.10 = (f32[9344]{0:T(1024)S(1)}, f32[9344]{0:T(1024)}, u32[]{:S(2)}) copy-start(f32[9344]{0:T(1024)} %custom-call) | copy-start | bytes 112132
  423.1 86.8 %copy-start.14 = (f32[8,768]{1,0:T(8,128)S(1)}, f32[8,768]{1,0:T(8,128)}, u32[]{:S(2)}) copy-start(f32[8,768]{1,0:T(8,128)} %get-tuple-element.191) | copy-start | bytes 73732
  423.1 87.8 %copy-start.11 = (f32[9344]{0:T(1024)S(1)}, f32[9344]{0:T(1024)}, u32[]{:S(2)}) copy-start(f32[9344]{0:T(1024)} %custom-call.1) | copy-start | bytes 112132
  500.9 11.0 %copy-start.3 = (f32[384,768]{1,0:T(8,128)S(1)}, f32[384,768]{1,0:T(8,128)}, u32[]{:S(2)}) copy-start(f32[384,768]{1,0:T(8,128)} %get-tuple-element.198) | copy-start | bytes 3538948
  512.8 77.0 %copy-start.2 = (f32[384,768]{1,0:T(8,128)S(1)}, f32[384,768]{1,0:T(8,128)}, u32[]{:S(2)}) copy-start(f32[384,768]{1,0:T(8,128)} %get-tuple-element.137) | copy-start | bytes 3538948
  586.9 5.7 copy-start.4
  587.9 4.6 copy-start.8
  590.7 13.8 %collective-permute-start = (bf16[384,768]{1,0:T(8,128)(2,1)}, bf16[384,768]{1,0:T(8,128)(2,1)S(1)}, u32[]{:S(2)}, u32[]{:S(2)}) collective-permute-start(bf16[384,768]{1,0:T(8,128)(2,1)} %convert_element_type.81), channel_id=1, source_target_pairs={{2,4},{4,2},{3,5},{5,3},{10,12},{12,10},{11,13},{13,11},{18,20},{2... | collective-permute-start | bytes 1769480 | tf_op jit(solution)/shard_map/ppermute | solution.py:623
  604.6 1.5 copy-start.6
  604.6 2.3 copy-start.5
  606.1 1.6 copy-start.1
Sparse Core Ops, SparseCore 0:
  11.5 79.0 all-gather.2

commit v4 on v2

--- a/solution.py
+++ b/solution.py
@@ -1,4 +1,5 @@
 import functools
+import types
 
 import jax, jax.numpy as jnp
 from jax import lax
@@ -707,36 +708,6 @@
             left.remove(ax)
         return v.reshape(-1, n)
 
-    def scatter_all(self, up, down, out):
-        n, e = up.shape[1], out.shape[1]
-        bits = len(self.dims)
-        view = lambda v: v.reshape(*([2] * bits), -1, v.shape[1])
-        mats = [view(up), view(down), view(out)]
-        pos = bits - 1
-        to_send = jnp.concatenate([pick(v, 1 - self.c, pos) for v in mats], axis=-1)
-        got = swap(to_send, self.core)
-        up, down, out = [
-            (pick(v, self.c, pos).astype(F32) + got[..., at : at + v.shape[-1]].astype(F32)).astype(BF)
-            for v, at in zip(mats, (0, n, 2 * n))
-        ]
-        down = jnp.concatenate([down, out], axis=-1)
-        res = []
-        for v, axes in ((up, self.plane), (down, self.plane[::-1])):
-            left = list(self.plane)
-            for ax in axes:
-                i, p = lax.axis_index(ax), left.index(ax)
-                got = swap(pick(v, 1 - i, p), ax)
-                v = (pick(v, i, p).astype(F32) + got.astype(F32)).astype(BF)
-                left.remove(ax)
-            res.append(v)
-        up, down = res
-        rows = up.shape[0]
-        cut = lambda v: v.reshape(rows, self.mp, -1)
-        v = jnp.concatenate([cut(up), cut(down[:, :n]), cut(down[:, n:])], axis=-1)
-        v = self.ring_scatter([pick(v, (self.z - r) % self.mp, 1) for r in range(self.mp)])
-        q = n // self.mp
-        return v[:, :q], v[:, q : 2 * q], v[:, 2 * q :]
-
     def ring_scatter(self, chunks):
         t = chunks[-1]
         for r in range(self.mp - 2, -1, -1):
@@ -771,7 +742,6 @@
     rel_small = jnp.stack([small] + plan.ring_gather(small))
     n_up = layers * ffq
     rel_bup = rel_small[:, :n_up].reshape(mp, layers, ffq).astype(F32)
-    bup = jnp.stack([pick(rel_bup, (plan.z - q) % mp, 0) for q in range(mp)])
     rel_bqv = rel_small[:, n_up:].reshape(mp, layers, 2, heads_w).astype(F32)
     mine = 2 * plan.c + plan.zl
     my_bqv = pick(rel_bqv, (plan.z - mine) % mp, 0)
@@ -788,13 +758,26 @@
         exts.append(jnp.concatenate([quarter, head0], axis=1))
 
     ups, downs, outs = [], [], []
-    order = ("zh", "zl") + dims
     for l in range(layers):
-        outs.append(lax.all_gather(plan.piece(w_out[l]), order, axis=0, tiled=True))
-        n_up = ffq // dp
-        piece = lax.dynamic_slice_in_dim(w_up[l], plan.d * n_up, n_up, 1)
-        ups.append(lax.all_gather(jnp.transpose(piece), order, axis=0, tiled=True))
-        downs.append(lax.all_gather(plan.piece(w_down[l]), order, axis=0, tiled=True))
+        po = plan.piece(w_out[l])
+        pu = jnp.concatenate([plan.piece(w_up[l]), po], axis=0)
+        pd = plan.piece(w_down[l])
+        n_out, n_d = po.shape[0], pd.shape[0]
+        both = plan.ring_gather(jnp.concatenate([pu, pd], axis=0))
+        stacked = jnp.stack(both)
+        n_u = pu.shape[0]
+        gu = plan.plane_gather(stacked[:, :n_u], fwd_axes)
+        gd = plan.plane_gather(stacked[:, n_u:], alt_axes)
+        up = gu[:, :, : n_u - n_out].reshape(mp - 1, d_model, ffq)
+        ups.append(jnp.concatenate([w_up[l]] + [up[r] for r in range(mp - 1)], axis=1))
+        out = gu[:, :, n_u - n_out :].reshape(mp - 1, heads_w, d_model)
+        out = jnp.concatenate([w_out[l][None], out], axis=0)
+        outs.append(
+            jnp.concatenate([pick(out, (plan.z - q) % mp, 0) for q in range(mp)], axis=0)
+        )
+        downs.append(
+            jnp.concatenate([w_down[l], gd.reshape((mp - 1) * ffq, d_model)], axis=0)
+        )
 
     dy = plan.relabel(jnp.concatenate([dy_long[0], dy_short[0]], axis=0))
 
@@ -803,6 +786,9 @@
     saved = []
     shares = []
     for l in range(layers):
+        normed, hat1, inv1 = normalize(resid, gain[l, 0], shift[l, 0])
+        normed = normed.astype(BF)
+        full = [plan.gather(normed[:rl]), plan.gather(normed[rl:])]
         bias = jnp.concatenate(
             [
                 my_bqv[l, 0],
@@ -812,24 +798,22 @@
                 jnp.zeros((HD,), F32),
             ]
         )
-        full_l, full_s, pj_l, pj_s = project(
-            plan.core, resid, gain[l, 0], shift[l, 0], exts[l], bias, rl, rs
-        )
-        full, proj = (full_l, full_s), (pj_l, pj_s)
-        attended, *att = attend_fwd_x(plan.core, pj_l, pj_s)
+        proj = [(dot(n, exts[l]) + bias).astype(BF) for n in full]
+        att = [attend_fwd(p) for p in proj]
         share = jnp.zeros((), F32)
-        for carry in att[4:]:
-            size = carry.shape[1]
-            sel = carry[size // BR]
+        for p, a in zip(proj, att):
+            size = p.shape[0]
+            sel = a[2][size // BR]
             left = (size - 1 - lax.broadcasted_iota(jnp.int32, (size,), 0)).astype(F32)
             share = share + jnp.sum(
                 jax.nn.sigmoid(4.0 * (sel / jnp.maximum(left, 1.0) - limits[l]))
             )
         shares.append(share)
+        attended = jnp.concatenate([plan.to_rows(a[0]) for a in att], axis=0)
         middle = resid + dot(attended, outs[l]) + b_out[l].astype(F32)
         normed2, hat2, inv2 = normalize(middle, gain[l, 1], shift[l, 1])
         normed2 = normed2.astype(BF)
-        upper = dot(normed2, ups[l], 1, 1) + bup[:, l].reshape(-1)
+        upper = dot(normed2, ups[l]) + rel_bup[:, l].reshape(-1)
         active = gelu_both(upper)[0].astype(BF)
         saved.append((resid, middle, full, proj, att, attended, normed2, upper, active))
         resid = middle + dot(active, downs[l]) + b_down[l].astype(F32)
@@ -849,7 +833,7 @@
         w_down_t = dot(gm, active, 0, 0).astype(BF)
         w_up_g = dot(normed2, gu, 0, 0).astype(BF)
         g_bup = jnp.sum(gu.astype(F32), axis=0)
-        gn2 = dot(gu, ups[l])
+        gn2 = dot(gu, ups[l], 1, 1)
         _, hat2, inv2 = normalize(middle, gain[l, 1], shift[l, 1])
         back, g_gain2, g_shift2 = normalize_back(gn2, hat2, inv2, gain[l, 1])
         gmid = g + back
@@ -857,14 +841,24 @@
         ga = gmid.astype(BF)
         go = dot(ga, outs[l], 1, 1).astype(BF)
         w_out_t = dot(ga, attended, 0, 0).astype(BF)
-        dext = attend_bwd_x(plan.core, *proj, go, *att)
-        new_g, ln1 = collect(plan.core, *dext, exts[l], resid, gain[l, 0], gmid)
-        g_gain1, g_shift1 = ln1[0], ln1[1]
+        gh = [plan.to_heads(go[:rl]), plan.to_heads(go[rl:])]
+        dext = [attend_bwd(p, h, a[0], a[1], a[2]) for p, h, a in zip(proj, gh, att)]
+        gn1 = jnp.concatenate(
+            [plan.scatter(dot(e, exts[l], 1, 1).astype(BF)) for e in dext], axis=0
+        )
         w_ext_g = sum(dot(n, e, 0, 0) for n, e in zip(full, dext)).astype(BF)
         g_bext = sum(jnp.sum(e.astype(F32), axis=0) for e in dext)
-        g = new_g
-
-        w_up_g, w_down_t, w_out_t = plan.scatter_all(w_up_g, w_down_t, w_out_t)
+        _, hat1, inv1 = normalize(resid, gain[l, 0], shift[l, 0])
+        back, g_gain1, g_shift1 = normalize_back(gn1, hat1, inv1, gain[l, 0])
+        g = gmid + back
+
+        w_up_g = plan.plane_scatter(w_up_g, (plan.core,) + core_rest)
+        w_up_g = plan.ring_scatter([w_up_g[:, r * ffq : (r + 1) * ffq] for r in range(mp)])
+        w_down_t = plan.plane_scatter(w_down_t, (plan.core,) + core_rest[::-1])
+        w_down_t = plan.ring_scatter([w_down_t[:, r * ffq : (r + 1) * ffq] for r in range(mp)])
+        w_out_t = plan.plane_scatter(w_out_t, (plan.core,) + core_rest)
+        w_out_t = w_out_t.reshape(-1, mp, heads_w)
+        w_out_t = plan.ring_scatter([pick(w_out_t, (plan.z - r) % mp, 1) for r in range(mp)])
         w_ext_g = plan.plane_scatter(w_ext_g, core_rest[::-1])
         w_ext_g = w_ext_g.reshape(2, -1, w_ext_g.shape[1])
         part, zero = w_ext_g[..., : 3 * heads_w], w_ext_g[..., 3 * heads_w :]
@@ -888,6 +882,8 @@
         gq = hot * g_bext[None, :heads_w]
         gv = hot * g_bext[None, 2 * heads_w : 3 * heads_w]
         gq = gq.reshape(-1).at[:HD].add(g_bext[3 * heads_w : 3 * heads_w + HD])
+        g_bup = g_bup.reshape(mp, ffq)
+        g_bup = jnp.stack([pick(g_bup, (plan.z - q) % mp, 0) for q in range(mp)])
         vec[l] = jnp.concatenate(
             [
                 g_gain1, g_gain2, g_shift1, g_shift2, g_bout, g_bdown,
@@ -896,19 +892,18 @@
         )
 
     dx = plan.relabel(g.astype(BF)).astype(F32)
-    total_v = jnp.stack([vec[l] for l in range(layers)])
-    total_v = total(dims + ("zh", "zl"), total_v.reshape(-1, 128)).reshape(total_v.shape)
+    total = lax.psum(jnp.stack([vec[l] for l in range(layers)]), dims + ("zh", "zl"))
     n = d_model
-    g_gain = total_v[:, : 2 * n].reshape(layers, 2, n)
-    g_bias = total_v[:, 2 * n : 4 * n].reshape(layers, 2, n)
-    g_bout = total_v[:, 4 * n : 5 * n]
-    g_bdown = total_v[:, 5 * n : 6 * n]
+    g_gain = total[:, : 2 * n].reshape(layers, 2, n)
+    g_bias = total[:, 2 * n : 4 * n].reshape(layers, 2, n)
+    g_bout = total[:, 4 * n : 5 * n]
+    g_bdown = total[:, 5 * n : 6 * n]
     at = 6 * n
-    g_bqv = total_v[:, at : at + 2 * mp * heads_w].reshape(layers, 2, mp, heads_w)
+    g_bqv = total[:, at : at + 2 * mp * heads_w].reshape(layers, 2, mp, heads_w)
     at += 2 * mp * heads_w
-    g_bup = total_v[:, at : at + mp * ffq].reshape(layers, mp, ffq)
+    g_bup = total[:, at : at + mp * ffq].reshape(layers, mp, ffq)
     at += mp * ffq
-    key_share = total_v[:, at] / (dp * (rows * mp))
+    key_share = total[:, at] / (dp * (rows * mp))
     return (
         y[None, :rl],
         y[None, rl:],
@@ -928,6 +923,1092 @@
     )
 
 
+MESH = pl.DeviceIdType.MESH
+ANY = pl.BlockSpec(memory_space=pl.ANY)
+
+
+class Net:
+    def __init__(self, dims):
+        self.dims = dims
+        self.y, self.x, self.c = (lax.axis_index(ax) for ax in dims)
+        self.zh, self.zl = lax.axis_index("zh"), lax.axis_index("zl")
+        self.z = 2 * self.zh + self.zl
+        self.yx = 2 * self.y + self.x
+        self.me = 2 * self.c + self.zl
+        self.moves = self.c != self.zh
+
+    def group(self, delta):
+        return {self.dims[2]: self.c ^ (delta >> 1), "zl": self.zl ^ (delta & 1)}
+
+    def member(self, m):
+        return {self.dims[2]: m >> 1, "zl": m & 1}
+
+    def plane(self, e):
+        return {self.dims[0]: self.y ^ (e >> 1), self.dims[1]: self.x ^ (e & 1)}
+
+    def line(self, r):
+        to = (self.z + r) % 4
+        return {"zh": to // 2, "zl": to % 2}
+
+    def partner(self):
+        return {self.dims[2]: 1 - self.c, "zh": 1 - self.zh}
+
+    def greet(self, peers):
+        barrier = pltpu.get_barrier_semaphore()
+        for peer in peers:
+            pl.semaphore_signal(barrier, inc=1, device_id=peer, device_id_type=MESH)
+        pl.semaphore_wait(barrier, len(peers))
+
+
+class Sems:
+    def __init__(self, ssem, rsem):
+        self.ssem, self.rsem, self.used = ssem, rsem, 0
+
+    def copy(self, src, dst, device):
+        i = self.used
+        self.used += 1
+        return send(src, dst, self.ssem.at[i], self.rsem.at[i], device)
+
+
+class Batch:
+    def __init__(self, copies, when=None):
+        self.copies, self.when = copies, when
+
+    def _do(self, f):
+        if self.when is None:
+            f()
+        else:
+            pl.when(self.when)(f)
+
+    def start(self):
+        self._do(lambda: [c.start() for c in self.copies] and None)
+
+    def recv(self):
+        self._do(lambda: [c.wait_recv() for c in self.copies] and None)
+
+    def sent(self):
+        self._do(lambda: [c.wait_send() for c in self.copies] and None)
+
+    def end(self):
+        self.recv()
+        self.sent()
+
+
+def aligned(v, n=16):
+    return pl.multiple_of(v, n)
+
+
+class Projections:
+    def __init__(self, net, sems, wq, w0, qland, zland, ext):
+        self.net, self.wq, self.w0, self.qland, self.zland, self.ext = net, wq, w0, qland, zland, ext
+        rows = qland.shape[1]
+        here = pl.ds(aligned(net.yx * rows), rows)
+        at = net.yx
+        self.q1 = Batch([sems.copy(wq.at[here], qland.at[at], net.partner())], net.moves)
+        self.q2 = Batch([sems.copy(qland.at[at], qland.at[at], net.plane(e)) for e in (1, 2, 3)], net.moves)
+        self.h1 = []
+        for r in (1, 2, 3):
+            copy = sems.copy(w0.at[here], zland.at[at], net.line(r))
+            self.h1.append(copy)
+        self.h2 = Batch([sems.copy(zland.at[at], zland.at[at], net.plane(e)) for e in (1, 2, 3)], net.z != 0)
+
+    def start(self):
+        self.q1.start()
+
+        @pl.when(self.net.z == 0)
+        def _():
+            for copy in self.h1:
+                copy.start()
+
+    def forward(self):
+        self.q1.recv()
+        self.q2.start()
+        for r in (1, 2, 3):
+            pl.when(self.net.z == r)(lambda: self.h1[r - 1].wait_recv())
+        self.h2.start()
+
+    def finish(self):
+        rows, n = self.qland.shape[1:]
+        self.q2.recv()
+        self.h2.recv()
+
+        @pl.when(self.net.moves)
+        def _():
+            for k in range(4):
+                self.ext[k * rows : (k + 1) * rows, :n] = self.qland[k]
+
+        @pl.when(jnp.logical_not(self.net.moves))
+        def _():
+            self.ext[:, :n] = self.wq[...]
+
+        @pl.when(self.net.z != 0)
+        def _():
+            for k in range(4):
+                self.ext[k * rows : (k + 1) * rows, n:] = self.zland[k]
+
+        @pl.when(self.net.z == 0)
+        def _():
+            self.ext[:, n:] = self.w0[...]
+
+        self.q1.sent()
+        self.q2.sent()
+        self.h2.sent()
+
+        @pl.when(self.net.z == 0)
+        def _():
+            for copy in self.h1:
+                copy.wait_send()
+
+
+def project_part(net, sems, resid, gain, shift, w, bias, fl, fs, pj_l, pj_s):
+    nl, ns = fl.shape[0] // 4, fs.shape[0] // 4
+    half = nl // 2
+    parts = ((fs, pj_s, ns, 0, ns, nl), (fl, pj_l, nl, 0, half, 0), (fl, pj_l, nl, half, half, half))
+    me = net.me
+
+    def rows(k, m):
+        ref, _, n, at, size, _ = parts[k]
+        return ref.at[pl.ds(aligned(m * n + at), size)]
+
+    def compute(k, m):
+        ref, out, n, at, size, _ = parts[k]
+        here = pl.ds(aligned(m * n + at), size)
+        out[here] = (mm(ref[here], w[...]) + bias[...]).astype(jnp.bfloat16)
+
+    chip = [sems.copy(rows(k, me), rows(k, me), net.group(1)) for k in range(3)]
+    core = [sems.copy(rows(k, me), rows(k, me), net.group(2)) for k in range(3)]
+    over = [sems.copy(rows(k, me ^ 1), rows(k, me ^ 1), net.group(2)) for k in range(3)]
+    for k in range(3):
+        ref, _, n, at, size, src = parts[k]
+        hat, _ = norm_rows(resid[src : src + size].astype(jnp.float32))
+        ref[pl.ds(aligned(me * n + at), size)] = (hat * gain[...] + shift[...]).astype(jnp.bfloat16)
+        chip[k].start()
+        core[k].start()
+    for k in range(3):
+        compute(k, me)
+    for k in range(3):
+        core[k].wait_recv()
+        compute(k, me ^ 2)
+    for k in range(3):
+        chip[k].wait_recv()
+        over[k].start()
+        compute(k, me ^ 1)
+    for k in range(3):
+        over[k].wait_recv()
+        compute(k, me ^ 3)
+    return chip + core + over
+
+
+def attend_part(net, sems, xl, xs, att, ol, os, lsel, lses, cl, cs, land):
+    nl, ns = xl.shape[0] // 4, xs.shape[0] // 4
+    w = ol.shape[1]
+    base = sems.used
+    sems.used += 8
+
+    def part(k):
+        return ((ol, nl, 0), (os, ns, nl))[k]
+
+    def copy(k, m):
+        src, n, at = part(k)
+        return send(
+            src.at[pl.ds(m * n, n)],
+            land.at[net.me, pl.ds(at, n)],
+            sems.ssem.at[base + 4 * k + m],
+            sems.rsem.at[base + 4 * k + net.me],
+            net.member(m),
+        )
+
+    def arrived(k, m):
+        src, n, at = part(k)
+        i = base + 4 * k + m
+        return send(src.at[pl.ds(0, n)], land.at[m, pl.ds(at, n)], sems.ssem.at[i], sems.rsem.at[i], net.member(m))
+
+    def start(k, m):
+        src, n, at = part(k)
+
+        @pl.when(net.me != m)
+        def _():
+            copy(k, m).start()
+
+        @pl.when(net.me == m)
+        def _():
+            land[m, at : at + n] = src[m * n : (m + 1) * n]
+
+    def started(k, n):
+        def done(b):
+            for m in range(b * BR // n, (b + 1) * BR // n):
+                start(k, m)
+
+        return done
+
+    fwd_one(xs, os, lses, cs, started(1, ns))
+    fwd_one(xl, ol, lsel, cl, started(0, nl))
+    for m in range(4):
+
+        @pl.when(net.me != m)
+        def _():
+            for k in range(2):
+                copy(k, m).wait_send()
+                arrived(k, m).wait_recv()
+
+    for m in range(4):
+        att[:, m * w : (m + 1) * w] = land[m]
+
+
+def gelu_pair(u):
+    k = 0.7978845608028654
+    sq = u * u
+    t = jnp.tanh(u * (k + k * 0.044715 * sq))
+    h = 0.5 * (1.0 + t)
+    act = u * h
+    slope = h + act * (1.0 - t) * (k + 3 * k * 0.044715 * sq)
+    return act, slope
+
+
+TN = (((0,), (0,)), ((), ()))
+
+
+def ext_scatter(net, sems, dw, land):
+    return [sems.copy(dw.at[net.yx ^ e], land.at[e - 1], net.plane(e)) for e in (1, 2, 3)]
+
+
+class FinishLine:
+    def __init__(self, net, sems, s, so, land, oland, own=None):
+        self.own = s.at[0] if own is None else own
+        self.net, self.s, self.so, self.land, self.oland = net, s, so, land, oland
+        self.main = Batch([sems.copy(s.at[r], land.at[3 - r], net.line(r)) for r in (1, 2, 3)])
+        self.out = []
+        for r in (1, 2, 3):
+            to = (net.z + r) % 4
+            copy = sems.copy(so.at[to % 2], oland.at[3 - r], net.line(r))
+            self.out.append((copy, to // 2 == net.c))
+        self.owner = net.zh == net.c
+
+    def start(self):
+        self.main.start()
+        for copy, use in self.out:
+            pl.when(use)(copy.start)
+
+    def finish(self, f_out, fo_out):
+        self.main.recv()
+        f_out[...] = (
+            self.own[...].astype(jnp.float32)
+            + self.land[0].astype(jnp.float32)
+            + self.land[1].astype(jnp.float32)
+            + self.land[2].astype(jnp.float32)
+        ).astype(f_out.dtype)
+
+        @pl.when(self.owner)
+        def _():
+            for copy, _ in self.out:
+                copy.wait_recv()
+            fo_out[...] = (
+                self.so[self.net.zl].astype(jnp.float32)
+                + self.oland[0].astype(jnp.float32)
+                + self.oland[1].astype(jnp.float32)
+                + self.oland[2].astype(jnp.float32)
+            ).astype(fo_out.dtype)
+
+        @pl.when(jnp.logical_not(self.owner))
+        def _():
+            fo_out[...] = jnp.zeros_like(fo_out)
+
+        self.main.sent()
+        for copy, use in self.out:
+            pl.when(use)(copy.wait_send)
+
+
+class Local:
+    def __init__(self, sem):
+        self.sem, self.copies = sem, []
+
+    def start(self, src, dst):
+        copy = pltpu.make_async_copy(src, dst, self.sem.at[len(self.copies)])
+        self.copies.append(copy)
+        copy.start()
+        return copy
+
+
+def z_weights(net, sems, layer, w_up, w_down, zup, zdn):
+    rows, n = zup.shape[0], zup.shape[1] // 3
+    part = zdn.shape[1]
+    out = []
+    for r in (1, 2, 3):
+        dev, slot = net.line(r), 3 - r
+        src = w_up.at[layer, pl.ds(aligned(net.yx * rows), rows), pl.ds(aligned(net.c * n, 128), n)]
+        out.append(sems.copy(src, zup.at[:, pl.ds(slot * n, n)], dev))
+        src = w_down.at[layer, pl.ds(aligned(net.c * n + net.yx * part), part)]
+        out.append(sems.copy(src, zdn.at[slot], dev))
+    return Batch(out)
+
+
+def plane_weights(net, sems, zup, zdn, wup, wdn):
+    rows, n = zup.shape[0], zup.shape[1] // 3
+    part = zdn.shape[1]
+    at_up = pl.ds(aligned(net.yx * rows), rows)
+    at_dn = pl.ds(aligned(net.yx * part), part)
+    out = []
+    for e in (1, 2, 3):
+        out.append(sems.copy(zup, wup.at[at_up, pl.ds(n, 3 * n)], net.plane(e)))
+        out.append(sems.copy(zdn, wdn.at[pl.ds(1, 3), at_dn], net.plane(e)))
+    return Batch(out)
+
+
+def first_x(dims, R):
+    net, sems = Net(dims), Sems(R.ssem, R.rsem)
+    nl = R.xl.shape[0]
+    moved = Batch(
+        [
+            sems.copy(R.xl, R.xr.at[pl.ds(0, nl)], net.partner()),
+            sems.copy(R.xs, R.xr.at[pl.ds(nl, R.xs.shape[0])], net.partner()),
+        ],
+        net.moves,
+    )
+    proj = Projections(net, sems, R.wq, R.w0, R.qland, R.zland, R.ext)
+    tiny = Batch([sems.copy(R.small, R.smalls.at[4 - r], net.line(r)) for r in (1, 2, 3)])
+    weights = z_weights(net, sems, 0, R.w_up, R.w_down, R.zup, R.zdn)
+    net.greet([net.partner()] + [net.line(r) for r in (1, 2, 3)] + [net.plane(e) for e in (1, 2, 3)])
+    proj.start()
+    moved.start()
+    tiny.start()
+    weights.start()
+    R.smalls[0] = R.small[...]
+
+    @pl.when(jnp.logical_not(net.moves))
+    def _():
+        R.xr[:nl] = R.xl[...]
+        R.xr[nl:] = R.xs[...]
+
+    proj.forward()
+    proj.finish()
+    moved.end()
+    tiny.end()
+    weights.end()
+
+
+def forward_x(dims, first, last, R):
+    net, sems, loc = Net(dims), Sems(R.ssem, R.rsem), Local(R.lsem)
+    n, d = R.resid.shape
+    f = R.own_up.shape[1]
+    weights = plane_weights(net, sems, R.zup, R.zdn, R.wup, R.wdn)
+    peers = [net.group(2), net.group(3), net.partner()]
+    peers += [net.plane(e) for e in (1, 2, 3)] + [net.line(r) for r in (1, 2, 3)]
+    if first:
+        proj = Projections(net, sems, R.wq, R.w0, R.qland, R.zland, R.ext_next)
+        later = z_weights(net, sems, 1, R.w_up, R.w_down, R.zup_next, R.zdn_next)
+    else:
+        nl = R.dl.shape[0]
+        moved = Batch(
+            [
+                sems.copy(R.dl, R.dyr.at[pl.ds(0, nl)], net.partner()),
+                sems.copy(R.ds, R.dyr.at[pl.ds(nl, R.ds.shape[0])], net.partner()),
+            ],
+            net.moves,
+        )
+    there = sems.copy(R.n2.at[pl.ds(0, n)], R.n2.at[pl.ds(n, n)], net.group(2))
+    back = sems.copy(R.out, R.got, net.group(2))
+    net.greet(peers)
+    weights.start()
+    pending = project_part(
+        net, sems, R.resid, R.gain1, R.shift1, R.ext, R.bias, R.fl, R.fs, R.pj_l, R.pj_s
+    )
+    if first:
+        proj.start()
+    else:
+        moved.start()
+
+        @pl.when(jnp.logical_not(net.moves))
+        def _():
+            R.dyr[:nl] = R.dl[...]
+            R.dyr[nl:] = R.ds[...]
+
+    for src, dst in ((R.fl, R.fl_o), (R.fs, R.fs_o), (R.pj_l, R.pjl_o), (R.pj_s, R.pjs_o)):
+        loc.start(src, dst)
+    R.wup[:, :f] = R.own_up[...]
+    R.wdn[0] = R.own_dn[...]
+    rows, part = R.zup.shape[0], R.zdn.shape[1]
+    R.wup[pl.ds(aligned(net.yx * rows), rows), f:] = R.zup[...]
+    for k in range(3):
+        R.wdn[k + 1, pl.ds(aligned(net.yx * part), part)] = R.zdn[k]
+    if first:
+        later.start()
+    attend_part(
+        net, sems, R.pj_l, R.pj_s, R.att, R.ol, R.os, R.lsel, R.lses, R.cl, R.cs, R.land
+    )
+    if first:
+        proj.forward()
+    share = jnp.zeros((1, 1), jnp.float32)
+    for carry in (R.cl, R.cs):
+        size = carry.shape[1]
+        left = (size - 1 - lax.broadcasted_iota(jnp.int32, (1, size), 1)).astype(jnp.float32)
+        ratio = carry[size // BR : size // BR + 1] / jnp.maximum(left, 1.0)
+        t = 4.0 * (ratio - R.limit[:1, :1])
+        share = share + jnp.sum(1.0 / (1.0 + jnp.exp(-t)), axis=1, keepdims=True)
+    R.share[...] = jnp.broadcast_to(share * 0.25, R.share.shape)
+    half = n // 2
+    for i in range(2):
+        at = slice(i * half, (i + 1) * half)
+        R.middle[at] = R.resid[at].astype(jnp.float32) + mm(R.att[at], R.wout[...]) + R.bout[...]
+        hat, _ = norm_rows(R.middle[at])
+        R.n2[at] = (hat * R.gain2[...] + R.shift2[...]).astype(jnp.bfloat16)
+    there.start()
+    weights.recv()
+    for src, dst in ((R.wup, R.wup_o), (R.wdn, R.wdn_o)):
+        loc.start(src, dst)
+
+    def hidden(at):
+        u = mm(R.n2[at], R.wup[...]) + R.bup[...]
+        a, s = gelu_pair(u)
+        low = a.astype(jnp.bfloat16)
+        for i in range(2):
+            R.act[i, at] = low[:, 2 * i * f : 2 * (i + 1) * f]
+            loc.start(R.act.at[i, at], R.act_o.at[i, at])
+        R.slope[at] = s.astype(jnp.bfloat16)
+        loc.start(R.slope.at[at], R.slope_o.at[at])
+
+    def down(at):
+        return mm(R.act[0, at], R.wdn[0:2].reshape(2 * f, d)) + mm(
+            R.act[1, at], R.wdn[2:4].reshape(2 * f, d)
+        )
+
+    quarter = n // 2
+    for i in range(2):
+        hidden(slice(i * quarter, (i + 1) * quarter))
+    there.wait_recv()
+    for i in range(2):
+        hidden(slice(n + i * quarter, n + (i + 1) * quarter))
+    for i in range(2):
+        R.out[i * half : (i + 1) * half] = down(slice(n + i * half, n + (i + 1) * half)).astype(
+            jnp.bfloat16
+        )
+    back.start()
+    for i in range(2):
+        at = slice(i * half, (i + 1) * half)
+        R.new[at] = R.middle[at] + down(at) + R.bdown[...]
+    back.wait_recv()
+    R.new[...] += R.got[...].astype(jnp.float32)
+    if last:
+        R.y[...] = R.new[...].astype(jnp.bfloat16)
+    there.wait_send()
+    back.wait_send()
+    for copy in pending:
+        copy.wait_send()
+    weights.sent()
+    if first:
+        proj.finish()
+        later.end()
+    else:
+        moved.end()
+    for copy in loc.copies:
+        copy.wait()
+
+
+def backward_x(dims, last, R):
+    net, sems, loc = Net(dims), Sems(R.ssem, R.rsem), Local(R.lsem)
+    f32, bf = jnp.float32, jnp.bfloat16
+    n, d = R.g.shape
+    f = R.wup.shape[1] // 4
+    nl, ns = R.pj_l.shape[0] // 4, R.pj_s.shape[0] // 4
+    wid = R.ol.shape[1]
+    me, yx = net.me, net.yx
+    there = sems.copy(R.gm.at[pl.ds(0, n)], R.gm.at[pl.ds(n, n)], net.group(2))
+    back = sems.copy(R.out.at[0], R.got.at[0], net.group(2))
+    cross = sems.copy(R.oself, R.olands, net.group(2))
+    big_dn = Batch([sems.copy(R.ddn.at[yx ^ e], R.rdn.at[e - 1], net.plane(e)) for e in (1, 2, 3)])
+    big_up = Batch(
+        [sems.copy(R.dup.at[yx ^ e], R.rup.at[e - 1], net.plane(e)) for e in (1, 2, 3)]
+        + [sems.copy(R.dout.at[yx ^ e], R.rout.at[e - 1], net.plane(e)) for e in (1, 2, 3)]
+    )
+    base = sems.used
+    sems.used += 8
+    peers = [net.group(d_) for d_ in (1, 2, 3)] + [net.plane(e) for e in (1, 2, 3)]
+    if last:
+        moved = Batch([sems.copy(R.y, R.yr, net.partner())], net.moves)
+        peers += [net.partner()]
+    else:
+        carry = FinishLine(net, sems, R.s_in, R.so_in, R.fland, R.foland, R.s_own)
+        ext = Batch(ext_scatter(net, sems, R.dq_in, R.qland) + ext_scatter(net, sems, R.d0_in, R.zland))
+        peers += [net.line(2), net.line(4 - net.zl * 2 - 1)]
+    R.gm[:n] = R.g[...].astype(bf)
+    net.greet(peers)
+    there.start()
+    fetched = [loc.start(R.act.at[i], R.buf.at[pl.ds(i * 2 * n, 2 * n)]) for i in range(2)]
+    for src, dst in ((R.pjl_i, R.pj_l), (R.pjs_i, R.pj_s), (R.ext_i, R.ext)):
+        loc.start(src, dst)
+    if last:
+        moved.start()
+
+        @pl.when(jnp.logical_not(net.moves))
+        def _():
+            R.yr[...] = R.y[...]
+
+    else:
+        ext.start()
+        carry.start()
+        for src, dst in ((R.s_in.at[0], R.s_own), (R.dq_in.at[yx], R.dq_own), (R.d0_in.at[yx], R.d0_own)):
+            loc.start(src, dst)
+    R.rows[...] = jnp.zeros_like(R.rows)
+    R.rows[5:6] = jnp.sum(R.g[...].astype(f32), axis=0, keepdims=True)
+    half = n // 2
+    wdn2 = lambda: R.wdn[...].reshape(4 * f, d)
+
+    def hidden(at):
+        u = mm(R.gm[at], wdn2(), NT)
+        R.gu[at] = (u * R.slope[at].astype(f32)).astype(bf)
+
+    for i in range(2):
+        hidden(slice(i * half, (i + 1) * half))
+    there.wait_recv()
+    for i in range(2):
+        hidden(slice(n + i * half, n + (i + 1) * half))
+    for i in range(2):
+        R.out[0, i * half : (i + 1) * half] = mm(
+            R.gu[n + i * half : n + (i + 1) * half], R.wup[...], NT
+        ).astype(bf)
+    back.start()
+    for i in range(2):
+        R.mine[i * half : (i + 1) * half] = mm(R.gu[i * half : (i + 1) * half], R.wup[...], NT)
+    chunk = d // 4
+
+    for c in fetched:
+        c.wait()
+    for k in range(4):
+        for i in range(2):
+            t = mm(R.gm[:, k * chunk : (k + 1) * chunk], R.buf[i * 2 * n : (i + 1) * 2 * n], TN)
+            t = t.astype(bf)
+            R.ddn[k, 2 * i] = t[:, :f]
+            R.ddn[k, 2 * i + 1] = t[:, f:]
+    big_dn.start()
+    fl, fs = R.buf.at[pl.ds(0, 4 * nl)], R.buf.at[pl.ds(4 * nl, 4 * ns)]
+    late = [loc.start(R.fl_i, fl), loc.start(R.fs_i, fs)]
+    back.wait_recv()
+    gn = R.mine[...] + R.got[0].astype(f32)
+    hat, inv = norm_rows(R.middle[...])
+    gh = gn * R.gain2[...]
+    a = jnp.mean(gh, axis=-1, keepdims=True)
+    b = jnp.mean(gh * hat, axis=-1, keepdims=True)
+    R.gmid[...] = R.g[...].astype(f32) + inv * (gh - a - hat * b)
+    R.rows[1:2] = jnp.sum(gn * hat, axis=0, keepdims=True)
+    R.rows[3:4] = jnp.sum(gn, axis=0, keepdims=True)
+    R.rows[4:5] = jnp.sum(R.gmid[...], axis=0, keepdims=True)
+    R.ga[...] = R.gmid[...].astype(bf)
+    go = mm(R.ga[...], R.wout[...], NT).astype(bf)
+    for m in range(4):
+        R.outg[m] = go[:, m * wid : (m + 1) * wid]
+
+    def part(k):
+        return ((R.gl, nl, 0), (R.gs, ns, nl))[k]
+
+    def copy(k, m):
+        dst, size, at = part(k)
+        return send(
+            R.outg.at[m, pl.ds(at, size)],
+            dst.at[pl.ds(aligned(me * size), size)],
+            sems.ssem.at[base + 4 * k + m],
+            sems.rsem.at[base + 4 * k + me],
+            net.member(m),
+        )
+
+    def arrived(k, m):
+        dst, size, at = part(k)
+        i = base + 4 * k + m
+        return send(
+            R.outg.at[m, pl.ds(at, size)], dst.at[pl.ds(m * size, size)], sems.ssem.at[i], sems.rsem.at[i], net.member(m)
+        )
+
+    for k in (1, 0):
+        for m in range(4):
+            dst, size, at = part(k)
+
+            @pl.when(me != m)
+            def _():
+                copy(k, m).start()
+
+            @pl.when(me == m)
+            def _():
+                dst[m * size : (m + 1) * size] = R.outg[m, at : at + size]
+
+    e = R.att.shape[1] // 2
+    other = R.att[:, pl.ds(aligned((1 - net.c) * e, 128), e)]
+    R.oself[...] = mm(R.ga[...], other, TN).astype(bf)
+    cross.start()
+    for k in range(4):
+        t = mm(R.n2[:, k * chunk : (k + 1) * chunk], R.gu[...], TN).astype(bf)
+        for r in range(4):
+            R.dup[k, r] = t[:, r * f : (r + 1) * f]
+    bup = jnp.sum(R.gu[...].astype(f32), axis=0, keepdims=True)
+    for c in range(2):
+
+        @pl.when(net.c == c)
+        def _():
+            for r in range(4):
+                R.rows[pl.ds(16 + (net.z + r) % 4, 1), c * f : (c + 1) * f] = bup[:, r * f : (r + 1) * f]
+
+    own = mm(R.ga[...], R.att[:, pl.ds(aligned(net.c * e, 128), e)], TN)
+    cross.wait_recv()
+    own = (own + R.olands[...].astype(f32)).astype(bf)
+    for k in range(4):
+        R.dout[k] = own[k * chunk : (k + 1) * chunk]
+    big_up.start()
+    done = [id(c) for c in fetched + late]
+    for c in loc.copies:
+        if id(c) not in done:
+            c.wait()
+    for k in (1, 0):
+        for m in range(4):
+
+            @pl.when(me != m)
+            def _():
+                arrived(k, m).wait_recv()
+
+        if k:
+            bwd_one(R.pj_s, R.gs, R.os, R.lses, R.cs, R.ds, R.acc, R.kt)
+        else:
+            bwd_one(R.pj_l, R.gl, R.ol, R.lsel, R.cl, R.dl, R.acc, R.kt)
+
+    def partial(m):
+        a = mm(R.dl[pl.ds(aligned(m * nl), nl)], R.ext[...], NT)
+        b = mm(R.ds[pl.ds(aligned(m * ns), ns)], R.ext[...], NT)
+        return jnp.concatenate([a, b], axis=0)
+
+    back.wait_send()
+    to_core = [sems.copy(R.out.at[k], R.got.at[k + 1], net.group(2)) for k in (0, 1)]
+    to_chip = sems.copy(R.out.at[2], R.got.at[3], net.group(1))
+    R.out[0] = partial(me ^ 3).astype(bf)
+    to_core[0].start()
+    R.mine[...] = partial(me ^ 1)
+    to_core[0].wait_recv()
+    R.out[2] = (R.mine[...] + R.got[1].astype(f32)).astype(bf)
+    to_chip.start()
+    R.out[1] = partial(me ^ 2).astype(bf)
+    to_core[1].start()
+    R.mine[...] = partial(me)
+    nq = R.dq.shape[2]
+    for c in late:
+        c.wait()
+    for k in range(4):
+        at = slice(k * chunk, (k + 1) * chunk)
+        both = mm(fl[:, at], R.dl[...], TN) + mm(fs[:, at], R.ds[...], TN)
+        R.dq[k] = both[:, :nq].astype(bf)
+        R.d0[k] = both[:, nq:].astype(bf)
+    bsum = jnp.sum(R.dl[...].astype(f32), axis=0, keepdims=True) + jnp.sum(
+        R.ds[...].astype(f32), axis=0, keepdims=True
+    )
+    R.rows[pl.ds(8 + me, 1), :wid] = bsum[:, :wid]
+    R.rows[pl.ds(12 + me, 1), :wid] = bsum[:, 2 * wid : 3 * wid]
+    R.rows[8:9, :HD] += bsum[:, nq : nq + HD]
+    hat, inv = norm_rows(R.resid[...].astype(f32))
+    to_core[1].wait_recv()
+    to_chip.wait_recv()
+    grad = R.mine[...] + R.got[2].astype(f32) + R.got[3].astype(f32)
+    gh = grad * R.gain1[...]
+    a = jnp.mean(gh, axis=-1, keepdims=True)
+    b = jnp.mean(gh * hat, axis=-1, keepdims=True)
+    R.g_new[...] = (R.gmid[...] + inv * (gh - a - hat * b)).astype(R.g_new.dtype)
+    R.rows[0:1] = jnp.sum(grad * hat, axis=0, keepdims=True)
+    R.rows[2:3] = jnp.sum(grad, axis=0, keepdims=True)
+    for c in to_core + [to_chip, there, cross]:
+        c.wait_send()
+    for m in range(4):
+
+        @pl.when(me != m)
+        def _():
+            for k in range(2):
+                copy(k, m).wait_send()
+
+    if last:
+        moved.end()
+    else:
+        ext.recv()
+        for own, lands, dst in ((R.dq_own, R.qland, R.q_out), (R.d0_own, R.zland, R.z_out)):
+            t = own[...].astype(f32)
+            for i in range(3):
+                t = t + lands[i].astype(f32)
+            dst[...] = t.astype(bf)
+        carry.finish(R.f_out, R.fo_out)
+        ext.sent()
+
+    def add_up(own, land, i):
+        for r in range(4):
+            t = own[yx, r].astype(f32)
+            for k in range(3):
+                t = t + land[k, r].astype(f32)
+            R.s[r, i] = t.astype(bf)
+
+    big_dn.recv()
+    add_up(R.ddn, R.rdn, 1)
+    big_up.recv()
+    add_up(R.dup, R.rup, 0)
+    t = R.dout[yx].astype(f32)
+    for k in range(3):
+        t = t + R.rout[k].astype(f32)
+    for i in range(2):
+        R.so[i] = t[:, i * wid : (i + 1) * wid].astype(bf)
+    big_dn.sent()
+    big_up.sent()
+
+
+def tail_x(axes, R):
+    dims = axes[:-2]
+    net, sems = Net(dims), Sems(R.ssem, R.rsem)
+    f32, bf = jnp.float32, jnp.bfloat16
+    moved = Batch([sems.copy(R.dx, R.dxr, net.partner())], net.moves)
+    line = FinishLine(net, sems, R.s, R.so, R.land, R.oland)
+    ext = Batch(ext_scatter(net, sems, R.dq, R.qland) + ext_scatter(net, sems, R.d0, R.zland))
+    nv = len(axes)
+    rounds = [{ax: 1 - lax.axis_index(ax)} for ax in axes]
+    steps = [sems.copy(R.vland.at[i], R.vland.at[nv + 1 + i], peer) for i, peer in enumerate(rounds)]
+    qsend = Batch([sems.copy(R.qs, R.qline, net.line(2))], net.moves)
+    qrecv = jnp.logical_not(net.moves)
+    zsend = [sems.copy(R.zs, R.zline.at[r - 1], net.line(r)) for r in (1, 2, 3)]
+    cross = Batch(
+        [sems.copy(R.fself, R.fland, net.group(2)), sems.copy(R.zself, R.zlands, net.group(2))]
+    )
+    owned = Batch(
+        [sems.copy(R.oself, R.olands, net.group(2)), sems.copy(R.qself, R.qlands, net.group(2))],
+        None,
+    )
+    net.greet(
+        [net.partner(), net.group(2)]
+        + [net.line(r) for r in (1, 2, 3)]
+        + [net.plane(e) for e in (1, 2, 3)]
+    )
+    ext.start()
+    line.start()
+    moved.start()
+    nr = R.rows0.shape[0]
+    R.vland[0, :nr] = R.rows0[...]
+    R.vland[0, nr:] = R.rows1[...]
+    R.vland[0, 6:7] = jnp.broadcast_to(R.share0[:1, :1], (1, R.rows0.shape[1]))
+    R.vland[0, nr + 6 : nr + 7] = jnp.broadcast_to(R.share1[:1, :1], (1, R.rows0.shape[1]))
+
+    def step(i):
+        steps[i].wait()
+        R.vland[i + 1] = R.vland[i] + R.vland[nv + 1 + i]
+        if i + 1 < nv:
+            steps[i + 1].start()
+
+    steps[0].start()
+    step(0)
+    step(1)
+    ext.recv()
+    yx = net.yx
+    for own, lands, dst in ((R.dq, R.qland, R.qs), (R.d0, R.zland, R.zs)):
+        t = own[yx].astype(f32)
+        for e in range(3):
+            t = t + lands[e].astype(f32)
+        dst[0] = t.astype(bf)
+    R.qs[1] = R.q1[...]
+    R.zs[1] = R.z1[...]
+    qsend.start()
+    for r in (1, 2, 3):
+        pl.when(net.z == 4 - r)(zsend[r - 1].start)
+    step(2)
+    step(3)
+    step(4)
+    nl = R.dx_l.shape[0]
+    half = R.f0.shape[1] // 2
+    theirs = pl.ds(aligned((1 - net.c) * half), half)
+    ours = pl.ds(aligned(net.c * half), half)
+
+    @pl.when(qrecv)
+    def _():
+        R.dx_l[...] = R.dx[:nl].astype(f32)
+        R.dx_s[...] = R.dx[nl:].astype(f32)
+        qsend.copies[0].wait_recv()
+        for l in range(2):
+            R.qself[l] = (R.qs[l, theirs].astype(f32) + R.qline[l, theirs].astype(f32)).astype(bf)
+            R.gqkv[l] = R.qs[l, ours].astype(f32) + R.qline[l, ours].astype(f32)
+
+    @pl.when(net.z == 0)
+    def _():
+        for r in (1, 2, 3):
+            zsend[r - 1].wait_recv()
+        for l in range(2):
+            t = R.zs[l].astype(f32)
+            for r in range(3):
+                t = t + R.zline[r, l].astype(f32)
+            R.zs[l] = t.astype(bf)
+
+    tot = R.vland.at[nv]
+    for l in range(2):
+        at = l * nr
+        for i in range(2):
+            R.g_gain[l, i : i + 1] = tot[at + i : at + i + 1]
+            R.g_bias[l, i : i + 1] = tot[at + 2 + i : at + 3 + i]
+            R.g_bqv[l, i : i + 1] = tot[pl.ds(at + 8 + 4 * i + net.z, 1), : R.g_bqv.shape[2]]
+        R.g_bout[l : l + 1] = tot[at + 4 : at + 5]
+        R.g_bdown[l : l + 1] = tot[at + 5 : at + 6]
+        R.g_bup[l : l + 1] = tot[pl.ds(at + 16 + net.z, 1)]
+        R.shares[l : l + 1] = tot[at + 6 : at + 7, :128]
+    line.finish(R.f0, R.fo0)
+
+    @pl.when(qrecv)
+    def _():
+        for l, fo in ((0, R.fo0), (1, R.fo1)):
+            R.oself[l] = fo[theirs].astype(bf)
+            R.gout[l] = jnp.transpose(fo[ours].astype(f32))
+        for c in owned.copies:
+            c.start()
+
+    for l, f in ((0, R.f0), (1, R.f1)):
+        for i in range(2):
+            R.fself[l, i] = f[i, theirs].astype(bf)
+        R.zself[l] = R.zs[l, theirs]
+    cross.start()
+    n = R.f0.shape[2]
+    for c in range(2):
+
+        @pl.when(net.c == c)
+        def _():
+            for l, f in ((0, R.f0), (1, R.f1)):
+                R.gup[l, :, c * n : (c + 1) * n] = f[0, ours].astype(f32)
+                R.gdn[l, c * n : (c + 1) * n] = jnp.transpose(f[1, ours].astype(f32))
+
+    cross.recv()
+    for c in range(2):
+
+        @pl.when(net.c != c)
+        def _():
+            for l in range(2):
+                R.gup[l, :, c * n : (c + 1) * n] = R.fland[l, 0].astype(f32)
+                R.gdn[l, c * n : (c + 1) * n] = jnp.transpose(R.fland[l, 1].astype(f32))
+
+    @pl.when(net.moves)
+    def _():
+        for c in owned.copies:
+            c.wait_recv()
+        R.gqkv[...] = R.qlands[...].astype(f32)
+        for l in range(2):
+            R.gout[l] = jnp.transpose(R.olands[l].astype(f32))
+
+    @pl.when(net.z == 0)
+    def _():
+        wid = R.gout.shape[1]
+        for l in range(2):
+            t = R.zs[l, ours].astype(f32) + R.zlands[l].astype(f32)
+            R.gqkv[l, :, :HD] += t[:, :HD]
+            R.gqkv[l, :, wid : wid + HD] += t[:, HD:]
+
+    moved.recv()
+
+    @pl.when(net.moves)
+    def _():
+        R.dx_l[...] = R.dxr[:nl].astype(f32)
+        R.dx_s[...] = R.dxr[nl:].astype(f32)
+
+    pl.when(qrecv)(lambda: [c.wait_send() for c in owned.copies] and None)
+    cross.sent()
+    qsend.sent()
+    for r in (1, 2, 3):
+        pl.when(net.z == 4 - r)(zsend[r - 1].wait_send)
+    ext.sent()
+    moved.sent()
+
+
+def run(kernel, static, ins, outs, scratch, ident, name, flops):
+    names = list(ins) + list(outs) + list(scratch)
+
+    def body_of(*refs):
+        kernel(*static, types.SimpleNamespace(**dict(zip(names, refs))))
+
+    res = pl.pallas_call(
+        body_of,
+        out_shape=tuple(jax.ShapeDtypeStruct(tuple(s), t) for s, t, _ in outs.values()),
+        in_specs=[VMEM if v else ANY for _, v in ins.values()],
+        out_specs=tuple(VMEM if v else ANY for _, _, v in outs.values()),
+        scratch_shapes=list(scratch.values()),
+        compiler_params=pltpu.CompilerParams(
+            vmem_limit_bytes=60 * 1024 * 1024, collective_id=ident, has_side_effects=True
+        ),
+        cost_estimate=pl.CostEstimate(flops=flops, bytes_accessed=10**7, transcendentals=10**6),
+        name=name,
+    )(*[a for a, _ in ins.values()])
+    return types.SimpleNamespace(**dict(zip(outs, res)))
+
+
+def fast_body(
+    dims, x_long, x_short, dy_long, dy_short, ln_gain, ln_bias, w_qkv, b_qv, w_out, b_out, w_up, b_up, w_down, b_down, threshold
+):
+    bf, f32 = jnp.bfloat16, jnp.float32
+    layers, d = w_qkv.shape[0], w_qkv.shape[1]
+    wid, ffq = w_qkv.shape[3], w_up.shape[2]
+    rl, rs = x_long.shape[1], x_short.shape[1]
+    n = rl + rs
+    sl, ss = 4 * rl, 4 * rs
+    nq, nx, n0 = 3 * wid, 3 * wid + 2 * HD, 2 * HD
+    nh = wid // HD
+    f = ffq // 2
+    ff = 4 * f
+    chunk, part = d // 4, f // 4
+    half = chunk // 2
+    net = Net(dims)
+    axes = dims + ("zh", "zl")
+    vm = lambda *s: pltpu.VMEM(tuple(s), bf)
+    vf = lambda *s: pltpu.VMEM(tuple(s), f32)
+    sem2 = lambda k: dict(ssem=DMA((k,)), rsem=DMA((k,)))
+
+    wqs = [w_qkv[l].reshape(d, nq) for l in range(layers)]
+    w0s = [w_qkv[l][:, :2, :HD].reshape(d, n0) for l in range(layers)]
+    flat = jnp.concatenate([b_up.reshape(-1), b_qv.reshape(-1)])
+    flat = jnp.pad(flat, (0, -flat.shape[0] % 4096)).reshape(16, -1)
+    share_rows = wid // 8
+    wo = lax.dynamic_slice_in_dim(w_out, (4 * net.y + 2 * net.x + net.c) * share_rows, share_rows, 1)
+    wo = [lax.all_gather(wo[l], ("zh", "zl") + dims, axis=0, tiled=True) for l in range(layers)]
+    own_up = [lax.dynamic_slice_in_dim(w_up[l], net.c * f, f, 1) for l in range(layers)]
+    own_dn = [lax.dynamic_slice_in_dim(w_down[l], net.c * f, f, 0) for l in range(layers)]
+
+    lands = dict(qland=vm(4, chunk, nq), zland=vm(4, chunk, n0))
+    P0 = run(
+        first_x,
+        (dims,),
+        dict(xl=(x_long[0], 1), xs=(x_short[0], 1), wq=(wqs[0], 1), w0=(w0s[0], 1), small=(flat, 1), w_up=(w_up, 0), w_down=(w_down, 0)),
+        dict(
+            xr=((n, d), bf, 1), ext=((d, nx), bf, 1), smalls=((4,) + flat.shape, bf, 1),
+            zup=((chunk, 3 * f), bf, 0), zdn=((3, part, d), bf, 0),
+        ),
+        dict(**lands, **sem2(24)),
+        1,
+        "first_x",
+        10**9,
+    )
+    n_up = layers * ffq
+    smalls = P0.smalls.reshape(4, -1)
+    rel_bup = smalls[:, :n_up].reshape(4, layers, 2, f).astype(f32)
+    rel_bup = lax.dynamic_index_in_dim(rel_bup, net.c, 2, keepdims=False)
+    rel_bup = jnp.swapaxes(rel_bup, 0, 1).reshape(layers, ff)
+    rel_bqv = smalls[:, n_up : n_up + layers * 2 * wid].reshape(4, layers, 2, wid).astype(f32)
+    my_bqv = lax.dynamic_index_in_dim(rel_bqv, (net.me - net.z) % 4, 0, keepdims=False)
+    zero_bq = lax.dynamic_index_in_dim(rel_bqv, (0 - net.z) % 4, 0, keepdims=False)[:, 0, :HD]
+    none = jnp.zeros((layers, wid), f32)
+    bias = jnp.concatenate([my_bqv[:, 0], none, my_bqv[:, 1], zero_bq, none[:, :HD]], axis=1)
+    gain, shift = ln_gain.astype(f32), ln_bias.astype(f32)
+    bo, bd = b_out.astype(f32), b_down.astype(f32)
+    limits = jnp.broadcast_to((threshold.astype(f32) / 64.0)[:, None, None], (layers, 8, 128))
+
+    resid, zup, zdn = P0.xr, P0.zup, P0.zdn
+    exts = [P0.ext]
+    saved = []
+    for l in range(layers):
+        first, last = l == 0, l == layers - 1
+        ins = dict(
+            resid=(resid, 1), gain1=(gain[l, :1], 1), shift1=(shift[l, :1], 1), gain2=(gain[l, 1:], 1), shift2=(shift[l, 1:], 1),
+            ext=(exts[l], 1), bias=(bias[l : l + 1], 1), own_up=(own_up[l], 1), own_dn=(own_dn[l], 1), zup=(zup, 1), zdn=(zdn, 1),
+            wout=(wo[l], 1), bout=(bo[l : l + 1], 1), bup=(rel_bup[l : l + 1], 1), bdown=(bd[l : l + 1], 1), limit=(limits[l], 1),
+        )
+        outs = dict(
+            fl_o=((sl, d), bf, 0), fs_o=((ss, d), bf, 0), pjl_o=((sl, nx), bf, 0), pjs_o=((ss, nx), bf, 0),
+            att=((n, 4 * wid), bf, 1), ol=((sl, wid), bf, 1), os=((ss, wid), bf, 1),
+            lsel=((8, sl), f32, 1), lses=((8, ss), f32, 1), cl=((8, sl), f32, 1), cs=((8, ss), f32, 1),
+            wup_o=((d, ff), bf, 0), wdn_o=((4, f, d), bf, 0), middle=((n, d), f32, 1), n2=((2 * n, d), bf, 1),
+            act_o=((2, 2 * n, 2 * f), bf, 0), slope_o=((2 * n, ff), bf, 0), new=((n, d), f32, 1), share=((8, 128), f32, 1),
+        )
+        scratch = dict(
+            fl=vm(sl, d), fs=vm(ss, d), pj_l=vm(sl, nx), pj_s=vm(ss, nx), wup=vm(d, ff), wdn=vm(4, f, d),
+            act=vm(2, 2 * n, 2 * f), slope=vm(2 * n, ff), land=vm(4, n, wid), out=vm(n, d), got=vm(n, d), lsem=DMA((24,)),
+            **sem2(48),
+        )
+        if first:
+            ins.update(wq=(wqs[1], 1), w0=(w0s[1], 1), w_up=(w_up, 0), w_down=(w_down, 0))
+            outs.update(ext_next=((d, nx), bf, 1), zup_next=((chunk, 3 * f), bf, 0), zdn_next=((3, part, d), bf, 0))
+            scratch.update(lands)
+        else:
+            ins.update(dl=(dy_long[0], 1), ds=(dy_short[0], 1))
+            outs.update(dyr=((n, d), bf, 1))
+        if last:
+            outs.update(y=((n, d), bf, 1))
+        A = run(forward_x, (dims, first, last), ins, outs, scratch, 2 + l, "forward_x", 10**10)
+        A.resid = resid
+        saved.append(A)
+        resid = A.new
+        if first:
+            exts.append(A.ext_next)
+            zup, zdn = A.zup_next, A.zdn_next
+
+    g = saved[-1].dyr
+    back = [None] * layers
+    B = None
+    for l in reversed(range(layers)):
+        A = saved[l]
+        last = l == layers - 1
+        ins = dict(
+            g=(g, 1), att=(A.att, 1), wout=(wo[l], 1), gain1=(gain[l, :1], 1), gain2=(gain[l, 1:], 1), wup=(A.wup_o, 1), wdn=(A.wdn_o, 1),
+            middle=(A.middle, 1), n2=(A.n2, 1), act=(A.act_o, 0), slope=(A.slope_o, 1), resid=(A.resid, 1),
+            pjl_i=(A.pjl_o, 0), pjs_i=(A.pjs_o, 0), ext_i=(exts[l], 0), fl_i=(A.fl_o, 0), fs_i=(A.fs_o, 0),
+            ol=(A.ol, 1), os=(A.os, 1), lsel=(A.lsel, 1), lses=(A.lses, 1), cl=(A.cl, 1), cs=(A.cs, 1),
+        )
+        outs = dict(
+            g_new=((n, d), f32 if l else bf, 1), rows=((24, d), f32, 1), dq=((4, chunk, nq), bf, 1), d0=((4, chunk, n0), bf, 1),
+            s=((4, 2, chunk, f), bf, 1), so=((2, chunk, wid), bf, 1),
+        )
+        scratch = dict(
+            gm=vm(2 * n, d), gu=vm(2 * n, ff), mine=vf(n, d), out=vm(3, n, d), got=vm(4, n, d), gmid=vf(n, d), ga=vm(n, d),
+            oself=vm(d, 2 * wid), olands=vm(d, 2 * wid), dup=vm(4, 4, chunk, f), ddn=vm(4, 4, chunk, f), dout=vm(4, chunk, 2 * wid),
+            rup=vm(3, 4, chunk, f), rdn=vm(3, 4, chunk, f), rout=vm(3, chunk, 2 * wid),
+            outg=vm(4, n, wid), gl=vm(sl, wid), gs=vm(ss, wid), pj_l=vm(sl, nx), pj_s=vm(ss, nx), ext=vm(d, nx),
+            buf=vm(sl + ss, d), dl=vm(sl, nx), ds=vm(ss, nx), acc=vf(2 * nh + 1, sl, HD), kt=vm(nh + 1, HD, sl),
+            lsem=DMA((12,)), **sem2(48),
+        )
+        if last:
+            ins.update(y=(A.y, 1))
+            outs.update(yr=((n, d), bf, 1))
+        else:
+            ins.update(s_in=(B.s, 0), so_in=(B.so, 1), dq_in=(B.dq, 0), d0_in=(B.d0, 0))
+            outs.update(
+                f_out=((2, chunk, f), bf, 1), fo_out=((chunk, wid), bf, 1), q_out=((chunk, nq), bf, 1), z_out=((chunk, n0), bf, 1)
+            )
+            scratch.update(
+                s_own=vm(2, chunk, f), dq_own=vm(chunk, nq), d0_own=vm(chunk, n0), fland=vm(3, 2, chunk, f), foland=vm(3, chunk, wid), qland=vm(3, chunk, nq), zland=vm(3, chunk, n0))
+        B = run(backward_x, (dims, last), ins, outs, scratch, 6 + l, "backward_x", 2 * 10**10)
+        back[l] = B
+        g = B.g_new
+        if last:
+            y = B.yr
+
+    nv = len(axes)
+    T = run(
+        tail_x,
+        (axes,),
+        dict(
+            s=(B.s, 1), so=(B.so, 1), dq=(B.dq, 1), d0=(B.d0, 1), f1=(B.f_out, 1), fo1=(B.fo_out, 1), q1=(B.q_out, 1), z1=(B.z_out, 1),
+            rows0=(back[0].rows, 1), rows1=(back[1].rows, 1), share0=(saved[0].share, 1), share1=(saved[1].share, 1), dx=(g, 1),
+        ),
+        dict(
+            gup=((2, half, ffq), f32, 1), gdn=((2, ffq, half), f32, 1), gout=((2, wid, half), f32, 1), gqkv=((2, half, nq), f32, 1),
+            dx_l=((rl, d), f32, 1), dx_s=((rs, d), f32, 1), g_gain=((2, 2, d), f32, 1), g_bias=((2, 2, d), f32, 1),
+            g_bqv=((2, 2, wid), f32, 1), g_bout=((2, d), f32, 1), g_bdown=((2, d), f32, 1), g_bup=((2, ffq), f32, 1),
+            shares=((2, 128), f32, 1),
+        ),
+        dict(
+            land=vm(3, 2, chunk, f), oland=vm(3, chunk, wid), f0=vf(2, chunk, f), fo0=vf(chunk, wid),
+            qland=vm(3, chunk, nq), zland=vm(3, chunk, n0), qs=vm(2, chunk, nq), zs=vm(2, chunk, n0), qline=vm(2, chunk, nq),
+            zline=vm(3, 2, chunk, n0), fself=vm(2, 2, half, f), fland=vm(2, 2, half, f), oself=vm(2, half, wid),
+            olands=vm(2, half, wid), qself=vm(2, half, nq), qlands=vm(2, half, nq), zself=vm(2, half, n0), zlands=vm(2, half, n0),
+            vland=vf(2 * nv + 1, 48, d), dxr=vm(n, d), **sem2(32),
+        ),
+        10,
+        "tail_x",
+        10**9,
+    )
+    return (
+        y[None, :rl],
+        y[None, rl:],
+        T.dx_l[None],
+        T.dx_s[None],
+        T.g_gain,
+        T.g_bias,
+        T.gqkv.reshape(layers, half, 3, wid),
+        T.g_bqv,
+        T.gout,
+        T.g_bout,
+        T.gup,
+        T.g_bup,
+        T.gdn,
+        T.g_bdown,
+        T.shares[:, 0] / (8 * 4 * n),
+    )
+
+
 def solution(mesh):
     dp, mp = mesh.shape["dp"], mesh.shape["mp"]
     bits = dp.bit_length() - 1
@@ -944,6 +2025,7 @@
         P(), P(), P(None, dims, None, z), P(None, None, z), P(None, z, dims), P(),
         P(None, dims, z), P(None, z), P(None, z, dims), P(), P(),
     )
+    run = functools.partial(fast_body, dims) if dp == 8 else functools.partial(body, dims, dp, mp)
     return jax.shard_map(
-        functools.partial(body, dims, dp, mp), mesh=fine, in_specs=in_specs, out_specs=out_specs, check_vma=False
+        run, mesh=fine, in_specs=in_specs, out_specs=out_specs, check_vma=False
     )

time: 902 us -> 487 us (0.54)
  waiting for transfers between devices: 304 us -> 9.45 us
  Pallas kernels: 215 us -> 415 us
  starting transfers between devices: 106 us -> 0.08 us
  matrix products: 92.8 us -> 0 us
  other arithmetic: 60.7 us -> 1.41 us
  local copies, waits for them, and re-layouts: 90.7 us -> 37.1 us
    pallas_call x9 -> x6, Pallas kernels: 215 us -> 415 us  [run(): pl.pallas_call(body_of, out_shape=tuple((jax.ShapeDtypeStruct(tuple(s), t...]
    all_gather x6 -> x2, waiting for transfers between devices: 166 us -> 8.74 us  [fast_body(): lax.all_gather(wo[l], ('zh', 'zl') + dims, axis=0, tiled=True)]
    ppermute x43 -> x0, waiting for transfers between devices: 138 us -> none  [the longest x20 92.7 us: swap(): lax.ppermute(v, axes if len(axes) > 1 else axes[0], [(i, count - 1 - i) f...]
    ppermute x43 -> x0, starting transfers between devices: 106 us -> none  [the longest x9 45.2 us: ring(): lax.ppermute(v, ('zh', 'zl'), [(i, (i + step) % n) for i in range(n)])]
    dot_general x22 -> x0, matrix products: 92.8 us -> none  [dot(): lax.dot_general(a, b, (((ca,), (cb,)), ((), ())), preferred_element_type=...]
    convert_element_type x32 -> x4, other arithmetic: 23.6 us -> 0.03 us  [the longest x2 0.01 us: fast_body(): gain, shift = (ln_gain.astype(f32), ln_bias.astype(f32))]
    unnamed x278 -> x54, local copies, waits for them, and re-layouts: 28.5 us -> 10.9 us
    dynamic_slice x22 -> x7, local copies, waits for them, and re-layouts: 16.8 us -> 3.5 us  [the longest x2 1.76 us: fast_body(): lax.dynamic_slice_in_dim(w_up[l], net.c * f, f, 1)]
  transfers between devices with their start and end apart: 49 -> 2, of which waited for: 25 -> 1; matrix products, arithmetic and copies ran while one was open for 17% -> 4% of each run, Pallas kernels for 14% -> 25%
where the time goes in v4:
time: 487 us; the launch traced here: 478 us
  Pallas kernels  415 us (85%)
  local copies, waits for them, and re-layouts  37.1 us (8%)
  between operations  14.6 us (3%)
  waiting for transfers between devices  9.45 us (2%)
    pallas_call x6, Pallas kernels, run(): pl.pallas_call(body_of, out_shape=tuple((jax.ShapeDtypeStruct(tuple(s), t...  415 us
    unnamed x54, local copies, waits for them, and re-layouts  10.9 us
  transfers between devices with their start and end apart: 2, of which 1 were waited for; matrix products, arithmetic and copies ran while one was open for 4% of the time, Pallas kernels for 25%

profile of v4, /device:TPU:1, one launch (start us, length us, event | category | flops | bytes accessed | tf_op | source)
XLA Modules:
  0.0 478.1 jit_solution(15954793177656090246)
XLA Ops:
  7.2 1.4 constant_dynamic-slice_fusion.2
  8.7 0.7 all-gather.7.cloned.1.call-update
  9.5 0.8 reshape.73
  10.3 0.7 reshape.72
  11.0 0.6 reshape.74.refs_4_
  11.6 2.9 fusion.4
  14.5 1.2 slice_bitcast_fusion.14
  15.7 0.8 copy.47.refs_3_
  16.5 1.4 copy.46.refs_2_
  17.9 49.4 %first_x.1 = (bf16[384,768]{1,0:T(8,128)(2,1)}, bf16[768,704]{1,0:T(8,128)(2,1)}, bf16[4,16,256]{2,1,0:T(8,128)(2,1)}, bf16[192,1152]{1,0:T(8,128)(2,1)}, bf16[3,96,768]{2,1,0:T(8,128)(2,1)}) custom-call(bf16[256,768]{1,0:T(8,128)(2,1)} %bitcast.76, bf16[128,768]{1,0:T(8,128)(2,1)} %bitcast.78, bf16[768,576]{1,0:T(8,128)(2,1)} %copy.46.refs_2_, ...), custom_call_target="tpu_custom_call" | custom-call | flops 1000000000 | bytes 10000000 | tf_op jit(solution)/shard_map/first_x/pallas_call | solution.py:1815
  67.3 0.8 copy.55
  68.2 0.9 dynamic-slice_bitcast_fusion.1.refs_7_
  69.0 0.9 dynamic-slice_bitcast_fusion.3.refs_7_
  69.9 0.9 slice.179
  70.9 0.8 copy.51.refs_17_
  71.7 1.3 copy.50.refs_16_
  73.1 0.6 copy.57
  73.8 0.6 copy.56
  74.5 0.6 fusion.8
  75.3 0.9 dynamic-slice_bitcast_fusion.refs_8_
  76.2 0.9 dynamic-slice_bitcast_fusion.2.refs_8_
  77.0 0.6 fusion.5
  77.6 0.6 fusion.6
  78.2 0.6 slice_bitcast_fusion.4
  78.8 8.7 %all-gather.5.cloned.1.call-done = bf16[1,768,768]{2,1,0:T(8,128)(2,1)} async-done(((bf16[1,24,768]{2,1,0:T(8,128)(2,1)}), bf16[1,768,768]{2,1,0:T(8,128)(2,1)}) %all-gather.5.cloned.1.call-update) | async-done | bytes 1179664 | tf_op jit(solution)/shard_map/all_gather | solution.py:1857
  87.6 1.1 broadcast_in_dim.29.refs_15_
  88.7 70.9 %forward_x.2 = (bf16[1024,768]{1,0:T(8,128)(2,1)}, bf16[512,768]{1,0:T(8,128)(2,1)}, bf16[1024,704]{1,0:T(8,128)(2,1)}, bf16[512,704]{1,0:T(8,128)(2,1)}, bf16[3...) custom-call(bf16[384,768]{1,0:T(8,128)(2,1)} %get-tuple-element.92.r, ...), custom_call_target="tpu_custom_call" | custom-call | flops 10000000000 | bytes 10000000 | tf_op jit(solution)/shard_map/forward_x/pallas_call | solution.py:1815
  159.6 1.2 broadcast_in_dim.31.refs_15_
  160.8 56.7 %forward_x.3 = (bf16[1024,768]{1,0:T(8,128)(2,1)}, bf16[512,768]{1,0:T(8,128)(2,1)}, bf16[1024,704]{1,0:T(8,128)(2,1)}, bf16[512,704]{1,0:T(8,128)(2,1)}, bf16[3...) custom-call(f32[384,768]{1,0:T(8,128)} %get-tuple-element.97.refs_0_, ...), custom_call_target="tpu_custom_call" | custom-call | flops 10000000000 | bytes 10000000 | tf_op jit(solution)/shard_map/forward_x/pallas_call | solution.py:1815
  217.5 78.1 %backward_x.2 = (f32[384,768]{1,0:T(8,128)}, f32[24,768]{1,0:T(8,128)}, bf16[4,192,576]{2,1,0:T(8,128)(2,1)}, bf16[4,192,128]{2,1,0:T(8,128)(2,1)}, bf16[4,2,192...) custom-call(bf16[384,768]{1,0:T(8,128)(2,1)} %get-tuple-element.101.refs_0_, ...), custom_call_target="tpu_custom_call" | custom-call | flops 20000000000 | bytes 10000000 | tf_op jit(solution)/shard_map/backward_x/pallas_call | solution.py:1815
  295.6 1.6 slice_bitcast_fusion.1
  297.2 1.8 slice_bitcast_fusion
  299.0 81.9 %backward_x.3 = (bf16[384,768]{1,0:T(8,128)(2,1)}, f32[24,768]{1,0:T(8,128)}, bf16[4,192,576]{2,1,0:T(8,128)(2,1)}, bf16[4,192,128]{2,1,0:T(8,128)(2,1)}, bf16[4...) custom-call(f32[384,768]{1,0:T(8,128)} %get-tuple-element.121.refs_0, ...), custom_call_target="tpu_custom_call" | custom-call | flops 20000000000 | bytes 10000000 | tf_op jit(solution)/shard_map/backward_x/pallas_call | solution.py:1815
  380.9 78.6 %tail_x.1 = (f32[2,96,768]{2,1,0:T(8,128)}, f32[2,768,96]{2,1,0:T(8,128)}, f32[2,192,96]{2,1,0:T(8,128)}, f32[2,96,576]{2,1,0:T(8,128)}, f32[256,768]{1,0:T(8,12...) custom-call(bf16[4,2,192,384]{3,2,1,0:T(8,128)(2,1)} %get-tuple-elem, ...), custom_call_target="tpu_custom_call" | custom-call | flops 1000000000 | bytes 10000000 | tf_op jit(solution)/shard_map/tail_x/pallas_call | solution.py:1815
  459.5 1.4 multiply_reduce_fusion
  460.9 1.3 copy.52
  462.1 1.1 copy.53
  463.2 1.1 copy.54
  464.3 0.9 copy.72
  465.2 0.7 copy.73
  466.0 0.6 copy.74
  466.6 0.6 copy.75
  467.2 0.6 copy.76
  467.8 0.7 copy.77
  468.5 0.6 copy.78
  469.1 0.8 copy.79
  469.9 0.6 copy.80
  470.5 0.6 copy.81
  (62 shorter events, 0.7 us)
Async XLA Ops:
  7.2 80.4 %all-gather.5.cloned.1.call-start = ((), (), s32[]{:S(2)}) async-start(), calls=%async_computation | async-start | bytes 1216512 | tf_op jit(solution)/shard_map/all_gather | solution.py:1857
  8.7 150.9 %all-gather.7.cloned.1.call-start = ((), (), s32[]{:S(2)}) async-start(), calls=%async_computation.1 | async-start | bytes 1216512 | tf_op jit(solution)/shard_map/all_gather | solution.py:1857
  11.6 2.9 copy-start.2
  17.9 50.2 %copy-start.18 = (s32[2]{0:T(128)S(1)}, s32[2]{0:T(128)}, u32[]{:S(2)}) copy-start(s32[2]{0:T(128)} %param.29) | copy-start | bytes 28
  17.9 50.2 %copy-start.15 = (bf16[2,2,768]{2,1,0:T(2,128)(2,1)S(1)}, bf16[2,2,768]{2,1,0:T(2,128)(2,1)}, u32[]{:S(2)}) copy-start(bf16[2,2,768]{2,1,0:T(2,128)(2,1)} %param.19) | copy-start | bytes 18436
  17.9 50.2 %copy-start.16 = (bf16[2,2,768]{2,1,0:T(2,128)(2,1)S(1)}, bf16[2,2,768]{2,1,0:T(2,128)(2,1)}, u32[]{:S(2)}) copy-start(bf16[2,2,768]{2,1,0:T(2,128)(2,1)} %param.20) | copy-start | bytes 18436
  17.9 50.3 %copy-start.1 = (bf16[1,768,768]{2,1,0:T(8,128)(2,1)S(1)}, bf16[1,768,768]{2,1,0:T(8,128)(2,1)}, u32[]{:S(2)}) copy-start(bf16[1,768,768]{2,1,0:T(8,128)(2,1)} %get-tuple-element.216) | copy-start | bytes 3538948
  70.9 4.2 copy-start
  75.3 2.3 copy-start.10
  75.3 2.3 copy-start.11
  459.5 3.7 copy-start.4
  462.1 2.2 copy-start.3
  463.2 2.0 copy-start.6
  464.3 1.7 copy-start.9
  464.3 2.3 copy-start.8
  464.3 2.9 copy-start.17
  464.3 3.5 copy-start.7
  464.3 4.1 copy-start.14
  464.3 4.7 copy-start.5
  465.2 4.6 copy-start.13
  465.2 5.2 %copy-start.12 = (f32[2,768]{1,0:T(2,128)S(1)}, f32[2,768]{1,0:T(2,128)}, u32[]{:S(2)}) copy-start(f32[2,768]{1,0:T(2,128)} %get-tuple-element.280) | copy-start | bytes 18436
Sparse Core Ops, SparseCore 0:
  11.5 76.0 all-gather.4
  91.0 65.7 all-gather.6

commit v5 on v4

--- a/solution.py
+++ b/solution.py
@@ -967,6 +967,7 @@
     def copy(self, src, dst, device):
         i = self.used
         self.used += 1
+        assert i < self.ssem.shape[0]
         return send(src, dst, self.ssem.at[i], self.rsem.at[i], device)
 
 
@@ -1223,23 +1224,47 @@
         self.sem, self.copies = sem, []
 
     def start(self, src, dst):
+        assert len(self.copies) < self.sem.shape[0]
         copy = pltpu.make_async_copy(src, dst, self.sem.at[len(self.copies)])
         self.copies.append(copy)
         copy.start()
         return copy
 
 
-def z_weights(net, sems, layer, w_up, w_down, zup, zdn):
-    rows, n = zup.shape[0], zup.shape[1] // 3
-    part = zdn.shape[1]
-    out = []
-    for r in (1, 2, 3):
-        dev, slot = net.line(r), 3 - r
-        src = w_up.at[layer, pl.ds(aligned(net.yx * rows), rows), pl.ds(aligned(net.c * n, 128), n)]
-        out.append(sems.copy(src, zup.at[:, pl.ds(slot * n, n)], dev))
-        src = w_down.at[layer, pl.ds(aligned(net.c * n + net.yx * part), part)]
-        out.append(sems.copy(src, zdn.at[slot], dev))
-    return Batch(out)
+class LineWeights:
+    def __init__(self, net, sems, layer, w_up, w_down, zup, zdn):
+        rows, n = zup.shape[0], zup.shape[1] // 3
+        part = zdn.shape[1]
+        own = (
+            w_up.at[layer, pl.ds(aligned(net.yx * rows), rows), pl.ds(aligned(net.c * n, 128), n)],
+            w_down.at[layer, pl.ds(aligned(net.c * n + net.yx * part), part)],
+        )
+
+        def slot(k):
+            return (zup.at[:, pl.ds(k * n, n)], zdn.at[k])
+
+        self.steps = []
+        for s in (1, 2, 3):
+            up_src = own if s == 1 else slot(4 - s)
+            dn_src = own if s == 1 else slot(s - 2)
+            up = [sems.copy(up_src[i], slot(3 - s)[i], net.line(1)) for i in range(2)]
+            dn = [sems.copy(dn_src[i], slot(s - 1)[i], net.line(3)) for i in range(2)]
+            sends_up = jnp.logical_and(net.z >= s - 1, net.z <= 2)
+            sends_dn = jnp.logical_and(net.z <= 4 - s, net.z >= 1)
+            self.steps.append(((up, sends_up, net.z >= s), (dn, sends_dn, net.z + s <= 3)))
+
+    def start(self, s):
+        for copies, sends, _ in self.steps[s]:
+            Batch(copies, sends).start()
+
+    def recv(self, s):
+        for copies, _, gets in self.steps[s]:
+            Batch(copies, gets).recv()
+
+    def sent(self):
+        for step in self.steps:
+            for copies, sends, _ in step:
+                Batch(copies, sends).sent()
 
 
 def plane_weights(net, sems, zup, zdn, wup, wdn):
@@ -1266,12 +1291,12 @@
     )
     proj = Projections(net, sems, R.wq, R.w0, R.qland, R.zland, R.ext)
     tiny = Batch([sems.copy(R.small, R.smalls.at[4 - r], net.line(r)) for r in (1, 2, 3)])
-    weights = z_weights(net, sems, 0, R.w_up, R.w_down, R.zup, R.zdn)
+    weights = LineWeights(net, sems, 0, R.w_up, R.w_down, R.zup, R.zdn)
     net.greet([net.partner()] + [net.line(r) for r in (1, 2, 3)] + [net.plane(e) for e in (1, 2, 3)])
     proj.start()
     moved.start()
     tiny.start()
-    weights.start()
+    weights.start(0)
     R.smalls[0] = R.small[...]
 
     @pl.when(jnp.logical_not(net.moves))
@@ -1280,22 +1305,28 @@
         R.xr[nl:] = R.xs[...]
 
     proj.forward()
+    weights.recv(0)
+    weights.start(1)
     proj.finish()
+    weights.recv(1)
+    weights.start(2)
     moved.end()
     tiny.end()
-    weights.end()
+    weights.recv(2)
+    weights.sent()
 
 
 def forward_x(dims, first, last, R):
     net, sems, loc = Net(dims), Sems(R.ssem, R.rsem), Local(R.lsem)
     n, d = R.resid.shape
-    f = R.own_up.shape[1]
+    f = R.wup.shape[1] // 4
+    layer = 0 if first else 1
     weights = plane_weights(net, sems, R.zup, R.zdn, R.wup, R.wdn)
     peers = [net.group(2), net.group(3), net.partner()]
     peers += [net.plane(e) for e in (1, 2, 3)] + [net.line(r) for r in (1, 2, 3)]
     if first:
         proj = Projections(net, sems, R.wq, R.w0, R.qland, R.zland, R.ext_next)
-        later = z_weights(net, sems, 1, R.w_up, R.w_down, R.zup_next, R.zdn_next)
+        later = LineWeights(net, sems, 1, R.w_up, R.w_down, R.zup_next, R.zdn_next)
     else:
         nl = R.dl.shape[0]
         moved = Batch(
@@ -1309,6 +1340,10 @@
     back = sems.copy(R.out, R.got, net.group(2))
     net.greet(peers)
     weights.start()
+    own = [
+        loc.start(R.w_up.at[layer, :, pl.ds(aligned(net.c * f, 128), f)], R.wup.at[:, pl.ds(0, f)]),
+        loc.start(R.w_down.at[layer, pl.ds(aligned(net.c * f), f)], R.wdn.at[0]),
+    ]
     pending = project_part(
         net, sems, R.resid, R.gain1, R.shift1, R.ext, R.bias, R.fl, R.fs, R.pj_l, R.pj_s
     )
@@ -1324,18 +1359,18 @@
 
     for src, dst in ((R.fl, R.fl_o), (R.fs, R.fs_o), (R.pj_l, R.pjl_o), (R.pj_s, R.pjs_o)):
         loc.start(src, dst)
-    R.wup[:, :f] = R.own_up[...]
-    R.wdn[0] = R.own_dn[...]
     rows, part = R.zup.shape[0], R.zdn.shape[1]
     R.wup[pl.ds(aligned(net.yx * rows), rows), f:] = R.zup[...]
     for k in range(3):
         R.wdn[k + 1, pl.ds(aligned(net.yx * part), part)] = R.zdn[k]
     if first:
-        later.start()
+        later.start(0)
     attend_part(
         net, sems, R.pj_l, R.pj_s, R.att, R.ol, R.os, R.lsel, R.lses, R.cl, R.cs, R.land
     )
     if first:
+        later.recv(0)
+        later.start(1)
         proj.forward()
     share = jnp.zeros((1, 1), jnp.float32)
     for carry in (R.cl, R.cs):
@@ -1353,6 +1388,8 @@
         R.n2[at] = (hat * R.gain2[...] + R.shift2[...]).astype(jnp.bfloat16)
     there.start()
     weights.recv()
+    for copy in own:
+        copy.wait()
     for src, dst in ((R.wup, R.wup_o), (R.wdn, R.wdn_o)):
         loc.start(src, dst)
 
@@ -1374,6 +1411,9 @@
     quarter = n // 2
     for i in range(2):
         hidden(slice(i * quarter, (i + 1) * quarter))
+    if first:
+        later.recv(1)
+        later.start(2)
     there.wait_recv()
     for i in range(2):
         hidden(slice(n + i * quarter, n + (i + 1) * quarter))
@@ -1396,10 +1436,11 @@
     weights.sent()
     if first:
         proj.finish()
-        later.end()
+        later.recv(2)
+        later.sent()
     else:
         moved.end()
-    for copy in loc.copies:
+    for copy in loc.copies[2:]:
         copy.wait()
 
 
@@ -1415,10 +1456,8 @@
     back = sems.copy(R.out.at[0], R.got.at[0], net.group(2))
     cross = sems.copy(R.oself, R.olands, net.group(2))
     big_dn = Batch([sems.copy(R.ddn.at[yx ^ e], R.rdn.at[e - 1], net.plane(e)) for e in (1, 2, 3)])
-    big_up = Batch(
-        [sems.copy(R.dup.at[yx ^ e], R.rup.at[e - 1], net.plane(e)) for e in (1, 2, 3)]
-        + [sems.copy(R.dout.at[yx ^ e], R.rout.at[e - 1], net.plane(e)) for e in (1, 2, 3)]
-    )
+    big_up = Batch([sems.copy(R.dup.at[yx ^ e], R.rup.at[e - 1], net.plane(e)) for e in (1, 2, 3)])
+    big_out = Batch([sems.copy(R.dout.at[yx ^ e], R.rout.at[e - 1], net.plane(e)) for e in (1, 2, 3)])
     base = sems.used
     sems.used += 8
     peers = [net.group(d_) for d_ in (1, 2, 3)] + [net.plane(e) for e in (1, 2, 3)]
@@ -1428,6 +1467,8 @@
     else:
         carry = FinishLine(net, sems, R.s_in, R.so_in, R.fland, R.foland, R.s_own)
         ext = Batch(ext_scatter(net, sems, R.dq_in, R.qland) + ext_scatter(net, sems, R.d0_in, R.zland))
+        ext_line = ExtLine(net, sems, R.q_sum, R.z_sum, R.qline, R.zline)
+        low = Batch([sems.copy(R.s.at[r, 1], R.dnland.at[3 - r], net.line(r)) for r in (1, 2, 3)])
         peers += [net.line(2), net.line(4 - net.zl * 2 - 1)]
     R.gm[:n] = R.g[...].astype(bf)
     net.greet(peers)
@@ -1536,6 +1577,7 @@
         t = mm(R.n2[:, k * chunk : (k + 1) * chunk], R.gu[...], TN).astype(bf)
         for r in range(4):
             R.dup[k, r] = t[:, r * f : (r + 1) * f]
+    big_up.start()
     bup = jnp.sum(R.gu[...].astype(f32), axis=0, keepdims=True)
     for c in range(2):
 
@@ -1549,7 +1591,9 @@
     own = (own + R.olands[...].astype(f32)).astype(bf)
     for k in range(4):
         R.dout[k] = own[k * chunk : (k + 1) * chunk]
-    big_up.start()
+    big_out.start()
+    if not last:
+        late.append(loc.start(R.resid, R.ga))
     done = [id(c) for c in fetched + late]
     for c in loc.copies:
         if id(c) not in done:
@@ -1563,8 +1607,28 @@
 
         if k:
             bwd_one(R.pj_s, R.gs, R.os, R.lses, R.cs, R.ds, R.acc, R.kt)
+            if not last:
+                ext.recv()
+                for own_, lands, dst in ((R.dq_own, R.qland, R.q_sum), (R.d0_own, R.zland, R.z_sum)):
+                    t = own_[...].astype(f32)
+                    for i in range(3):
+                        t = t + lands[i].astype(f32)
+                    dst[...] = t.astype(bf)
+                ext_line.start()
         else:
             bwd_one(R.pj_l, R.gl, R.ol, R.lsel, R.cl, R.dl, R.acc, R.kt)
+
+    def add_up(own, land, i):
+        for r in range(4):
+            t = own[yx, r].astype(f32)
+            for k in range(3):
+                t = t + land[k, r].astype(f32)
+            R.s[r, i] = t.astype(bf)
+
+    big_dn.recv()
+    add_up(R.ddn, R.rdn, 1)
+    if not last:
+        low.start()
 
     def partial(m):
         a = mm(R.dl[pl.ds(aligned(m * nl), nl)], R.ext[...], NT)
@@ -1597,7 +1661,7 @@
     R.rows[pl.ds(8 + me, 1), :wid] = bsum[:, :wid]
     R.rows[pl.ds(12 + me, 1), :wid] = bsum[:, 2 * wid : 3 * wid]
     R.rows[8:9, :HD] += bsum[:, nq : nq + HD]
-    hat, inv = norm_rows(R.resid[...].astype(f32))
+    hat, inv = norm_rows(R.resid[...] if last else R.ga[...].astype(f32))
     to_core[1].wait_recv()
     to_chip.wait_recv()
     grad = R.mine[...] + R.got[2].astype(f32) + R.got[3].astype(f32)
@@ -1619,26 +1683,19 @@
     if last:
         moved.end()
     else:
-        ext.recv()
-        for own, lands, dst in ((R.dq_own, R.qland, R.q_out), (R.d0_own, R.zland, R.z_out)):
-            t = own[...].astype(f32)
-            for i in range(3):
-                t = t + lands[i].astype(f32)
-            dst[...] = t.astype(bf)
         carry.finish(R.f_out, R.fo_out)
         ext.sent()
-
-    def add_up(own, land, i):
-        for r in range(4):
-            t = own[yx, r].astype(f32)
-            for k in range(3):
-                t = t + land[k, r].astype(f32)
-            R.s[r, i] = t.astype(bf)
-
-    big_dn.recv()
-    add_up(R.ddn, R.rdn, 1)
+        ext_line.finish(R.q_out, R.z_out)
+        low.recv()
+        t = R.s[0, 1].astype(f32)
+        for k in range(3):
+            t = t + R.dnland[k].astype(f32)
+        R.dn_out[...] = t.astype(bf)
+        low.sent()
+
     big_up.recv()
     add_up(R.dup, R.rup, 0)
+    big_out.recv()
     t = R.dout[yx].astype(f32)
     for k in range(3):
         t = t + R.rout[k].astype(f32)
@@ -1646,6 +1703,42 @@
         R.so[i] = t[:, i * wid : (i + 1) * wid].astype(bf)
     big_dn.sent()
     big_up.sent()
+    big_out.sent()
+
+
+class ExtLine:
+    def __init__(self, net, sems, q, z, qline, zline):
+        self.net, self.q, self.z, self.qline, self.zline = net, q, z, qline, zline
+        self.qsend = Batch([sems.copy(q, qline, net.line(2))], net.moves)
+        self.stays = jnp.logical_not(net.moves)
+        self.zsend = [sems.copy(z, zline.at[r - 1], net.line(r)) for r in (1, 2, 3)]
+
+    def start(self):
+        self.qsend.start()
+        for r in (1, 2, 3):
+            pl.when(self.net.z == 4 - r)(self.zsend[r - 1].start)
+
+    def finish(self, q_out, z_out):
+        f32 = jnp.float32
+        q_out[...] = self.q[...].astype(q_out.dtype)
+        z_out[...] = self.z[...].astype(z_out.dtype)
+
+        @pl.when(self.stays)
+        def _():
+            self.qsend.copies[0].wait_recv()
+            q_out[...] = (self.q[...].astype(f32) + self.qline[...].astype(f32)).astype(q_out.dtype)
+
+        @pl.when(self.net.z == 0)
+        def _():
+            t = self.z[...].astype(f32)
+            for r in (1, 2, 3):
+                self.zsend[r - 1].wait_recv()
+                t = t + self.zline[r - 1].astype(f32)
+            z_out[...] = t.astype(z_out.dtype)
+
+        self.qsend.sent()
+        for r in (1, 2, 3):
+            pl.when(self.net.z == 4 - r)(self.zsend[r - 1].wait_send)
 
 
 def tail_x(axes, R):
@@ -1653,14 +1746,13 @@
     net, sems = Net(dims), Sems(R.ssem, R.rsem)
     f32, bf = jnp.float32, jnp.bfloat16
     moved = Batch([sems.copy(R.dx, R.dxr, net.partner())], net.moves)
-    line = FinishLine(net, sems, R.s, R.so, R.land, R.oland)
+    line = FinishLine(net, sems, R.s.at[:, pl.ds(0, 1)], R.so, R.land, R.oland)
     ext = Batch(ext_scatter(net, sems, R.dq, R.qland) + ext_scatter(net, sems, R.d0, R.zland))
     nv = len(axes)
     rounds = [{ax: 1 - lax.axis_index(ax)} for ax in axes]
     steps = [sems.copy(R.vland.at[i], R.vland.at[nv + 1 + i], peer) for i, peer in enumerate(rounds)]
-    qsend = Batch([sems.copy(R.qs, R.qline, net.line(2))], net.moves)
+    ext_line = ExtLine(net, sems, R.q_sum, R.z_sum, R.qline, R.zline)
     qrecv = jnp.logical_not(net.moves)
-    zsend = [sems.copy(R.zs, R.zline.at[r - 1], net.line(r)) for r in (1, 2, 3)]
     cross = Batch(
         [sems.copy(R.fself, R.fland, net.group(2)), sems.copy(R.zself, R.zlands, net.group(2))]
     )
@@ -1693,16 +1785,12 @@
     step(1)
     ext.recv()
     yx = net.yx
-    for own, lands, dst in ((R.dq, R.qland, R.qs), (R.d0, R.zland, R.zs)):
+    for own, lands, dst in ((R.dq, R.qland, R.q_sum), (R.d0, R.zland, R.z_sum)):
         t = own[yx].astype(f32)
         for e in range(3):
             t = t + lands[e].astype(f32)
-        dst[0] = t.astype(bf)
-    R.qs[1] = R.q1[...]
-    R.zs[1] = R.z1[...]
-    qsend.start()
-    for r in (1, 2, 3):
-        pl.when(net.z == 4 - r)(zsend[r - 1].start)
+        dst[...] = t.astype(bf)
+    ext_line.start()
     step(2)
     step(3)
     step(4)
@@ -1715,20 +1803,14 @@
     def _():
         R.dx_l[...] = R.dx[:nl].astype(f32)
         R.dx_s[...] = R.dx[nl:].astype(f32)
-        qsend.copies[0].wait_recv()
-        for l in range(2):
-            R.qself[l] = (R.qs[l, theirs].astype(f32) + R.qline[l, theirs].astype(f32)).astype(bf)
-            R.gqkv[l] = R.qs[l, ours].astype(f32) + R.qline[l, ours].astype(f32)
-
-    @pl.when(net.z == 0)
+
+    ext_line.finish(R.q0, R.z0)
+
+    @pl.when(qrecv)
     def _():
-        for r in (1, 2, 3):
-            zsend[r - 1].wait_recv()
-        for l in range(2):
-            t = R.zs[l].astype(f32)
-            for r in range(3):
-                t = t + R.zline[r, l].astype(f32)
-            R.zs[l] = t.astype(bf)
+        for l, q in ((0, R.q0), (1, R.q1)):
+            R.qself[l] = q[theirs].astype(bf)
+            R.gqkv[l] = q[ours].astype(f32)
 
     tot = R.vland.at[nv]
     for l in range(2):
@@ -1751,19 +1833,20 @@
         for c in owned.copies:
             c.start()
 
-    for l, f in ((0, R.f0), (1, R.f1)):
+    for l, fs in ((0, (R.f0.at[0], R.dn0)), (1, (R.f1.at[0], R.f1.at[1]))):
         for i in range(2):
-            R.fself[l, i] = f[i, theirs].astype(bf)
-        R.zself[l] = R.zs[l, theirs]
+            R.fself[l, i] = fs[i][theirs].astype(bf)
+    for l, z in ((0, R.z0), (1, R.z1)):
+        R.zself[l] = z[theirs].astype(bf)
     cross.start()
     n = R.f0.shape[2]
     for c in range(2):
 
         @pl.when(net.c == c)
         def _():
-            for l, f in ((0, R.f0), (1, R.f1)):
-                R.gup[l, :, c * n : (c + 1) * n] = f[0, ours].astype(f32)
-                R.gdn[l, c * n : (c + 1) * n] = jnp.transpose(f[1, ours].astype(f32))
+            for l, fs in ((0, (R.f0.at[0], R.dn0)), (1, (R.f1.at[0], R.f1.at[1]))):
+                R.gup[l, :, c * n : (c + 1) * n] = fs[0][ours].astype(f32)
+                R.gdn[l, c * n : (c + 1) * n] = jnp.transpose(fs[1][ours].astype(f32))
 
     cross.recv()
     for c in range(2):
@@ -1785,8 +1868,8 @@
     @pl.when(net.z == 0)
     def _():
         wid = R.gout.shape[1]
-        for l in range(2):
-            t = R.zs[l, ours].astype(f32) + R.zlands[l].astype(f32)
+        for l, z in ((0, R.z0), (1, R.z1)):
+            t = z[ours].astype(f32) + R.zlands[l].astype(f32)
             R.gqkv[l, :, :HD] += t[:, :HD]
             R.gqkv[l, :, wid : wid + HD] += t[:, HD:]
 
@@ -1799,11 +1882,25 @@
 
     pl.when(qrecv)(lambda: [c.wait_send() for c in owned.copies] and None)
     cross.sent()
-    qsend.sent()
-    for r in (1, 2, 3):
-        pl.when(net.z == 4 - r)(zsend[r - 1].wait_send)
     ext.sent()
     moved.sent()
+
+
+def results_k(*refs):
+    k = len(refs) // 2
+    for src, dst in zip(refs[:k], refs[k:]):
+        dst[...] = src[...]
+
+
+def results(arrays):
+    return pl.pallas_call(
+        results_k,
+        out_shape=tuple(jax.ShapeDtypeStruct(a.shape, a.dtype) for a in arrays),
+        in_specs=[VMEM] * len(arrays),
+        out_specs=(VMEM,) * len(arrays),
+        compiler_params=pltpu.CompilerParams(vmem_limit_bytes=40 * 1024 * 1024),
+        name="results_k",
+    )(*arrays)
 
 
 def run(kernel, static, ins, outs, scratch, ident, name, flops):
@@ -1855,8 +1952,6 @@
     share_rows = wid // 8
     wo = lax.dynamic_slice_in_dim(w_out, (4 * net.y + 2 * net.x + net.c) * share_rows, share_rows, 1)
     wo = [lax.all_gather(wo[l], ("zh", "zl") + dims, axis=0, tiled=True) for l in range(layers)]
-    own_up = [lax.dynamic_slice_in_dim(w_up[l], net.c * f, f, 1) for l in range(layers)]
-    own_dn = [lax.dynamic_slice_in_dim(w_down[l], net.c * f, f, 0) for l in range(layers)]
 
     lands = dict(qland=vm(4, chunk, nq), zland=vm(4, chunk, n0))
     P0 = run(
@@ -1867,7 +1962,7 @@
             xr=((n, d), bf, 1), ext=((d, nx), bf, 1), smalls=((4,) + flat.shape, bf, 1),
             zup=((chunk, 3 * f), bf, 0), zdn=((3, part, d), bf, 0),
         ),
-        dict(**lands, **sem2(24)),
+        dict(**lands, **sem2(32)),
         1,
         "first_x",
         10**9,
@@ -1893,7 +1988,7 @@
         first, last = l == 0, l == layers - 1
         ins = dict(
             resid=(resid, 1), gain1=(gain[l, :1], 1), shift1=(shift[l, :1], 1), gain2=(gain[l, 1:], 1), shift2=(shift[l, 1:], 1),
-            ext=(exts[l], 1), bias=(bias[l : l + 1], 1), own_up=(own_up[l], 1), own_dn=(own_dn[l], 1), zup=(zup, 1), zdn=(zdn, 1),
+            ext=(exts[l], 1), bias=(bias[l : l + 1], 1), w_up=(w_up, 0), w_down=(w_down, 0), zup=(zup, 1), zdn=(zdn, 1),
             wout=(wo[l], 1), bout=(bo[l : l + 1], 1), bup=(rel_bup[l : l + 1], 1), bdown=(bd[l : l + 1], 1), limit=(limits[l], 1),
         )
         outs = dict(
@@ -1909,7 +2004,7 @@
             **sem2(48),
         )
         if first:
-            ins.update(wq=(wqs[1], 1), w0=(w0s[1], 1), w_up=(w_up, 0), w_down=(w_down, 0))
+            ins.update(wq=(wqs[1], 1), w0=(w0s[1], 1))
             outs.update(ext_next=((d, nx), bf, 1), zup_next=((chunk, 3 * f), bf, 0), zdn_next=((3, part, d), bf, 0))
             scratch.update(lands)
         else:
@@ -1933,7 +2028,7 @@
         last = l == layers - 1
         ins = dict(
             g=(g, 1), att=(A.att, 1), wout=(wo[l], 1), gain1=(gain[l, :1], 1), gain2=(gain[l, 1:], 1), wup=(A.wup_o, 1), wdn=(A.wdn_o, 1),
-            middle=(A.middle, 1), n2=(A.n2, 1), act=(A.act_o, 0), slope=(A.slope_o, 1), resid=(A.resid, 1),
+            middle=(A.middle, 1), n2=(A.n2, 1), act=(A.act_o, 0), slope=(A.slope_o, 1), resid=(A.resid, int(last)),
             pjl_i=(A.pjl_o, 0), pjs_i=(A.pjs_o, 0), ext_i=(exts[l], 0), fl_i=(A.fl_o, 0), fs_i=(A.fs_o, 0),
             ol=(A.ol, 1), os=(A.os, 1), lsel=(A.lsel, 1), lses=(A.lses, 1), cl=(A.cl, 1), cs=(A.cs, 1),
         )
@@ -1955,9 +2050,10 @@
         else:
             ins.update(s_in=(B.s, 0), so_in=(B.so, 1), dq_in=(B.dq, 0), d0_in=(B.d0, 0))
             outs.update(
-                f_out=((2, chunk, f), bf, 1), fo_out=((chunk, wid), bf, 1), q_out=((chunk, nq), bf, 1), z_out=((chunk, n0), bf, 1)
+                dn_out=((chunk, f), bf, 1), f_out=((2, chunk, f), bf, 1), fo_out=((chunk, wid), bf, 1), q_out=((chunk, nq), bf, 1), z_out=((chunk, n0), bf, 1)
             )
             scratch.update(
+                q_sum=vm(chunk, nq), z_sum=vm(chunk, n0), qline=vm(chunk, nq), zline=vm(3, chunk, n0), dnland=vm(3, chunk, f),
                 s_own=vm(2, chunk, f), dq_own=vm(chunk, nq), d0_own=vm(chunk, n0), fland=vm(3, 2, chunk, f), foland=vm(3, chunk, wid), qland=vm(3, chunk, nq), zland=vm(3, chunk, n0))
         B = run(backward_x, (dims, last), ins, outs, scratch, 6 + l, "backward_x", 2 * 10**10)
         back[l] = B
@@ -1971,7 +2067,7 @@
         (axes,),
         dict(
             s=(B.s, 1), so=(B.so, 1), dq=(B.dq, 1), d0=(B.d0, 1), f1=(B.f_out, 1), fo1=(B.fo_out, 1), q1=(B.q_out, 1), z1=(B.z_out, 1),
-            rows0=(back[0].rows, 1), rows1=(back[1].rows, 1), share0=(saved[0].share, 1), share1=(saved[1].share, 1), dx=(g, 1),
+            rows0=(back[0].rows, 1), dn0=(B.dn_out, 1), rows1=(back[1].rows, 1), share0=(saved[0].share, 1), share1=(saved[1].share, 1), dx=(g, 1),
         ),
         dict(
             gup=((2, half, ffq), f32, 1), gdn=((2, ffq, half), f32, 1), gout=((2, wid, half), f32, 1), gqkv=((2, half, nq), f32, 1),
@@ -1980,9 +2076,9 @@
             shares=((2, 128), f32, 1),
         ),
         dict(
-            land=vm(3, 2, chunk, f), oland=vm(3, chunk, wid), f0=vf(2, chunk, f), fo0=vf(chunk, wid),
-            qland=vm(3, chunk, nq), zland=vm(3, chunk, n0), qs=vm(2, chunk, nq), zs=vm(2, chunk, n0), qline=vm(2, chunk, nq),
-            zline=vm(3, 2, chunk, n0), fself=vm(2, 2, half, f), fland=vm(2, 2, half, f), oself=vm(2, half, wid),
+            land=vm(3, 1, chunk, f), oland=vm(3, chunk, wid), f0=vf(1, chunk, f), fo0=vf(chunk, wid), q0=vf(chunk, nq), z0=vf(chunk, n0),
+            qland=vm(3, chunk, nq), zland=vm(3, chunk, n0), q_sum=vm(chunk, nq), z_sum=vm(chunk, n0), qline=vm(chunk, nq),
+            zline=vm(3, chunk, n0), fself=vm(2, 2, half, f), fland=vm(2, 2, half, f), oself=vm(2, half, wid),
             olands=vm(2, half, wid), qself=vm(2, half, nq), qlands=vm(2, half, nq), zself=vm(2, half, n0), zlands=vm(2, half, n0),
             vland=vf(2 * nv + 1, 48, d), dxr=vm(n, d), **sem2(32),
         ),
@@ -1990,22 +2086,15 @@
         "tail_x",
         10**9,
     )
+    done = results(
+        (
+            T.dx_l, T.dx_s, T.g_gain, T.g_bias, T.g_bqv, T.gout, T.g_bout, T.gup, T.g_bup, T.gdn, T.g_bdown
+        )
+    )
+    dx_l, dx_s, g_gain, g_bias, g_bqv, gout, g_bout, gup, g_bup, gdn, g_bdown = done
     return (
-        y[None, :rl],
-        y[None, rl:],
-        T.dx_l[None],
-        T.dx_s[None],
-        T.g_gain,
-        T.g_bias,
-        T.gqkv.reshape(layers, half, 3, wid),
-        T.g_bqv,
-        T.gout,
-        T.g_bout,
-        T.gup,
-        T.g_bup,
-        T.gdn,
-        T.g_bdown,
-        T.shares[:, 0] / (8 * 4 * n),
+        y[None, :rl], y[None, rl:], dx_l[None], dx_s[None], g_gain, g_bias, T.gqkv.reshape(layers, half, 3, wid),
+        g_bqv, gout, g_bout, gup, g_bup, gdn, g_bdown, T.shares[:, 0] / (8 * 4 * n),
     )
 
 

time: 487 us -> 455 us (0.934)
  Pallas kernels: 415 us -> 394 us
  local copies, waits for them, and re-layouts: 37.1 us -> 31.9 us
  waiting for transfers between devices: 9.45 us -> 4.26 us
    pallas_call x6, Pallas kernels: 415 us -> 393 us  [run(): pl.pallas_call(body_of, out_shape=tuple((jax.ShapeDtypeStruct(tuple(s), t...]
    all_gather x2, waiting for transfers between devices: 8.74 us -> 3.55 us  [fast_body(): lax.all_gather(wo[l], ('zh', 'zl') + dims, axis=0, tiled=True)]
    unnamed x54 -> x40, local copies, waits for them, and re-layouts: 10.9 us -> 13.6 us
  transfers between devices with their start and end apart: 2 -> 2, of which waited for: 1 -> 1; matrix products, arithmetic and copies ran while one was open for 4% -> 3% of each run, Pallas kernels for 25% -> 27%
where the time goes in v5:
time: 455 us; the launch traced here: 446 us
  Pallas kernels  394 us (87%)
  local copies, waits for them, and re-layouts  31.9 us (7%)
  between operations  14.5 us (3%)
    pallas_call x6, Pallas kernels, run(): pl.pallas_call(body_of, out_shape=tuple((jax.ShapeDtypeStruct(tuple(s), t...  393 us
    unnamed x40, local copies, waits for them, and re-layouts  13.6 us
  transfers between devices with their start and end apart: 2, of which 1 were waited for; matrix products, arithmetic and copies ran while one was open for 3% of the time, Pallas kernels for 27%

profile of v5, /device:TPU:1, one launch (start us, length us, event | category | flops | bytes accessed | tf_op | source)
XLA Modules:
  0.0 446.2 jit_solution(770520124653827222)
XLA Ops:
  7.2 0.0 all-gather.5.cloned.1.call-start
  7.2 1.4 constant_dynamic-slice_fusion.2
  8.7 0.0 all-gather.7.cloned.1.call-start
  8.7 0.7 all-gather.7.cloned.1.call-update
  9.5 0.8 reshape.69
  10.3 0.7 reshape.68
  11.0 0.6 reshape.70.refs_4_
  11.6 1.7 slice_bitcast_fusion.14
  13.3 0.8 copy.47.refs_3_
  14.1 1.3 copy.46.refs_2_
  15.5 49.2 %first_x.1 = (bf16[384,768]{1,0:T(8,128)(2,1)}, bf16[768,704]{1,0:T(8,128)(2,1)}, bf16[4,16,256]{2,1,0:T(8,128)(2,1)}, bf16[192,1152]{1,0:T(8,128)(2,1)}, bf16[3,96,768]{2,1,0:T(8,128)(2,1)}) custom-call(bf16[256,768]{1,0:T(8,128)(2,1)} %bitcast.67, bf16[128,768]{1,0:T(8,128)(2,1)} %bitcast.68, bf16[768,576]{1,0:T(8,128)(2,1)} %copy.46.refs_2_, ...), custom_call_target="tpu_custom_call" | custom-call | flops 1000000000 | bytes 10000000 | tf_op jit(solution)/shard_map/first_x/pallas_call | solution.py:1912
  64.7 0.8 copy.55
  65.6 0.8 copy.51.refs_17_
  66.5 1.3 copy.50.refs_16_
  67.8 0.6 copy.57
  68.4 0.1 reshape.74
  68.5 0.6 copy.56
  69.1 0.1 concatenate.7
  69.2 0.6 fusion.6
  69.8 0.6 fusion.3
  70.4 0.6 fusion.4
  71.0 0.6 slice_bitcast_fusion.4
  71.7 3.5 all-gather.5.cloned.1.call-done
  75.2 1.3 broadcast_in_dim.29.refs_15_
  76.5 69.4 %forward_x.2 = (bf16[1024,768]{1,0:T(8,128)(2,1)}, bf16[512,768]{1,0:T(8,128)(2,1)}, bf16[1024,704]{1,0:T(8,128)(2,1)}, bf16[512,704]{1,0:T(8,128)(2,1)}, bf16[3...) custom-call(bf16[384,768]{1,0:T(8,128)(2,1)} %get-tuple-element.104., ...), custom_call_target="tpu_custom_call" | custom-call | flops 10000000000 | bytes 10000000 | tf_op jit(solution)/shard_map/forward_x/pallas_call | solution.py:1912
  145.9 1.2 broadcast_in_dim.31.refs_15_
  147.1 56.2 %forward_x.3 = (bf16[1024,768]{1,0:T(8,128)(2,1)}, bf16[512,768]{1,0:T(8,128)(2,1)}, bf16[1024,704]{1,0:T(8,128)(2,1)}, bf16[512,704]{1,0:T(8,128)(2,1)}, bf16[3...) custom-call(f32[384,768]{1,0:T(8,128)} %get-tuple-element.109.refs_0, ...), custom_call_target="tpu_custom_call" | custom-call | flops 10000000000 | bytes 10000000 | tf_op jit(solution)/shard_map/forward_x/pallas_call | solution.py:1912
  203.4 77.4 %backward_x.2 = (f32[384,768]{1,0:T(8,128)}, f32[24,768]{1,0:T(8,128)}, bf16[4,192,576]{2,1,0:T(8,128)(2,1)}, bf16[4,192,128]{2,1,0:T(8,128)(2,1)}, bf16[4,2,192...) custom-call(bf16[384,768]{1,0:T(8,128)(2,1)} %get-tuple-element.113.refs_0_, ...), custom_call_target="tpu_custom_call" | custom-call | flops 20000000000 | bytes 10000000 | tf_op jit(solution)/shard_map/backward_x/pallas_call | solution.py:1912
  280.8 1.6 slice_bitcast_fusion.1
  282.4 1.8 slice_bitcast_fusion
  284.2 81.7 %backward_x.3 = (bf16[384,768]{1,0:T(8,128)(2,1)}, f32[24,768]{1,0:T(8,128)}, bf16[4,192,576]{2,1,0:T(8,128)(2,1)}, bf16[4,192,128]{2,1,0:T(8,128)(2,1)}, bf16[4...) custom-call(f32[384,768]{1,0:T(8,128)} %get-tuple-element.133.refs_0, ...), custom_call_target="tpu_custom_call" | custom-call | flops 20000000000 | bytes 10000000 | tf_op jit(solution)/shard_map/backward_x/pallas_call | solution.py:1912
  365.9 58.7 %tail_x.1 = (f32[2,96,768]{2,1,0:T(8,128)}, f32[2,768,96]{2,1,0:T(8,128)}, f32[2,192,96]{2,1,0:T(8,128)}, f32[2,96,576]{2,1,0:T(8,128)}, f32[256,768]{1,0:T(8,12...) custom-call(bf16[4,2,192,384]{3,2,1,0:T(8,128)(2,1)} %get-tuple-elem, ...), custom_call_target="tpu_custom_call" | custom-call | flops 1000000000 | bytes 10000000 | tf_op jit(solution)/shard_map/tail_x/pallas_call | solution.py:1912
  424.6 1.2 multiply_reduce_fusion
  425.9 1.1 copy-done
  427.0 1.1 copy-done.1
  428.2 1.1 copy-done.2
  429.2 1.0 copy-done.3
  430.2 0.9 copy-done.4
  431.2 0.7 copy-done.5
  431.9 0.7 copy-done.6
  432.6 0.7 copy-done.7
  433.3 0.7 copy-done.8
  434.0 0.7 copy-done.9
  434.6 0.7 copy-done.10
  435.3 1.4 results_k.1
  436.8 1.1 copy.54
  437.8 0.2 copy.52
  438.1 1.1 copy.53
  (43 shorter events, 0.2 us)
Async XLA Ops:
  7.2 68.0 %all-gather.5.cloned.1.call-start = ((), (), s32[]{:S(2)}) async-start(), calls=%async_computation | async-start | bytes 1216512 | tf_op jit(solution)/shard_map/all_gather | solution.py:1954
  8.7 137.2 %all-gather.7.cloned.1.call-start = ((), (), s32[]{:S(2)}) async-start(), calls=%async_computation.1 | async-start | bytes 1216512 | tf_op jit(solution)/shard_map/all_gather | solution.py:1954
  15.5 50.1 %copy-start.14 = (bf16[2,2,768]{2,1,0:T(2,128)(2,1)S(1)}, bf16[2,2,768]{2,1,0:T(2,128)(2,1)}, u32[]{:S(2)}) copy-start(bf16[2,2,768]{2,1,0:T(2,128)(2,1)} %param.19) | copy-start | bytes 18436
  15.5 50.1 %copy-start.15 = (bf16[2,2,768]{2,1,0:T(2,128)(2,1)S(1)}, bf16[2,2,768]{2,1,0:T(2,128)(2,1)}, u32[]{:S(2)}) copy-start(bf16[2,2,768]{2,1,0:T(2,128)(2,1)} %param.20) | copy-start | bytes 18436
  64.6 4.6 %copy-start.16 = (s32[2]{0:T(128)S(1)}, s32[2]{0:T(128)}, u32[]{:S(2)}) copy-start(s32[2]{0:T(128)} %param.29) | copy-start | bytes 28
  64.7 5.8 %copy-start.12 = (bf16[2,768]{1,0:T(2,128)(2,1)S(1)}, bf16[2,768]{1,0:T(2,128)(2,1)}, u32[]{:S(2)}) copy-start(bf16[2,768]{1,0:T(2,128)(2,1)} %param.28) | copy-start | bytes 9220
  64.7 5.8 %copy-start.13 = (bf16[2,768]{1,0:T(2,128)(2,1)S(1)}, bf16[2,768]{1,0:T(2,128)(2,1)}, u32[]{:S(2)}) copy-start(bf16[2,768]{1,0:T(2,128)(2,1)} %param.24) | copy-start | bytes 9220
  425.9 1.1 copy-start
  427.0 1.1 copy-start.1
  428.2 1.1 copy-start.2
  429.2 1.0 copy-start.3
  430.2 0.9 copy-start.4
  431.2 0.7 copy-start.5
  431.9 0.7 copy-start.6
  432.6 0.7 copy-start.7
  433.3 0.7 copy-start.8
  434.0 0.7 copy-start.9
  434.6 0.7 copy-start.10
  435.3 2.5 copy-start.11
Sparse Core Ops, SparseCore 0:
  11.5 63.6 all-gather.4
  78.7 57.7 all-gather.6

commit v6 on v5

--- a/solution.py
+++ b/solution.py
@@ -89,7 +89,7 @@
             done(b)
 
 
-def bwd_one(x_ref, g_ref, o_ref, lse_ref, carry_ref, d_ref, acc, kt):
+def bwd_one(x_ref, g_ref, o_ref, lse_ref, carry_ref, d_ref, acc, kt, midway=None):
     size = x_ref.shape[0]
     nh = (x_ref.shape[1] - 2 * HD) // (3 * HD)
     w = nh * HD
@@ -177,7 +177,8 @@
             else:
                 acc[2 * nh, cols] += dk
         d_ref[rows, 3 * w : 3 * w + HD] = jnp.transpose(dqt * 0.125).astype(jnp.bfloat16)
-        own = pl.ds(b * BR, BR)
+        if midway is not None:
+            midway(b)
     for h in range(nh):
         d_ref[:, w + h * HD : w + (h + 1) * HD] = acc[h, :size].astype(jnp.bfloat16)
         d_ref[:, 2 * w + h * HD : 2 * w + (h + 1) * HD] = acc[nh + h, :size].astype(jnp.bfloat16)
@@ -1061,7 +1062,7 @@
                 copy.wait_send()
 
 
-def project_part(net, sems, resid, gain, shift, w, bias, fl, fs, pj_l, pj_s):
+def project_part(net, sems, resid, gain, shift, w, bias, fl, fs, pj_l, pj_s, after_chip):
     nl, ns = fl.shape[0] // 4, fs.shape[0] // 4
     half = nl // 2
     parts = ((fs, pj_s, ns, 0, ns, nl), (fl, pj_l, nl, 0, half, 0), (fl, pj_l, nl, half, half, half))
@@ -1093,6 +1094,8 @@
     for k in range(3):
         chip[k].wait_recv()
         over[k].start()
+        if k == 2:
+            after_chip()
         compute(k, me ^ 1)
     for k in range(3):
         over[k].wait_recv()
@@ -1100,7 +1103,7 @@
     return chip + core + over
 
 
-def attend_part(net, sems, xl, xs, att, ol, os, lsel, lses, cl, cs, land):
+def attend_part(net, sems, xl, xs, att, ol, os, lsel, lses, cl, cs, land, hooks):
     nl, ns = xl.shape[0] // 4, xs.shape[0] // 4
     w = ol.shape[1]
     base = sems.used
@@ -1139,6 +1142,8 @@
         def done(b):
             for m in range(b * BR // n, (b + 1) * BR // n):
                 start(k, m)
+            if k == 0 and b in hooks:
+                hooks[b]()
 
         return done
 
@@ -1177,7 +1182,10 @@
     def __init__(self, net, sems, s, so, land, oland, own=None):
         self.own = s.at[0] if own is None else own
         self.net, self.s, self.so, self.land, self.oland = net, s, so, land, oland
-        self.main = Batch([sems.copy(s.at[r], land.at[3 - r], net.line(r)) for r in (1, 2, 3)])
+        self.main = [
+            Batch([sems.copy(s.at[r, i], land.at[3 - r, i], net.line(r)) for r in (1, 2, 3)])
+            for i in range(land.shape[1])
+        ]
         self.out = []
         for r in (1, 2, 3):
             to = (net.z + r) % 4
@@ -1186,12 +1194,17 @@
         self.owner = net.zh == net.c
 
     def start(self):
-        self.main.start()
+        for part in self.main:
+            part.start()
+        self.start_rest()
+
+    def start_rest(self):
         for copy, use in self.out:
             pl.when(use)(copy.start)
 
     def finish(self, f_out, fo_out):
-        self.main.recv()
+        for part in self.main:
+            part.recv()
         f_out[...] = (
             self.own[...].astype(jnp.float32)
             + self.land[0].astype(jnp.float32)
@@ -1214,7 +1227,8 @@
         def _():
             fo_out[...] = jnp.zeros_like(fo_out)
 
-        self.main.sent()
+        for part in self.main:
+            part.sent()
         for copy, use in self.out:
             pl.when(use)(copy.wait_send)
 
@@ -1344,13 +1358,24 @@
         loc.start(R.w_up.at[layer, :, pl.ds(aligned(net.c * f, 128), f)], R.wup.at[:, pl.ds(0, f)]),
         loc.start(R.w_down.at[layer, pl.ds(aligned(net.c * f), f)], R.wdn.at[0]),
     ]
+    hooks = {}
+    if first:
+
+        def after_chip():
+            proj.start()
+            later.start(0)
+
+        def second():
+            later.recv(0)
+            later.start(1)
+
+        hooks = {1: second}
+    else:
+        after_chip = moved.start
     pending = project_part(
-        net, sems, R.resid, R.gain1, R.shift1, R.ext, R.bias, R.fl, R.fs, R.pj_l, R.pj_s
+        net, sems, R.resid, R.gain1, R.shift1, R.ext, R.bias, R.fl, R.fs, R.pj_l, R.pj_s, after_chip
     )
-    if first:
-        proj.start()
-    else:
-        moved.start()
+    if not first:
 
         @pl.when(jnp.logical_not(net.moves))
         def _():
@@ -1363,21 +1388,19 @@
     R.wup[pl.ds(aligned(net.yx * rows), rows), f:] = R.zup[...]
     for k in range(3):
         R.wdn[k + 1, pl.ds(aligned(net.yx * part), part)] = R.zdn[k]
-    if first:
-        later.start(0)
     attend_part(
-        net, sems, R.pj_l, R.pj_s, R.att, R.ol, R.os, R.lsel, R.lses, R.cl, R.cs, R.land
+        net, sems, R.pj_l, R.pj_s, R.att, R.ol, R.os, R.lsel, R.lses, R.cl, R.cs, R.land, hooks
     )
     if first:
-        later.recv(0)
-        later.start(1)
+        later.recv(1)
+        later.start(2)
         proj.forward()
     share = jnp.zeros((1, 1), jnp.float32)
     for carry in (R.cl, R.cs):
         size = carry.shape[1]
         left = (size - 1 - lax.broadcasted_iota(jnp.int32, (1, size), 1)).astype(jnp.float32)
         ratio = carry[size // BR : size // BR + 1] / jnp.maximum(left, 1.0)
-        t = 4.0 * (ratio - R.limit[:1, :1])
+        t = 4.0 * (ratio - R.limit[...])
         share = share + jnp.sum(1.0 / (1.0 + jnp.exp(-t)), axis=1, keepdims=True)
     R.share[...] = jnp.broadcast_to(share * 0.25, R.share.shape)
     half = n // 2
@@ -1411,9 +1434,6 @@
     quarter = n // 2
     for i in range(2):
         hidden(slice(i * quarter, (i + 1) * quarter))
-    if first:
-        later.recv(1)
-        later.start(2)
     there.wait_recv()
     for i in range(2):
         hidden(slice(n + i * quarter, n + (i + 1) * quarter))
@@ -1452,6 +1472,7 @@
     nl, ns = R.pj_l.shape[0] // 4, R.pj_s.shape[0] // 4
     wid = R.ol.shape[1]
     me, yx = net.me, net.yx
+    chunk = d // 4
     there = sems.copy(R.gm.at[pl.ds(0, n)], R.gm.at[pl.ds(n, n)], net.group(2))
     back = sems.copy(R.out.at[0], R.got.at[0], net.group(2))
     cross = sems.copy(R.oself, R.olands, net.group(2))
@@ -1462,7 +1483,13 @@
     sems.used += 8
     peers = [net.group(d_) for d_ in (1, 2, 3)] + [net.plane(e) for e in (1, 2, 3)]
     if last:
-        moved = Batch([sems.copy(R.y, R.yr, net.partner())], net.moves)
+        moved = Batch(
+            [
+                sems.copy(R.y.at[pl.ds(0, nl)], R.yr_l, net.partner()),
+                sems.copy(R.y.at[pl.ds(nl, ns)], R.yr_s, net.partner()),
+            ],
+            net.moves,
+        )
         peers += [net.partner()]
     else:
         carry = FinishLine(net, sems, R.s_in, R.so_in, R.fland, R.foland, R.s_own)
@@ -1481,11 +1508,11 @@
 
         @pl.when(jnp.logical_not(net.moves))
         def _():
-            R.yr[...] = R.y[...]
+            R.yr_l[...] = R.y[:nl]
+            R.yr_s[...] = R.y[nl:]
 
     else:
-        ext.start()
-        carry.start()
+        carry.main[0].start()
         for src, dst in ((R.s_in.at[0], R.s_own), (R.dq_in.at[yx], R.dq_own), (R.d0_in.at[yx], R.d0_own)):
             loc.start(src, dst)
     R.rows[...] = jnp.zeros_like(R.rows)
@@ -1497,9 +1524,22 @@
         u = mm(R.gm[at], wdn2(), NT)
         R.gu[at] = (u * R.slope[at].astype(f32)).astype(bf)
 
-    for i in range(2):
-        hidden(slice(i * half, (i + 1) * half))
+    hidden(slice(0, half))
     there.wait_recv()
+    for c in fetched:
+        c.wait()
+    for k in range(4):
+        for i in range(2):
+            t = mm(R.gm[:, k * chunk : (k + 1) * chunk], R.buf[i * 2 * n : (i + 1) * 2 * n], TN)
+            t = t.astype(bf)
+            R.ddn[k, 2 * i] = t[:, :f]
+            R.ddn[k, 2 * i + 1] = t[:, f:]
+    big_dn.start()
+    if not last:
+        ext.start()
+    fl, fs = R.buf.at[pl.ds(0, 4 * nl)], R.buf.at[pl.ds(4 * nl, 4 * ns)]
+    late = [loc.start(R.fl_i, fl), loc.start(R.fs_i, fs)]
+    hidden(slice(half, n))
     for i in range(2):
         hidden(slice(n + i * half, n + (i + 1) * half))
     for i in range(2):
@@ -1509,19 +1549,7 @@
     back.start()
     for i in range(2):
         R.mine[i * half : (i + 1) * half] = mm(R.gu[i * half : (i + 1) * half], R.wup[...], NT)
-    chunk = d // 4
-
-    for c in fetched:
-        c.wait()
-    for k in range(4):
-        for i in range(2):
-            t = mm(R.gm[:, k * chunk : (k + 1) * chunk], R.buf[i * 2 * n : (i + 1) * 2 * n], TN)
-            t = t.astype(bf)
-            R.ddn[k, 2 * i] = t[:, :f]
-            R.ddn[k, 2 * i + 1] = t[:, f:]
-    big_dn.start()
-    fl, fs = R.buf.at[pl.ds(0, 4 * nl)], R.buf.at[pl.ds(4 * nl, 4 * ns)]
-    late = [loc.start(R.fl_i, fl), loc.start(R.fs_i, fs)]
+
     back.wait_recv()
     gn = R.mine[...] + R.got[0].astype(f32)
     hat, inv = norm_rows(R.middle[...])
@@ -1598,6 +1626,19 @@
     for c in loc.copies:
         if id(c) not in done:
             c.wait()
+    def add_up(own, land, i):
+        for r in range(4):
+            t = own[yx, r].astype(f32)
+            for k in range(3):
+                t = t + land[k, r].astype(f32)
+            R.s[r, i] = t.astype(bf)
+
+    def midway(b):
+        if b == 2 and not last:
+            big_dn.recv()
+            add_up(R.ddn, R.rdn, 1)
+            low.start()
+
     for k in (1, 0):
         for m in range(4):
 
@@ -1606,6 +1647,9 @@
                 arrived(k, m).wait_recv()
 
         if k:
+            if not last:
+                carry.main[1].start()
+                carry.start_rest()
             bwd_one(R.pj_s, R.gs, R.os, R.lses, R.cs, R.ds, R.acc, R.kt)
             if not last:
                 ext.recv()
@@ -1616,19 +1660,8 @@
                     dst[...] = t.astype(bf)
                 ext_line.start()
         else:
-            bwd_one(R.pj_l, R.gl, R.ol, R.lsel, R.cl, R.dl, R.acc, R.kt)
-
-    def add_up(own, land, i):
-        for r in range(4):
-            t = own[yx, r].astype(f32)
-            for k in range(3):
-                t = t + land[k, r].astype(f32)
-            R.s[r, i] = t.astype(bf)
-
-    big_dn.recv()
-    add_up(R.ddn, R.rdn, 1)
-    if not last:
-        low.start()
+            bwd_one(R.pj_l, R.gl, R.ol, R.lsel, R.cl, R.dl, R.acc, R.kt, midway)
+
 
     def partial(m):
         a = mm(R.dl[pl.ds(aligned(m * nl), nl)], R.ext[...], NT)
@@ -1693,6 +1726,9 @@
         R.dn_out[...] = t.astype(bf)
         low.sent()
 
+    if last:
+        big_dn.recv()
+        add_up(R.ddn, R.rdn, 1)
     big_up.recv()
     add_up(R.dup, R.rup, 0)
     big_out.recv()
@@ -1749,7 +1785,7 @@
     line = FinishLine(net, sems, R.s.at[:, pl.ds(0, 1)], R.so, R.land, R.oland)
     ext = Batch(ext_scatter(net, sems, R.dq, R.qland) + ext_scatter(net, sems, R.d0, R.zland))
     nv = len(axes)
-    rounds = [{ax: 1 - lax.axis_index(ax)} for ax in axes]
+    rounds = [{ax: 1 - lax.axis_index(ax)} for ax in axes[::-1]]
     steps = [sems.copy(R.vland.at[i], R.vland.at[nv + 1 + i], peer) for i, peer in enumerate(rounds)]
     ext_line = ExtLine(net, sems, R.q_sum, R.z_sum, R.qline, R.zline)
     qrecv = jnp.logical_not(net.moves)
@@ -1767,7 +1803,6 @@
     )
     ext.start()
     line.start()
-    moved.start()
     nr = R.rows0.shape[0]
     R.vland[0, :nr] = R.rows0[...]
     R.vland[0, nr:] = R.rows1[...]
@@ -1791,6 +1826,7 @@
             t = t + lands[e].astype(f32)
         dst[...] = t.astype(bf)
     ext_line.start()
+    moved.start()
     step(2)
     step(3)
     step(4)
@@ -1804,13 +1840,19 @@
         R.dx_l[...] = R.dx[:nl].astype(f32)
         R.dx_s[...] = R.dx[nl:].astype(f32)
 
+    wq = R.gqkv.shape[3]
+
+    def put(l, v):
+        for i in range(3):
+            R.gqkv[l, i] = v[:, i * wq : (i + 1) * wq]
+
     ext_line.finish(R.q0, R.z0)
 
     @pl.when(qrecv)
     def _():
         for l, q in ((0, R.q0), (1, R.q1)):
             R.qself[l] = q[theirs].astype(bf)
-            R.gqkv[l] = q[ours].astype(f32)
+            put(l, q[ours].astype(f32))
 
     tot = R.vland.at[nv]
     for l in range(2):
@@ -1822,7 +1864,7 @@
         R.g_bout[l : l + 1] = tot[at + 4 : at + 5]
         R.g_bdown[l : l + 1] = tot[at + 5 : at + 6]
         R.g_bup[l : l + 1] = tot[pl.ds(at + 16 + net.z, 1)]
-        R.shares[l : l + 1] = tot[at + 6 : at + 7, :128]
+        R.shares[l : l + 1] = tot[at + 6 : at + 7, :128] / (32 * R.dx.shape[0])
     line.finish(R.f0, R.fo0)
 
     @pl.when(qrecv)
@@ -1846,7 +1888,7 @@
         def _():
             for l, fs in ((0, (R.f0.at[0], R.dn0)), (1, (R.f1.at[0], R.f1.at[1]))):
                 R.gup[l, :, c * n : (c + 1) * n] = fs[0][ours].astype(f32)
-                R.gdn[l, c * n : (c + 1) * n] = jnp.transpose(fs[1][ours].astype(f32))
+                R.gdn[l, :, c * n : (c + 1) * n] = fs[1][ours].astype(f32)
 
     cross.recv()
     for c in range(2):
@@ -1855,14 +1897,14 @@
         def _():
             for l in range(2):
                 R.gup[l, :, c * n : (c + 1) * n] = R.fland[l, 0].astype(f32)
-                R.gdn[l, c * n : (c + 1) * n] = jnp.transpose(R.fland[l, 1].astype(f32))
+                R.gdn[l, :, c * n : (c + 1) * n] = R.fland[l, 1].astype(f32)
 
     @pl.when(net.moves)
     def _():
         for c in owned.copies:
             c.wait_recv()
-        R.gqkv[...] = R.qlands[...].astype(f32)
         for l in range(2):
+            put(l, R.qlands[l].astype(f32))
             R.gout[l] = jnp.transpose(R.olands[l].astype(f32))
 
     @pl.when(net.z == 0)
@@ -1870,8 +1912,8 @@
         wid = R.gout.shape[1]
         for l, z in ((0, R.z0), (1, R.z1)):
             t = z[ours].astype(f32) + R.zlands[l].astype(f32)
-            R.gqkv[l, :, :HD] += t[:, :HD]
-            R.gqkv[l, :, wid : wid + HD] += t[:, HD:]
+            R.gqkv[l, 0, :, :HD] += t[:, :HD]
+            R.gqkv[l, 1, :, :HD] += t[:, HD:]
 
     moved.recv()
 
@@ -1888,17 +1930,22 @@
 
 def results_k(*refs):
     k = len(refs) // 2
-    for src, dst in zip(refs[:k], refs[k:]):
-        dst[...] = src[...]
+    sem = refs[-1]
+    copies = [pltpu.make_async_copy(refs[i], refs[k + i], sem.at[i]) for i in range(k)]
+    for copy in copies:
+        copy.start()
+    for copy in copies:
+        copy.wait()
 
 
 def results(arrays):
     return pl.pallas_call(
         results_k,
         out_shape=tuple(jax.ShapeDtypeStruct(a.shape, a.dtype) for a in arrays),
-        in_specs=[VMEM] * len(arrays),
+        in_specs=[ANY] * len(arrays),
         out_specs=(VMEM,) * len(arrays),
-        compiler_params=pltpu.CompilerParams(vmem_limit_bytes=40 * 1024 * 1024),
+        scratch_shapes=[DMA((len(arrays),))],
+        compiler_params=pltpu.CompilerParams(vmem_limit_bytes=60 * 1024 * 1024),
         name="results_k",
     )(*arrays)
 
@@ -1979,7 +2026,7 @@
     bias = jnp.concatenate([my_bqv[:, 0], none, my_bqv[:, 1], zero_bq, none[:, :HD]], axis=1)
     gain, shift = ln_gain.astype(f32), ln_bias.astype(f32)
     bo, bd = b_out.astype(f32), b_down.astype(f32)
-    limits = jnp.broadcast_to((threshold.astype(f32) / 64.0)[:, None, None], (layers, 8, 128))
+    limits = (threshold.astype(f32) / 64.0)[:, None]
 
     resid, zup, zdn = P0.xr, P0.zup, P0.zdn
     exts = [P0.ext]
@@ -1989,7 +2036,7 @@
         ins = dict(
             resid=(resid, 1), gain1=(gain[l, :1], 1), shift1=(shift[l, :1], 1), gain2=(gain[l, 1:], 1), shift2=(shift[l, 1:], 1),
             ext=(exts[l], 1), bias=(bias[l : l + 1], 1), w_up=(w_up, 0), w_down=(w_down, 0), zup=(zup, 1), zdn=(zdn, 1),
-            wout=(wo[l], 1), bout=(bo[l : l + 1], 1), bup=(rel_bup[l : l + 1], 1), bdown=(bd[l : l + 1], 1), limit=(limits[l], 1),
+            wout=(wo[l], 1), bout=(bo[l : l + 1], 1), bup=(rel_bup[l : l + 1], 1), bdown=(bd[l : l + 1], 1), limit=(limits[l : l + 1], 1),
         )
         outs = dict(
             fl_o=((sl, d), bf, 0), fs_o=((ss, d), bf, 0), pjl_o=((sl, nx), bf, 0), pjs_o=((ss, nx), bf, 0),
@@ -2046,7 +2093,7 @@
         )
         if last:
             ins.update(y=(A.y, 1))
-            outs.update(yr=((n, d), bf, 1))
+            outs.update(yr_l=((rl, d), bf, 1), yr_s=((rs, d), bf, 1))
         else:
             ins.update(s_in=(B.s, 0), so_in=(B.so, 1), dq_in=(B.dq, 0), d0_in=(B.d0, 0))
             outs.update(
@@ -2059,7 +2106,7 @@
         back[l] = B
         g = B.g_new
         if last:
-            y = B.yr
+            y_l, y_s = B.yr_l, B.yr_s
 
     nv = len(axes)
     T = run(
@@ -2070,7 +2117,7 @@
             rows0=(back[0].rows, 1), dn0=(B.dn_out, 1), rows1=(back[1].rows, 1), share0=(saved[0].share, 1), share1=(saved[1].share, 1), dx=(g, 1),
         ),
         dict(
-            gup=((2, half, ffq), f32, 1), gdn=((2, ffq, half), f32, 1), gout=((2, wid, half), f32, 1), gqkv=((2, half, nq), f32, 1),
+            gup=((2, half, ffq), f32, 1), gdn=((2, half, ffq), f32, 1), gout=((2, wid, half), f32, 1), gqkv=((2, 3, half, wid), f32, 1),
             dx_l=((rl, d), f32, 1), dx_s=((rs, d), f32, 1), g_gain=((2, 2, d), f32, 1), g_bias=((2, 2, d), f32, 1),
             g_bqv=((2, 2, wid), f32, 1), g_bout=((2, d), f32, 1), g_bdown=((2, d), f32, 1), g_bup=((2, ffq), f32, 1),
             shares=((2, 128), f32, 1),
@@ -2088,13 +2135,13 @@
     )
     done = results(
         (
-            T.dx_l, T.dx_s, T.g_gain, T.g_bias, T.g_bqv, T.gout, T.g_bout, T.gup, T.g_bup, T.gdn, T.g_bdown
+            y_l, y_s, T.dx_l, T.dx_s, T.g_gain, T.g_bias, T.gqkv, T.g_bqv, T.gout, T.g_bout, T.gup, T.g_bup, T.gdn, T.g_bdown
         )
     )
-    dx_l, dx_s, g_gain, g_bias, g_bqv, gout, g_bout, gup, g_bup, gdn, g_bdown = done
+    y_l, y_s, dx_l, dx_s, g_gain, g_bias, gqkv, g_bqv, gout, g_bout, gup, g_bup, gdn, g_bdown = done
     return (
-        y[None, :rl], y[None, rl:], dx_l[None], dx_s[None], g_gain, g_bias, T.gqkv.reshape(layers, half, 3, wid),
-        g_bqv, gout, g_bout, gup, g_bup, gdn, g_bdown, T.shares[:, 0] / (8 * 4 * n),
+        y_l[None], y_s[None], dx_l[None], dx_s[None], g_gain, g_bias, jnp.swapaxes(gqkv, 1, 2), g_bqv, gout, g_bout, gup, g_bup,
+        jnp.swapaxes(gdn, 1, 2), g_bdown, T.shares[:, 0],
     )
 
 

time: 455 us -> 434 us (0.954)
  local copies, waits for them, and re-layouts: 31.9 us -> 15.4 us
    unnamed x40 -> x14, local copies, waits for them, and re-layouts: 13.6 us -> 2.03 us
    broadcast_in_dim x4 -> x0, local copies, waits for them, and re-layouts: 5.9 us -> none  [the longest x2 2.52 us: fast_body(): jnp.broadcast_to((threshold.astype(f32) / 64.0)[:, None, None], (layers,...]
    pallas_call x6, Pallas kernels: 393 us -> 387 us  [run(): pl.pallas_call(body_of, out_shape=tuple((jax.ShapeDtypeStruct(tuple(s), t...]
where the time goes in v6:
time: 434 us; the launch traced here: 426 us
  Pallas kernels  391 us (90%)
  local copies, waits for them, and re-layouts  15.4 us (4%)
  between operations  14.5 us (3%)
    pallas_call x6, Pallas kernels, run(): pl.pallas_call(body_of, out_shape=tuple((jax.ShapeDtypeStruct(tuple(s), t...  387 us
  transfers between devices with their start and end apart: 2, of which 1 were waited for; matrix products, arithmetic and copies ran while one was open for 3% of the time, Pallas kernels for 27%

profile of v6, /device:TPU:1, one launch (start us, length us, event | category | flops | bytes accessed | tf_op | source)
XLA Modules:
  0.0 425.6 jit_solution(17682695665626300292)
XLA Ops:
  7.2 0.0 all-gather.5.cloned.1.call-start
  7.2 1.4 constant_dynamic-slice_fusion.2
  8.7 0.0 all-gather.5.cloned.1.call-update
  8.7 0.0 all-gather.7.cloned.1.call-start
  8.7 0.7 all-gather.7.cloned.1.call-update
  9.5 0.8 reshape.61
  10.3 0.7 reshape.60
  11.0 0.6 reshape.62.refs_4_
  11.6 1.7 slice_bitcast_fusion.12
  13.3 0.8 copy.42.refs_3_
  14.1 1.3 copy.41.refs_2_
  15.4 0.0 copy-start.2
  15.4 0.0 copy-start.3
  15.4 49.2 %first_x.1 = (bf16[384,768]{1,0:T(8,128)(2,1)}, bf16[768,704]{1,0:T(8,128)(2,1)}, bf16[4,16,256]{2,1,0:T(8,128)(2,1)}, bf16[192,1152]{1,0:T(8,128)(2,1)}, bf16[3,96,768]{2,1,0:T(8,128)(2,1)}) custom-call(bf16[256,768]{1,0:T(8,128)(2,1)} %bitcast.65, bf16[128,768]{1,0:T(8,128)(2,1)} %bitcast.66, bf16[768,576]{1,0:T(8,128)(2,1)} %copy.41.refs_2_, ...), custom_call_target="tpu_custom_call" | custom-call | flops 1000000000 | bytes 10000000 | tf_op jit(solution)/shard_map/first_x/pallas_call | solution.py:1959
  64.6 0.0 copy-start.4
  64.6 0.0 copy-start
  64.6 0.0 copy-start.1
  64.6 0.8 copy.47
  65.5 0.0 copy-done.2
  65.5 0.0 copy-done.3
  65.5 0.8 copy.46.refs_17_
  66.4 1.3 copy.45.refs_16_
  67.8 0.6 copy.49
  68.4 0.1 reshape.65
  68.5 0.6 copy.48
  69.1 0.1 concatenate.7
  69.2 0.0 copy-done.4
  69.2 0.6 fusion.6
  69.8 0.6 fusion.3
  70.4 0.0 copy-done
  70.4 0.0 copy-done.1
  70.4 0.6 fusion.4
  71.0 0.6 slice_bitcast_fusion.2
  71.6 3.5 all-gather.5.cloned.1.call-done
  75.2 65.8 %forward_x.2 = (bf16[1024,768]{1,0:T(8,128)(2,1)}, bf16[512,768]{1,0:T(8,128)(2,1)}, bf16[1024,704]{1,0:T(8,128)(2,1)}, bf16[512,704]{1,0:T(8,128)(2,1)}, bf16[3...) custom-call(bf16[384,768]{1,0:T(8,128)(2,1)} %get-tuple-element.108., ...), custom_call_target="tpu_custom_call" | custom-call | flops 10000000000 | bytes 10000000 | tf_op jit(solution)/shard_map/forward_x/pallas_call | solution.py:1959
  140.9 0.0 all-gather.7.cloned.1.call-done
  141.0 55.4 %forward_x.3 = (bf16[1024,768]{1,0:T(8,128)(2,1)}, bf16[512,768]{1,0:T(8,128)(2,1)}, bf16[1024,704]{1,0:T(8,128)(2,1)}, bf16[512,704]{1,0:T(8,128)(2,1)}, bf16[3...) custom-call(f32[384,768]{1,0:T(8,128)} %get-tuple-element.113.refs_0, ...), custom_call_target="tpu_custom_call" | custom-call | flops 10000000000 | bytes 10000000 | tf_op jit(solution)/shard_map/forward_x/pallas_call | solution.py:1959
  196.4 72.5 %backward_x.2 = (f32[384,768]{1,0:T(8,128)}, f32[24,768]{1,0:T(8,128)}, bf16[4,192,576]{2,1,0:T(8,128)(2,1)}, bf16[4,192,128]{2,1,0:T(8,128)(2,1)}, bf16[4,2,192...) custom-call(bf16[384,768]{1,0:T(8,128)(2,1)} %get-tuple-element.117.re, ...), custom_call_target="tpu_custom_call" | custom-call | flops 20000000000 | bytes 10000000 | tf_op jit(solution)/shard_map/backward_x/pallas_call | solution.py:1959
  268.9 89.4 %backward_x.3 = (bf16[384,768]{1,0:T(8,128)(2,1)}, f32[24,768]{1,0:T(8,128)}, bf16[4,192,576]{2,1,0:T(8,128)(2,1)}, bf16[4,192,128]{2,1,0:T(8,128)(2,1)}, bf16[4...) custom-call(f32[384,768]{1,0:T(8,128)} %get-tuple-element.138.refs_0, ...), custom_call_target="tpu_custom_call" | custom-call | flops 20000000000 | bytes 10000000 | tf_op jit(solution)/shard_map/backward_x/pallas_call | solution.py:1959
  358.3 54.8 %tail_x.1 = (f32[2,96,768]{2,1,0:T(8,128)}, f32[2,96,768]{2,1,0:T(8,128)}, f32[2,192,96]{2,1,0:T(8,128)}, f32[2,3,96,192]{3,2,1,0:T(8,128)}, f32[256,768]{1,0:T(...) custom-call(bf16[4,2,192,384]{3,2,1,0:T(8,128)(2,1)} %get-tuple-elem, ...), custom_call_target="tpu_custom_call" | custom-call | flops 1000000000 | bytes 10000000 | tf_op jit(solution)/shard_map/tail_x/pallas_call | solution.py:1959
  413.2 1.3 slice_reduce_fusion
  414.4 4.1 results_k.1
  (18 shorter events, 0.1 us)
Async XLA Ops:
  7.2 68.0 %all-gather.5.cloned.1.call-start = ((), (), s32[]{:S(2)}) async-start(), calls=%async_computation | async-start | bytes 1216512 | tf_op jit(solution)/shard_map/all_gather | solution.py:2001
  8.7 132.3 %all-gather.7.cloned.1.call-start = ((), (), s32[]{:S(2)}) async-start(), calls=%async_computation.1 | async-start | bytes 1216512 | tf_op jit(solution)/shard_map/all_gather | solution.py:2001
  15.4 50.0 %copy-start.2 = (bf16[2,2,768]{2,1,0:T(2,128)(2,1)S(1)}, bf16[2,2,768]{2,1,0:T(2,128)(2,1)}, u32[]{:S(2)}) copy-start(bf16[2,2,768]{2,1,0:T(2,128)(2,1)} %param.19) | copy-start | bytes 18436
  15.4 50.1 %copy-start.3 = (bf16[2,2,768]{2,1,0:T(2,128)(2,1)S(1)}, bf16[2,2,768]{2,1,0:T(2,128)(2,1)}, u32[]{:S(2)}) copy-start(bf16[2,2,768]{2,1,0:T(2,128)(2,1)} %param.20) | copy-start | bytes 18436
  64.6 4.6 %copy-start.4 = (s32[2]{0:T(128)S(1)}, s32[2]{0:T(128)}, u32[]{:S(2)}) copy-start(s32[2]{0:T(128)} %param.29) | copy-start | bytes 28
  64.6 5.8 %copy-start = (bf16[2,768]{1,0:T(2,128)(2,1)S(1)}, bf16[2,768]{1,0:T(2,128)(2,1)}, u32[]{:S(2)}) copy-start(bf16[2,768]{1,0:T(2,128)(2,1)} %param.28) | copy-start | bytes 9220
  64.6 5.8 %copy-start.1 = (bf16[2,768]{1,0:T(2,128)(2,1)S(1)}, bf16[2,768]{1,0:T(2,128)(2,1)}, u32[]{:S(2)}) copy-start(bf16[2,768]{1,0:T(2,128)(2,1)} %param.24) | copy-start | bytes 9220
Sparse Core Ops, SparseCore 0:
  11.5 63.6 all-gather.4
  78.6 56.1 all-gather.6

commit v7 on v6

--- a/solution.py
+++ b/solution.py
@@ -1512,7 +1512,8 @@
             R.yr_s[...] = R.y[nl:]
 
     else:
-        carry.main[0].start()
+        ext.start()
+        carry.start()
         for src, dst in ((R.s_in.at[0], R.s_own), (R.dq_in.at[yx], R.dq_own), (R.d0_in.at[yx], R.d0_own)):
             loc.start(src, dst)
     R.rows[...] = jnp.zeros_like(R.rows)
@@ -1535,8 +1536,6 @@
             R.ddn[k, 2 * i] = t[:, :f]
             R.ddn[k, 2 * i + 1] = t[:, f:]
     big_dn.start()
-    if not last:
-        ext.start()
     fl, fs = R.buf.at[pl.ds(0, 4 * nl)], R.buf.at[pl.ds(4 * nl, 4 * ns)]
     late = [loc.start(R.fl_i, fl), loc.start(R.fs_i, fs)]
     hidden(slice(half, n))
@@ -1647,9 +1646,6 @@
                 arrived(k, m).wait_recv()
 
         if k:
-            if not last:
-                carry.main[1].start()
-                carry.start_rest()
             bwd_one(R.pj_s, R.gs, R.os, R.lses, R.cs, R.ds, R.acc, R.kt)
             if not last:
                 ext.recv()

time: 434 us -> 424 us (0.977)
  Pallas kernels: 391 us -> 382 us
    pallas_call x6, Pallas kernels: 387 us -> 378 us  [run(): pl.pallas_call(body_of, out_shape=tuple((jax.ShapeDtypeStruct(tuple(s), t...]
  transfers between devices with their start and end apart: 2 -> 2, of which waited for: 1 -> 1; matrix products, arithmetic and copies ran while one was open for 3% -> 3% of each run, Pallas kernels for 27% -> 28%
where the time goes in v7:
time: 424 us; the launch traced here: 416 us
  Pallas kernels  382 us (90%)
  local copies, waits for them, and re-layouts  15.4 us (4%)
  between operations  14.5 us (3%)
  waiting for transfers between devices  4.28 us (1%)
    pallas_call x6, Pallas kernels, run(): pl.pallas_call(body_of, out_shape=tuple((jax.ShapeDtypeStruct(tuple(s), t...  378 us
  transfers between devices with their start and end apart: 2, of which 1 were waited for; matrix products, arithmetic and copies ran while one was open for 3% of the time, Pallas kernels for 28%

profile of v7, /device:TPU:1, one launch (start us, length us, event | category | flops | bytes accessed | tf_op | source)
XLA Modules:
  0.0 416.1 jit_solution(1133141261814492766)
XLA Ops:
  7.2 0.0 all-gather.5.cloned.1.call-start
  7.2 1.4 constant_dynamic-slice_fusion.2
  8.7 0.0 all-gather.5.cloned.1.call-update
  8.7 0.0 all-gather.7.cloned.1.call-start
  8.7 0.7 all-gather.7.cloned.1.call-update
  9.5 0.8 reshape.61
  10.3 0.7 reshape.60
  11.0 0.6 reshape.62.refs_4_
  11.6 1.7 slice_bitcast_fusion.12
  13.3 0.8 copy.42.refs_3_
  14.1 1.3 copy.41.refs_2_
  15.4 0.0 copy-start.2
  15.4 0.0 copy-start.3
  15.4 49.2 %first_x.1 = (bf16[384,768]{1,0:T(8,128)(2,1)}, bf16[768,704]{1,0:T(8,128)(2,1)}, bf16[4,16,256]{2,1,0:T(8,128)(2,1)}, bf16[192,1152]{1,0:T(8,128)(2,1)}, bf16[3,96,768]{2,1,0:T(8,128)(2,1)}) custom-call(bf16[256,768]{1,0:T(8,128)(2,1)} %bitcast.65, bf16[128,768]{1,0:T(8,128)(2,1)} %bitcast.66, bf16[768,576]{1,0:T(8,128)(2,1)} %copy.41.refs_2_, ...), custom_call_target="tpu_custom_call" | custom-call | flops 1000000000 | bytes 10000000 | tf_op jit(solution)/shard_map/first_x/pallas_call | solution.py:1955
  64.6 0.0 copy-start.4
  64.6 0.0 copy-start
  64.6 0.0 copy-start.1
  64.6 0.8 copy.47
  65.5 0.0 copy-done.2
  65.5 0.0 copy-done.3
  65.5 0.8 copy.46.refs_17_
  66.4 1.3 copy.45.refs_16_
  67.8 0.6 copy.49
  68.4 0.1 reshape.65
  68.5 0.6 copy.48
  69.1 0.1 concatenate.7
  69.2 0.0 copy-done.4
  69.2 0.6 fusion.6
  69.8 0.6 fusion.3
  70.4 0.0 copy-done
  70.4 0.0 copy-done.1
  70.4 0.6 fusion.4
  71.0 0.6 slice_bitcast_fusion.2
  71.6 3.5 all-gather.5.cloned.1.call-done
  75.2 65.8 %forward_x.2 = (bf16[1024,768]{1,0:T(8,128)(2,1)}, bf16[512,768]{1,0:T(8,128)(2,1)}, bf16[1024,704]{1,0:T(8,128)(2,1)}, bf16[512,704]{1,0:T(8,128)(2,1)}, bf16[3...) custom-call(bf16[384,768]{1,0:T(8,128)(2,1)} %get-tuple-element.108., ...), custom_call_target="tpu_custom_call" | custom-call | flops 10000000000 | bytes 10000000 | tf_op jit(solution)/shard_map/forward_x/pallas_call | solution.py:1955
  140.9 0.0 all-gather.7.cloned.1.call-done
  141.0 55.4 %forward_x.3 = (bf16[1024,768]{1,0:T(8,128)(2,1)}, bf16[512,768]{1,0:T(8,128)(2,1)}, bf16[1024,704]{1,0:T(8,128)(2,1)}, bf16[512,704]{1,0:T(8,128)(2,1)}, bf16[3...) custom-call(f32[384,768]{1,0:T(8,128)} %get-tuple-element.113.refs_0, ...), custom_call_target="tpu_custom_call" | custom-call | flops 10000000000 | bytes 10000000 | tf_op jit(solution)/shard_map/forward_x/pallas_call | solution.py:1955
  196.4 72.5 %backward_x.2 = (f32[384,768]{1,0:T(8,128)}, f32[24,768]{1,0:T(8,128)}, bf16[4,192,576]{2,1,0:T(8,128)(2,1)}, bf16[4,192,128]{2,1,0:T(8,128)(2,1)}, bf16[4,2,192...) custom-call(bf16[384,768]{1,0:T(8,128)(2,1)} %get-tuple-element.117.re, ...), custom_call_target="tpu_custom_call" | custom-call | flops 20000000000 | bytes 10000000 | tf_op jit(solution)/shard_map/backward_x/pallas_call | solution.py:1955
  268.9 80.7 %backward_x.3 = (bf16[384,768]{1,0:T(8,128)(2,1)}, f32[24,768]{1,0:T(8,128)}, bf16[4,192,576]{2,1,0:T(8,128)(2,1)}, bf16[4,192,128]{2,1,0:T(8,128)(2,1)}, bf16[4...) custom-call(f32[384,768]{1,0:T(8,128)} %get-tuple-element.138.refs_0, ...), custom_call_target="tpu_custom_call" | custom-call | flops 20000000000 | bytes 10000000 | tf_op jit(solution)/shard_map/backward_x/pallas_call | solution.py:1955
  349.6 54.1 %tail_x.1 = (f32[2,96,768]{2,1,0:T(8,128)}, f32[2,96,768]{2,1,0:T(8,128)}, f32[2,192,96]{2,1,0:T(8,128)}, f32[2,3,96,192]{3,2,1,0:T(8,128)}, f32[256,768]{1,0:T(...) custom-call(bf16[4,2,192,384]{3,2,1,0:T(8,128)(2,1)} %get-tuple-elem, ...), custom_call_target="tpu_custom_call" | custom-call | flops 1000000000 | bytes 10000000 | tf_op jit(solution)/shard_map/tail_x/pallas_call | solution.py:1955
  403.7 1.3 slice_reduce_fusion
  404.9 4.1 results_k.1
  (18 shorter events, 0.1 us)
Async XLA Ops:
  7.2 68.0 %all-gather.5.cloned.1.call-start = ((), (), s32[]{:S(2)}) async-start(), calls=%async_computation | async-start | bytes 1216512 | tf_op jit(solution)/shard_map/all_gather | solution.py:1997
  8.7 132.3 %all-gather.7.cloned.1.call-start = ((), (), s32[]{:S(2)}) async-start(), calls=%async_computation.1 | async-start | bytes 1216512 | tf_op jit(solution)/shard_map/all_gather | solution.py:1997
  15.4 50.0 %copy-start.2 = (bf16[2,2,768]{2,1,0:T(2,128)(2,1)S(1)}, bf16[2,2,768]{2,1,0:T(2,128)(2,1)}, u32[]{:S(2)}) copy-start(bf16[2,2,768]{2,1,0:T(2,128)(2,1)} %param.19) | copy-start | bytes 18436
  15.4 50.1 %copy-start.3 = (bf16[2,2,768]{2,1,0:T(2,128)(2,1)S(1)}, bf16[2,2,768]{2,1,0:T(2,128)(2,1)}, u32[]{:S(2)}) copy-start(bf16[2,2,768]{2,1,0:T(2,128)(2,1)} %param.20) | copy-start | bytes 18436
  64.6 4.6 %copy-start.4 = (s32[2]{0:T(128)S(1)}, s32[2]{0:T(128)}, u32[]{:S(2)}) copy-start(s32[2]{0:T(128)} %param.29) | copy-start | bytes 28
  64.6 5.8 %copy-start = (bf16[2,768]{1,0:T(2,128)(2,1)S(1)}, bf16[2,768]{1,0:T(2,128)(2,1)}, u32[]{:S(2)}) copy-start(bf16[2,768]{1,0:T(2,128)(2,1)} %param.28) | copy-start | bytes 9220
  64.6 5.8 %copy-start.1 = (bf16[2,768]{1,0:T(2,128)(2,1)S(1)}, bf16[2,768]{1,0:T(2,128)(2,1)}, u32[]{:S(2)}) copy-start(bf16[2,768]{1,0:T(2,128)(2,1)} %param.24) | copy-start | bytes 9220
Sparse Core Ops, SparseCore 0:
  11.5 63.6 all-gather.4
  78.6 56.1 all-gather.6
